TPU v7x, 32 devices: a whole 2x2x4 slice. The times are simulated.
32 devices in a mesh: tile: 16 (over z, y, x), mode: 2 (over core).
Axes of the slice: x: 2, y: 2, z: 4, core: 2. Of those that a mesh axis runs over, the one named last changes fastest.
Arguments:
- object_field: float32 [2, 4096, 512], P(None, 'tile'), may hold values from -4.2 to 4.2
- probe: float32 [2, 2, 256, 256], P('mode'), may hold values from -2.1 to 2.1
- positions: int32 [2, 32, 2], P(None, 'tile'), may hold values from 0 to 3840, as said below
- measured: float32 [2, 32, 256, 256], P(None, 'tile'), may hold values from 0.1 to 30
Outputs:
- refined_object: float32 [2, 4096, 512], P(None, 'tile')
- refined_probe: float32 [2, 2, 256, 256], P('mode')
Inputs may be any that keep to these rules, and one draw needn't show every extreme that they name: positions[b, j] = (row, column). Position j belongs to tile t = j // 2; its row lies from t * 256 - 256 / 2 to t * 256 - 256 / 2 + 256, both ends reached in some tile, and every pattern lies inside the object of 4096 x 512.
All inputs are finite; a program needn't handle non-finite values.
Results may differ from a plain program's by a relative error of at most 0.0001.
Values sent between devices are 32-bit elements; how exact they have to be, the bound alone decides.
No kernel may reach another device: no remote copies, remote signals or barrier semaphores. Data moves between devices by JAX's collectives and lax.ppermute only.
A program may use at most 64 MiB of HBM per device.

v0:
```python
import functools
import math

import jax
import jax.numpy as jnp
import numpy as np
from jax import lax
from jax.experimental import pallas as pl
from jax.experimental.pallas import tpu as pltpu
from jax.sharding import PartitionSpec as P

F32 = jnp.float32
BF16 = jnp.bfloat16
VMEM_BYTES = 16 * 1024 * 1024
GROUP = 4


def padded(block, sides, width):
    for axis, dim in sides:
        count = lax.axis_size(axis)
        forward = [(i, i + 1) for i in range(count - 1)]
        backward = [(target, source) for source, target in forward]
        low = lax.ppermute(
            lax.slice_in_dim(block, block.shape[dim] - width, None, axis=dim), axis, forward
        )
        high = lax.ppermute(lax.slice_in_dim(block, 0, width, axis=dim), axis, backward)
        block = jnp.concatenate([low, block, high], axis=dim)
    return block


def tables(length):
    index_values = jnp.arange(length, dtype=jnp.int32)
    product = index_values[:, None] * index_values[None, :] % length
    angles = product.astype(jnp.float32) * (2.0 * math.pi / length)
    scaling = 1.0 / math.sqrt(length)
    return (jnp.cos(angles) * scaling, jnp.sin(angles) * scaling)


def apply_left(matrix, target):
    return jnp.einsum("ab,pbc->pac", matrix, target, precision=lax.Precision.HIGHEST)


def apply_right(target, matrix):
    return jnp.einsum("pab,bc->pac", target, matrix, precision=lax.Precision.HIGHEST)


def transform(real_part, imag_part, cosine, sine_table, direction):
    left_real = apply_left(cosine, real_part) + direction * apply_left(sine_table, imag_part)
    left_imag = apply_left(cosine, imag_part) - direction * apply_left(sine_table, real_part)
    out_real = apply_right(left_real, cosine) + direction * apply_right(left_imag, sine_table)
    out_imag = apply_right(left_imag, cosine) - direction * apply_right(left_real, sine_table)
    return (out_real, out_imag)


def place_add(target, placed, row_start, col_start):
    zero_index = jnp.int32(0)
    current = lax.dynamic_slice(target, (zero_index, row_start, col_start), placed.shape)
    return lax.dynamic_update_slice(target, current + placed, (zero_index, row_start, col_start))


def shards_by_mode(object_field, probe, positions, measured):
    strip_rows = object_field.shape[1]
    object_width = object_field.shape[2]
    pattern = probe.shape[2]
    half_pattern = pattern // 2
    count = positions.shape[1]
    cosine, sine_table = tables(pattern)
    tile_index = lax.axis_index("tile")
    offset = tile_index * strip_rows - half_pattern
    for minibatch in range(measured.shape[0]):
        extended = padded(object_field, (("tile", 1),), half_pattern)
        row_offsets = positions[minibatch, :, 0] - offset
        column_offsets = positions[minibatch, :, 1]

        def cut_one(row_start, col_start):
            return lax.dynamic_slice(
                extended, (jnp.int32(0), row_start, col_start), (2, pattern, pattern)
            )

        patches = jax.vmap(cut_one)(row_offsets, column_offsets)
        obj_real = patches[:, 0]
        obj_imag = patches[:, 1]
        probe_real = probe[0, 0]
        probe_imag = probe[0, 1]
        exit_real = probe_real * obj_real - probe_imag * obj_imag
        exit_imag = probe_real * obj_imag + probe_imag * obj_real
        far_real, far_imag = transform(exit_real, exit_imag, cosine, sine_table, 1.0)
        observed = measured[minibatch]
        intensity = lax.psum(far_real * far_real + far_imag * far_imag, "mode")
        modulus = jnp.sqrt((observed + 1.0) / (intensity + 1.0)) - 1.0
        chi_real, chi_imag = transform(
            modulus * far_real, modulus * far_imag, cosine, sine_table, -1.0
        )
        grad_real = probe_real * chi_real + probe_imag * chi_imag
        grad_imag = probe_real * chi_imag - probe_imag * chi_real
        probe_power = probe_real * probe_real + probe_imag * probe_imag
        step_real = jnp.sum(obj_real * chi_real + obj_imag * chi_imag, axis=0)
        step_imag = jnp.sum(obj_real * chi_imag - obj_imag * chi_real, axis=0)
        coverage = jnp.sum(obj_real * obj_real + obj_imag * obj_imag, axis=0)
        accumulated = jnp.zeros((3, strip_rows + pattern, object_width), jnp.float32)
        for position in range(count):
            placed = jnp.stack([grad_real[position], grad_imag[position], probe_power])
            accumulated = place_add(
                accumulated, placed, row_offsets[position], column_offsets[position]
            )
        rim_rows = jnp.concatenate(
            [accumulated[:, :half_pattern], accumulated[:, strip_rows + half_pattern :]], axis=1
        )
        received = padded(rim_rows, (("tile", 1),), half_pattern)
        own_strip = accumulated[:, half_pattern : half_pattern + strip_rows]
        own_strip = own_strip.at[:, :half_pattern].add(received[:, :half_pattern])
        own_strip = own_strip.at[:, strip_rows - half_pattern :].add(
            received[:, pattern + half_pattern :]
        )
        summed = lax.psum(own_strip, "mode")
        divisor = summed[2] + 1.0
        object_field = jnp.stack(
            [object_field[0] + summed[0] / divisor, object_field[1] + summed[1] / divisor]
        )
        step_stack = jnp.stack([jnp.stack([step_real, step_imag])])
        step_total, coverage_total = lax.psum((step_stack, coverage), "tile")
        probe = probe + step_total / (coverage_total + 1.0)
    return (object_field, probe)


def table_of(length):
    index_values = np.arange(length)
    angles = (index_values[:, None] * index_values[None, :] % length) * (2.0 * np.pi / length)
    scaling = 1.0 / np.sqrt(length)
    return np.stack([np.cos(angles) * scaling, np.sin(angles) * scaling]).astype(np.float32)


def spot(info, size, minibatch, side, slot):
    tiles, strip, pattern = size
    place = (((side + 1) * 2 + minibatch) * 2 + slot) * 2
    tile = info[24]
    row = info[place] - tile * strip + pattern // 2
    if side < 0:
        row = jnp.where(tile == 0, -pattern, row)
    if side > 0:
        row = jnp.where(tile == tiles - 1, strip + pattern, row)
    return row, info[place + 1]


def take_columns(block, column, width):
    total = block.shape[-1]
    return pltpu.roll(block, lax.rem(total - column, total), 1)[:, :width]


def add_at(tall, block, row, column):
    rows, width = block.shape
    total = tall.shape[1]
    shift = lax.rem(row, 8)
    start = pl.multiple_of(row - shift, 8)
    turned = pltpu.roll(block.reshape(rows // 8, 8, width), shift, 1)
    empty = jnp.zeros((1, 8, width), block.dtype)
    inside = lax.broadcasted_iota(jnp.int32, (rows // 8 + 1, 8, width), 1) >= shift
    moved = jnp.where(
        inside,
        jnp.concatenate([turned, empty], axis=0),
        jnp.concatenate([empty, turned], axis=0),
    ).reshape(rows + 8, width)
    wide = jnp.concatenate([moved, jnp.zeros((rows + 8, total - width), block.dtype)], axis=1)
    tall[pl.ds(start, rows + 8), :] += pltpu.roll(wide, column, 1)


def rows_at(ref, row, rows):
    width = ref.shape[1]
    shift = lax.rem(row, 8)
    start = pl.multiple_of(row - shift, 8)
    block = ref[pl.ds(start, rows + 8), :].reshape(rows // 8 + 1, 8, width)
    turned = pltpu.roll(block, lax.rem(8 - shift, 8), 1)
    inside = lax.broadcasted_iota(jnp.int32, (rows // 8, 8, width), 1) < 8 - shift
    return jnp.where(inside, turned[:-1], turned[1:]).reshape(rows, width)


def halves(value):
    high = value.astype(BF16)
    return high, (value - high.astype(F32)).astype(BF16)


def product(left, right):
    dot = functools.partial(jnp.dot, preferred_element_type=F32)
    return dot(left[0], right[0]) + (dot(left[0], right[1]) + dot(left[1], right[0]))


def cut_patch(size, info, minibatch, strip_ref, below, above, window, part):
    tiles, rows, width = size
    half = width // 2
    row, column = spot(info, size, minibatch, 0, info[25])

    def columns(block):
        return block if block.shape[1] == width else take_columns(block, column, width)

    window[:half] = columns(below)
    window[half : half + rows] = columns(strip_ref[part])
    window[half + rows : rows + width] = columns(above)
    return rows_at(window, row, width)


def illumination_kernel(size, minibatch, info, own, other, out, tall):
    tiles, strip, pattern = size
    half = pattern // 2
    kept = slice(pattern + half, pattern + half + strip)
    tall[kept] = jnp.zeros((strip, tall.shape[1]), F32)
    (pr0, pi0), (pr1, pi1) = ((ref[0], ref[1]) for ref in (own, other))
    power = pr0 * pr0 + pi0 * pi0 + (pr1 * pr1 + pi1 * pi1)
    for side in (-1, 0, 1):
        for slot in range(2):
            row, column = spot(info, size, minibatch, side, slot)
            add_at(tall, power, row + pattern, column)
    out[...] = tall[kept]


def ready_kernel(info, probe, measured, table, own, observed, split):
    own[...] = probe[...]
    for minibatch in range(2):
        observed[minibatch] = measured[minibatch, info[25]]
    for i in range(2):
        split[2 * i], split[2 * i + 1] = halves(table[i])


def field_kernel(size, minibatch, info, strip_ref, *refs):
    tiles, strip, pattern = size
    slot = info[25]
    count = 2 if minibatch else 4
    edges, (own, other, measured, table) = refs[:count], refs[count : count + 4]
    gradient, step_own, step_other, window = refs[count + 4 :]

    def edge(side, part):
        if len(edges) == 2:
            return edges[side][part]
        return jnp.where(slot == part, edges[2 * side][...], edges[2 * side + 1][...])

    obj_real, obj_imag = (
        cut_patch(size, info, minibatch, strip_ref, edge(0, part), edge(1, part), window, part)
        for part in range(2)
    )
    cos_high, cos_low, sin_high, sin_low = (table[i] for i in range(4))

    def block(top_left, top_right, low_left, low_right):
        return jnp.concatenate(
            [
                jnp.concatenate([top_left, top_right], axis=1),
                jnp.concatenate([low_left, low_right], axis=1),
            ],
            axis=0,
        )

    first = (
        block(cos_high, sin_high, -sin_high, cos_high),
        block(cos_low, sin_low, -sin_low, cos_low),
    )
    second = (
        block(cos_high, -sin_high, sin_high, cos_high),
        block(cos_low, -sin_low, sin_low, cos_low),
    )
    probes = [(ref[0], ref[1]) for ref in (own, other)]

    def both(fields, left, right):
        (r0, i0), (r1, i1) = fields
        y = product(left, halves(block(r0, r1, i0, i1)))
        y = block(
            y[:pattern, :pattern], y[pattern:, :pattern], y[:pattern, pattern:], y[pattern:, pattern:]
        )
        y = product(halves(y), right)
        return (
            (y[:pattern, :pattern], y[:pattern, pattern:]),
            (y[pattern:, :pattern], y[pattern:, pattern:]),
        )

    exits = [(pr * obj_real - pi * obj_imag, pr * obj_imag + pi * obj_real) for pr, pi in probes]
    far = both(exits, first, second)
    intensity = (far[0][0] * far[0][0] + far[0][1] * far[0][1]) + (
        far[1][0] * far[1][0] + far[1][1] * far[1][1]
    )
    factor = jnp.sqrt((measured[minibatch] + 1.0) / (intensity + 1.0)) - 1.0
    chi = both([(factor * fr, factor * fi) for fr, fi in far], second, first)
    (pr0, pi0), (pr1, pi1) = probes
    (cr0, ci0), (cr1, ci1) = chi
    gradient[0] = (pr0 * cr0 + pi0 * ci0) + (pr1 * cr1 + pi1 * ci1)
    gradient[1] = (pr0 * ci0 - pi0 * cr0) + (pr1 * ci1 - pi1 * cr1)
    coverage = obj_real * obj_real + obj_imag * obj_imag
    rows = pattern // GROUP
    mate = lax.rem(info[24], GROUP)
    for step, keeper, (cr, ci) in ((step_own, slot, chi[0]), (step_other, 1 - slot, chi[1])):
        real = obj_real * cr + obj_imag * ci
        imag = obj_real * ci - obj_imag * cr
        for k in range(GROUP):
            start = k * rows
            block = step.at[mate ^ k]
            block[:rows] = real[start : start + rows]
            block[rows : 2 * rows] = imag[start : start + rows]
            middle = start + rows // 2
            block[2 * rows :] = jnp.where(
                keeper == 0, coverage[start:middle], coverage[middle : start + rows]
            )


def update_kernel(size, minibatch, info, strip_ref, illum, own, other, b0, a0, b1, a1, *outs):
    strip_out, *edges, tall = outs
    tiles, strip, pattern = size
    half = pattern // 2
    slot = info[25]
    kept = slice(pattern + half, pattern + half + strip)
    grads = (
        (0, slot, own, 0),
        (0, 1 - slot, other, 0),
        (-1, slot, b0, half),
        (1, slot, a0, 0),
        (-1, 1 - slot, b1, half),
        (1, 1 - slot, a1, 0),
    )
    for part in range(2):
        tall[kept] = jnp.zeros((strip, tall.shape[1]), F32)
        for side, place, ref, start in grads:
            row, column = spot(info, size, minibatch, side, place)
            add_at(tall, ref[part], row + pattern + start, column)
        fresh = strip_ref[part] + tall[kept] / (illum[...] + 1.0)
        strip_out[part] = fresh
        if edges:
            column_below = spot(info, size, minibatch + 1, -1, slot)[1]
            column_above = spot(info, size, minibatch + 1, 1, slot)[1]
            edges[0][part] = take_columns(fresh[:half], column_below, pattern)
            edges[1][part] = take_columns(fresh[strip - half :], column_above, pattern)


def probe_kernel(info, own_totals, other_totals, *refs):
    probes, outs = refs[: len(refs) // 2], refs[len(refs) // 2 :]
    slot = info[25]
    rows = outs[0].shape[1] // GROUP
    mate = lax.rem(info[24], GROUP)
    for k in range(GROUP):
        where = pl.ds(pl.multiple_of((mate ^ k) * rows, rows), rows)
        mine, theirs = own_totals[k], other_totals[k]
        own_half, other_half = mine[2 * rows :], theirs[theirs.shape[0] - rows // 2 :]
        coverage = jnp.concatenate(
            [
                jnp.where(slot == 0, own_half, other_half),
                jnp.where(slot == 0, other_half, own_half),
            ],
            axis=0,
        )
        divisor = coverage + 1.0
        for totals, probe, out in zip((mine, theirs), probes, outs):
            for part in range(2):
                change = totals[part * rows : (part + 1) * rows] / divisor
                out[part, where, :] = probe[part, where, :] + change


def call(kernel, name, outs, inputs, scratch=(), flops=0):
    shapes = [
        shape if isinstance(shape, jax.ShapeDtypeStruct) else jax.ShapeDtypeStruct(shape, F32)
        for shape in outs
    ]
    size = sum(value.size * value.dtype.itemsize for value in (*shapes, *inputs))
    smem = pl.BlockSpec(memory_space=pltpu.SMEM)
    vmem = pl.BlockSpec(memory_space=pltpu.VMEM)
    return pl.pallas_call(
        kernel,
        out_shape=shapes,
        in_specs=[smem] + [vmem] * (len(inputs) - 1),
        out_specs=[vmem] * len(shapes),
        scratch_shapes=[pltpu.VMEM(shape, F32) for shape in scratch],
        compiler_params=pltpu.CompilerParams(vmem_limit_bytes=VMEM_BYTES),
        cost_estimate=pl.CostEstimate(flops=flops, bytes_accessed=size, transcendentals=0),
        name=name,
    )(*inputs)


def shards_by_position(object_field, probe, positions, measured):
    strip = object_field.shape[1]
    width = object_field.shape[2]
    pattern = probe.shape[2]
    half = pattern // 2
    tiles = lax.axis_size("tile")
    size = (tiles, strip, pattern)
    field = (2, pattern, pattern)
    tall = (3 * pattern + strip + 8, width)
    window = (pattern + strip + 8, pattern)
    up = [(i, i + 1) for i in range(tiles - 1)]
    down = [(i + 1, i) for i in range(tiles - 1)]

    def swap(value):
        return lax.ppermute(value, "mode", [(0, 1), (1, 0)])

    def across(value, k):
        return lax.ppermute(value, "tile", [(i, i ^ k) for i in range(tiles)])

    def scatter(blocks, unit):
        mates = [across(blocks[k], unit * k) for k in range(1, GROUP)]
        return functools.reduce(jnp.add, mates, blocks[0])

    def exchange(piece, unit):
        piece = piece + across(piece, unit)
        return piece + across(piece, 2 * unit)

    def gather(piece, unit):
        return jnp.stack([piece] + [across(piece, unit * k) for k in range(1, GROUP)])

    def from_below(value):
        return lax.ppermute(value, "tile", up)

    def from_above(value):
        return lax.ppermute(value, "tile", down)

    def bind(kernel, *args):
        return functools.partial(kernel, *args)

    tile, slot = lax.axis_index("tile"), lax.axis_index("mode")
    index = jnp.stack([tile, slot]).astype(jnp.int32)
    here = jnp.concatenate([positions.ravel()] * 3 + [index])
    one_part = lax.dynamic_index_in_dim(object_field, slot, 0, keepdims=False)
    edges = [from_below(one_part[strip - half :]), from_above(one_part[:half])]
    below, above = from_below(positions), from_above(positions)
    other = swap(probe[0])
    own, observed, table = call(
        ready_kernel,
        "ready",
        [field, field, jax.ShapeDtypeStruct((4, pattern, pattern), BF16)],
        (here, probe[0], measured, jnp.asarray(table_of(pattern))),
    )
    *edges, below, above, own, observed, table = lax.optimization_barrier(
        (*edges, below, above, own, observed, table)
    )
    edges = [edges[0], swap(edges[0]), edges[1], swap(edges[1])]
    info = jnp.concatenate([below.ravel(), positions.ravel(), above.ravel(), index])

    for minibatch in range(2):
        last = minibatch == 1
        rows = pattern // GROUP
        blocks = (GROUP, 2 * rows + rows // 2, pattern)
        gradient, step_own, step_other = call(
            bind(field_kernel, size, minibatch),
            "field",
            [field, blocks, blocks],
            (here, object_field, *edges, own, other, observed, table),
            [window],
            flops=2 * 12 * 512**3,
        )
        (illum,) = call(
            bind(illumination_kernel, size, minibatch),
            "illumination",
            [(strip, width)],
            (info, own, other),
            [tall],
        )
        steps = step_own + swap(step_other)
        piece = scatter(steps, 1)
        if last:
            gradient, piece, illum = lax.optimization_barrier((gradient, piece, illum))
        rim_below, rim_above = from_below(gradient[:, half:]), from_above(gradient[:, :half])
        if not last:
            gradient, rim_below, rim_above, piece, illum = lax.optimization_barrier(
                (gradient, rim_below, rim_above, piece, illum)
            )
        rims = (gradient, swap(gradient), rim_below, rim_above, swap(rim_below), swap(rim_above))
        object_field, *edges = call(
            bind(update_kernel, size, minibatch),
            "update",
            [object_field.shape] + ([] if last else [(2, half, pattern)] * 2),
            (info, object_field, illum, *rims),
            [tall],
        )
        piece = exchange(piece, GROUP)
        if not last:
            edges = [from_below(edges[1]), from_above(edges[0])]
            piece, *edges = lax.optimization_barrier((piece, *edges))
        totals = gather(piece, 1)
        if last:
            totals, object_field = lax.optimization_barrier((totals, object_field))
            others = swap(totals[:, 2 * rows :])
            (own,) = call(probe_kernel, "probe", [field], (here, totals, others, own))
        else:
            own, other = call(
                probe_kernel, "probe", [field] * 2, (here, totals, swap(totals), own, other)
            )
    return (object_field, own[None])


def solution(mesh):
    in_specs = (
        P(None, "tile", None),
        P("mode", None, None, None),
        P(None, "tile", None),
        P(None, "tile", None, None),
    )
    out_specs = (P(None, "tile", None), P("mode", None, None, None))

    def whole(object_field, probe, positions, measured):
        tiles, pair = mesh.shape["tile"], mesh.shape["mode"]
        by_position = (
            pair == 2
            and probe.shape[0] == 2
            and positions.shape[:2] == (2, 2 * tiles)
            and tiles == GROUP * GROUP
            and probe.shape[2] % (16 * 2 * GROUP) == 0
            and object_field.shape[1] == tiles * probe.shape[2]
        )
        shards = shards_by_position if by_position else shards_by_mode
        return jax.shard_map(
            shards, mesh=mesh, in_specs=in_specs, out_specs=out_specs, check_vma=False
        )(object_field, probe, positions, measured)

    return whole
```

profile of v0, /device:TPU:0, one launch (start us, length us, event | category | flops | bytes accessed | tf_op | source)
XLA Modules:
  0.0 145.5 jit_solution(1488693497900867466)
XLA Ops:
  0.6 2.0 %dynamic-slice_bitcast_fusion = (f32[128,512]{1,0:T(8,128)}, f32[128,512]{1,0:T(8,128)}) fusion(f32[2,256,512]{2,1,0:T(8,128)} %strip_ref.3, s32[]{:T(128)S(6)} %select_n.4, s32[]{:T(128)S(6)} %add.53), kind=kLoop, calls=%fused_computation.2 | loop fusion | bytes 1048584 | tf_op jit(solution)/shard_map/slice | solution.py:414
  2.6 1.4 collective-permute-start.1
  4.0 6.2 %collective-permute-start = (f32[128,512]{1,0:T(8,128)}, f32[128,512]{1,0:T(8,128)}, u32[]{:S(2)}, u32[]{:S(2)}) collective-permute-start(f32[128,512]{1,0:T(8,128)} %get-tuple-element.71), channel_id=1, source_target_pairs={{0,2},{2,4},{4,6},{6,8},{8,10},{10,12},{12,14},{14,16},{16,18},{18... | collective-permute-start | bytes 786440 | tf_op jit(solution)/shard_map/ppermute | solution.py:402
  10.2 1.3 collective-permute-start.3
  11.5 4.8 %collective-permute-start.2 = (s32[2,2,2]{2,1,0:T(2,128)S(1)}, s32[2,2,2]{2,1,0:T(2,128)S(1)}, u32[]{:S(2)}, u32[]{:S(2)}) collective-permute-start(s32[2,2,2]{2,1,0:T(2,128)S(1)} %copy-done.9), channel_id=1, source_target_pairs={{0,2},{2,4},{4,6},{6,8},{8,10},{10,12},{12,14},{14,16},{16,18},{18... | collective-permute-start | bytes 104 | tf_op jit(solution)/shard_map/ppermute | solution.py:402
  16.5 1.0 copy-done.2
  17.6 1.0 copy-done.3
  19.7 1.2 collective-permute-done.2
  21.5 1.2 collective-permute-done.4.refs_1_
  22.9 5.7 %field.2 = (f32[2,256,256]{2,1,0:T(8,128)S(1)}, f32[4,160,256]{2,1,0:T(8,128)S(1)}, f32[4,160,256]{2,1,0:T(8,128)S(1)}) custom-call(s32[26]{0:T(128)S(1)} %concatenate.8.info, f32[2,256,512]{2,1,0:T(8,128)S(1)} %copy-done, f32[128,512]{1,0:T(8,128)} %collective-permute-done.refs_0_, f32[128,512]{1,0:T(8,128)S(1)} %collective-permute-done.4.refs_1_, ...), custom_call_target="tpu_custom_call" | custom-call | flops 3221225472 | bytes 6029416 | tf_op jit(solution)/shard_map/field/pallas_call | solution.py:359
  28.8 2.0 %collective-permute-done.9 = f32[4,160,256]{2,1,0:T(8,128)S(1)} collective-permute-done((f32[4,160,256]{2,1,0:T(8,128)S(1)}, f32[4,160,256]{2,1,0:T(8,128)S(1)}, u32[]{:S(2)}, u32[]{:S(2)}) %collective-permute-start.9) | collective-permute-done | bytes 655392 | tf_op jit(solution)/shard_map/ppermute | solution.py:385
  31.7 2.5 %collective-permute-start.10 = (f32[160,256]{1,0:T(8,128)}, f32[160,256]{1,0:T(8,128)}, u32[]{:S(2)}, u32[]{:S(2)}) collective-permute-start(f32[160,256]{1,0:T(8,128)} %get-tuple-element.75), channel_id=1, source_target_pairs={{0,2},{2,0},{4,6},{6,4},{8,10},{10,8},{12,14},{14,12},{16,18},{18,... | collective-permute-start | bytes 491528 | tf_op jit(solution)/shard_map/ppermute | solution.py:388
  34.2 1.6 %collective-permute-start.12 = (f32[160,256]{1,0:T(8,128)}, f32[160,256]{1,0:T(8,128)}, u32[]{:S(2)}, u32[]{:S(2)}) collective-permute-start(f32[160,256]{1,0:T(8,128)} %get-tuple-element.76), channel_id=1, source_target_pairs={{0,6},{2,4},{4,2},{6,0},{8,14},{10,12},{12,10},{14,8},{16,22},{18,... | collective-permute-start | bytes 491528 | tf_op jit(solution)/shard_map/ppermute | solution.py:388
  37.2 1.3 collective-permute-start.8
  38.4 4.6 %collective-permute-start.7 = (f32[2,128,256]{2,1,0:T(8,128)S(1)}, f32[2,128,256]{2,1,0:T(8,128)S(1)}, u32[]{:S(2)}, u32[]{:S(2)}) collective-permute-start(f32[2,128,256]{2,1,0:T(8,128)S(1)} %get-tuple-element.81), channel_id=1, source_target_pairs={{0,2},{2,4},{4,6},{6,8},{8,10},{10,12},{12,14},{14,16},{16,18},{18... | collective-permute-start | bytes 786440 | tf_op jit(solution)/shard_map/ppermute | solution.py:402
  43.3 1.7 %illumination.2.illum = f32[256,512]{1,0:T(8,128)S(1)} custom-call(s32[26]{0:T(128)S(1)} %concatenate.9.info, f32[2,256,256]{2,1,0:T(8,128)S(1)} %get-tuple-element.43.refs_4_.own.refs_0_, f32[2,256,256]{2,1,0:T(8,128)S(1)} %collective-permute-done.6.refs_5_.other.refs_1_), custom_call_target="tpu_custom_call" | custom-call | bytes 1572968 | tf_op jit(solution)/shard_map/illumination/pallas_call | solution.py:359
  45.6 1.2 fusion.5
  46.8 2.0 %collective-permute-done.8.a0 = f32[2,128,256]{2,1,0:T(8,128)S(1)} collective-permute-done((f32[2,128,256]{2,1,0:T(8,128)}, f32[2,128,256]{2,1,0:T(8,128)S(1)}, u32[]{:S(2)}, u32[]{:S(2)}) %collective-permute-start.8) | collective-permute-done | bytes 262176 | tf_op jit(solution)/shard_map/ppermute | solution.py:405
  48.8 4.9 %collective-permute-done.7.b0 = f32[2,128,256]{2,1,0:T(8,128)S(1)} collective-permute-done((f32[2,128,256]{2,1,0:T(8,128)S(1)}, f32[2,128,256]{2,1,0:T(8,128)S(1)}, u32[]{:S(2)}, u32[]{:S(2)}) %collective-permute-start.7) | collective-permute-done | bytes 262176 | tf_op jit(solution)/shard_map/ppermute | solution.py:402
  54.1 1.7 %collective-permute-start.16 = (f32[160,256]{1,0:T(8,128)S(1)}, f32[160,256]{1,0:T(8,128)S(1)}, u32[]{:S(2)}, u32[]{:S(2)}) collective-permute-start(f32[160,256]{1,0:T(8,128)S(1)} %fusion.5), channel_id=1, source_target_pairs={{0,8},{2,10},{4,12},{6,14},{8,0},{10,2},{12,4},{14,6},{16,24},{18,... | collective-permute-start | bytes 491528 | tf_op jit(solution)/shard_map/ppermute | solution.py:388
  56.3 2.3 %update.2 = (f32[2,256,512]{2,1,0:T(8,128)S(1)}, f32[2,128,256]{2,1,0:T(8,128)S(1)}, f32[2,128,256]{2,1,0:T(8,128)S(1)}) custom-call(s32[26]{0:T(128)S(1)} %concatenate.9.info, f32[2,256,512]{2,1,0:T(8,128)S(1)} %copy-done, f32[256,512]{1,0:T(8,128)S(1)} %illumination.2.illum, f32[2,256,256]{2,1,0:T(8,128)S(1)} %get-tuple-element.50.own, ...), custom_call_target="tpu_custom_call" | custom-call | bytes 5242984 | tf_op jit(solution)/shard_map/update/pallas_call | solution.py:359
  58.6 4.4 %collective-permute-start.18 = (f32[2,128,256]{2,1,0:T(8,128)S(1)}, f32[2,128,256]{2,1,0:T(8,128)S(1)}, u32[]{:S(2)}, u32[]{:S(2)}) collective-permute-start(f32[2,128,256]{2,1,0:T(8,128)S(1)} %get-tuple-element.55), channel_id=1, source_target_pairs={{0,2},{2,4},{4,6},{6,8},{8,10},{10,12},{12,14},{14,16},{16,18},{18... | collective-permute-start | bytes 786440 | tf_op jit(solution)/shard_map/ppermute | solution.py:402
  63.1 1.5 %collective-permute-start.19 = (f32[2,128,256]{2,1,0:T(8,128)S(1)}, f32[2,128,256]{2,1,0:T(8,128)S(1)}, u32[]{:S(2)}, u32[]{:S(2)}) collective-permute-start(f32[2,128,256]{2,1,0:T(8,128)S(1)} %get-tuple-element.56), channel_id=1, source_target_pairs={{2,0},{4,2},{6,4},{8,6},{10,8},{12,10},{14,12},{16,14},{18,16},{20... | collective-permute-start | bytes 786440 | tf_op jit(solution)/shard_map/ppermute | solution.py:405
  64.6 4.7 %collective-permute-start.17 = (f32[160,256]{1,0:T(8,128)S(1)}, f32[160,256]{1,0:T(8,128)S(1)}, u32[]{:S(2)}, u32[]{:S(2)}) collective-permute-start(f32[160,256]{1,0:T(8,128)S(1)} %add.45), channel_id=1, source_target_pairs={{0,16},{2,18},{4,20},{6,22},{8,24},{10,26},{12,28},{14,30},{16,0},... | collective-permute-start | bytes 491528 | tf_op jit(solution)/shard_map/ppermute | solution.py:388
  69.3 12.8 %collective-permute-done.17 = f32[160,256]{1,0:T(8,128)S(1)} collective-permute-done((f32[160,256]{1,0:T(8,128)S(1)}, f32[160,256]{1,0:T(8,128)S(1)}, u32[]{:S(2)}, u32[]{:S(2)}) %collective-permute-start.17) | collective-permute-done | bytes 163872 | tf_op jit(solution)/shard_map/ppermute | solution.py:388
  82.3 3.4 %collective-permute-start.20 = (f32[160,256]{1,0:T(8,128)S(1)}, f32[160,256]{1,0:T(8,128)S(1)}, u32[]{:S(2)}, u32[]{:S(2)}) collective-permute-start(f32[160,256]{1,0:T(8,128)S(1)} %add.46), channel_id=1, source_target_pairs={{0,2},{2,0},{4,6},{6,4},{8,10},{10,8},{12,14},{14,12},{16,18},{18,... | collective-permute-start | bytes 491528 | tf_op jit(solution)/shard_map/ppermute | solution.py:388
  85.7 4.4 %collective-permute-done.22 = f32[160,256]{1,0:T(8,128)S(1)} collective-permute-done((f32[160,256]{1,0:T(8,128)S(1)}, f32[160,256]{1,0:T(8,128)S(1)}, u32[]{:S(2)}, u32[]{:S(2)}) %collective-permute-start.22) | collective-permute-done | bytes 163872 | tf_op jit(solution)/shard_map/ppermute | solution.py:388
  90.0 0.9 collective-permute-done.21
  91.1 2.1 %collective-permute-done.23.other_totals = f32[4,160,256]{2,1,0:T(8,128)S(1)} collective-permute-done((f32[4,160,256]{2,1,0:T(8,128)S(1)}, f32[4,160,256]{2,1,0:T(8,128)S(1)}, u32[]{:S(2)}, u32[]{:S(2)}) %collective-permute-start.23) | collective-permute-done | bytes 655392 | tf_op jit(solution)/shard_map/ppermute | solution.py:385
  93.9 5.0 %field.3 = (f32[2,256,256]{2,1,0:T(8,128)S(1)}, f32[4,160,256]{2,1,0:T(8,128)S(1)}, f32[4,160,256]{2,1,0:T(8,128)S(1)}) custom-call(s32[26]{0:T(128)S(1)} %concatenate.8.info, f32[2,256,512]{2,1,0:T(8,128)S(1)} %get-tuple-element.53.strip_ref, f32[2,128,256]{2,1,0:T(8,128)S(1)} %collective-permute-done.18.refs_0_, ...), custom_call_target="tpu_custom_call" | custom-call | flops 3221225472 | bytes 5505128 | tf_op jit(solution)/shard_map/field/pallas_call | solution.py:359
  99.0 2.0 %collective-permute-done.24 = f32[4,160,256]{2,1,0:T(8,128)S(1)} collective-permute-done((f32[4,160,256]{2,1,0:T(8,128)S(1)}, f32[4,160,256]{2,1,0:T(8,128)S(1)}, u32[]{:S(2)}, u32[]{:S(2)}) %collective-permute-start.24) | collective-permute-done | bytes 655392 | tf_op jit(solution)/shard_map/ppermute | solution.py:385
  101.4 2.7 %collective-permute-start.27 = (f32[160,256]{1,0:T(8,128)S(1)}, f32[160,256]{1,0:T(8,128)S(1)}, u32[]{:S(2)}, u32[]{:S(2)}) collective-permute-start(f32[160,256]{1,0:T(8,128)S(1)} %get-tuple-element.73), channel_id=1, source_target_pairs={{0,6},{2,4},{4,2},{6,0},{8,14},{10,12},{12,10},{14,8},{16,22},{18,... | collective-permute-start | bytes 491528 | tf_op jit(solution)/shard_map/ppermute | solution.py:388
  104.7 1.7 %illumination.3.illum = f32[256,512]{1,0:T(8,128)S(1)} custom-call(s32[26]{0:T(128)S(1)} %concatenate.9.info, f32[2,256,256]{2,1,0:T(8,128)S(1)} %get-tuple-element.60.refs_2_.own.refs_0_, f32[2,256,256]{2,1,0:T(8,128)S(1)} %get-tuple-element.61.refs_3_.other), custom_call_target="tpu_custom_call" | custom-call | bytes 1572968 | tf_op jit(solution)/shard_map/illumination/pallas_call | solution.py:359
  106.4 1.9 %collective-permute-done.25 = f32[160,256]{1,0:T(8,128)S(1)} collective-permute-done((f32[160,256]{1,0:T(8,128)S(1)}, f32[160,256]{1,0:T(8,128)S(1)}, u32[]{:S(2)}, u32[]{:S(2)}) %collective-permute-start.25) | collective-permute-done | bytes 163872 | tf_op jit(solution)/shard_map/ppermute | solution.py:388
  108.3 3.7 %collective-permute-done.27 = f32[160,256]{1,0:T(8,128)S(1)} collective-permute-done((f32[160,256]{1,0:T(8,128)S(1)}, f32[160,256]{1,0:T(8,128)S(1)}, u32[]{:S(2)}, u32[]{:S(2)}) %collective-permute-start.27) | collective-permute-done | bytes 163872 | tf_op jit(solution)/shard_map/ppermute | solution.py:388
  111.9 1.4 collective-permute-done.26
  113.4 5.3 %collective-permute-done.28 = f32[160,256]{1,0:T(8,128)S(1)} collective-permute-done((f32[160,256]{1,0:T(8,128)S(1)}, f32[160,256]{1,0:T(8,128)S(1)}, u32[]{:S(2)}, u32[]{:S(2)}) %collective-permute-start.28) | collective-permute-done | bytes 163872 | tf_op jit(solution)/shard_map/ppermute | solution.py:388
  118.9 1.3 collective-permute-start.35
  120.2 4.6 %collective-permute-start.34 = (f32[2,128,256]{2,1,0:T(8,128)S(1)}, f32[2,128,256]{2,1,0:T(8,128)S(1)}, u32[]{:S(2)}, u32[]{:S(2)}) collective-permute-start(f32[2,128,256]{2,1,0:T(8,128)S(1)} %get-tuple-element.79), channel_id=1, source_target_pairs={{0,2},{2,4},{4,6},{6,8},{8,10},{10,12},{12,14},{14,16},{16,18},{18... | collective-permute-start | bytes 786440 | tf_op jit(solution)/shard_map/ppermute | solution.py:402
  124.8 3.6 %collective-permute-done.29 = f32[160,256]{1,0:T(8,128)S(1)} collective-permute-done((f32[160,256]{1,0:T(8,128)S(1)}, f32[160,256]{1,0:T(8,128)S(1)}, u32[]{:S(2)}, u32[]{:S(2)}) %collective-permute-start.29) | collective-permute-done | bytes 163872 | tf_op jit(solution)/shard_map/ppermute | solution.py:388
  128.6 1.2 collective-permute-done.35.a0
  129.9 2.2 %collective-permute-start.30 = (f32[160,256]{1,0:T(8,128)S(1)}, f32[160,256]{1,0:T(8,128)S(1)}, u32[]{:S(2)}, u32[]{:S(2)}) collective-permute-start(f32[160,256]{1,0:T(8,128)S(1)} %add.52), channel_id=1, source_target_pairs={{0,2},{2,0},{4,6},{6,4},{8,10},{10,8},{12,14},{14,12},{16,18},{18,... | collective-permute-start | bytes 491528 | tf_op jit(solution)/shard_map/ppermute | solution.py:388
  132.0 1.5 %collective-permute-done.34.b0 = f32[2,128,256]{2,1,0:T(8,128)S(1)} collective-permute-done((f32[2,128,256]{2,1,0:T(8,128)S(1)}, f32[2,128,256]{2,1,0:T(8,128)S(1)}, u32[]{:S(2)}, u32[]{:S(2)}) %collective-permute-start.34) | collective-permute-done | bytes 262176 | tf_op jit(solution)/shard_map/ppermute | solution.py:402
  133.5 3.6 %collective-permute-done.32 = f32[160,256]{1,0:T(8,128)S(1)} collective-permute-done((f32[160,256]{1,0:T(8,128)S(1)}, f32[160,256]{1,0:T(8,128)S(1)}, u32[]{:S(2)}, u32[]{:S(2)}) %collective-permute-start.32) | collective-permute-done | bytes 163872 | tf_op jit(solution)/shard_map/ppermute | solution.py:388
  137.9 1.6 %collective-permute-done.30 = f32[160,256]{1,0:T(8,128)S(1)} collective-permute-done((f32[160,256]{1,0:T(8,128)S(1)}, f32[160,256]{1,0:T(8,128)S(1)}, u32[]{:S(2)}, u32[]{:S(2)}) %collective-permute-start.30) | collective-permute-done | bytes 163872 | tf_op jit(solution)/shard_map/ppermute | solution.py:388
  139.6 3.1 %update.3 = f32[2,256,512]{2,1,0:T(8,128)} custom-call(s32[26]{0:T(128)S(1)} %concatenate.9.info, f32[2,256,512]{2,1,0:T(8,128)S(1)} %get-tuple-element.53.strip_ref, f32[256,512]{1,0:T(8,128)S(1)} %illumination.3.illum, f32[2,256,256]{2,1,0:T(8,128)S(1)} %get-tuple-element.67.own, f32[2,256,256]{2,1,0:T(8,128)S(1)} %collective-permute-done.33.other, ...), custom_call_target="tpu_custom_call" | custom-call | bytes 4718696 | tf_op jit(solution)/shard_map/update/pallas_call | solution.py:359
  142.8 1.3 collective-permute-done.38.other_totals
  144.1 1.4 probe.3
  (80 shorter events, 10.0 us)
Async XLA Ops:
  0.6 15.9 %copy-start.1 = (f32[2,2,256,256]{3,2,1,0:T(8,128)S(1)}, f32[2,2,256,256]{3,2,1,0:T(8,128)}, u32[]{:S(2)}) copy-start(f32[2,2,256,256]{3,2,1,0:T(8,128)} %measured.1) | copy-start | bytes 3145732
  2.6 7.6 %copy-start.9 = (s32[2,2,2]{2,1,0:T(2,128)S(1)}, s32[2,2,2]{2,1,0:T(2,128)}, u32[]{:S(2)}) copy-start(s32[2,2,2]{2,1,0:T(2,128)} %param.7) | copy-start | bytes 100
  2.6 18.4 %collective-permute-start.1 = (f32[128,512]{1,0:T(8,128)}, f32[128,512]{1,0:T(8,128)S(1)}, u32[]{:S(2)}, u32[]{:S(2)}) collective-permute-start(f32[128,512]{1,0:T(8,128)} %get-tuple-element.70), channel_id=1, source_target_pairs={{2,0},{4,2},{6,4},{8,6},{10,8},{12,10},{14,12},{16,14},{18,16},{20... | collective-permute-start | bytes 786440 | tf_op jit(solution)/shard_map/ppermute | solution.py:405
  4.0 17.0 %collective-permute-start = (f32[128,512]{1,0:T(8,128)}, f32[128,512]{1,0:T(8,128)}, u32[]{:S(2)}, u32[]{:S(2)}) collective-permute-start(f32[128,512]{1,0:T(8,128)} %get-tuple-element.71), channel_id=1, source_target_pairs={{0,2},{2,4},{4,6},{6,8},{8,10},{10,12},{12,14},{14,16},{16,18},{18... | collective-permute-start | bytes 786440 | tf_op jit(solution)/shard_map/ppermute | solution.py:402
  10.2 11.3 %collective-permute-start.6 = (f32[2,256,256]{2,1,0:T(8,128)}, f32[2,256,256]{2,1,0:T(8,128)S(1)}, u32[]{:S(2)}, u32[]{:S(2)}) collective-permute-start(f32[2,256,256]{2,1,0:T(8,128)} %bitcast.44), channel_id=1, source_target_pairs={{0,1},{1,0},{2,3},{3,2},{4,5},{5,4},{6,7},{7,6},{8,9},{9,8},{10,11... | collective-permute-start | bytes 1572872 | tf_op jit(solution)/shard_map/ppermute | solution.py:385
  10.2 9.5 %collective-permute-start.3 = (s32[2,2,2]{2,1,0:T(2,128)S(1)}, s32[2,2,2]{2,1,0:T(2,128)S(1)}, u32[]{:S(2)}, u32[]{:S(2)}) collective-permute-start(s32[2,2,2]{2,1,0:T(2,128)S(1)} %copy-done.9), channel_id=1, source_target_pairs={{2,0},{4,2},{6,4},{8,6},{10,8},{12,10},{14,12},{16,14},{18,16},{20... | collective-permute-start | bytes 104 | tf_op jit(solution)/shard_map/ppermute | solution.py:405
  11.5 9.5 %collective-permute-start.2 = (s32[2,2,2]{2,1,0:T(2,128)S(1)}, s32[2,2,2]{2,1,0:T(2,128)S(1)}, u32[]{:S(2)}, u32[]{:S(2)}) collective-permute-start(s32[2,2,2]{2,1,0:T(2,128)S(1)} %copy-done.9), channel_id=1, source_target_pairs={{0,2},{2,4},{4,6},{6,8},{8,10},{10,12},{12,14},{14,16},{16,18},{18... | collective-permute-start | bytes 104 | tf_op jit(solution)/shard_map/ppermute | solution.py:402
  16.5 1.0 copy-start.2
  18.6 4.3 %copy-start = (f32[2,256,512]{2,1,0:T(8,128)S(1)}, f32[2,256,512]{2,1,0:T(8,128)}, u32[]{:S(2)}) copy-start(f32[2,256,512]{2,1,0:T(8,128)} %strip_ref.3) | copy-start | bytes 3145732
  19.3 9.3 %copy-start.4 = (f32[2,256,256]{2,1,0:T(8,128)}, f32[2,256,256]{2,1,0:T(8,128)S(1)}, u32[]{:S(2)}) copy-start(f32[2,256,256]{2,1,0:T(8,128)S(1)} %get-tuple-element.44.refs_6_.refs_4_) | copy-start | bytes 1572868
  19.3 9.3 %copy-start.6 = (bf16[4,256,256]{2,1,0:T(8,128)(2,1)}, bf16[4,256,256]{2,1,0:T(8,128)(2,1)S(1)}, u32[]{:S(2)}) copy-start(bf16[4,256,256]{2,1,0:T(8,128)(2,1)S(1)} %get-tuple-element.45.refs_7_.refs_5_) | copy-start | bytes 1572868
  21.0 1.7 %collective-permute-start.4 = (f32[128,512]{1,0:T(8,128)}, f32[128,512]{1,0:T(8,128)S(1)}, u32[]{:S(2)}, u32[]{:S(2)}) collective-permute-start(f32[128,512]{1,0:T(8,128)} %collective-permute-done.refs_0_), channel_id=1, source_target_pairs={{0,1},{1,0},{2,3},{3,2},{4,5},{5,4},{6,7},{7,6},{8,9},{9,8},{10,11... | collective-permute-start | bytes 786440 | tf_op jit(solution)/shard_map/ppermute | solution.py:385
  21.0 1.9 %collective-permute-start.5 = (f32[128,512]{1,0:T(8,128)S(1)}, f32[128,512]{1,0:T(8,128)S(1)}, u32[]{:S(2)}, u32[]{:S(2)}) collective-permute-start(f32[128,512]{1,0:T(8,128)S(1)} %collective-permute-done.1.refs_2_), channel_id=1, source_target_pairs={{0,1},{1,0},{2,3},{3,2},{4,5},{5,4},{6,7},{7,6},{8,9},{9,8},{10,11... | collective-permute-start | bytes 786440 | tf_op jit(solution)/shard_map/ppermute | solution.py:385
  28.6 2.2 %collective-permute-start.9 = (f32[4,160,256]{2,1,0:T(8,128)S(1)}, f32[4,160,256]{2,1,0:T(8,128)S(1)}, u32[]{:S(2)}, u32[]{:S(2)}) collective-permute-start(f32[4,160,256]{2,1,0:T(8,128)S(1)} %get-tuple-element.48), channel_id=1, source_target_pairs={{0,1},{1,0},{2,3},{3,2},{4,5},{5,4},{6,7},{7,6},{8,9},{9,8},{10,11... | collective-permute-start | bytes 1966088 | tf_op jit(solution)/shard_map/ppermute | solution.py:385
  30.8 6.3 %copy-start.8 = (f32[4,160,256]{2,1,0:T(8,128)}, f32[4,160,256]{2,1,0:T(8,128)S(1)}, u32[]{:S(2)}) copy-start(f32[4,160,256]{2,1,0:T(8,128)S(1)} %add.41) | copy-start | bytes 1966084
  31.7 13.2 %collective-permute-start.10 = (f32[160,256]{1,0:T(8,128)}, f32[160,256]{1,0:T(8,128)}, u32[]{:S(2)}, u32[]{:S(2)}) collective-permute-start(f32[160,256]{1,0:T(8,128)} %get-tuple-element.75), channel_id=1, source_target_pairs={{0,2},{2,0},{4,6},{6,4},{8,10},{10,8},{12,14},{14,12},{16,18},{18,... | collective-permute-start | bytes 491528 | tf_op jit(solution)/shard_map/ppermute | solution.py:388
  34.2 10.8 %collective-permute-start.12 = (f32[160,256]{1,0:T(8,128)}, f32[160,256]{1,0:T(8,128)}, u32[]{:S(2)}, u32[]{:S(2)}) collective-permute-start(f32[160,256]{1,0:T(8,128)} %get-tuple-element.76), channel_id=1, source_target_pairs={{0,6},{2,4},{4,2},{6,0},{8,14},{10,12},{12,10},{14,8},{16,22},{18,... | collective-permute-start | bytes 491528 | tf_op jit(solution)/shard_map/ppermute | solution.py:388
  35.8 9.8 %collective-permute-start.11 = (f32[160,256]{1,0:T(8,128)}, f32[160,256]{1,0:T(8,128)}, u32[]{:S(2)}, u32[]{:S(2)}) collective-permute-start(f32[160,256]{1,0:T(8,128)} %get-tuple-element.77), channel_id=1, source_target_pairs={{0,4},{2,6},{4,0},{6,2},{8,12},{10,14},{12,8},{14,10},{16,20},{18,... | collective-permute-start | bytes 491528 | tf_op jit(solution)/shard_map/ppermute | solution.py:388
  37.2 11.6 %collective-permute-start.8 = (f32[2,128,256]{2,1,0:T(8,128)}, f32[2,128,256]{2,1,0:T(8,128)S(1)}, u32[]{:S(2)}, u32[]{:S(2)}) collective-permute-start(f32[2,128,256]{2,1,0:T(8,128)} %get-tuple-element.80), channel_id=1, source_target_pairs={{2,0},{4,2},{6,4},{8,6},{10,8},{12,10},{14,12},{16,14},{18,16},{20... | collective-permute-start | bytes 786440 | tf_op jit(solution)/shard_map/ppermute | solution.py:405
  38.4 15.2 %collective-permute-start.7 = (f32[2,128,256]{2,1,0:T(8,128)S(1)}, f32[2,128,256]{2,1,0:T(8,128)S(1)}, u32[]{:S(2)}, u32[]{:S(2)}) collective-permute-start(f32[2,128,256]{2,1,0:T(8,128)S(1)} %get-tuple-element.81), channel_id=1, source_target_pairs={{0,2},{2,4},{4,6},{6,8},{8,10},{10,12},{12,14},{14,16},{16,18},{18... | collective-permute-start | bytes 786440 | tf_op jit(solution)/shard_map/ppermute | solution.py:402
  53.6 2.7 %collective-permute-start.13 = (f32[2,256,256]{2,1,0:T(8,128)S(1)}, f32[2,256,256]{2,1,0:T(8,128)S(1)}, u32[]{:S(2)}, u32[]{:S(2)}) collective-permute-start(f32[2,256,256]{2,1,0:T(8,128)S(1)} %get-tuple-element.50.own), channel_id=1, source_target_pairs={{0,1},{1,0},{2,3},{3,2},{4,5},{5,4},{6,7},{7,6},{8,9},{9,8},{10,11... | collective-permute-start | bytes 1572872 | tf_op jit(solution)/shard_map/ppermute | solution.py:385
  53.6 2.3 %collective-permute-start.14 = (f32[2,128,256]{2,1,0:T(8,128)S(1)}, f32[2,128,256]{2,1,0:T(8,128)S(1)}, u32[]{:S(2)}, u32[]{:S(2)}) collective-permute-start(f32[2,128,256]{2,1,0:T(8,128)S(1)} %collective-permute-done.7.b0), channel_id=1, source_target_pairs={{0,1},{1,0},{2,3},{3,2},{4,5},{5,4},{6,7},{7,6},{8,9},{9,8},{10,11... | collective-permute-start | bytes 786440 | tf_op jit(solution)/shard_map/ppermute | solution.py:385
  54.1 2.1 %collective-permute-start.15 = (f32[2,128,256]{2,1,0:T(8,128)S(1)}, f32[2,128,256]{2,1,0:T(8,128)S(1)}, u32[]{:S(2)}, u32[]{:S(2)}) collective-permute-start(f32[2,128,256]{2,1,0:T(8,128)S(1)} %collective-permute-done.8.a0), channel_id=1, source_target_pairs={{0,1},{1,0},{2,3},{3,2},{4,5},{5,4},{6,7},{7,6},{8,9},{9,8},{10,11... | collective-permute-start | bytes 786440 | tf_op jit(solution)/shard_map/ppermute | solution.py:385
  54.1 10.4 %collective-permute-start.16 = (f32[160,256]{1,0:T(8,128)S(1)}, f32[160,256]{1,0:T(8,128)S(1)}, u32[]{:S(2)}, u32[]{:S(2)}) collective-permute-start(f32[160,256]{1,0:T(8,128)S(1)} %fusion.5), channel_id=1, source_target_pairs={{0,8},{2,10},{4,12},{6,14},{8,0},{10,2},{12,4},{14,6},{16,24},{18,... | collective-permute-start | bytes 491528 | tf_op jit(solution)/shard_map/ppermute | solution.py:388
  58.6 23.4 %collective-permute-start.18 = (f32[2,128,256]{2,1,0:T(8,128)S(1)}, f32[2,128,256]{2,1,0:T(8,128)S(1)}, u32[]{:S(2)}, u32[]{:S(2)}) collective-permute-start(f32[2,128,256]{2,1,0:T(8,128)S(1)} %get-tuple-element.55), channel_id=1, source_target_pairs={{0,2},{2,4},{4,6},{6,8},{8,10},{10,12},{12,14},{14,16},{16,18},{18... | collective-permute-start | bytes 786440 | tf_op jit(solution)/shard_map/ppermute | solution.py:402
  63.1 19.0 %collective-permute-start.19 = (f32[2,128,256]{2,1,0:T(8,128)S(1)}, f32[2,128,256]{2,1,0:T(8,128)S(1)}, u32[]{:S(2)}, u32[]{:S(2)}) collective-permute-start(f32[2,128,256]{2,1,0:T(8,128)S(1)} %get-tuple-element.56), channel_id=1, source_target_pairs={{2,0},{4,2},{6,4},{8,6},{10,8},{12,10},{14,12},{16,14},{18,16},{20... | collective-permute-start | bytes 786440 | tf_op jit(solution)/shard_map/ppermute | solution.py:405
  64.6 17.5 %collective-permute-start.17 = (f32[160,256]{1,0:T(8,128)S(1)}, f32[160,256]{1,0:T(8,128)S(1)}, u32[]{:S(2)}, u32[]{:S(2)}) collective-permute-start(f32[160,256]{1,0:T(8,128)S(1)} %add.45), channel_id=1, source_target_pairs={{0,16},{2,18},{4,20},{6,22},{8,24},{10,26},{12,28},{14,30},{16,0},... | collective-permute-start | bytes 491528 | tf_op jit(solution)/shard_map/ppermute | solution.py:388
  82.1 7.9 %collective-permute-start.22 = (f32[160,256]{1,0:T(8,128)S(1)}, f32[160,256]{1,0:T(8,128)S(1)}, u32[]{:S(2)}, u32[]{:S(2)}) collective-permute-start(f32[160,256]{1,0:T(8,128)S(1)} %add.46), channel_id=1, source_target_pairs={{0,6},{2,4},{4,2},{6,0},{8,14},{10,12},{12,10},{14,8},{16,22},{18,... | collective-permute-start | bytes 491528 | tf_op jit(solution)/shard_map/ppermute | solution.py:388
  82.2 8.7 %collective-permute-start.21 = (f32[160,256]{1,0:T(8,128)S(1)}, f32[160,256]{1,0:T(8,128)S(1)}, u32[]{:S(2)}, u32[]{:S(2)}) collective-permute-start(f32[160,256]{1,0:T(8,128)S(1)} %add.46), channel_id=1, source_target_pairs={{0,4},{2,6},{4,0},{6,2},{8,12},{10,14},{12,8},{14,10},{16,20},{18,... | collective-permute-start | bytes 491528 | tf_op jit(solution)/shard_map/ppermute | solution.py:388
  82.3 8.6 %collective-permute-start.20 = (f32[160,256]{1,0:T(8,128)S(1)}, f32[160,256]{1,0:T(8,128)S(1)}, u32[]{:S(2)}, u32[]{:S(2)}) collective-permute-start(f32[160,256]{1,0:T(8,128)S(1)} %add.46), channel_id=1, source_target_pairs={{0,2},{2,0},{4,6},{6,4},{8,10},{10,8},{12,14},{14,12},{16,18},{18,... | collective-permute-start | bytes 491528 | tf_op jit(solution)/shard_map/ppermute | solution.py:388
  91.0 2.9 %copy-start.5 = (f32[2,256,256]{2,1,0:T(8,128)S(1)}, f32[2,256,256]{2,1,0:T(8,128)}, u32[]{:S(2)}) copy-start(f32[2,256,256]{2,1,0:T(8,128)} %copy-done.4) | copy-start | bytes 1572868
  91.0 2.9 %copy-start.7 = (bf16[4,256,256]{2,1,0:T(8,128)(2,1)S(1)}, bf16[4,256,256]{2,1,0:T(8,128)(2,1)}, u32[]{:S(2)}) copy-start(bf16[4,256,256]{2,1,0:T(8,128)(2,1)} %copy-done.6) | copy-start | bytes 1572868
  91.0 2.2 %collective-permute-start.23 = (f32[4,160,256]{2,1,0:T(8,128)S(1)}, f32[4,160,256]{2,1,0:T(8,128)S(1)}, u32[]{:S(2)}, u32[]{:S(2)}) collective-permute-start(f32[4,160,256]{2,1,0:T(8,128)S(1)} %pad_maximum_fusion.own_totals), channel_id=1, source_target_pairs={{0,1},{1,0},{2,3},{3,2},{4,5},{5,4},{6,7},{7,6},{8,9},{9,8},{10,11... | collective-permute-start | bytes 1966088 | tf_op jit(solution)/shard_map/ppermute | solution.py:385
  98.8 2.2 %collective-permute-start.24 = (f32[4,160,256]{2,1,0:T(8,128)S(1)}, f32[4,160,256]{2,1,0:T(8,128)S(1)}, u32[]{:S(2)}, u32[]{:S(2)}) collective-permute-start(f32[4,160,256]{2,1,0:T(8,128)S(1)} %get-tuple-element.64), channel_id=1, source_target_pairs={{0,1},{1,0},{2,3},{3,2},{4,5},{5,4},{6,7},{7,6},{8,9},{9,8},{10,11... | collective-permute-start | bytes 1966088 | tf_op jit(solution)/shard_map/ppermute | solution.py:385
  101.1 7.1 %collective-permute-start.25 = (f32[160,256]{1,0:T(8,128)S(1)}, f32[160,256]{1,0:T(8,128)S(1)}, u32[]{:S(2)}, u32[]{:S(2)}) collective-permute-start(f32[160,256]{1,0:T(8,128)S(1)} %get-tuple-element.72), channel_id=1, source_target_pairs={{0,2},{2,0},{4,6},{6,4},{8,10},{10,8},{12,14},{14,12},{16,18},{18,... | collective-permute-start | bytes 491528 | tf_op jit(solution)/shard_map/ppermute | solution.py:388
  101.4 10.5 %collective-permute-start.27 = (f32[160,256]{1,0:T(8,128)S(1)}, f32[160,256]{1,0:T(8,128)S(1)}, u32[]{:S(2)}, u32[]{:S(2)}) collective-permute-start(f32[160,256]{1,0:T(8,128)S(1)} %get-tuple-element.73), channel_id=1, source_target_pairs={{0,6},{2,4},{4,2},{6,0},{8,14},{10,12},{12,10},{14,8},{16,22},{18,... | collective-permute-start | bytes 491528 | tf_op jit(solution)/shard_map/ppermute | solution.py:388
  104.1 9.2 %collective-permute-start.26 = (f32[160,256]{1,0:T(8,128)S(1)}, f32[160,256]{1,0:T(8,128)S(1)}, u32[]{:S(2)}, u32[]{:S(2)}) collective-permute-start(f32[160,256]{1,0:T(8,128)S(1)} %get-tuple-element.74), channel_id=1, source_target_pairs={{0,4},{2,6},{4,0},{6,2},{8,12},{10,14},{12,8},{14,10},{16,20},{18,... | collective-permute-start | bytes 491528 | tf_op jit(solution)/shard_map/ppermute | solution.py:388
  113.3 5.4 %collective-permute-start.28 = (f32[160,256]{1,0:T(8,128)S(1)}, f32[160,256]{1,0:T(8,128)S(1)}, u32[]{:S(2)}, u32[]{:S(2)}) collective-permute-start(f32[160,256]{1,0:T(8,128)S(1)} %fusion.2), channel_id=1, source_target_pairs={{0,8},{2,10},{4,12},{6,14},{8,0},{10,2},{12,4},{14,6},{16,24},{18,... | collective-permute-start | bytes 491528 | tf_op jit(solution)/shard_map/ppermute | solution.py:388
  118.7 9.7 %collective-permute-start.29 = (f32[160,256]{1,0:T(8,128)S(1)}, f32[160,256]{1,0:T(8,128)S(1)}, u32[]{:S(2)}, u32[]{:S(2)}) collective-permute-start(f32[160,256]{1,0:T(8,128)S(1)} %add.51), channel_id=1, source_target_pairs={{0,16},{2,18},{4,20},{6,22},{8,24},{10,26},{12,28},{14,30},{16,0},... | collective-permute-start | bytes 491528 | tf_op jit(solution)/shard_map/ppermute | solution.py:388
  118.9 11.0 %collective-permute-start.35 = (f32[2,128,256]{2,1,0:T(8,128)S(1)}, f32[2,128,256]{2,1,0:T(8,128)S(1)}, u32[]{:S(2)}, u32[]{:S(2)}) collective-permute-start(f32[2,128,256]{2,1,0:T(8,128)S(1)} %get-tuple-element.78), channel_id=1, source_target_pairs={{2,0},{4,2},{6,4},{8,6},{10,8},{12,10},{14,12},{16,14},{18,16},{20... | collective-permute-start | bytes 786440 | tf_op jit(solution)/shard_map/ppermute | solution.py:405
  120.2 13.4 %collective-permute-start.34 = (f32[2,128,256]{2,1,0:T(8,128)S(1)}, f32[2,128,256]{2,1,0:T(8,128)S(1)}, u32[]{:S(2)}, u32[]{:S(2)}) collective-permute-start(f32[2,128,256]{2,1,0:T(8,128)S(1)} %get-tuple-element.79), channel_id=1, source_target_pairs={{0,2},{2,4},{4,6},{6,8},{8,10},{10,12},{12,14},{14,16},{16,18},{18... | collective-permute-start | bytes 786440 | tf_op jit(solution)/shard_map/ppermute | solution.py:402
  124.7 14.8 %collective-permute-start.33 = (f32[2,256,256]{2,1,0:T(8,128)S(1)}, f32[2,256,256]{2,1,0:T(8,128)S(1)}, u32[]{:S(2)}, u32[]{:S(2)}) collective-permute-start(f32[2,256,256]{2,1,0:T(8,128)S(1)} %get-tuple-element.67.own), channel_id=1, source_target_pairs={{0,1},{1,0},{2,3},{3,2},{4,5},{5,4},{6,7},{7,6},{8,9},{9,8},{10,11... | collective-permute-start | bytes 1572872 | tf_op jit(solution)/shard_map/ppermute | solution.py:385
  128.5 8.6 %collective-permute-start.32 = (f32[160,256]{1,0:T(8,128)S(1)}, f32[160,256]{1,0:T(8,128)S(1)}, u32[]{:S(2)}, u32[]{:S(2)}) collective-permute-start(f32[160,256]{1,0:T(8,128)S(1)} %add.52), channel_id=1, source_target_pairs={{0,6},{2,4},{4,2},{6,0},{8,14},{10,12},{12,10},{14,8},{16,22},{18,... | collective-permute-start | bytes 491528 | tf_op jit(solution)/shard_map/ppermute | solution.py:388
  128.5 9.4 %collective-permute-start.31 = (f32[160,256]{1,0:T(8,128)S(1)}, f32[160,256]{1,0:T(8,128)S(1)}, u32[]{:S(2)}, u32[]{:S(2)}) collective-permute-start(f32[160,256]{1,0:T(8,128)S(1)} %add.52), channel_id=1, source_target_pairs={{0,4},{2,6},{4,0},{6,2},{8,12},{10,14},{12,8},{14,10},{16,20},{18,... | collective-permute-start | bytes 491528 | tf_op jit(solution)/shard_map/ppermute | solution.py:388
  129.9 9.6 %collective-permute-start.30 = (f32[160,256]{1,0:T(8,128)S(1)}, f32[160,256]{1,0:T(8,128)S(1)}, u32[]{:S(2)}, u32[]{:S(2)}) collective-permute-start(f32[160,256]{1,0:T(8,128)S(1)} %add.52), channel_id=1, source_target_pairs={{0,2},{2,0},{4,6},{6,4},{8,10},{10,8},{12,14},{14,12},{16,18},{18,... | collective-permute-start | bytes 491528 | tf_op jit(solution)/shard_map/ppermute | solution.py:388
  133.5 6.0 %collective-permute-start.37 = (f32[2,128,256]{2,1,0:T(8,128)S(1)}, f32[2,128,256]{2,1,0:T(8,128)S(1)}, u32[]{:S(2)}, u32[]{:S(2)}) collective-permute-start(f32[2,128,256]{2,1,0:T(8,128)S(1)} %collective-permute-done.35.a0), channel_id=1, source_target_pairs={{0,1},{1,0},{2,3},{3,2},{4,5},{5,4},{6,7},{7,6},{8,9},{9,8},{10,11... | collective-permute-start | bytes 786440 | tf_op jit(solution)/shard_map/ppermute | solution.py:385
  137.1 2.5 %collective-permute-start.36 = (f32[2,128,256]{2,1,0:T(8,128)S(1)}, f32[2,128,256]{2,1,0:T(8,128)S(1)}, u32[]{:S(2)}, u32[]{:S(2)}) collective-permute-start(f32[2,128,256]{2,1,0:T(8,128)S(1)} %collective-permute-done.34.b0), channel_id=1, source_target_pairs={{0,1},{1,0},{2,3},{3,2},{4,5},{5,4},{6,7},{7,6},{8,9},{9,8},{10,11... | collective-permute-start | bytes 786440 | tf_op jit(solution)/shard_map/ppermute | solution.py:385
  142.7 1.4 collective-permute-start.38
  (1 other events, 1.0 us)
where the time goes:
time: 146 us
  waiting for transfers between devices  60.9 us (42%)
  starting transfers between devices  53.6 us (37%)
  Pallas kernels  22.2 us (15%)
  local copies, waits for them, and re-layouts  6.17 us (4%)
  other arithmetic  1.58 us (1%)
    ppermute x16, waiting for transfers between devices, across(): return lax.ppermute(value, 'tile', [(i, i ^ k) for i in range(tiles)])  40.5 us
    ppermute x5, starting transfers between devices, from_below(): return lax.ppermute(value, 'tile', up)  24.5 us
    pallas_call x9, Pallas kernels, call(): pl.pallas_call(kernel, out_shape=shapes, in_specs=[smem] + [vmem] * (len(...  22.2 us
    ppermute x16, starting transfers between devices, across(): return lax.ppermute(value, 'tile', [(i, i ^ k) for i in range(tiles)])  20.6 us
    ppermute x13, waiting for transfers between devices, swap(): return lax.ppermute(value, 'mode', [(0, 1), (1, 0)])  9.22 us
    ppermute x5, waiting for transfers between devices, from_below(): return lax.ppermute(value, 'tile', up)  7.61 us
    ppermute x5, starting transfers between devices, from_above(): return lax.ppermute(value, 'tile', down)  6.74 us
    ppermute x5, waiting for transfers between devices, from_above(): return lax.ppermute(value, 'tile', down)  3.58 us
  transfers between devices with their start and end apart: 39, of which 26 were waited for; matrix products, arithmetic and copies ran while one was open for 2% of the time, Pallas kernels for 4%

commit v1 on v0

--- a/solution.py
+++ b/solution.py
@@ -212,6 +212,13 @@
     out[...] = tall[kept]
 
 
+def patch_kernel(size, minibatch, info, strip_ref, below, above, patch, window):
+    for part in range(2):
+        patch[part] = cut_patch(
+            size, info, minibatch, strip_ref, below[part], above[part], window, part
+        )
+
+
 def ready_kernel(info, probe, measured, table, own, observed, split):
     own[...] = probe[...]
     for minibatch in range(2):
@@ -223,19 +230,18 @@
 def field_kernel(size, minibatch, info, strip_ref, *refs):
     tiles, strip, pattern = size
     slot = info[25]
-    count = 2 if minibatch else 4
-    edges, (own, other, measured, table) = refs[:count], refs[count : count + 4]
-    gradient, step_own, step_other, window = refs[count + 4 :]
-
-    def edge(side, part):
-        if len(edges) == 2:
-            return edges[side][part]
-        return jnp.where(slot == part, edges[2 * side][...], edges[2 * side + 1][...])
-
-    obj_real, obj_imag = (
-        cut_patch(size, info, minibatch, strip_ref, edge(0, part), edge(1, part), window, part)
-        for part in range(2)
-    )
+    if minibatch:
+        own, other, measured, table, gradient, top, bottom, step_own, step_other = refs
+        obj_real, obj_imag = strip_ref[0], strip_ref[1]
+    else:
+        *edges, own, other, measured, table = refs[:-6]
+        gradient, top, bottom, step_own, step_other, window = refs[-6:]
+        sides = (jnp.where(slot == 0, edges[i][...], edges[i + 1][...]) for i in (0, 2))
+        others = (jnp.where(slot == 0, edges[i + 1][...], edges[i][...]) for i in (0, 2))
+        obj_real, obj_imag = (
+            cut_patch(size, info, minibatch, strip_ref, *ends, window, part)
+            for part, ends in enumerate((sides, others))
+        )
     cos_high, cos_low, sin_high, sin_low = (table[i] for i in range(4))
 
     def block(top_left, top_right, low_left, low_right):
@@ -278,8 +284,12 @@
     chi = both([(factor * fr, factor * fi) for fr, fi in far], second, first)
     (pr0, pi0), (pr1, pi1) = probes
     (cr0, ci0), (cr1, ci1) = chi
-    gradient[0] = (pr0 * cr0 + pi0 * ci0) + (pr1 * cr1 + pi1 * ci1)
-    gradient[1] = (pr0 * ci0 - pi0 * cr0) + (pr1 * ci1 - pi1 * cr1)
+    half = top.shape[1]
+    for part, value in (
+        (0, (pr0 * cr0 + pi0 * ci0) + (pr1 * cr1 + pi1 * ci1)),
+        (1, (pr0 * ci0 - pi0 * cr0) + (pr1 * ci1 - pi1 * cr1)),
+    ):
+        gradient[part], top[part], bottom[part] = value, value[:half], value[half:]
     coverage = obj_real * obj_real + obj_imag * obj_imag
     rows = pattern // GROUP
     mate = lax.rem(info[24], GROUP)
@@ -391,9 +401,11 @@
         mates = [across(blocks[k], unit * k) for k in range(1, GROUP)]
         return functools.reduce(jnp.add, mates, blocks[0])
 
-    def exchange(piece, unit):
-        piece = piece + across(piece, unit)
-        return piece + across(piece, 2 * unit)
+    def exchange(piece, unit, pairwise):
+        if pairwise:
+            piece = piece + across(piece, unit)
+            return piece + across(piece, 2 * unit)
+        return scatter([piece] * GROUP, unit)
 
     def gather(piece, unit):
         return jnp.stack([piece] + [across(piece, unit * k) for k in range(1, GROUP)])
@@ -430,12 +442,18 @@
         last = minibatch == 1
         rows = pattern // GROUP
         blocks = (GROUP, 2 * rows + rows // 2, pattern)
-        gradient, step_own, step_other = call(
+        cut = (object_field, *edges)
+        if last:
+            cut = call(
+                bind(patch_kernel, size, minibatch), "patch", [field], (here, *cut), [window], 10**10
+            )
+        rim = (2, half, pattern)
+        gradient, top, bottom, step_own, step_other = call(
             bind(field_kernel, size, minibatch),
             "field",
-            [field, blocks, blocks],
-            (here, object_field, *edges, own, other, observed, table),
-            [window],
+            [field, rim, rim, blocks, blocks],
+            (here, *cut, own, other, observed, table),
+            [] if last else [window],
             flops=2 * 12 * 512**3,
         )
         (illum,) = call(
@@ -445,24 +463,28 @@
             (info, own, other),
             [tall],
         )
-        steps = step_own + swap(step_other)
+        brought = swap(step_other)
+        steps = [step_own[k] + brought[k] for k in range(GROUP)]
         piece = scatter(steps, 1)
         if last:
-            gradient, piece, illum = lax.optimization_barrier((gradient, piece, illum))
-        rim_below, rim_above = from_below(gradient[:, half:]), from_above(gradient[:, :half])
+            gradient, top, bottom, piece, illum = lax.optimization_barrier(
+                (gradient, top, bottom, piece, illum)
+            )
+        rim_below, rim_above = from_below(bottom), from_above(top)
         if not last:
-            gradient, rim_below, rim_above, piece, illum = lax.optimization_barrier(
-                (gradient, rim_below, rim_above, piece, illum)
+            gradient, rim_below, rim_above, illum = lax.optimization_barrier(
+                (gradient, rim_below, rim_above, illum)
             )
         rims = (gradient, swap(gradient), rim_below, rim_above, swap(rim_below), swap(rim_above))
         object_field, *edges = call(
             bind(update_kernel, size, minibatch),
             "update",
-            [object_field.shape] + ([] if last else [(2, half, pattern)] * 2),
+            [object_field.shape] + ([] if last else [rim] * 2),
             (info, object_field, illum, *rims),
             [tall],
-        )
-        piece = exchange(piece, GROUP)
+            flops=0,
+        )
+        piece = exchange(piece, GROUP, last)
         if not last:
             edges = [from_below(edges[1]), from_above(edges[0])]
             piece, *edges = lax.optimization_barrier((piece, *edges))

time: 146 us -> 147 us (level)
  waiting for transfers between devices: 60.9 us -> 56.4 us
  starting transfers between devices: 53.6 us -> 55.8 us
  Pallas kernels: 22.2 us -> 23.8 us
    ppermute x16 -> x17, waiting for transfers between devices: 40.5 us -> 31.1 us  [across(): return lax.ppermute(value, 'tile', [(i, i ^ k) for i in range(tiles)])]
    ppermute x5, waiting for transfers between devices: 3.58 us -> 12.4 us  [from_above(): return lax.ppermute(value, 'tile', down)]
    ppermute x16 -> x17, starting transfers between devices: 20.6 us -> 28.8 us  [across(): return lax.ppermute(value, 'tile', [(i, i ^ k) for i in range(tiles)])]
    ppermute x5, starting transfers between devices: 24.5 us -> 18.4 us  [from_below(): return lax.ppermute(value, 'tile', up)]
    ppermute x13, waiting for transfers between devices: 9.22 us -> 6.83 us  [swap(): return lax.ppermute(value, 'mode', [(0, 1), (1, 0)])]
    pallas_call x9 -> x10, Pallas kernels: 22.2 us -> 23.8 us  [call(): pl.pallas_call(kernel, out_shape=shapes, in_specs=[smem] + [vmem] * (len(...]
    ppermute x5, waiting for transfers between devices: 7.61 us -> 6.08 us  [from_below(): return lax.ppermute(value, 'tile', up)]
  transfers between devices with their start and end apart: 39 -> 40, of which waited for: 26 -> 24; matrix products, arithmetic and copies ran while one was open for 2% -> 3% of each run, Pallas kernels for 4% -> 5%
where the time goes in v1:
time: 147 us; the launch traced here: 146 us
  waiting for transfers between devices  56.4 us (38%)
  starting transfers between devices  55.8 us (38%)
  Pallas kernels  23.8 us (16%)
  local copies, waits for them, and re-layouts  6.38 us (4%)
  other arithmetic  2.38 us (2%)
    ppermute x17, waiting for transfers between devices, across(): return lax.ppermute(value, 'tile', [(i, i ^ k) for i in range(tiles)])  31.1 us
    ppermute x17, starting transfers between devices, across(): return lax.ppermute(value, 'tile', [(i, i ^ k) for i in range(tiles)])  28.8 us
    pallas_call x10, Pallas kernels, call(): pl.pallas_call(kernel, out_shape=shapes, in_specs=[smem] + [vmem] * (len(...  23.8 us
    ppermute x5, starting transfers between devices, from_below(): return lax.ppermute(value, 'tile', up)  18.4 us
    ppermute x5, waiting for transfers between devices, from_above(): return lax.ppermute(value, 'tile', down)  12.4 us
    ppermute x13, waiting for transfers between devices, swap(): return lax.ppermute(value, 'mode', [(0, 1), (1, 0)])  6.83 us
    ppermute x5, starting transfers between devices, from_above(): return lax.ppermute(value, 'tile', down)  6.64 us
    ppermute x5, waiting for transfers between devices, from_below(): return lax.ppermute(value, 'tile', up)  6.08 us
  transfers between devices with their start and end apart: 40, of which 24 were waited for; matrix products, arithmetic and copies ran while one was open for 3% of the time, Pallas kernels for 5%

profile of v1, /device:TPU:0, one launch (start us, length us, event | category | flops | bytes accessed | tf_op | source)
XLA Modules:
  0.0 145.8 jit_solution(5733398437757501423)
XLA Ops:
  0.6 2.0 %dynamic-slice_bitcast_fusion = (f32[128,512]{1,0:T(8,128)}, f32[128,512]{1,0:T(8,128)}) fusion(f32[2,256,512]{2,1,0:T(8,128)} %strip_ref.3, s32[]{:T(128)S(6)} %select_n.4, s32[]{:T(128)S(6)} %add.113), kind=kLoop, calls=%fused_computation.2 | loop fusion | bytes 1048584 | tf_op jit(solution)/shard_map/slice | solution.py:426
  2.6 5.0 %collective-permute-start = (f32[128,512]{1,0:T(8,128)}, f32[128,512]{1,0:T(8,128)S(1)}, u32[]{:S(2)}, u32[]{:S(2)}) collective-permute-start(f32[128,512]{1,0:T(8,128)} %get-tuple-element.87), channel_id=1, source_target_pairs={{0,2},{2,4},{4,6},{6,8},{8,10},{10,12},{12,14},{14,16},{16,18},{18... | collective-permute-start | bytes 786440 | tf_op jit(solution)/shard_map/ppermute | solution.py:414
  7.6 1.3 collective-permute-start.1
  9.0 4.5 %collective-permute-start.2 = (s32[2,2,2]{2,1,0:T(2,128)S(1)}, s32[2,2,2]{2,1,0:T(2,128)S(1)}, u32[]{:S(2)}, u32[]{:S(2)}) collective-permute-start(s32[2,2,2]{2,1,0:T(2,128)S(1)} %copy-done.9), channel_id=1, source_target_pairs={{0,2},{2,4},{4,6},{6,8},{8,10},{10,12},{12,14},{14,16},{16,18},{18... | collective-permute-start | bytes 104 | tf_op jit(solution)/shard_map/ppermute | solution.py:414
  13.5 1.3 collective-permute-start.3
  17.8 1.3 collective-permute-done.2
  19.1 1.9 %collective-permute-done.3 = s32[2,2,2]{2,1,0:T(2,128)S(1)} collective-permute-done((s32[2,2,2]{2,1,0:T(2,128)S(1)}, s32[2,2,2]{2,1,0:T(2,128)S(1)}, u32[]{:S(2)}, u32[]{:S(2)}) %collective-permute-start.3) | collective-permute-done | bytes 64 | tf_op jit(solution)/shard_map/ppermute | solution.py:417
  23.2 6.4 %field.2 = (f32[2,256,256]{2,1,0:T(8,128)S(1)}, f32[2,128,256]{2,1,0:T(8,128)}, f32[2,128,256]{2,1,0:T(8,128)}, f32[4,160,256]{2,1,0:T(8,128)S(1)}, f32[4,160,256]{2,1,0:T(8,128)S(1)}) custom-call(s32[26]{0:T(128)S(1)} %concatenate.8.info, f32[2,256,512]{2,1,0:T(8,128)S(1)} %copy-done, f32[128,512]{1,0:T(8,128)S(1)} %collective-permute-done.refs_0_, ...), custom_call_target="tpu_custom_call" | custom-call | flops 3221225472 | bytes 6553704 | tf_op jit(solution)/shard_map/field/pallas_call | solution.py:369
  29.8 3.4 %collective-permute-start.7 = (f32[2,128,256]{2,1,0:T(8,128)}, f32[2,128,256]{2,1,0:T(8,128)S(1)}, u32[]{:S(2)}, u32[]{:S(2)}) collective-permute-start(f32[2,128,256]{2,1,0:T(8,128)} %get-tuple-element.52), channel_id=1, source_target_pairs={{0,2},{2,4},{4,6},{6,8},{8,10},{10,12},{12,14},{14,16},{16,18},{18... | collective-permute-start | bytes 786440 | tf_op jit(solution)/shard_map/ppermute | solution.py:414
  33.2 1.3 collective-permute-start.8
  35.5 2.6 %collective-permute-start.13 = (f32[160,256]{1,0:T(8,128)}, f32[160,256]{1,0:T(8,128)}, u32[]{:S(2)}, u32[]{:S(2)}) collective-permute-start(f32[160,256]{1,0:T(8,128)} %get-tuple-element.83), channel_id=1, source_target_pairs={{0,2},{2,0},{4,6},{6,4},{8,10},{10,8},{12,14},{14,12},{16,18},{18,... | collective-permute-start | bytes 491528 | tf_op jit(solution)/shard_map/ppermute | solution.py:398
  38.2 3.1 %collective-permute-start.14 = (f32[160,256]{1,0:T(8,128)}, f32[160,256]{1,0:T(8,128)}, u32[]{:S(2)}, u32[]{:S(2)}) collective-permute-start(f32[160,256]{1,0:T(8,128)} %get-tuple-element.85), channel_id=1, source_target_pairs={{0,4},{2,6},{4,0},{6,2},{8,12},{10,14},{12,8},{14,10},{16,20},{18,... | collective-permute-start | bytes 491528 | tf_op jit(solution)/shard_map/ppermute | solution.py:398
  43.3 1.7 %illumination.2.illum = f32[256,512]{1,0:T(8,128)S(1)} custom-call(s32[26]{0:T(128)S(1)} %concatenate.9.info, f32[2,256,256]{2,1,0:T(8,128)S(1)} %get-tuple-element.48.refs_4_.own.refs_0_, f32[2,256,256]{2,1,0:T(8,128)S(1)} %collective-permute-done.6.refs_5_.other.refs_1_), custom_call_target="tpu_custom_call" | custom-call | bytes 1572968 | tf_op jit(solution)/shard_map/illumination/pallas_call | solution.py:369
  45.0 2.6 %collective-permute-done.8.a0 = f32[2,128,256]{2,1,0:T(8,128)} collective-permute-done((f32[2,128,256]{2,1,0:T(8,128)}, f32[2,128,256]{2,1,0:T(8,128)}, u32[]{:S(2)}, u32[]{:S(2)}) %collective-permute-start.8) | collective-permute-done | bytes 262176 | tf_op jit(solution)/shard_map/ppermute | solution.py:417
  48.1 3.0 %collective-permute-done.13 = f32[160,256]{1,0:T(8,128)} collective-permute-done((f32[160,256]{1,0:T(8,128)}, f32[160,256]{1,0:T(8,128)}, u32[]{:S(2)}, u32[]{:S(2)}) %collective-permute-start.13) | collective-permute-done | bytes 163872 | tf_op jit(solution)/shard_map/ppermute | solution.py:398
  51.1 2.1 %collective-permute-done.15 = f32[160,256]{1,0:T(8,128)} collective-permute-done((f32[160,256]{1,0:T(8,128)}, f32[160,256]{1,0:T(8,128)}, u32[]{:S(2)}, u32[]{:S(2)}) %collective-permute-start.15) | collective-permute-done | bytes 163872 | tf_op jit(solution)/shard_map/ppermute | solution.py:398
  53.3 1.2 fusion.13
  54.5 5.0 %collective-permute-start.16 = (f32[160,256]{1,0:T(8,128)S(1)}, f32[160,256]{1,0:T(8,128)S(1)}, u32[]{:S(2)}, u32[]{:S(2)}) collective-permute-start(f32[160,256]{1,0:T(8,128)S(1)} %fusion.13), channel_id=1, source_target_pairs={{0,8},{2,10},{4,12},{6,14},{8,0},{10,2},{12,4},{14,6},{16,24},{18,... | collective-permute-start | bytes 491528 | tf_op jit(solution)/shard_map/ppermute | solution.py:398
  59.4 2.3 %collective-permute-start.17 = (f32[160,256]{1,0:T(8,128)S(1)}, f32[160,256]{1,0:T(8,128)S(1)}, u32[]{:S(2)}, u32[]{:S(2)}) collective-permute-start(f32[160,256]{1,0:T(8,128)S(1)} %fusion.13), channel_id=1, source_target_pairs={{0,16},{2,18},{4,20},{6,22},{8,24},{10,26},{12,28},{14,30},{16,0},... | collective-permute-start | bytes 491528 | tf_op jit(solution)/shard_map/ppermute | solution.py:398
  61.9 2.8 %update.2 = (f32[2,256,512]{2,1,0:T(8,128)S(1)}, f32[2,128,256]{2,1,0:T(8,128)S(1)}, f32[2,128,256]{2,1,0:T(8,128)S(1)}) custom-call(s32[26]{0:T(128)S(1)} %concatenate.9.info, f32[2,256,512]{2,1,0:T(8,128)S(1)} %copy-done, f32[256,512]{1,0:T(8,128)S(1)} %illumination.2.illum, f32[2,256,256]{2,1,0:T(8,128)S(1)} %get-tuple-element.55.own, ...), custom_call_target="tpu_custom_call" | custom-call | bytes 5242984 | tf_op jit(solution)/shard_map/update/pallas_call | solution.py:369
  64.7 2.9 %collective-permute-start.19 = (f32[2,128,256]{2,1,0:T(8,128)S(1)}, f32[2,128,256]{2,1,0:T(8,128)S(1)}, u32[]{:S(2)}, u32[]{:S(2)}) collective-permute-start(f32[2,128,256]{2,1,0:T(8,128)S(1)} %get-tuple-element.61), channel_id=1, source_target_pairs={{0,2},{2,4},{4,6},{6,8},{8,10},{10,12},{12,14},{14,16},{16,18},{18... | collective-permute-start | bytes 786440 | tf_op jit(solution)/shard_map/ppermute | solution.py:414
  67.7 1.5 %collective-permute-start.20 = (f32[2,128,256]{2,1,0:T(8,128)S(1)}, f32[2,128,256]{2,1,0:T(8,128)S(1)}, u32[]{:S(2)}, u32[]{:S(2)}) collective-permute-start(f32[2,128,256]{2,1,0:T(8,128)S(1)} %get-tuple-element.62), channel_id=1, source_target_pairs={{2,0},{4,2},{6,4},{8,6},{10,8},{12,10},{14,12},{16,14},{18,16},{20... | collective-permute-start | bytes 786440 | tf_op jit(solution)/shard_map/ppermute | solution.py:417
  69.1 5.3 %collective-permute-done.17 = f32[160,256]{1,0:T(8,128)S(1)} collective-permute-done((f32[160,256]{1,0:T(8,128)S(1)}, f32[160,256]{1,0:T(8,128)S(1)}, u32[]{:S(2)}, u32[]{:S(2)}) %collective-permute-start.17) | collective-permute-done | bytes 163872 | tf_op jit(solution)/shard_map/ppermute | solution.py:398
  74.5 3.9 %collective-permute-done.20.above = f32[2,128,256]{2,1,0:T(8,128)S(1)} collective-permute-done((f32[2,128,256]{2,1,0:T(8,128)S(1)}, f32[2,128,256]{2,1,0:T(8,128)S(1)}, u32[]{:S(2)}, u32[]{:S(2)}) %collective-permute-start.20) | collective-permute-done | bytes 262176 | tf_op jit(solution)/shard_map/ppermute | solution.py:417
  78.4 1.4 collective-permute-start.21
  79.8 2.5 %collective-permute-start.22 = (f32[160,256]{1,0:T(8,128)S(1)}, f32[160,256]{1,0:T(8,128)S(1)}, u32[]{:S(2)}, u32[]{:S(2)}) collective-permute-start(f32[160,256]{1,0:T(8,128)S(1)} %add_add_fusion), channel_id=1, source_target_pairs={{0,4},{2,6},{4,0},{6,2},{8,12},{10,14},{12,8},{14,10},{16,20},{18,... | collective-permute-start | bytes 491528 | tf_op jit(solution)/shard_map/ppermute | solution.py:398
  82.3 2.1 %collective-permute-done.21 = f32[160,256]{1,0:T(8,128)S(1)} collective-permute-done((f32[160,256]{1,0:T(8,128)S(1)}, f32[160,256]{1,0:T(8,128)S(1)}, u32[]{:S(2)}, u32[]{:S(2)}) %collective-permute-start.21) | collective-permute-done | bytes 163872 | tf_op jit(solution)/shard_map/ppermute | solution.py:398
  84.4 4.7 %collective-permute-done.22 = f32[160,256]{1,0:T(8,128)S(1)} collective-permute-done((f32[160,256]{1,0:T(8,128)S(1)}, f32[160,256]{1,0:T(8,128)S(1)}, u32[]{:S(2)}, u32[]{:S(2)}) %collective-permute-start.22) | collective-permute-done | bytes 163872 | tf_op jit(solution)/shard_map/ppermute | solution.py:398
  92.1 4.5 %field.3 = (f32[2,256,256]{2,1,0:T(8,128)S(1)}, f32[2,128,256]{2,1,0:T(8,128)S(1)}, f32[2,128,256]{2,1,0:T(8,128)S(1)}, f32[4,160,256]{2,1,0:T(8,128)S(1)}, f32[4,160,256]{2,1,0:T(8,128)S(1)}) custom-call(s32[26]{0:T(128)S(1)} %concatenate.8.info, f32[2,256,256]{2,1,0:T(8,128)S(1)} %patch.1.strip_ref, f32[2,256,256]{2,1,0:T(8,128)S(1)} %get-tuple-element.66.refs_0_.own, ...), custom_call_target="tpu_custom_call" | custom-call | flops 3221225472 | bytes 4980840 | tf_op jit(solution)/shard_map/field/pallas_call | solution.py:369
  96.8 2.0 %collective-permute-done.25 = f32[4,160,256]{2,1,0:T(8,128)S(1)} collective-permute-done((f32[4,160,256]{2,1,0:T(8,128)S(1)}, f32[4,160,256]{2,1,0:T(8,128)S(1)}, u32[]{:S(2)}, u32[]{:S(2)}) %collective-permute-start.25) | collective-permute-done | bytes 655392 | tf_op jit(solution)/shard_map/ppermute | solution.py:395
  98.8 1.3 collective-permute-start.26
  100.7 1.7 %collective-permute-start.28 = (f32[160,256]{1,0:T(8,128)S(1)}, f32[160,256]{1,0:T(8,128)S(1)}, u32[]{:S(2)}, u32[]{:S(2)}) collective-permute-start(f32[160,256]{1,0:T(8,128)S(1)} %get-tuple-element.81), channel_id=1, source_target_pairs={{0,6},{2,4},{4,2},{6,0},{8,14},{10,12},{12,10},{14,8},{16,22},{18,... | collective-permute-start | bytes 491528 | tf_op jit(solution)/shard_map/ppermute | solution.py:398
  102.4 1.7 %illumination.3.illum = f32[256,512]{1,0:T(8,128)S(1)} custom-call(s32[26]{0:T(128)S(1)} %concatenate.9.info, f32[2,256,256]{2,1,0:T(8,128)S(1)} %get-tuple-element.66.refs_0_.own, f32[2,256,256]{2,1,0:T(8,128)S(1)} %get-tuple-element.67.refs_1_.other), custom_call_target="tpu_custom_call" | custom-call | bytes 1572968 | tf_op jit(solution)/shard_map/illumination/pallas_call | solution.py:369
  104.1 1.9 %collective-permute-done.26 = f32[160,256]{1,0:T(8,128)S(1)} collective-permute-done((f32[160,256]{1,0:T(8,128)S(1)}, f32[160,256]{1,0:T(8,128)S(1)}, u32[]{:S(2)}, u32[]{:S(2)}) %collective-permute-start.26) | collective-permute-done | bytes 163872 | tf_op jit(solution)/shard_map/ppermute | solution.py:398
  106.9 2.7 %collective-permute-done.28 = f32[160,256]{1,0:T(8,128)S(1)} collective-permute-done((f32[160,256]{1,0:T(8,128)S(1)}, f32[160,256]{1,0:T(8,128)S(1)}, u32[]{:S(2)}, u32[]{:S(2)}) %collective-permute-start.28) | collective-permute-done | bytes 163872 | tf_op jit(solution)/shard_map/ppermute | solution.py:398
  109.6 3.8 %collective-permute-start.29 = (f32[160,256]{1,0:T(8,128)S(1)}, f32[160,256]{1,0:T(8,128)S(1)}, u32[]{:S(2)}, u32[]{:S(2)}) collective-permute-start(f32[160,256]{1,0:T(8,128)S(1)} %fusion.6), channel_id=1, source_target_pairs={{0,8},{2,10},{4,12},{6,14},{8,0},{10,2},{12,4},{14,6},{16,24},{18,... | collective-permute-start | bytes 491528 | tf_op jit(solution)/shard_map/ppermute | solution.py:398
  113.4 3.5 %collective-permute-done.29 = f32[160,256]{1,0:T(8,128)S(1)} collective-permute-done((f32[160,256]{1,0:T(8,128)S(1)}, f32[160,256]{1,0:T(8,128)S(1)}, u32[]{:S(2)}, u32[]{:S(2)}) %collective-permute-start.29) | collective-permute-done | bytes 163872 | tf_op jit(solution)/shard_map/ppermute | solution.py:398
  117.0 2.7 %collective-permute-start.30 = (f32[160,256]{1,0:T(8,128)S(1)}, f32[160,256]{1,0:T(8,128)S(1)}, u32[]{:S(2)}, u32[]{:S(2)}) collective-permute-start(f32[160,256]{1,0:T(8,128)S(1)} %add.111), channel_id=1, source_target_pairs={{0,16},{2,18},{4,20},{6,22},{8,24},{10,26},{12,28},{14,30},{16,0},... | collective-permute-start | bytes 491528 | tf_op jit(solution)/shard_map/ppermute | solution.py:398
  119.7 2.6 %collective-permute-start.35 = (f32[2,128,256]{2,1,0:T(8,128)S(1)}, f32[2,128,256]{2,1,0:T(8,128)S(1)}, u32[]{:S(2)}, u32[]{:S(2)}) collective-permute-start(f32[2,128,256]{2,1,0:T(8,128)S(1)} %get-tuple-element.76), channel_id=1, source_target_pairs={{0,2},{2,4},{4,6},{6,8},{8,10},{10,12},{12,14},{14,16},{16,18},{18... | collective-permute-start | bytes 786440 | tf_op jit(solution)/shard_map/ppermute | solution.py:414
  122.2 1.3 collective-permute-start.36
  123.6 2.5 %collective-permute-done.30 = f32[160,256]{1,0:T(8,128)S(1)} collective-permute-done((f32[160,256]{1,0:T(8,128)S(1)}, f32[160,256]{1,0:T(8,128)S(1)}, u32[]{:S(2)}, u32[]{:S(2)}) %collective-permute-start.30) | collective-permute-done | bytes 163872 | tf_op jit(solution)/shard_map/ppermute | solution.py:398
  126.1 1.2 collective-permute-start.31
  127.8 4.8 %collective-permute-done.35.b0 = f32[2,128,256]{2,1,0:T(8,128)S(1)} collective-permute-done((f32[2,128,256]{2,1,0:T(8,128)S(1)}, f32[2,128,256]{2,1,0:T(8,128)S(1)}, u32[]{:S(2)}, u32[]{:S(2)}) %collective-permute-start.35) | collective-permute-done | bytes 262176 | tf_op jit(solution)/shard_map/ppermute | solution.py:414
  132.6 3.9 %collective-permute-done.36.a0 = f32[2,128,256]{2,1,0:T(8,128)S(1)} collective-permute-done((f32[2,128,256]{2,1,0:T(8,128)S(1)}, f32[2,128,256]{2,1,0:T(8,128)S(1)}, u32[]{:S(2)}, u32[]{:S(2)}) %collective-permute-start.36) | collective-permute-done | bytes 262176 | tf_op jit(solution)/shard_map/ppermute | solution.py:417
  136.6 1.8 %collective-permute-done.31 = f32[160,256]{1,0:T(8,128)S(1)} collective-permute-done((f32[160,256]{1,0:T(8,128)S(1)}, f32[160,256]{1,0:T(8,128)S(1)}, u32[]{:S(2)}, u32[]{:S(2)}) %collective-permute-start.31) | collective-permute-done | bytes 163872 | tf_op jit(solution)/shard_map/ppermute | solution.py:398
  139.9 3.1 %update.3 = f32[2,256,512]{2,1,0:T(8,128)} custom-call(s32[26]{0:T(128)S(1)} %concatenate.9.info, f32[2,256,512]{2,1,0:T(8,128)S(1)} %get-tuple-element.58.strip_ref, f32[256,512]{1,0:T(8,128)S(1)} %illumination.3.illum, f32[2,256,256]{2,1,0:T(8,128)S(1)} %get-tuple-element.75.own, f32[2,256,256]{2,1,0:T(8,128)S(1)} %collective-permute-done.34.other, ...), custom_call_target="tpu_custom_call" | custom-call | bytes 4718696 | tf_op jit(solution)/shard_map/update/pallas_call | solution.py:369
  143.2 1.2 collective-permute-done.39.other_totals
  144.4 1.4 probe.3
  (84 shorter events, 16.2 us)
Async XLA Ops:
  0.6 14.4 %copy-start.1 = (f32[2,2,256,256]{3,2,1,0:T(8,128)S(1)}, f32[2,2,256,256]{3,2,1,0:T(8,128)}, u32[]{:S(2)}) copy-start(f32[2,2,256,256]{3,2,1,0:T(8,128)} %measured.1) | copy-start | bytes 3145732
  2.6 6.4 %copy-start.9 = (s32[2,2,2]{2,1,0:T(2,128)S(1)}, s32[2,2,2]{2,1,0:T(2,128)}, u32[]{:S(2)}) copy-start(s32[2,2,2]{2,1,0:T(2,128)} %param.7) | copy-start | bytes 100
  2.6 18.4 %collective-permute-start = (f32[128,512]{1,0:T(8,128)}, f32[128,512]{1,0:T(8,128)S(1)}, u32[]{:S(2)}, u32[]{:S(2)}) collective-permute-start(f32[128,512]{1,0:T(8,128)} %get-tuple-element.87), channel_id=1, source_target_pairs={{0,2},{2,4},{4,6},{6,8},{8,10},{10,12},{12,14},{14,16},{16,18},{18... | collective-permute-start | bytes 786440 | tf_op jit(solution)/shard_map/ppermute | solution.py:414
  7.6 13.5 %collective-permute-start.1 = (f32[128,512]{1,0:T(8,128)}, f32[128,512]{1,0:T(8,128)}, u32[]{:S(2)}, u32[]{:S(2)}) collective-permute-start(f32[128,512]{1,0:T(8,128)} %get-tuple-element.86), channel_id=1, source_target_pairs={{2,0},{4,2},{6,4},{8,6},{10,8},{12,10},{14,12},{16,14},{18,16},{20... | collective-permute-start | bytes 786440 | tf_op jit(solution)/shard_map/ppermute | solution.py:417
  8.9 14.4 %collective-permute-start.6 = (f32[2,256,256]{2,1,0:T(8,128)}, f32[2,256,256]{2,1,0:T(8,128)S(1)}, u32[]{:S(2)}, u32[]{:S(2)}) collective-permute-start(f32[2,256,256]{2,1,0:T(8,128)} %bitcast.44), channel_id=1, source_target_pairs={{0,1},{1,0},{2,3},{3,2},{4,5},{5,4},{6,7},{7,6},{8,9},{9,8},{10,11... | collective-permute-start | bytes 1572872 | tf_op jit(solution)/shard_map/ppermute | solution.py:395
  9.0 10.1 %collective-permute-start.2 = (s32[2,2,2]{2,1,0:T(2,128)S(1)}, s32[2,2,2]{2,1,0:T(2,128)S(1)}, u32[]{:S(2)}, u32[]{:S(2)}) collective-permute-start(s32[2,2,2]{2,1,0:T(2,128)S(1)} %copy-done.9), channel_id=1, source_target_pairs={{0,2},{2,4},{4,6},{6,8},{8,10},{10,12},{12,14},{14,16},{16,18},{18... | collective-permute-start | bytes 104 | tf_op jit(solution)/shard_map/ppermute | solution.py:414
  13.5 7.5 %collective-permute-start.3 = (s32[2,2,2]{2,1,0:T(2,128)S(1)}, s32[2,2,2]{2,1,0:T(2,128)S(1)}, u32[]{:S(2)}, u32[]{:S(2)}) collective-permute-start(s32[2,2,2]{2,1,0:T(2,128)S(1)} %copy-done.9), channel_id=1, source_target_pairs={{2,0},{4,2},{6,4},{8,6},{10,8},{12,10},{14,12},{16,14},{18,16},{20... | collective-permute-start | bytes 104 | tf_op jit(solution)/shard_map/ppermute | solution.py:417
  17.1 6.2 %copy-start = (f32[2,256,512]{2,1,0:T(8,128)S(1)}, f32[2,256,512]{2,1,0:T(8,128)}, u32[]{:S(2)}) copy-start(f32[2,256,512]{2,1,0:T(8,128)} %strip_ref.3) | copy-start | bytes 3145732
  17.8 11.9 %copy-start.4 = (f32[2,256,256]{2,1,0:T(8,128)}, f32[2,256,256]{2,1,0:T(8,128)S(1)}, u32[]{:S(2)}) copy-start(f32[2,256,256]{2,1,0:T(8,128)S(1)} %get-tuple-element.49.refs_6_.refs_2_) | copy-start | bytes 1572868
  17.8 11.9 %copy-start.6 = (bf16[4,256,256]{2,1,0:T(8,128)(2,1)}, bf16[4,256,256]{2,1,0:T(8,128)(2,1)S(1)}, u32[]{:S(2)}) copy-start(bf16[4,256,256]{2,1,0:T(8,128)(2,1)S(1)} %get-tuple-element.50.refs_7_.refs_3_) | copy-start | bytes 1572868
  21.0 2.2 %copy-start.10 = (s32[2,2,2]{2,1,0:T(2,128)}, s32[2,2,2]{2,1,0:T(2,128)S(1)}, u32[]{:S(2)}) copy-start(s32[2,2,2]{2,1,0:T(2,128)S(1)} %collective-permute-done.3) | copy-start | bytes 100
  21.1 1.6 %collective-permute-start.4 = (f32[128,512]{1,0:T(8,128)S(1)}, f32[128,512]{1,0:T(8,128)S(1)}, u32[]{:S(2)}, u32[]{:S(2)}) collective-permute-start(f32[128,512]{1,0:T(8,128)S(1)} %collective-permute-done.refs_0_), channel_id=1, source_target_pairs={{0,1},{1,0},{2,3},{3,2},{4,5},{5,4},{6,7},{7,6},{8,9},{9,8},{10,11... | collective-permute-start | bytes 786440 | tf_op jit(solution)/shard_map/ppermute | solution.py:395
  21.1 2.1 %collective-permute-start.5 = (f32[128,512]{1,0:T(8,128)}, f32[128,512]{1,0:T(8,128)S(1)}, u32[]{:S(2)}, u32[]{:S(2)}) collective-permute-start(f32[128,512]{1,0:T(8,128)} %collective-permute-done.1.refs_2_), channel_id=1, source_target_pairs={{0,1},{1,0},{2,3},{3,2},{4,5},{5,4},{6,7},{7,6},{8,9},{9,8},{10,11... | collective-permute-start | bytes 786440 | tf_op jit(solution)/shard_map/ppermute | solution.py:395
  29.7 4.9 %collective-permute-start.12 = (f32[4,160,256]{2,1,0:T(8,128)S(1)}, f32[4,160,256]{2,1,0:T(8,128)S(1)}, u32[]{:S(2)}, u32[]{:S(2)}) collective-permute-start(f32[4,160,256]{2,1,0:T(8,128)S(1)} %get-tuple-element.60), channel_id=1, source_target_pairs={{0,1},{1,0},{2,3},{3,2},{4,5},{5,4},{6,7},{7,6},{8,9},{9,8},{10,11... | collective-permute-start | bytes 1966088 | tf_op jit(solution)/shard_map/ppermute | solution.py:395
  29.8 15.2 %collective-permute-start.7 = (f32[2,128,256]{2,1,0:T(8,128)}, f32[2,128,256]{2,1,0:T(8,128)S(1)}, u32[]{:S(2)}, u32[]{:S(2)}) collective-permute-start(f32[2,128,256]{2,1,0:T(8,128)} %get-tuple-element.52), channel_id=1, source_target_pairs={{0,2},{2,4},{4,6},{6,8},{8,10},{10,12},{12,14},{14,16},{16,18},{18... | collective-permute-start | bytes 786440 | tf_op jit(solution)/shard_map/ppermute | solution.py:414
  33.2 14.4 %collective-permute-start.8 = (f32[2,128,256]{2,1,0:T(8,128)}, f32[2,128,256]{2,1,0:T(8,128)}, u32[]{:S(2)}, u32[]{:S(2)}) collective-permute-start(f32[2,128,256]{2,1,0:T(8,128)} %get-tuple-element.53), channel_id=1, source_target_pairs={{2,0},{4,2},{6,4},{8,6},{10,8},{12,10},{14,12},{16,14},{18,16},{20... | collective-permute-start | bytes 786440 | tf_op jit(solution)/shard_map/ppermute | solution.py:417
  35.5 15.6 %collective-permute-start.13 = (f32[160,256]{1,0:T(8,128)}, f32[160,256]{1,0:T(8,128)}, u32[]{:S(2)}, u32[]{:S(2)}) collective-permute-start(f32[160,256]{1,0:T(8,128)} %get-tuple-element.83), channel_id=1, source_target_pairs={{0,2},{2,0},{4,6},{6,4},{8,10},{10,8},{12,14},{14,12},{16,18},{18,... | collective-permute-start | bytes 491528 | tf_op jit(solution)/shard_map/ppermute | solution.py:398
  38.2 3.7 %copy-start.11 = (s32[2,2,2]{2,1,0:T(2,128)S(1)}, s32[2,2,2]{2,1,0:T(2,128)}, u32[]{:S(2)}) copy-start(s32[2,2,2]{2,1,0:T(2,128)} %copy-done.10) | copy-start | bytes 100
  38.2 12.9 %collective-permute-start.14 = (f32[160,256]{1,0:T(8,128)}, f32[160,256]{1,0:T(8,128)}, u32[]{:S(2)}, u32[]{:S(2)}) collective-permute-start(f32[160,256]{1,0:T(8,128)} %get-tuple-element.85), channel_id=1, source_target_pairs={{0,4},{2,6},{4,0},{6,2},{8,12},{10,14},{12,8},{14,10},{16,20},{18,... | collective-permute-start | bytes 491528 | tf_op jit(solution)/shard_map/ppermute | solution.py:398
  41.3 12.0 %collective-permute-start.15 = (f32[160,256]{1,0:T(8,128)}, f32[160,256]{1,0:T(8,128)}, u32[]{:S(2)}, u32[]{:S(2)}) collective-permute-start(f32[160,256]{1,0:T(8,128)} %get-tuple-element.84), channel_id=1, source_target_pairs={{0,6},{2,4},{4,2},{6,0},{8,14},{10,12},{12,10},{14,8},{16,22},{18,... | collective-permute-start | bytes 491528 | tf_op jit(solution)/shard_map/ppermute | solution.py:398
  47.6 14.3 %collective-permute-start.9 = (f32[2,256,256]{2,1,0:T(8,128)S(1)}, f32[2,256,256]{2,1,0:T(8,128)S(1)}, u32[]{:S(2)}, u32[]{:S(2)}) collective-permute-start(f32[2,256,256]{2,1,0:T(8,128)S(1)} %get-tuple-element.55.own), channel_id=1, source_target_pairs={{0,1},{1,0},{2,3},{3,2},{4,5},{5,4},{6,7},{7,6},{8,9},{9,8},{10,11... | collective-permute-start | bytes 1572872 | tf_op jit(solution)/shard_map/ppermute | solution.py:395
  47.6 14.1 %collective-permute-start.10 = (f32[2,128,256]{2,1,0:T(8,128)S(1)}, f32[2,128,256]{2,1,0:T(8,128)S(1)}, u32[]{:S(2)}, u32[]{:S(2)}) collective-permute-start(f32[2,128,256]{2,1,0:T(8,128)S(1)} %collective-permute-done.7.b0), channel_id=1, source_target_pairs={{0,1},{1,0},{2,3},{3,2},{4,5},{5,4},{6,7},{7,6},{8,9},{9,8},{10,11... | collective-permute-start | bytes 786440 | tf_op jit(solution)/shard_map/ppermute | solution.py:395
  51.1 10.8 %collective-permute-start.11 = (f32[2,128,256]{2,1,0:T(8,128)}, f32[2,128,256]{2,1,0:T(8,128)S(1)}, u32[]{:S(2)}, u32[]{:S(2)}) collective-permute-start(f32[2,128,256]{2,1,0:T(8,128)} %collective-permute-done.8.a0), channel_id=1, source_target_pairs={{0,1},{1,0},{2,3},{3,2},{4,5},{5,4},{6,7},{7,6},{8,9},{9,8},{10,11... | collective-permute-start | bytes 786440 | tf_op jit(solution)/shard_map/ppermute | solution.py:395
  54.5 14.7 %collective-permute-start.16 = (f32[160,256]{1,0:T(8,128)S(1)}, f32[160,256]{1,0:T(8,128)S(1)}, u32[]{:S(2)}, u32[]{:S(2)}) collective-permute-start(f32[160,256]{1,0:T(8,128)S(1)} %fusion.13), channel_id=1, source_target_pairs={{0,8},{2,10},{4,12},{6,14},{8,0},{10,2},{12,4},{14,6},{16,24},{18,... | collective-permute-start | bytes 491528 | tf_op jit(solution)/shard_map/ppermute | solution.py:398
  59.4 15.0 %collective-permute-start.17 = (f32[160,256]{1,0:T(8,128)S(1)}, f32[160,256]{1,0:T(8,128)S(1)}, u32[]{:S(2)}, u32[]{:S(2)}) collective-permute-start(f32[160,256]{1,0:T(8,128)S(1)} %fusion.13), channel_id=1, source_target_pairs={{0,16},{2,18},{4,20},{6,22},{8,24},{10,26},{12,28},{14,30},{16,0},... | collective-permute-start | bytes 491528 | tf_op jit(solution)/shard_map/ppermute | solution.py:398
  61.7 12.7 %collective-permute-start.18 = (f32[160,256]{1,0:T(8,128)S(1)}, f32[160,256]{1,0:T(8,128)S(1)}, u32[]{:S(2)}, u32[]{:S(2)}) collective-permute-start(f32[160,256]{1,0:T(8,128)S(1)} %fusion.13), channel_id=1, source_target_pairs={{0,24},{2,26},{4,28},{6,30},{8,16},{10,18},{12,20},{14,22},{16,8},... | collective-permute-start | bytes 491528 | tf_op jit(solution)/shard_map/ppermute | solution.py:398
  64.7 9.8 %collective-permute-start.19 = (f32[2,128,256]{2,1,0:T(8,128)S(1)}, f32[2,128,256]{2,1,0:T(8,128)S(1)}, u32[]{:S(2)}, u32[]{:S(2)}) collective-permute-start(f32[2,128,256]{2,1,0:T(8,128)S(1)} %get-tuple-element.61), channel_id=1, source_target_pairs={{0,2},{2,4},{4,6},{6,8},{8,10},{10,12},{12,14},{14,16},{16,18},{18... | collective-permute-start | bytes 786440 | tf_op jit(solution)/shard_map/ppermute | solution.py:414
  67.7 10.8 %collective-permute-start.20 = (f32[2,128,256]{2,1,0:T(8,128)S(1)}, f32[2,128,256]{2,1,0:T(8,128)S(1)}, u32[]{:S(2)}, u32[]{:S(2)}) collective-permute-start(f32[2,128,256]{2,1,0:T(8,128)S(1)} %get-tuple-element.62), channel_id=1, source_target_pairs={{2,0},{4,2},{6,4},{8,6},{10,8},{12,10},{14,12},{16,14},{18,16},{20... | collective-permute-start | bytes 786440 | tf_op jit(solution)/shard_map/ppermute | solution.py:417
  78.4 6.0 %collective-permute-start.21 = (f32[160,256]{1,0:T(8,128)S(1)}, f32[160,256]{1,0:T(8,128)S(1)}, u32[]{:S(2)}, u32[]{:S(2)}) collective-permute-start(f32[160,256]{1,0:T(8,128)S(1)} %add_add_fusion), channel_id=1, source_target_pairs={{0,2},{2,0},{4,6},{6,4},{8,10},{10,8},{12,14},{14,12},{16,18},{18,... | collective-permute-start | bytes 491528 | tf_op jit(solution)/shard_map/ppermute | solution.py:398
  79.8 9.3 %collective-permute-start.22 = (f32[160,256]{1,0:T(8,128)S(1)}, f32[160,256]{1,0:T(8,128)S(1)}, u32[]{:S(2)}, u32[]{:S(2)}) collective-permute-start(f32[160,256]{1,0:T(8,128)S(1)} %add_add_fusion), channel_id=1, source_target_pairs={{0,4},{2,6},{4,0},{6,2},{8,12},{10,14},{12,8},{14,10},{16,20},{18,... | collective-permute-start | bytes 491528 | tf_op jit(solution)/shard_map/ppermute | solution.py:398
  82.3 6.8 %collective-permute-start.23 = (f32[160,256]{1,0:T(8,128)S(1)}, f32[160,256]{1,0:T(8,128)S(1)}, u32[]{:S(2)}, u32[]{:S(2)}) collective-permute-start(f32[160,256]{1,0:T(8,128)S(1)} %add_add_fusion), channel_id=1, source_target_pairs={{0,6},{2,4},{4,2},{6,0},{8,14},{10,12},{12,10},{14,8},{16,22},{18,... | collective-permute-start | bytes 491528 | tf_op jit(solution)/shard_map/ppermute | solution.py:398
  89.2 2.2 %collective-permute-start.24 = (f32[4,160,256]{2,1,0:T(8,128)S(1)}, f32[4,160,256]{2,1,0:T(8,128)S(1)}, u32[]{:S(2)}, u32[]{:S(2)}) collective-permute-start(f32[4,160,256]{2,1,0:T(8,128)S(1)} %pad_maximum_fusion.own_totals), channel_id=1, source_target_pairs={{0,1},{1,0},{2,3},{3,2},{4,5},{5,4},{6,7},{7,6},{8,9},{9,8},{10,11... | collective-permute-start | bytes 1966088 | tf_op jit(solution)/shard_map/ppermute | solution.py:395
  90.3 1.8 %copy-start.5 = (f32[2,256,256]{2,1,0:T(8,128)S(1)}, f32[2,256,256]{2,1,0:T(8,128)}, u32[]{:S(2)}) copy-start(f32[2,256,256]{2,1,0:T(8,128)} %copy-done.4) | copy-start | bytes 1572868
  96.6 2.2 %collective-permute-start.25 = (f32[4,160,256]{2,1,0:T(8,128)S(1)}, f32[4,160,256]{2,1,0:T(8,128)S(1)}, u32[]{:S(2)}, u32[]{:S(2)}) collective-permute-start(f32[4,160,256]{2,1,0:T(8,128)S(1)} %get-tuple-element.72), channel_id=1, source_target_pairs={{0,1},{1,0},{2,3},{3,2},{4,5},{5,4},{6,7},{7,6},{8,9},{9,8},{10,11... | collective-permute-start | bytes 1966088 | tf_op jit(solution)/shard_map/ppermute | solution.py:395
  98.8 7.1 %collective-permute-start.26 = (f32[160,256]{1,0:T(8,128)S(1)}, f32[160,256]{1,0:T(8,128)S(1)}, u32[]{:S(2)}, u32[]{:S(2)}) collective-permute-start(f32[160,256]{1,0:T(8,128)S(1)} %get-tuple-element.80), channel_id=1, source_target_pairs={{0,2},{2,0},{4,6},{6,4},{8,10},{10,8},{12,14},{14,12},{16,18},{18,... | collective-permute-start | bytes 491528 | tf_op jit(solution)/shard_map/ppermute | solution.py:398
  100.1 6.8 %collective-permute-start.27 = (f32[160,256]{1,0:T(8,128)S(1)}, f32[160,256]{1,0:T(8,128)S(1)}, u32[]{:S(2)}, u32[]{:S(2)}) collective-permute-start(f32[160,256]{1,0:T(8,128)S(1)} %get-tuple-element.82), channel_id=1, source_target_pairs={{0,4},{2,6},{4,0},{6,2},{8,12},{10,14},{12,8},{14,10},{16,20},{18,... | collective-permute-start | bytes 491528 | tf_op jit(solution)/shard_map/ppermute | solution.py:398
  100.7 8.9 %collective-permute-start.28 = (f32[160,256]{1,0:T(8,128)S(1)}, f32[160,256]{1,0:T(8,128)S(1)}, u32[]{:S(2)}, u32[]{:S(2)}) collective-permute-start(f32[160,256]{1,0:T(8,128)S(1)} %get-tuple-element.81), channel_id=1, source_target_pairs={{0,6},{2,4},{4,2},{6,0},{8,14},{10,12},{12,10},{14,8},{16,22},{18,... | collective-permute-start | bytes 491528 | tf_op jit(solution)/shard_map/ppermute | solution.py:398
  109.6 7.3 %collective-permute-start.29 = (f32[160,256]{1,0:T(8,128)S(1)}, f32[160,256]{1,0:T(8,128)S(1)}, u32[]{:S(2)}, u32[]{:S(2)}) collective-permute-start(f32[160,256]{1,0:T(8,128)S(1)} %fusion.6), channel_id=1, source_target_pairs={{0,8},{2,10},{4,12},{6,14},{8,0},{10,2},{12,4},{14,6},{16,24},{18,... | collective-permute-start | bytes 491528 | tf_op jit(solution)/shard_map/ppermute | solution.py:398
  117.0 9.2 %collective-permute-start.30 = (f32[160,256]{1,0:T(8,128)S(1)}, f32[160,256]{1,0:T(8,128)S(1)}, u32[]{:S(2)}, u32[]{:S(2)}) collective-permute-start(f32[160,256]{1,0:T(8,128)S(1)} %add.111), channel_id=1, source_target_pairs={{0,16},{2,18},{4,20},{6,22},{8,24},{10,26},{12,28},{14,30},{16,0},... | collective-permute-start | bytes 491528 | tf_op jit(solution)/shard_map/ppermute | solution.py:398
  119.7 13.0 %collective-permute-start.35 = (f32[2,128,256]{2,1,0:T(8,128)S(1)}, f32[2,128,256]{2,1,0:T(8,128)S(1)}, u32[]{:S(2)}, u32[]{:S(2)}) collective-permute-start(f32[2,128,256]{2,1,0:T(8,128)S(1)} %get-tuple-element.76), channel_id=1, source_target_pairs={{0,2},{2,4},{4,6},{6,8},{8,10},{10,12},{12,14},{14,16},{16,18},{18... | collective-permute-start | bytes 786440 | tf_op jit(solution)/shard_map/ppermute | solution.py:414
  122.2 14.3 %collective-permute-start.36 = (f32[2,128,256]{2,1,0:T(8,128)S(1)}, f32[2,128,256]{2,1,0:T(8,128)S(1)}, u32[]{:S(2)}, u32[]{:S(2)}) collective-permute-start(f32[2,128,256]{2,1,0:T(8,128)S(1)} %get-tuple-element.77), channel_id=1, source_target_pairs={{2,0},{4,2},{6,4},{8,6},{10,8},{12,10},{14,12},{16,14},{18,16},{20... | collective-permute-start | bytes 786440 | tf_op jit(solution)/shard_map/ppermute | solution.py:417
  123.5 15.4 %collective-permute-start.34 = (f32[2,256,256]{2,1,0:T(8,128)S(1)}, f32[2,256,256]{2,1,0:T(8,128)S(1)}, u32[]{:S(2)}, u32[]{:S(2)}) collective-permute-start(f32[2,256,256]{2,1,0:T(8,128)S(1)} %get-tuple-element.75.own), channel_id=1, source_target_pairs={{0,1},{1,0},{2,3},{3,2},{4,5},{5,4},{6,7},{7,6},{8,9},{9,8},{10,11... | collective-permute-start | bytes 1572872 | tf_op jit(solution)/shard_map/ppermute | solution.py:395
  126.1 12.2 %collective-permute-start.31 = (f32[160,256]{1,0:T(8,128)S(1)}, f32[160,256]{1,0:T(8,128)S(1)}, u32[]{:S(2)}, u32[]{:S(2)}) collective-permute-start(f32[160,256]{1,0:T(8,128)S(1)} %add.112), channel_id=1, source_target_pairs={{0,2},{2,0},{4,6},{6,4},{8,10},{10,8},{12,14},{14,12},{16,18},{18,... | collective-permute-start | bytes 491528 | tf_op jit(solution)/shard_map/ppermute | solution.py:398
  127.3 11.0 %collective-permute-start.32 = (f32[160,256]{1,0:T(8,128)S(1)}, f32[160,256]{1,0:T(8,128)S(1)}, u32[]{:S(2)}, u32[]{:S(2)}) collective-permute-start(f32[160,256]{1,0:T(8,128)S(1)} %add.112), channel_id=1, source_target_pairs={{0,4},{2,6},{4,0},{6,2},{8,12},{10,14},{12,8},{14,10},{16,20},{18,... | collective-permute-start | bytes 491528 | tf_op jit(solution)/shard_map/ppermute | solution.py:398
  132.6 6.2 %collective-permute-start.33 = (f32[160,256]{1,0:T(8,128)S(1)}, f32[160,256]{1,0:T(8,128)S(1)}, u32[]{:S(2)}, u32[]{:S(2)}) collective-permute-start(f32[160,256]{1,0:T(8,128)S(1)} %add.112), channel_id=1, source_target_pairs={{0,6},{2,4},{4,2},{6,0},{8,14},{10,12},{12,10},{14,8},{16,22},{18,... | collective-permute-start | bytes 491528 | tf_op jit(solution)/shard_map/ppermute | solution.py:398
  136.6 2.3 %collective-permute-start.37 = (f32[2,128,256]{2,1,0:T(8,128)S(1)}, f32[2,128,256]{2,1,0:T(8,128)S(1)}, u32[]{:S(2)}, u32[]{:S(2)}) collective-permute-start(f32[2,128,256]{2,1,0:T(8,128)S(1)} %collective-permute-done.35.b0), channel_id=1, source_target_pairs={{0,1},{1,0},{2,3},{3,2},{4,5},{5,4},{6,7},{7,6},{8,9},{9,8},{10,11... | collective-permute-start | bytes 786440 | tf_op jit(solution)/shard_map/ppermute | solution.py:395
  138.3 1.5 %collective-permute-start.38 = (f32[2,128,256]{2,1,0:T(8,128)S(1)}, f32[2,128,256]{2,1,0:T(8,128)S(1)}, u32[]{:S(2)}, u32[]{:S(2)}) collective-permute-start(f32[2,128,256]{2,1,0:T(8,128)S(1)} %collective-permute-done.36.a0), channel_id=1, source_target_pairs={{0,1},{1,0},{2,3},{3,2},{4,5},{5,4},{6,7},{7,6},{8,9},{9,8},{10,11... | collective-permute-start | bytes 786440 | tf_op jit(solution)/shard_map/ppermute | solution.py:395
  143.0 1.4 collective-permute-start.39
  (5 other events, 5.5 us)

commit v2 on v1

--- a/solution.py
+++ b/solution.py
@@ -13,6 +13,7 @@
 BF16 = jnp.bfloat16
 VMEM_BYTES = 16 * 1024 * 1024
 GROUP = 4
+UNITS = ((2, 1), (4, 8))
 
 
 def padded(block, sides, width):
@@ -140,6 +141,11 @@
     if side > 0:
         row = jnp.where(tile == tiles - 1, strip + pattern, row)
     return row, info[place + 1]
+
+
+def mates(tile):
+    line = lax.div(tile, GROUP)
+    return lax.rem(tile, GROUP), 2 * lax.rem(line, 2) + lax.div(line, 2)
 
 
 def take_columns(block, column, width):
@@ -291,20 +297,20 @@
     ):
         gradient[part], top[part], bottom[part] = value, value[:half], value[half:]
     coverage = obj_real * obj_real + obj_imag * obj_imag
-    rows = pattern // GROUP
-    mate = lax.rem(info[24], GROUP)
+    rows = pattern // (2 * GROUP)
     for step, keeper, (cr, ci) in ((step_own, slot, chi[0]), (step_other, 1 - slot, chi[1])):
         real = obj_real * cr + obj_imag * ci
         imag = obj_real * ci - obj_imag * cr
-        for k in range(GROUP):
-            start = k * rows
-            block = step.at[mate ^ k]
-            block[:rows] = real[start : start + rows]
-            block[rows : 2 * rows] = imag[start : start + rows]
-            middle = start + rows // 2
-            block[2 * rows :] = jnp.where(
-                keeper == 0, coverage[start:middle], coverage[middle : start + rows]
-            )
+        for which, mate in enumerate(mates(info[24])):
+            for k in range(GROUP):
+                start = (which * GROUP + k) * rows
+                block = step.at[which, mate ^ k]
+                block[:rows] = real[start : start + rows]
+                block[rows : 2 * rows] = imag[start : start + rows]
+                middle = start + rows // 2
+                block[2 * rows :] = jnp.where(
+                    keeper == 0, coverage[start:middle], coverage[middle : start + rows]
+                )
 
 
 def update_kernel(size, minibatch, info, strip_ref, illum, own, other, b0, a0, b1, a1, *outs):
@@ -338,24 +344,25 @@
 def probe_kernel(info, own_totals, other_totals, *refs):
     probes, outs = refs[: len(refs) // 2], refs[len(refs) // 2 :]
     slot = info[25]
-    rows = outs[0].shape[1] // GROUP
-    mate = lax.rem(info[24], GROUP)
-    for k in range(GROUP):
-        where = pl.ds(pl.multiple_of((mate ^ k) * rows, rows), rows)
-        mine, theirs = own_totals[k], other_totals[k]
-        own_half, other_half = mine[2 * rows :], theirs[theirs.shape[0] - rows // 2 :]
-        coverage = jnp.concatenate(
-            [
-                jnp.where(slot == 0, own_half, other_half),
-                jnp.where(slot == 0, other_half, own_half),
-            ],
-            axis=0,
-        )
-        divisor = coverage + 1.0
-        for totals, probe, out in zip((mine, theirs), probes, outs):
-            for part in range(2):
-                change = totals[part * rows : (part + 1) * rows] / divisor
-                out[part, where, :] = probe[part, where, :] + change
+    rows = outs[0].shape[1] // (2 * GROUP)
+    for which, mate in enumerate(mates(info[24])):
+        for k in range(GROUP):
+            start = which * GROUP * rows + pl.multiple_of((mate ^ k) * rows, rows)
+            where = pl.ds(start, rows)
+            mine, theirs = own_totals[which, k], other_totals[which, k]
+            own_half, other_half = mine[2 * rows :], theirs[theirs.shape[0] - rows // 2 :]
+            coverage = jnp.concatenate(
+                [
+                    jnp.where(slot == 0, own_half, other_half),
+                    jnp.where(slot == 0, other_half, own_half),
+                ],
+                axis=0,
+            )
+            divisor = coverage + 1.0
+            for totals, probe, out in zip((mine, theirs), probes, outs):
+                for part in range(2):
+                    change = totals[part * rows : (part + 1) * rows] / divisor
+                    out[part, where, :] = probe[part, where, :] + change
 
 
 def call(kernel, name, outs, inputs, scratch=(), flops=0):
@@ -397,18 +404,17 @@
     def across(value, k):
         return lax.ppermute(value, "tile", [(i, i ^ k) for i in range(tiles)])
 
-    def scatter(blocks, unit):
-        mates = [across(blocks[k], unit * k) for k in range(1, GROUP)]
-        return functools.reduce(jnp.add, mates, blocks[0])
-
-    def exchange(piece, unit, pairwise):
-        if pairwise:
+    def halve(kept, sent, units):
+        pair = kept + across(sent, units[0])
+        return pair[0] + across(pair[1], units[1])
+
+    def exchange(piece, units):
+        for unit in units:
             piece = piece + across(piece, unit)
-            return piece + across(piece, 2 * unit)
-        return scatter([piece] * GROUP, unit)
-
-    def gather(piece, unit):
-        return jnp.stack([piece] + [across(piece, unit * k) for k in range(1, GROUP)])
+        return piece
+
+    def double(block, unit):
+        return jnp.concatenate([block, across(block, unit)])
 
     def from_below(value):
         return lax.ppermute(value, "tile", up)
@@ -440,8 +446,8 @@
 
     for minibatch in range(2):
         last = minibatch == 1
-        rows = pattern // GROUP
-        blocks = (GROUP, 2 * rows + rows // 2, pattern)
+        rows = pattern // (2 * GROUP)
+        blocks = (2, GROUP, 2 * rows + rows // 2, pattern)
         cut = (object_field, *edges)
         if last:
             cut = call(
@@ -464,16 +470,21 @@
             [tall],
         )
         brought = swap(step_other)
-        steps = [step_own[k] + brought[k] for k in range(GROUP)]
-        piece = scatter(steps, 1)
+        kept, sent = ([step_own[i, at] + brought[i, at] for i in range(2)] for at in (slice(2), slice(2, 4)))
+        pieces = [halve(kept[i], sent[i], UNITS[i]) for i in range(2)]
         if last:
-            gradient, top, bottom, piece, illum = lax.optimization_barrier(
-                (gradient, top, bottom, piece, illum)
+            gradient, top, bottom, illum, pieces[0] = lax.optimization_barrier(
+                (gradient, top, bottom, illum, pieces[0])
             )
         rim_below, rim_above = from_below(bottom), from_above(top)
         if not last:
             gradient, rim_below, rim_above, illum = lax.optimization_barrier(
                 (gradient, rim_below, rim_above, illum)
+            )
+        pieces = [exchange(pieces[i], UNITS[1 - i])[None] for i in range(2)]
+        if last:
+            rim_below, rim_above, *pieces = lax.optimization_barrier(
+                (rim_below, rim_above, *pieces)
             )
         rims = (gradient, swap(gradient), rim_below, rim_above, swap(rim_below), swap(rim_above))
         object_field, *edges = call(
@@ -482,16 +493,16 @@
             [object_field.shape] + ([] if last else [rim] * 2),
             (info, object_field, illum, *rims),
             [tall],
-            flops=0,
-        )
-        piece = exchange(piece, GROUP, last)
+        )
+        pieces = [double(pieces[i], UNITS[i][1]) for i in range(2)]
         if not last:
-            edges = [from_below(edges[1]), from_above(edges[0])]
-            piece, *edges = lax.optimization_barrier((piece, *edges))
-        totals = gather(piece, 1)
+            pieces_and_edges = (*pieces, from_below(edges[1]), from_above(edges[0]))
+            *pieces, edge_below, edge_above = lax.optimization_barrier(pieces_and_edges)
+            edges = [edge_below, edge_above]
+        totals = jnp.stack([double(pieces[i], UNITS[i][0]) for i in range(2)])
         if last:
             totals, object_field = lax.optimization_barrier((totals, object_field))
-            others = swap(totals[:, 2 * rows :])
+            others = swap(totals[:, :, 2 * rows :])
             (own,) = call(probe_kernel, "probe", [field], (here, totals, others, own))
         else:
             own, other = call(

time: 147 us -> 158 us (1.075)
  waiting for transfers between devices: 56.4 us -> 67.1 us
    ppermute x17 -> x24, waiting for transfers between devices: 31.1 us -> 55.9 us  [across(): return lax.ppermute(value, 'tile', [(i, i ^ k) for i in range(tiles)])]
    ppermute x5, waiting for transfers between devices: 12.4 us -> 3.93 us  [from_above(): return lax.ppermute(value, 'tile', down)]
    ppermute x5, waiting for transfers between devices: 6.08 us -> 1.3 us  [from_below(): return lax.ppermute(value, 'tile', up)]
    ppermute x17 -> x24, starting transfers between devices: 28.8 us -> 27.8 us  [across(): return lax.ppermute(value, 'tile', [(i, i ^ k) for i in range(tiles)])]
  transfers between devices with their start and end apart: 40 -> 47, of which waited for: 24 -> 26; matrix products, arithmetic and copies ran while one was open for 3% -> 3% of each run, Pallas kernels for 5% -> 5%
where the time goes in v2:
time: 158 us; the launch traced here: 157 us
  waiting for transfers between devices  67.1 us (42%)
  starting transfers between devices  55.6 us (35%)
  Pallas kernels  23.9 us (15%)
  local copies, waits for them, and re-layouts  7.22 us (5%)
  other arithmetic  2.31 us (1%)
    ppermute x24, waiting for transfers between devices, across(): return lax.ppermute(value, 'tile', [(i, i ^ k) for i in range(tiles)])  55.9 us
    ppermute x24, starting transfers between devices, across(): return lax.ppermute(value, 'tile', [(i, i ^ k) for i in range(tiles)])  27.8 us
    pallas_call x10, Pallas kernels, call(): pl.pallas_call(kernel, out_shape=shapes, in_specs=[smem] + [vmem] * (len(...  23.9 us
    ppermute x5, starting transfers between devices, from_below(): return lax.ppermute(value, 'tile', up)  18.8 us
    ppermute x5, starting transfers between devices, from_above(): return lax.ppermute(value, 'tile', down)  6.64 us
    ppermute x13, waiting for transfers between devices, swap(): return lax.ppermute(value, 'mode', [(0, 1), (1, 0)])  6.01 us
    ppermute x5, waiting for transfers between devices, from_above(): return lax.ppermute(value, 'tile', down)  3.93 us
  transfers between devices with their start and end apart: 47, of which 26 were waited for; matrix products, arithmetic and copies ran while one was open for 3% of the time, Pallas kernels for 5%

profile of v2, /device:TPU:0, one launch (start us, length us, event | category | flops | bytes accessed | tf_op | source)
XLA Modules:
  0.0 157.3 jit_solution(694837430786123368)
XLA Ops:
  0.6 1.9 %dynamic-slice_bitcast_fusion = (f32[128,512]{1,0:T(8,128)}, f32[128,512]{1,0:T(8,128)}) fusion(f32[2,256,512]{2,1,0:T(8,128)} %strip_ref.3, s32[]{:T(128)S(6)} %select_n.4, s32[]{:T(128)S(6)} %add.133), kind=kLoop, calls=%fused_computation.6 | loop fusion | bytes 1048584 | tf_op jit(solution)/shard_map/slice | solution.py:432
  2.6 5.0 %collective-permute-start = (f32[128,512]{1,0:T(8,128)}, f32[128,512]{1,0:T(8,128)S(1)}, u32[]{:S(2)}, u32[]{:S(2)}) collective-permute-start(f32[128,512]{1,0:T(8,128)} %get-tuple-element.99), channel_id=1, source_target_pairs={{0,2},{2,4},{4,6},{6,8},{8,10},{10,12},{12,14},{14,16},{16,18},{18... | collective-permute-start | bytes 786440 | tf_op jit(solution)/shard_map/ppermute | solution.py:420
  7.6 1.3 collective-permute-start.1
  9.0 4.5 %collective-permute-start.2 = (s32[2,2,2]{2,1,0:T(2,128)S(1)}, s32[2,2,2]{2,1,0:T(2,128)S(1)}, u32[]{:S(2)}, u32[]{:S(2)}) collective-permute-start(s32[2,2,2]{2,1,0:T(2,128)S(1)} %copy-done.10), channel_id=1, source_target_pairs={{0,2},{2,4},{4,6},{6,8},{8,10},{10,12},{12,14},{14,16},{16,18},{18... | collective-permute-start | bytes 104 | tf_op jit(solution)/shard_map/ppermute | solution.py:420
  13.5 1.3 collective-permute-start.3
  17.8 1.3 collective-permute-done.2
  19.1 1.9 %collective-permute-done.3 = s32[2,2,2]{2,1,0:T(2,128)S(1)} collective-permute-done((s32[2,2,2]{2,1,0:T(2,128)S(1)}, s32[2,2,2]{2,1,0:T(2,128)S(1)}, u32[]{:S(2)}, u32[]{:S(2)}) %collective-permute-start.3) | collective-permute-done | bytes 64 | tf_op jit(solution)/shard_map/ppermute | solution.py:423
  23.2 6.4 %field.2 = (f32[2,256,256]{2,1,0:T(8,128)S(1)}, f32[2,128,256]{2,1,0:T(8,128)}, f32[2,128,256]{2,1,0:T(8,128)}, f32[2,4,80,256]{3,2,1,0:T(8,128)S(1)}, f32[2,4,80,256]{3,2,1,0:T(8,128)S(1)}) custom-call(s32[26]{0:T(128)S(1)} %concatenate.34.info, f32[2,256,512]{2,1,0:T(8,128)S(1)} %copy-done, f32[128,512]{1,0:T(8,128)S(1)} %collective-permute-done.refs_0_, ...), custom_call_target="tpu_custom_call" | custom-call | flops 3221225472 | bytes 6553704 | tf_op jit(solution)/shard_map/field/pallas_call | solution.py:376
  29.8 3.4 %collective-permute-start.7 = (f32[2,128,256]{2,1,0:T(8,128)}, f32[2,128,256]{2,1,0:T(8,128)S(1)}, u32[]{:S(2)}, u32[]{:S(2)}) collective-permute-start(f32[2,128,256]{2,1,0:T(8,128)} %get-tuple-element.57), channel_id=1, source_target_pairs={{0,2},{2,4},{4,6},{6,8},{8,10},{10,12},{12,14},{14,16},{16,18},{18... | collective-permute-start | bytes 786440 | tf_op jit(solution)/shard_map/ppermute | solution.py:420
  33.2 1.3 collective-permute-start.8
  36.2 3.7 %collective-permute-start.13 = (f32[2,80,256]{2,1,0:T(8,128)}, f32[2,80,256]{2,1,0:T(8,128)}, u32[]{:S(2)}, u32[]{:S(2)}) collective-permute-start(f32[2,80,256]{2,1,0:T(8,128)} %get-tuple-element.97), channel_id=1, source_target_pairs={{0,4},{2,6},{4,0},{6,2},{8,12},{10,14},{12,8},{14,10},{16,20},{18,... | collective-permute-start | bytes 491528 | tf_op jit(solution)/shard_map/ppermute | solution.py:405
  39.9 2.4 %collective-permute-start.18 = (f32[2,80,256]{2,1,0:T(8,128)}, f32[2,80,256]{2,1,0:T(8,128)}, u32[]{:S(2)}, u32[]{:S(2)}) collective-permute-start(f32[2,80,256]{2,1,0:T(8,128)} %get-tuple-element.96), channel_id=1, source_target_pairs={{0,8},{2,10},{4,12},{6,14},{8,0},{10,2},{12,4},{14,6},{16,24},{18,... | collective-permute-start | bytes 491528 | tf_op jit(solution)/shard_map/ppermute | solution.py:405
  44.3 1.7 %illumination.2.illum = f32[256,512]{1,0:T(8,128)S(1)} custom-call(s32[26]{0:T(128)S(1)} %concatenate.35.info, f32[2,256,256]{2,1,0:T(8,128)S(1)} %get-tuple-element.53.refs_4_.own.refs_0_, f32[2,256,256]{2,1,0:T(8,128)S(1)} %collective-permute-done.6.refs_5_.other.refs_1_), custom_call_target="tpu_custom_call" | custom-call | bytes 1572968 | tf_op jit(solution)/shard_map/illumination/pallas_call | solution.py:376
  47.6 3.1 %collective-permute-done.18 = f32[2,80,256]{2,1,0:T(8,128)} collective-permute-done((f32[2,80,256]{2,1,0:T(8,128)}, f32[2,80,256]{2,1,0:T(8,128)}, u32[]{:S(2)}, u32[]{:S(2)}) %collective-permute-start.18) | collective-permute-done | bytes 163872 | tf_op jit(solution)/shard_map/ppermute | solution.py:405
  51.7 2.7 %collective-permute-start.19 = (f32[80,256]{1,0:T(8,128)S(1)}, f32[80,256]{1,0:T(8,128)S(1)}, u32[]{:S(2)}, u32[]{:S(2)}) collective-permute-start(f32[80,256]{1,0:T(8,128)S(1)} %slice_bitcast_fusion.4), channel_id=1, source_target_pairs={{0,16},{2,18},{4,20},{6,22},{8,24},{10,26},{12,28},{14,30},{16,0},... | collective-permute-start | bytes 245768 | tf_op jit(solution)/shard_map/ppermute | solution.py:405
  54.4 1.3 collective-permute-start.14
  55.7 1.6 collective-permute-done.19
  57.3 2.1 %collective-permute-start.20 = (f32[80,256]{1,0:T(8,128)S(1)}, f32[80,256]{1,0:T(8,128)S(1)}, u32[]{:S(2)}, u32[]{:S(2)}) collective-permute-start(f32[80,256]{1,0:T(8,128)S(1)} %fusion.14), channel_id=1, source_target_pairs={{0,4},{2,6},{4,0},{6,2},{8,12},{10,14},{12,8},{14,10},{16,20},{18,... | collective-permute-start | bytes 245768 | tf_op jit(solution)/shard_map/ppermute | solution.py:405
  60.0 1.9 %collective-permute-done.20 = f32[80,256]{1,0:T(8,128)S(1)} collective-permute-done((f32[80,256]{1,0:T(8,128)S(1)}, f32[80,256]{1,0:T(8,128)S(1)}, u32[]{:S(2)}, u32[]{:S(2)}) %collective-permute-start.20) | collective-permute-done | bytes 81952 | tf_op jit(solution)/shard_map/ppermute | solution.py:405
  61.9 2.5 %collective-permute-start.21 = (f32[80,256]{1,0:T(8,128)S(1)}, f32[80,256]{1,0:T(8,128)S(1)}, u32[]{:S(2)}, u32[]{:S(2)}) collective-permute-start(f32[80,256]{1,0:T(8,128)S(1)} %add.115), channel_id=1, source_target_pairs={{0,2},{2,0},{4,6},{6,4},{8,10},{10,8},{12,14},{14,12},{16,18},{18,... | collective-permute-start | bytes 245768 | tf_op jit(solution)/shard_map/ppermute | solution.py:405
  64.4 2.8 %update.2 = (f32[2,256,512]{2,1,0:T(8,128)S(1)}, f32[2,128,256]{2,1,0:T(8,128)S(1)}, f32[2,128,256]{2,1,0:T(8,128)S(1)}) custom-call(s32[26]{0:T(128)S(1)} %concatenate.35.info, f32[2,256,512]{2,1,0:T(8,128)S(1)} %copy-done, f32[256,512]{1,0:T(8,128)S(1)} %illumination.2.illum, f32[2,256,256]{2,1,0:T(8,128)S(1)} %get-tuple-element.60.own, ...), custom_call_target="tpu_custom_call" | custom-call | bytes 5242984 | tf_op jit(solution)/shard_map/update/pallas_call | solution.py:376
  67.2 2.0 %collective-permute-start.23 = (f32[2,128,256]{2,1,0:T(8,128)S(1)}, f32[2,128,256]{2,1,0:T(8,128)S(1)}, u32[]{:S(2)}, u32[]{:S(2)}) collective-permute-start(f32[2,128,256]{2,1,0:T(8,128)S(1)} %get-tuple-element.66), channel_id=1, source_target_pairs={{0,2},{2,4},{4,6},{6,8},{8,10},{10,12},{12,14},{14,16},{16,18},{18... | collective-permute-start | bytes 786440 | tf_op jit(solution)/shard_map/ppermute | solution.py:420
  69.2 1.5 collective-permute-start.24
  70.7 5.8 %collective-permute-start.16 = (f32[80,256]{1,0:T(8,128)S(1)}, f32[80,256]{1,0:T(8,128)S(1)}, u32[]{:S(2)}, u32[]{:S(2)}) collective-permute-start(f32[80,256]{1,0:T(8,128)S(1)} %add.107), channel_id=1, source_target_pairs={{0,16},{2,18},{4,20},{6,22},{8,24},{10,26},{12,28},{14,30},{16,0},... | collective-permute-start | bytes 245768 | tf_op jit(solution)/shard_map/ppermute | solution.py:405
  76.6 9.1 %collective-permute-done.16 = f32[80,256]{1,0:T(8,128)S(1)} collective-permute-done((f32[80,256]{1,0:T(8,128)S(1)}, f32[80,256]{1,0:T(8,128)S(1)}, u32[]{:S(2)}, u32[]{:S(2)}) %collective-permute-start.16) | collective-permute-done | bytes 81952 | tf_op jit(solution)/shard_map/ppermute | solution.py:405
  86.5 3.6 %collective-permute-done.17 = f32[1,80,256]{2,1,0:T(8,128)S(1)} collective-permute-done((f32[1,80,256]{2,1,0:T(8,128)S(1)}, f32[1,80,256]{2,1,0:T(8,128)S(1)}, u32[]{:S(2)}, u32[]{:S(2)}) %collective-permute-start.17) | collective-permute-done | bytes 81952 | tf_op jit(solution)/shard_map/ppermute | solution.py:405
  90.4 5.2 %collective-permute-done.25 = f32[2,80,256]{2,1,0:T(8,128)S(1)} collective-permute-done((f32[2,80,256]{2,1,0:T(8,128)S(1)}, f32[2,80,256]{2,1,0:T(8,128)S(1)}, u32[]{:S(2)}, u32[]{:S(2)}) %collective-permute-start.25) | collective-permute-done | bytes 163872 | tf_op jit(solution)/shard_map/ppermute | solution.py:405
  96.8 1.1 collective-permute-done.27.other_totals
  98.7 4.5 %field.3 = (f32[2,256,256]{2,1,0:T(8,128)S(1)}, f32[2,128,256]{2,1,0:T(8,128)S(1)}, f32[2,128,256]{2,1,0:T(8,128)S(1)}, f32[2,4,80,256]{3,2,1,0:T(8,128)S(1)}, f32[2,4,80,256]{3,2,1,0:T(8,128)S(1)}) custom-call(s32[26]{0:T(128)S(1)} %concatenate.34.info, f32[2,256,256]{2,1,0:T(8,128)S(1)} %patch.1.strip_ref, ...), custom_call_target="tpu_custom_call" | custom-call | flops 3221225472 | bytes 4980840 | tf_op jit(solution)/shard_map/field/pallas_call | solution.py:376
  103.4 2.0 %collective-permute-done.28 = f32[2,4,80,256]{3,2,1,0:T(8,128)S(1)} collective-permute-done((f32[2,4,80,256]{3,2,1,0:T(8,128)S(1)}, f32[2,4,80,256]{3,2,1,0:T(8,128)S(1)}, u32[]{:S(2)}, u32[]{:S(2)}) %collective-permute-start.28) | collective-permute-done | bytes 655392 | tf_op jit(solution)/shard_map/ppermute | solution.py:402
  105.4 2.0 %collective-permute-start.29 = (f32[2,80,256]{2,1,0:T(8,128)S(1)}, f32[2,80,256]{2,1,0:T(8,128)S(1)}, u32[]{:S(2)}, u32[]{:S(2)}) collective-permute-start(f32[2,80,256]{2,1,0:T(8,128)S(1)} %get-tuple-element.93), channel_id=1, source_target_pairs={{0,4},{2,6},{4,0},{6,2},{8,12},{10,14},{12,8},{14,10},{16,20},{18,... | collective-permute-start | bytes 491528 | tf_op jit(solution)/shard_map/ppermute | solution.py:405
  107.4 1.7 %illumination.3.illum = f32[256,512]{1,0:T(8,128)S(1)} custom-call(s32[26]{0:T(128)S(1)} %concatenate.35.info, f32[2,256,256]{2,1,0:T(8,128)S(1)} %get-tuple-element.72.refs_0_.own, f32[2,256,256]{2,1,0:T(8,128)S(1)} %get-tuple-element.73.refs_1_.other), custom_call_target="tpu_custom_call" | custom-call | bytes 1572968 | tf_op jit(solution)/shard_map/illumination/pallas_call | solution.py:376
  109.1 2.8 %collective-permute-done.29 = f32[2,80,256]{2,1,0:T(8,128)S(1)} collective-permute-done((f32[2,80,256]{2,1,0:T(8,128)S(1)}, f32[2,80,256]{2,1,0:T(8,128)S(1)}, u32[]{:S(2)}, u32[]{:S(2)}) %collective-permute-start.29) | collective-permute-done | bytes 163872 | tf_op jit(solution)/shard_map/ppermute | solution.py:405
  111.9 1.5 collective-permute-done.35
  113.6 5.9 %collective-permute-done.36 = f32[80,256]{1,0:T(8,128)S(1)} collective-permute-done((f32[80,256]{1,0:T(8,128)S(1)}, f32[80,256]{1,0:T(8,128)S(1)}, u32[]{:S(2)}, u32[]{:S(2)}) %collective-permute-start.36) | collective-permute-done | bytes 81952 | tf_op jit(solution)/shard_map/ppermute | solution.py:405
  120.4 3.7 %collective-permute-done.37 = f32[80,256]{1,0:T(8,128)S(1)} collective-permute-done((f32[80,256]{1,0:T(8,128)S(1)}, f32[80,256]{1,0:T(8,128)S(1)}, u32[]{:S(2)}, u32[]{:S(2)}) %collective-permute-start.37) | collective-permute-done | bytes 81952 | tf_op jit(solution)/shard_map/ppermute | solution.py:405
  124.1 3.9 %collective-permute-start.31 = (f32[2,128,256]{2,1,0:T(8,128)S(1)}, f32[2,128,256]{2,1,0:T(8,128)S(1)}, u32[]{:S(2)}, u32[]{:S(2)}) collective-permute-start(f32[2,128,256]{2,1,0:T(8,128)S(1)} %get-tuple-element.79), channel_id=1, source_target_pairs={{0,2},{2,4},{4,6},{6,8},{8,10},{10,12},{12,14},{14,16},{16,18},{18... | collective-permute-start | bytes 786440 | tf_op jit(solution)/shard_map/ppermute | solution.py:420
  128.1 1.3 collective-permute-start.32
  129.4 2.0 %collective-permute-start.34 = (f32[80,256]{1,0:T(8,128)S(1)}, f32[80,256]{1,0:T(8,128)S(1)}, u32[]{:S(2)}, u32[]{:S(2)}) collective-permute-start(f32[80,256]{1,0:T(8,128)S(1)} %add.123), channel_id=1, source_target_pairs={{0,16},{2,18},{4,20},{6,22},{8,24},{10,26},{12,28},{14,30},{16,0},... | collective-permute-start | bytes 245768 | tf_op jit(solution)/shard_map/ppermute | solution.py:405
  131.4 6.8 %collective-permute-done.34 = f32[80,256]{1,0:T(8,128)S(1)} collective-permute-done((f32[80,256]{1,0:T(8,128)S(1)}, f32[80,256]{1,0:T(8,128)S(1)}, u32[]{:S(2)}, u32[]{:S(2)}) %collective-permute-start.34) | collective-permute-done | bytes 81952 | tf_op jit(solution)/shard_map/ppermute | solution.py:405
  139.2 1.3 collective-permute-start.39
  140.5 3.2 %collective-permute-done.39 = f32[1,80,256]{2,1,0:T(8,128)S(1)} collective-permute-done((f32[1,80,256]{2,1,0:T(8,128)S(1)}, f32[1,80,256]{2,1,0:T(8,128)S(1)}, u32[]{:S(2)}, u32[]{:S(2)}) %collective-permute-start.39) | collective-permute-done | bytes 81952 | tf_op jit(solution)/shard_map/ppermute | solution.py:405
  143.9 2.0 %collective-permute-done.41 = f32[1,80,256]{2,1,0:T(8,128)S(1)} collective-permute-done((f32[1,80,256]{2,1,0:T(8,128)S(1)}, f32[1,80,256]{2,1,0:T(8,128)S(1)}, u32[]{:S(2)}, u32[]{:S(2)}) %collective-permute-start.41) | collective-permute-done | bytes 81952 | tf_op jit(solution)/shard_map/ppermute | solution.py:405
  146.5 2.6 %collective-permute-done.40 = f32[2,80,256]{2,1,0:T(8,128)S(1)} collective-permute-done((f32[2,80,256]{2,1,0:T(8,128)S(1)}, f32[2,80,256]{2,1,0:T(8,128)S(1)}, u32[]{:S(2)}, u32[]{:S(2)}) %collective-permute-start.40) | collective-permute-done | bytes 163872 | tf_op jit(solution)/shard_map/ppermute | solution.py:405
  149.1 2.1 %collective-permute-done.42 = f32[2,80,256]{2,1,0:T(8,128)S(1)} collective-permute-done((f32[2,80,256]{2,1,0:T(8,128)S(1)}, f32[2,80,256]{2,1,0:T(8,128)S(1)}, u32[]{:S(2)}, u32[]{:S(2)}) %collective-permute-start.42) | collective-permute-done | bytes 163872 | tf_op jit(solution)/shard_map/ppermute | solution.py:405
  151.4 3.1 %update.3 = f32[2,256,512]{2,1,0:T(8,128)} custom-call(s32[26]{0:T(128)S(1)} %concatenate.35.info, f32[2,256,512]{2,1,0:T(8,128)S(1)} %get-tuple-element.63.strip_ref, f32[256,512]{1,0:T(8,128)S(1)} %illumination.3.illum, f32[2,256,256]{2,1,0:T(8,128)S(1)} %get-tuple-element.85.own, f32[2,256,256]{2,1,0:T(8,128)S(1)} %collective-permute-done.43.other, ...), custom_call_target="tpu_custom_call" | custom-call | bytes 4718696 | tf_op jit(solution)/shard_map/update/pallas_call | solution.py:376
  154.6 1.3 collective-permute-done.46.other_totals
  155.9 1.4 probe.3
  (121 shorter events, 18.8 us)
Async XLA Ops:
  0.6 14.4 %copy-start.1 = (f32[2,2,256,256]{3,2,1,0:T(8,128)S(1)}, f32[2,2,256,256]{3,2,1,0:T(8,128)}, u32[]{:S(2)}) copy-start(f32[2,2,256,256]{3,2,1,0:T(8,128)} %measured.1) | copy-start | bytes 3145732
  2.6 18.4 %collective-permute-start = (f32[128,512]{1,0:T(8,128)}, f32[128,512]{1,0:T(8,128)S(1)}, u32[]{:S(2)}, u32[]{:S(2)}) collective-permute-start(f32[128,512]{1,0:T(8,128)} %get-tuple-element.99), channel_id=1, source_target_pairs={{0,2},{2,4},{4,6},{6,8},{8,10},{10,12},{12,14},{14,16},{16,18},{18... | collective-permute-start | bytes 786440 | tf_op jit(solution)/shard_map/ppermute | solution.py:420
  7.6 13.5 %collective-permute-start.1 = (f32[128,512]{1,0:T(8,128)}, f32[128,512]{1,0:T(8,128)}, u32[]{:S(2)}, u32[]{:S(2)}) collective-permute-start(f32[128,512]{1,0:T(8,128)} %get-tuple-element.98), channel_id=1, source_target_pairs={{2,0},{4,2},{6,4},{8,6},{10,8},{12,10},{14,12},{16,14},{18,16},{20... | collective-permute-start | bytes 786440 | tf_op jit(solution)/shard_map/ppermute | solution.py:423
  8.9 14.4 %collective-permute-start.6 = (f32[2,256,256]{2,1,0:T(8,128)}, f32[2,256,256]{2,1,0:T(8,128)S(1)}, u32[]{:S(2)}, u32[]{:S(2)}) collective-permute-start(f32[2,256,256]{2,1,0:T(8,128)} %bitcast.72), channel_id=1, source_target_pairs={{0,1},{1,0},{2,3},{3,2},{4,5},{5,4},{6,7},{7,6},{8,9},{9,8},{10,11... | collective-permute-start | bytes 1572872 | tf_op jit(solution)/shard_map/ppermute | solution.py:402
  9.0 10.1 %collective-permute-start.2 = (s32[2,2,2]{2,1,0:T(2,128)S(1)}, s32[2,2,2]{2,1,0:T(2,128)S(1)}, u32[]{:S(2)}, u32[]{:S(2)}) collective-permute-start(s32[2,2,2]{2,1,0:T(2,128)S(1)} %copy-done.10), channel_id=1, source_target_pairs={{0,2},{2,4},{4,6},{6,8},{8,10},{10,12},{12,14},{14,16},{16,18},{18... | collective-permute-start | bytes 104 | tf_op jit(solution)/shard_map/ppermute | solution.py:420
  13.5 7.5 %collective-permute-start.3 = (s32[2,2,2]{2,1,0:T(2,128)S(1)}, s32[2,2,2]{2,1,0:T(2,128)S(1)}, u32[]{:S(2)}, u32[]{:S(2)}) collective-permute-start(s32[2,2,2]{2,1,0:T(2,128)S(1)} %copy-done.10), channel_id=1, source_target_pairs={{2,0},{4,2},{6,4},{8,6},{10,8},{12,10},{14,12},{16,14},{18,16},{20... | collective-permute-start | bytes 104 | tf_op jit(solution)/shard_map/ppermute | solution.py:423
  21.0 1.6 %collective-permute-start.4 = (f32[128,512]{1,0:T(8,128)S(1)}, f32[128,512]{1,0:T(8,128)S(1)}, u32[]{:S(2)}, u32[]{:S(2)}) collective-permute-start(f32[128,512]{1,0:T(8,128)S(1)} %collective-permute-done.refs_0_), channel_id=1, source_target_pairs={{0,1},{1,0},{2,3},{3,2},{4,5},{5,4},{6,7},{7,6},{8,9},{9,8},{10,11... | collective-permute-start | bytes 786440 | tf_op jit(solution)/shard_map/ppermute | solution.py:402
  21.1 2.1 %collective-permute-start.5 = (f32[128,512]{1,0:T(8,128)}, f32[128,512]{1,0:T(8,128)S(1)}, u32[]{:S(2)}, u32[]{:S(2)}) collective-permute-start(f32[128,512]{1,0:T(8,128)} %collective-permute-done.1.refs_2_), channel_id=1, source_target_pairs={{0,1},{1,0},{2,3},{3,2},{4,5},{5,4},{6,7},{7,6},{8,9},{9,8},{10,11... | collective-permute-start | bytes 786440 | tf_op jit(solution)/shard_map/ppermute | solution.py:402
  29.7 4.9 %collective-permute-start.12 = (f32[2,4,80,256]{3,2,1,0:T(8,128)S(1)}, f32[2,4,80,256]{3,2,1,0:T(8,128)S(1)}, u32[]{:S(2)}, u32[]{:S(2)}) collective-permute-start(f32[2,4,80,256]{3,2,1,0:T(8,128)S(1)} %get-tuple-element.65), channel_id=1, source_target_pairs={{0,1},{1,0},{2,3},{3,2},{4,5},{5,4},{6,7},{7,6},{8,9},{9,8},{10,11... | collective-permute-start | bytes 1966088 | tf_op jit(solution)/shard_map/ppermute | solution.py:402
  29.8 16.2 %collective-permute-start.7 = (f32[2,128,256]{2,1,0:T(8,128)}, f32[2,128,256]{2,1,0:T(8,128)S(1)}, u32[]{:S(2)}, u32[]{:S(2)}) collective-permute-start(f32[2,128,256]{2,1,0:T(8,128)} %get-tuple-element.57), channel_id=1, source_target_pairs={{0,2},{2,4},{4,6},{6,8},{8,10},{10,12},{12,14},{14,16},{16,18},{18... | collective-permute-start | bytes 786440 | tf_op jit(solution)/shard_map/ppermute | solution.py:420
  33.2 13.8 %collective-permute-start.8 = (f32[2,128,256]{2,1,0:T(8,128)}, f32[2,128,256]{2,1,0:T(8,128)}, u32[]{:S(2)}, u32[]{:S(2)}) collective-permute-start(f32[2,128,256]{2,1,0:T(8,128)} %get-tuple-element.58), channel_id=1, source_target_pairs={{2,0},{4,2},{6,4},{8,6},{10,8},{12,10},{14,12},{16,14},{18,16},{20... | collective-permute-start | bytes 786440 | tf_op jit(solution)/shard_map/ppermute | solution.py:423
  36.2 11.4 %collective-permute-start.13 = (f32[2,80,256]{2,1,0:T(8,128)}, f32[2,80,256]{2,1,0:T(8,128)}, u32[]{:S(2)}, u32[]{:S(2)}) collective-permute-start(f32[2,80,256]{2,1,0:T(8,128)} %get-tuple-element.97), channel_id=1, source_target_pairs={{0,4},{2,6},{4,0},{6,2},{8,12},{10,14},{12,8},{14,10},{16,20},{18,... | collective-permute-start | bytes 491528 | tf_op jit(solution)/shard_map/ppermute | solution.py:405
  39.9 10.8 %collective-permute-start.18 = (f32[2,80,256]{2,1,0:T(8,128)}, f32[2,80,256]{2,1,0:T(8,128)}, u32[]{:S(2)}, u32[]{:S(2)}) collective-permute-start(f32[2,80,256]{2,1,0:T(8,128)} %get-tuple-element.96), channel_id=1, source_target_pairs={{0,8},{2,10},{4,12},{6,14},{8,0},{10,2},{12,4},{14,6},{16,24},{18,... | collective-permute-start | bytes 491528 | tf_op jit(solution)/shard_map/ppermute | solution.py:405
  47.0 17.4 %collective-permute-start.9 = (f32[2,256,256]{2,1,0:T(8,128)S(1)}, f32[2,256,256]{2,1,0:T(8,128)S(1)}, u32[]{:S(2)}, u32[]{:S(2)}) collective-permute-start(f32[2,256,256]{2,1,0:T(8,128)S(1)} %get-tuple-element.60.own), channel_id=1, source_target_pairs={{0,1},{1,0},{2,3},{3,2},{4,5},{5,4},{6,7},{7,6},{8,9},{9,8},{10,11... | collective-permute-start | bytes 1572872 | tf_op jit(solution)/shard_map/ppermute | solution.py:402
  47.0 17.4 %collective-permute-start.10 = (f32[2,128,256]{2,1,0:T(8,128)S(1)}, f32[2,128,256]{2,1,0:T(8,128)S(1)}, u32[]{:S(2)}, u32[]{:S(2)}) collective-permute-start(f32[2,128,256]{2,1,0:T(8,128)S(1)} %collective-permute-done.7.b0), channel_id=1, source_target_pairs={{0,1},{1,0},{2,3},{3,2},{4,5},{5,4},{6,7},{7,6},{8,9},{9,8},{10,11... | collective-permute-start | bytes 786440 | tf_op jit(solution)/shard_map/ppermute | solution.py:402
  47.6 16.9 %collective-permute-start.11 = (f32[2,128,256]{2,1,0:T(8,128)}, f32[2,128,256]{2,1,0:T(8,128)S(1)}, u32[]{:S(2)}, u32[]{:S(2)}) collective-permute-start(f32[2,128,256]{2,1,0:T(8,128)} %collective-permute-done.8.a0), channel_id=1, source_target_pairs={{0,1},{1,0},{2,3},{3,2},{4,5},{5,4},{6,7},{7,6},{8,9},{9,8},{10,11... | collective-permute-start | bytes 786440 | tf_op jit(solution)/shard_map/ppermute | solution.py:402
  51.7 5.5 %collective-permute-start.19 = (f32[80,256]{1,0:T(8,128)S(1)}, f32[80,256]{1,0:T(8,128)S(1)}, u32[]{:S(2)}, u32[]{:S(2)}) collective-permute-start(f32[80,256]{1,0:T(8,128)S(1)} %slice_bitcast_fusion.4), channel_id=1, source_target_pairs={{0,16},{2,18},{4,20},{6,22},{8,24},{10,26},{12,28},{14,30},{16,0},... | collective-permute-start | bytes 245768 | tf_op jit(solution)/shard_map/ppermute | solution.py:405
  54.4 4.9 %collective-permute-start.14 = (f32[80,256]{1,0:T(8,128)S(1)}, f32[80,256]{1,0:T(8,128)S(1)}, u32[]{:S(2)}, u32[]{:S(2)}) collective-permute-start(f32[80,256]{1,0:T(8,128)S(1)} %slice_bitcast_fusion.6), channel_id=1, source_target_pairs={{0,2},{2,0},{4,6},{6,4},{8,10},{10,8},{12,14},{14,12},{16,18},{18,... | collective-permute-start | bytes 245768 | tf_op jit(solution)/shard_map/ppermute | solution.py:405
  57.3 4.6 %collective-permute-start.20 = (f32[80,256]{1,0:T(8,128)S(1)}, f32[80,256]{1,0:T(8,128)S(1)}, u32[]{:S(2)}, u32[]{:S(2)}) collective-permute-start(f32[80,256]{1,0:T(8,128)S(1)} %fusion.14), channel_id=1, source_target_pairs={{0,4},{2,6},{4,0},{6,2},{8,12},{10,14},{12,8},{14,10},{16,20},{18,... | collective-permute-start | bytes 245768 | tf_op jit(solution)/shard_map/ppermute | solution.py:405
  59.4 11.3 %collective-permute-start.15 = (f32[80,256]{1,0:T(8,128)S(1)}, f32[80,256]{1,0:T(8,128)S(1)}, u32[]{:S(2)}, u32[]{:S(2)}) collective-permute-start(f32[80,256]{1,0:T(8,128)S(1)} %fusion.15), channel_id=1, source_target_pairs={{0,8},{2,10},{4,12},{6,14},{8,0},{10,2},{12,4},{14,6},{16,24},{18,... | collective-permute-start | bytes 245768 | tf_op jit(solution)/shard_map/ppermute | solution.py:405
  61.9 14.6 %collective-permute-start.21 = (f32[80,256]{1,0:T(8,128)S(1)}, f32[80,256]{1,0:T(8,128)S(1)}, u32[]{:S(2)}, u32[]{:S(2)}) collective-permute-start(f32[80,256]{1,0:T(8,128)S(1)} %add.115), channel_id=1, source_target_pairs={{0,2},{2,0},{4,6},{6,4},{8,10},{10,8},{12,14},{14,12},{16,18},{18,... | collective-permute-start | bytes 245768 | tf_op jit(solution)/shard_map/ppermute | solution.py:405
  67.2 23.0 %collective-permute-start.23 = (f32[2,128,256]{2,1,0:T(8,128)S(1)}, f32[2,128,256]{2,1,0:T(8,128)S(1)}, u32[]{:S(2)}, u32[]{:S(2)}) collective-permute-start(f32[2,128,256]{2,1,0:T(8,128)S(1)} %get-tuple-element.66), channel_id=1, source_target_pairs={{0,2},{2,4},{4,6},{6,8},{8,10},{10,12},{12,14},{14,16},{16,18},{18... | collective-permute-start | bytes 786440 | tf_op jit(solution)/shard_map/ppermute | solution.py:420
  69.2 21.0 %collective-permute-start.24 = (f32[2,128,256]{2,1,0:T(8,128)S(1)}, f32[2,128,256]{2,1,0:T(8,128)S(1)}, u32[]{:S(2)}, u32[]{:S(2)}) collective-permute-start(f32[2,128,256]{2,1,0:T(8,128)S(1)} %get-tuple-element.67), channel_id=1, source_target_pairs={{2,0},{4,2},{6,4},{8,6},{10,8},{12,10},{14,12},{16,14},{18,16},{20... | collective-permute-start | bytes 786440 | tf_op jit(solution)/shard_map/ppermute | solution.py:423
  70.7 15.0 %collective-permute-start.16 = (f32[80,256]{1,0:T(8,128)S(1)}, f32[80,256]{1,0:T(8,128)S(1)}, u32[]{:S(2)}, u32[]{:S(2)}) collective-permute-start(f32[80,256]{1,0:T(8,128)S(1)} %add.107), channel_id=1, source_target_pairs={{0,16},{2,18},{4,20},{6,22},{8,24},{10,26},{12,28},{14,30},{16,0},... | collective-permute-start | bytes 245768 | tf_op jit(solution)/shard_map/ppermute | solution.py:405
  76.5 10.0 %collective-permute-start.22 = (f32[1,80,256]{2,1,0:T(8,128)S(1)}, f32[1,80,256]{2,1,0:T(8,128)S(1)}, u32[]{:S(2)}, u32[]{:S(2)}) collective-permute-start(f32[1,80,256]{2,1,0:T(8,128)S(1)} %add_bitcast_fusion.2), channel_id=1, source_target_pairs={{0,16},{2,18},{4,20},{6,22},{8,24},{10,26},{12,28},{14,30},{16,0},... | collective-permute-start | bytes 245768 | tf_op jit(solution)/shard_map/ppermute | solution.py:405
  85.7 4.5 %collective-permute-start.17 = (f32[1,80,256]{2,1,0:T(8,128)S(1)}, f32[1,80,256]{2,1,0:T(8,128)S(1)}, u32[]{:S(2)}, u32[]{:S(2)}) collective-permute-start(f32[1,80,256]{2,1,0:T(8,128)S(1)} %add_bitcast_fusion.3), channel_id=1, source_target_pairs={{0,2},{2,0},{4,6},{6,4},{8,10},{10,8},{12,14},{14,12},{16,18},{18,... | collective-permute-start | bytes 245768 | tf_op jit(solution)/shard_map/ppermute | solution.py:405
  90.2 5.4 %collective-permute-start.25 = (f32[2,80,256]{2,1,0:T(8,128)S(1)}, f32[2,80,256]{2,1,0:T(8,128)S(1)}, u32[]{:S(2)}, u32[]{:S(2)}) collective-permute-start(f32[2,80,256]{2,1,0:T(8,128)S(1)} %pad_maximum_fusion.2), channel_id=1, source_target_pairs={{0,4},{2,6},{4,0},{6,2},{8,12},{10,14},{12,8},{14,10},{16,20},{18,... | collective-permute-start | bytes 491528 | tf_op jit(solution)/shard_map/ppermute | solution.py:405
  90.3 5.4 %collective-permute-start.26 = (f32[2,80,256]{2,1,0:T(8,128)S(1)}, f32[2,80,256]{2,1,0:T(8,128)S(1)}, u32[]{:S(2)}, u32[]{:S(2)}) collective-permute-start(f32[2,80,256]{2,1,0:T(8,128)S(1)} %pad_maximum_fusion.3), channel_id=1, source_target_pairs={{0,8},{2,10},{4,12},{6,14},{8,0},{10,2},{12,4},{14,6},{16,24},{18,... | collective-permute-start | bytes 491528 | tf_op jit(solution)/shard_map/ppermute | solution.py:405
  95.7 2.2 %collective-permute-start.27 = (f32[2,4,80,256]{3,2,1,0:T(8,128)S(1)}, f32[2,4,80,256]{3,2,1,0:T(8,128)S(1)}, u32[]{:S(2)}, u32[]{:S(2)}) collective-permute-start(f32[2,4,80,256]{3,2,1,0:T(8,128)S(1)} %pad_maximum_fusion.own_totals), channel_id=1, source_target_pairs={{0,1},{1,0},{2,3},{3,2},{4,5},{5,4},{6,7},{7,6},{8,9},{9,8},{10,11... | collective-permute-start | bytes 1966088 | tf_op jit(solution)/shard_map/ppermute | solution.py:402
  103.2 2.2 %collective-permute-start.28 = (f32[2,4,80,256]{3,2,1,0:T(8,128)S(1)}, f32[2,4,80,256]{3,2,1,0:T(8,128)S(1)}, u32[]{:S(2)}, u32[]{:S(2)}) collective-permute-start(f32[2,4,80,256]{3,2,1,0:T(8,128)S(1)} %get-tuple-element.78), channel_id=1, source_target_pairs={{0,1},{1,0},{2,3},{3,2},{4,5},{5,4},{6,7},{7,6},{8,9},{9,8},{10,11... | collective-permute-start | bytes 1966088 | tf_op jit(solution)/shard_map/ppermute | solution.py:402
  105.4 6.5 %collective-permute-start.29 = (f32[2,80,256]{2,1,0:T(8,128)S(1)}, f32[2,80,256]{2,1,0:T(8,128)S(1)}, u32[]{:S(2)}, u32[]{:S(2)}) collective-permute-start(f32[2,80,256]{2,1,0:T(8,128)S(1)} %get-tuple-element.93), channel_id=1, source_target_pairs={{0,4},{2,6},{4,0},{6,2},{8,12},{10,14},{12,8},{14,10},{16,20},{18,... | collective-permute-start | bytes 491528 | tf_op jit(solution)/shard_map/ppermute | solution.py:405
  107.4 6.0 %collective-permute-start.35 = (f32[2,80,256]{2,1,0:T(8,128)S(1)}, f32[2,80,256]{2,1,0:T(8,128)S(1)}, u32[]{:S(2)}, u32[]{:S(2)}) collective-permute-start(f32[2,80,256]{2,1,0:T(8,128)S(1)} %get-tuple-element.92), channel_id=1, source_target_pairs={{0,8},{2,10},{4,12},{6,14},{8,0},{10,2},{12,4},{14,6},{16,24},{18,... | collective-permute-start | bytes 491528 | tf_op jit(solution)/shard_map/ppermute | solution.py:405
  113.5 6.1 %collective-permute-start.36 = (f32[80,256]{1,0:T(8,128)S(1)}, f32[80,256]{1,0:T(8,128)S(1)}, u32[]{:S(2)}, u32[]{:S(2)}) collective-permute-start(f32[80,256]{1,0:T(8,128)S(1)} %slice_bitcast_fusion), channel_id=1, source_target_pairs={{0,16},{2,18},{4,20},{6,22},{8,24},{10,26},{12,28},{14,30},{16,0},... | collective-permute-start | bytes 245768 | tf_op jit(solution)/shard_map/ppermute | solution.py:405
  113.6 6.7 %collective-permute-start.30 = (f32[80,256]{1,0:T(8,128)S(1)}, f32[80,256]{1,0:T(8,128)S(1)}, u32[]{:S(2)}, u32[]{:S(2)}) collective-permute-start(f32[80,256]{1,0:T(8,128)S(1)} %slice_bitcast_fusion.2), channel_id=1, source_target_pairs={{0,2},{2,0},{4,6},{6,4},{8,10},{10,8},{12,14},{14,12},{16,18},{18,... | collective-permute-start | bytes 245768 | tf_op jit(solution)/shard_map/ppermute | solution.py:405
  119.5 4.5 %collective-permute-start.37 = (f32[80,256]{1,0:T(8,128)S(1)}, f32[80,256]{1,0:T(8,128)S(1)}, u32[]{:S(2)}, u32[]{:S(2)}) collective-permute-start(f32[80,256]{1,0:T(8,128)S(1)} %fusion.12), channel_id=1, source_target_pairs={{0,4},{2,6},{4,0},{6,2},{8,12},{10,14},{12,8},{14,10},{16,20},{18,... | collective-permute-start | bytes 245768 | tf_op jit(solution)/shard_map/ppermute | solution.py:405
  120.3 9.1 %collective-permute-start.33 = (f32[80,256]{1,0:T(8,128)S(1)}, f32[80,256]{1,0:T(8,128)S(1)}, u32[]{:S(2)}, u32[]{:S(2)}) collective-permute-start(f32[80,256]{1,0:T(8,128)S(1)} %fusion.13), channel_id=1, source_target_pairs={{0,8},{2,10},{4,12},{6,14},{8,0},{10,2},{12,4},{14,6},{16,24},{18,... | collective-permute-start | bytes 245768 | tf_op jit(solution)/shard_map/ppermute | solution.py:405
  124.1 7.4 %collective-permute-start.38 = (f32[80,256]{1,0:T(8,128)S(1)}, f32[80,256]{1,0:T(8,128)S(1)}, u32[]{:S(2)}, u32[]{:S(2)}) collective-permute-start(f32[80,256]{1,0:T(8,128)S(1)} %add.131), channel_id=1, source_target_pairs={{0,2},{2,0},{4,6},{6,4},{8,10},{10,8},{12,14},{14,12},{16,18},{18,... | collective-permute-start | bytes 245768 | tf_op jit(solution)/shard_map/ppermute | solution.py:405
  124.1 14.1 %collective-permute-start.31 = (f32[2,128,256]{2,1,0:T(8,128)S(1)}, f32[2,128,256]{2,1,0:T(8,128)S(1)}, u32[]{:S(2)}, u32[]{:S(2)}) collective-permute-start(f32[2,128,256]{2,1,0:T(8,128)S(1)} %get-tuple-element.79), channel_id=1, source_target_pairs={{0,2},{2,4},{4,6},{6,8},{8,10},{10,12},{12,14},{14,16},{16,18},{18... | collective-permute-start | bytes 786440 | tf_op jit(solution)/shard_map/ppermute | solution.py:420
  128.1 11.2 %collective-permute-start.32 = (f32[2,128,256]{2,1,0:T(8,128)S(1)}, f32[2,128,256]{2,1,0:T(8,128)S(1)}, u32[]{:S(2)}, u32[]{:S(2)}) collective-permute-start(f32[2,128,256]{2,1,0:T(8,128)S(1)} %get-tuple-element.80), channel_id=1, source_target_pairs={{2,0},{4,2},{6,4},{8,6},{10,8},{12,10},{14,12},{16,14},{18,16},{20... | collective-permute-start | bytes 786440 | tf_op jit(solution)/shard_map/ppermute | solution.py:423
  129.4 8.9 %collective-permute-start.34 = (f32[80,256]{1,0:T(8,128)S(1)}, f32[80,256]{1,0:T(8,128)S(1)}, u32[]{:S(2)}, u32[]{:S(2)}) collective-permute-start(f32[80,256]{1,0:T(8,128)S(1)} %add.123), channel_id=1, source_target_pairs={{0,16},{2,18},{4,20},{6,22},{8,24},{10,26},{12,28},{14,30},{16,0},... | collective-permute-start | bytes 245768 | tf_op jit(solution)/shard_map/ppermute | solution.py:405
  139.2 4.4 %collective-permute-start.39 = (f32[1,80,256]{2,1,0:T(8,128)S(1)}, f32[1,80,256]{2,1,0:T(8,128)S(1)}, u32[]{:S(2)}, u32[]{:S(2)}) collective-permute-start(f32[1,80,256]{2,1,0:T(8,128)S(1)} %add_bitcast_fusion.1), channel_id=1, source_target_pairs={{0,2},{2,0},{4,6},{6,4},{8,10},{10,8},{12,14},{14,12},{16,18},{18,... | collective-permute-start | bytes 245768 | tf_op jit(solution)/shard_map/ppermute | solution.py:405
  140.5 5.3 %collective-permute-start.41 = (f32[1,80,256]{2,1,0:T(8,128)S(1)}, f32[1,80,256]{2,1,0:T(8,128)S(1)}, u32[]{:S(2)}, u32[]{:S(2)}) collective-permute-start(f32[1,80,256]{2,1,0:T(8,128)S(1)} %add_bitcast_fusion), channel_id=1, source_target_pairs={{0,16},{2,18},{4,20},{6,22},{8,24},{10,26},{12,28},{14,30},{16,0},... | collective-permute-start | bytes 245768 | tf_op jit(solution)/shard_map/ppermute | solution.py:405
  143.7 5.4 %collective-permute-start.40 = (f32[2,80,256]{2,1,0:T(8,128)S(1)}, f32[2,80,256]{2,1,0:T(8,128)S(1)}, u32[]{:S(2)}, u32[]{:S(2)}) collective-permute-start(f32[2,80,256]{2,1,0:T(8,128)S(1)} %pad_maximum_fusion.4), channel_id=1, source_target_pairs={{0,4},{2,6},{4,0},{6,2},{8,12},{10,14},{12,8},{14,10},{16,20},{18,... | collective-permute-start | bytes 491528 | tf_op jit(solution)/shard_map/ppermute | solution.py:405
  143.8 7.6 %collective-permute-start.43 = (f32[2,256,256]{2,1,0:T(8,128)S(1)}, f32[2,256,256]{2,1,0:T(8,128)S(1)}, u32[]{:S(2)}, u32[]{:S(2)}) collective-permute-start(f32[2,256,256]{2,1,0:T(8,128)S(1)} %get-tuple-element.85.own), channel_id=1, source_target_pairs={{0,1},{1,0},{2,3},{3,2},{4,5},{5,4},{6,7},{7,6},{8,9},{9,8},{10,11... | collective-permute-start | bytes 1572872 | tf_op jit(solution)/shard_map/ppermute | solution.py:402
  145.9 5.4 %collective-permute-start.42 = (f32[2,80,256]{2,1,0:T(8,128)S(1)}, f32[2,80,256]{2,1,0:T(8,128)S(1)}, u32[]{:S(2)}, u32[]{:S(2)}) collective-permute-start(f32[2,80,256]{2,1,0:T(8,128)S(1)} %pad_maximum_fusion.5), channel_id=1, source_target_pairs={{0,8},{2,10},{4,12},{6,14},{8,0},{10,2},{12,4},{14,6},{16,24},{18,... | collective-permute-start | bytes 491528 | tf_op jit(solution)/shard_map/ppermute | solution.py:405
  146.0 5.4 %collective-permute-start.44 = (f32[2,128,256]{2,1,0:T(8,128)S(1)}, f32[2,128,256]{2,1,0:T(8,128)S(1)}, u32[]{:S(2)}, u32[]{:S(2)}) collective-permute-start(f32[2,128,256]{2,1,0:T(8,128)S(1)} %collective-permute-done.31.b0), channel_id=1, source_target_pairs={{0,1},{1,0},{2,3},{3,2},{4,5},{5,4},{6,7},{7,6},{8,9},{9,8},{10,11... | collective-permute-start | bytes 786440 | tf_op jit(solution)/shard_map/ppermute | solution.py:402
  146.0 5.3 %collective-permute-start.45 = (f32[2,128,256]{2,1,0:T(8,128)S(1)}, f32[2,128,256]{2,1,0:T(8,128)S(1)}, u32[]{:S(2)}, u32[]{:S(2)}) collective-permute-start(f32[2,128,256]{2,1,0:T(8,128)S(1)} %collective-permute-done.32.a0), channel_id=1, source_target_pairs={{0,1},{1,0},{2,3},{3,2},{4,5},{5,4},{6,7},{7,6},{8,9},{9,8},{10,11... | collective-permute-start | bytes 786440 | tf_op jit(solution)/shard_map/ppermute | solution.py:402
  154.5 1.4 collective-permute-start.46
  (13 other events, 58.9 us)

commit v3 on v1

--- a/solution.py
+++ b/solution.py
@@ -13,6 +13,8 @@
 BF16 = jnp.bfloat16
 VMEM_BYTES = 16 * 1024 * 1024
 GROUP = 4
+NEAR_STEP = 2
+FAR_STEPS = (1, 8, 9)
 
 
 def padded(block, sides, width):
@@ -292,7 +294,7 @@
         gradient[part], top[part], bottom[part] = value, value[:half], value[half:]
     coverage = obj_real * obj_real + obj_imag * obj_imag
     rows = pattern // GROUP
-    mate = lax.rem(info[24], GROUP)
+    mate = lax.rem(lax.div(info[24], NEAR_STEP), GROUP)
     for step, keeper, (cr, ci) in ((step_own, slot, chi[0]), (step_other, 1 - slot, chi[1])):
         real = obj_real * cr + obj_imag * ci
         imag = obj_real * ci - obj_imag * cr
@@ -339,7 +341,7 @@
     probes, outs = refs[: len(refs) // 2], refs[len(refs) // 2 :]
     slot = info[25]
     rows = outs[0].shape[1] // GROUP
-    mate = lax.rem(info[24], GROUP)
+    mate = lax.rem(lax.div(info[24], NEAR_STEP), GROUP)
     for k in range(GROUP):
         where = pl.ds(pl.multiple_of((mate ^ k) * rows, rows), rows)
         mine, theirs = own_totals[k], other_totals[k]
@@ -401,11 +403,9 @@
         mates = [across(blocks[k], unit * k) for k in range(1, GROUP)]
         return functools.reduce(jnp.add, mates, blocks[0])
 
-    def exchange(piece, unit, pairwise):
-        if pairwise:
-            piece = piece + across(piece, unit)
-            return piece + across(piece, 2 * unit)
-        return scatter([piece] * GROUP, unit)
+    def exchange(piece):
+        first, second, third = (across(piece, steps) for steps in FAR_STEPS)
+        return (piece + first) + (second + third)
 
     def gather(piece, unit):
         return jnp.stack([piece] + [across(piece, unit * k) for k in range(1, GROUP)])
@@ -465,16 +465,11 @@
         )
         brought = swap(step_other)
         steps = [step_own[k] + brought[k] for k in range(GROUP)]
-        piece = scatter(steps, 1)
-        if last:
-            gradient, top, bottom, piece, illum = lax.optimization_barrier(
-                (gradient, top, bottom, piece, illum)
-            )
+        piece = scatter(steps, NEAR_STEP)
         rim_below, rim_above = from_below(bottom), from_above(top)
-        if not last:
-            gradient, rim_below, rim_above, illum = lax.optimization_barrier(
-                (gradient, rim_below, rim_above, illum)
-            )
+        gradient, rim_below, rim_above, illum = lax.optimization_barrier(
+            (gradient, rim_below, rim_above, illum)
+        )
         rims = (gradient, swap(gradient), rim_below, rim_above, swap(rim_below), swap(rim_above))
         object_field, *edges = call(
             bind(update_kernel, size, minibatch),
@@ -482,13 +477,12 @@
             [object_field.shape] + ([] if last else [rim] * 2),
             (info, object_field, illum, *rims),
             [tall],
-            flops=0,
-        )
-        piece = exchange(piece, GROUP, last)
+        )
+        piece = exchange(piece)
         if not last:
             edges = [from_below(edges[1]), from_above(edges[0])]
             piece, *edges = lax.optimization_barrier((piece, *edges))
-        totals = gather(piece, 1)
+        totals = gather(piece, NEAR_STEP)
         if last:
             totals, object_field = lax.optimization_barrier((totals, object_field))
             others = swap(totals[:, 2 * rows :])

time: 147 us -> 145 us (0.986)
  waiting for transfers between devices: 56.4 us -> 50.6 us
  starting transfers between devices: 55.8 us -> 59 us
    ppermute x5, waiting for transfers between devices: 12.4 us -> 6.85 us  [from_above(): return lax.ppermute(value, 'tile', down)]
    ppermute x5, waiting for transfers between devices: 6.08 us -> 8.82 us  [from_below(): return lax.ppermute(value, 'tile', up)]
    ppermute x5, starting transfers between devices: 18.4 us -> 20.6 us  [from_below(): return lax.ppermute(value, 'tile', up)]
    ppermute x17 -> x18, waiting for transfers between devices: 31.1 us -> 28.9 us  [across(): return lax.ppermute(value, 'tile', [(i, i ^ k) for i in range(tiles)])]
    ppermute x17 -> x18, starting transfers between devices: 28.8 us -> 29.6 us  [across(): return lax.ppermute(value, 'tile', [(i, i ^ k) for i in range(tiles)])]
  transfers between devices with their start and end apart: 40 -> 41, of which waited for: 24 -> 23; matrix products, arithmetic and copies ran while one was open for 3% -> 3% of each run, Pallas kernels for 5% -> 8%
where the time goes in v3:
time: 145 us; the launch traced here: 143 us
  starting transfers between devices  59 us (41%)
  waiting for transfers between devices  50.6 us (35%)
  Pallas kernels  23.9 us (16%)
  local copies, waits for them, and re-layouts  6.36 us (4%)
  other arithmetic  2.37 us (2%)
    ppermute x18, starting transfers between devices, across(): return lax.ppermute(value, 'tile', [(i, i ^ k) for i in range(tiles)])  29.6 us
    ppermute x18, waiting for transfers between devices, across(): return lax.ppermute(value, 'tile', [(i, i ^ k) for i in range(tiles)])  28.9 us
    pallas_call x10, Pallas kernels, call(): pl.pallas_call(kernel, out_shape=shapes, in_specs=[smem] + [vmem] * (len(...  23.9 us
    ppermute x5, starting transfers between devices, from_below(): return lax.ppermute(value, 'tile', up)  20.6 us
    ppermute x5, waiting for transfers between devices, from_below(): return lax.ppermute(value, 'tile', up)  8.82 us
    ppermute x5, waiting for transfers between devices, from_above(): return lax.ppermute(value, 'tile', down)  6.85 us
    ppermute x5, starting transfers between devices, from_above(): return lax.ppermute(value, 'tile', down)  6.64 us
    ppermute x13, waiting for transfers between devices, swap(): return lax.ppermute(value, 'mode', [(0, 1), (1, 0)])  6.02 us
  transfers between devices with their start and end apart: 41, of which 23 were waited for; matrix products, arithmetic and copies ran while one was open for 3% of the time, Pallas kernels for 8%

profile of v3, /device:TPU:0, one launch (start us, length us, event | category | flops | bytes accessed | tf_op | source)
XLA Modules:
  0.0 143.2 jit_solution(5115635923032995732)
XLA Ops:
  0.6 1.9 %dynamic-slice_bitcast_fusion = (f32[128,512]{1,0:T(8,128)}, f32[128,512]{1,0:T(8,128)}) fusion(f32[2,256,512]{2,1,0:T(8,128)} %strip_ref.3, s32[]{:T(128)S(6)} %select_n.4, s32[]{:T(128)S(6)} %add.117), kind=kLoop, calls=%fused_computation.2 | loop fusion | bytes 1048584 | tf_op jit(solution)/shard_map/slice | solution.py:426
  2.6 5.0 %collective-permute-start = (f32[128,512]{1,0:T(8,128)}, f32[128,512]{1,0:T(8,128)S(1)}, u32[]{:S(2)}, u32[]{:S(2)}) collective-permute-start(f32[128,512]{1,0:T(8,128)} %get-tuple-element.85), channel_id=1, source_target_pairs={{0,2},{2,4},{4,6},{6,8},{8,10},{10,12},{12,14},{14,16},{16,18},{18... | collective-permute-start | bytes 786440 | tf_op jit(solution)/shard_map/ppermute | solution.py:414
  7.6 1.3 collective-permute-start.1
  9.0 4.5 %collective-permute-start.2 = (s32[2,2,2]{2,1,0:T(2,128)S(1)}, s32[2,2,2]{2,1,0:T(2,128)S(1)}, u32[]{:S(2)}, u32[]{:S(2)}) collective-permute-start(s32[2,2,2]{2,1,0:T(2,128)S(1)} %copy-done.9), channel_id=1, source_target_pairs={{0,2},{2,4},{4,6},{6,8},{8,10},{10,12},{12,14},{14,16},{16,18},{18... | collective-permute-start | bytes 104 | tf_op jit(solution)/shard_map/ppermute | solution.py:414
  13.5 1.3 collective-permute-start.3
  17.8 1.3 collective-permute-done.2
  19.1 1.9 %collective-permute-done.3 = s32[2,2,2]{2,1,0:T(2,128)S(1)} collective-permute-done((s32[2,2,2]{2,1,0:T(2,128)S(1)}, s32[2,2,2]{2,1,0:T(2,128)S(1)}, u32[]{:S(2)}, u32[]{:S(2)}) %collective-permute-start.3) | collective-permute-done | bytes 64 | tf_op jit(solution)/shard_map/ppermute | solution.py:417
  23.2 6.4 %field.2 = (f32[2,256,256]{2,1,0:T(8,128)S(1)}, f32[2,128,256]{2,1,0:T(8,128)}, f32[2,128,256]{2,1,0:T(8,128)}, f32[4,160,256]{2,1,0:T(8,128)S(1)}, f32[4,160,256]{2,1,0:T(8,128)S(1)}) custom-call(s32[26]{0:T(128)S(1)} %concatenate.8.info, f32[2,256,512]{2,1,0:T(8,128)S(1)} %copy-done, f32[128,512]{1,0:T(8,128)S(1)} %collective-permute-done.refs_0_, ...), custom_call_target="tpu_custom_call" | custom-call | flops 3221225472 | bytes 6553704 | tf_op jit(solution)/shard_map/field/pallas_call | solution.py:371
  29.8 3.4 %collective-permute-start.7 = (f32[2,128,256]{2,1,0:T(8,128)}, f32[2,128,256]{2,1,0:T(8,128)S(1)}, u32[]{:S(2)}, u32[]{:S(2)}) collective-permute-start(f32[2,128,256]{2,1,0:T(8,128)} %get-tuple-element.51), channel_id=1, source_target_pairs={{0,2},{2,4},{4,6},{6,8},{8,10},{10,12},{12,14},{14,16},{16,18},{18... | collective-permute-start | bytes 786440 | tf_op jit(solution)/shard_map/ppermute | solution.py:414
  33.2 1.3 collective-permute-start.8
  35.5 3.7 %collective-permute-start.13 = (f32[160,256]{1,0:T(8,128)}, f32[160,256]{1,0:T(8,128)}, u32[]{:S(2)}, u32[]{:S(2)}) collective-permute-start(f32[160,256]{1,0:T(8,128)} %get-tuple-element.81), channel_id=1, source_target_pairs={{0,4},{2,6},{4,0},{6,2},{8,12},{10,14},{12,8},{14,10},{16,20},{18,... | collective-permute-start | bytes 491528 | tf_op jit(solution)/shard_map/ppermute | solution.py:400
  39.2 2.4 %collective-permute-start.14 = (f32[160,256]{1,0:T(8,128)}, f32[160,256]{1,0:T(8,128)}, u32[]{:S(2)}, u32[]{:S(2)}) collective-permute-start(f32[160,256]{1,0:T(8,128)} %get-tuple-element.83), channel_id=1, source_target_pairs={{0,8},{2,10},{4,12},{6,14},{8,0},{10,2},{12,4},{14,6},{16,24},{18,... | collective-permute-start | bytes 491528 | tf_op jit(solution)/shard_map/ppermute | solution.py:400
  41.6 1.5 %collective-permute-start.15 = (f32[160,256]{1,0:T(8,128)}, f32[160,256]{1,0:T(8,128)}, u32[]{:S(2)}, u32[]{:S(2)}) collective-permute-start(f32[160,256]{1,0:T(8,128)} %get-tuple-element.82), channel_id=1, source_target_pairs={{0,12},{2,14},{4,8},{6,10},{8,4},{10,6},{12,0},{14,2},{16,28},{18,... | collective-permute-start | bytes 491528 | tf_op jit(solution)/shard_map/ppermute | solution.py:400
  45.1 1.7 %illumination.2.illum = f32[256,512]{1,0:T(8,128)S(1)} custom-call(s32[26]{0:T(128)S(1)} %concatenate.9.info, f32[2,256,256]{2,1,0:T(8,128)S(1)} %get-tuple-element.47.refs_4_.own.refs_0_, f32[2,256,256]{2,1,0:T(8,128)S(1)} %collective-permute-done.6.refs_5_.other.refs_1_), custom_call_target="tpu_custom_call" | custom-call | bytes 1572968 | tf_op jit(solution)/shard_map/illumination/pallas_call | solution.py:371
  47.6 4.1 %collective-permute-done.14 = f32[160,256]{1,0:T(8,128)} collective-permute-done((f32[160,256]{1,0:T(8,128)}, f32[160,256]{1,0:T(8,128)}, u32[]{:S(2)}, u32[]{:S(2)}) %collective-permute-start.14) | collective-permute-done | bytes 163872 | tf_op jit(solution)/shard_map/ppermute | solution.py:400
  51.6 1.2 fusion.13
  52.8 3.3 %collective-permute-start.16 = (f32[160,256]{1,0:T(8,128)S(1)}, f32[160,256]{1,0:T(8,128)S(1)}, u32[]{:S(2)}, u32[]{:S(2)}) collective-permute-start(f32[160,256]{1,0:T(8,128)S(1)} %fusion.13), channel_id=1, source_target_pairs={{0,2},{2,0},{4,6},{6,4},{8,10},{10,8},{12,14},{14,12},{16,18},{18,... | collective-permute-start | bytes 491528 | tf_op jit(solution)/shard_map/ppermute | solution.py:400
  56.1 2.6 %collective-permute-start.17 = (f32[160,256]{1,0:T(8,128)S(1)}, f32[160,256]{1,0:T(8,128)S(1)}, u32[]{:S(2)}, u32[]{:S(2)}) collective-permute-start(f32[160,256]{1,0:T(8,128)S(1)} %fusion.13), channel_id=1, source_target_pairs={{0,16},{2,18},{4,20},{6,22},{8,24},{10,26},{12,28},{14,30},{16,0},... | collective-permute-start | bytes 491528 | tf_op jit(solution)/shard_map/ppermute | solution.py:400
  58.8 2.8 %update.2 = (f32[2,256,512]{2,1,0:T(8,128)S(1)}, f32[2,128,256]{2,1,0:T(8,128)S(1)}, f32[2,128,256]{2,1,0:T(8,128)S(1)}) custom-call(s32[26]{0:T(128)S(1)} %concatenate.9.info, f32[2,256,512]{2,1,0:T(8,128)S(1)} %copy-done, f32[256,512]{1,0:T(8,128)S(1)} %illumination.2.illum, f32[2,256,256]{2,1,0:T(8,128)S(1)} %get-tuple-element.54.own, ...), custom_call_target="tpu_custom_call" | custom-call | bytes 5242984 | tf_op jit(solution)/shard_map/update/pallas_call | solution.py:371
  61.5 3.7 %collective-permute-start.19 = (f32[2,128,256]{2,1,0:T(8,128)S(1)}, f32[2,128,256]{2,1,0:T(8,128)S(1)}, u32[]{:S(2)}, u32[]{:S(2)}) collective-permute-start(f32[2,128,256]{2,1,0:T(8,128)S(1)} %get-tuple-element.60), channel_id=1, source_target_pairs={{0,2},{2,4},{4,6},{6,8},{8,10},{10,12},{12,14},{14,16},{16,18},{18... | collective-permute-start | bytes 786440 | tf_op jit(solution)/shard_map/ppermute | solution.py:414
  65.2 1.5 %collective-permute-start.20 = (f32[2,128,256]{2,1,0:T(8,128)S(1)}, f32[2,128,256]{2,1,0:T(8,128)S(1)}, u32[]{:S(2)}, u32[]{:S(2)}) collective-permute-start(f32[2,128,256]{2,1,0:T(8,128)S(1)} %get-tuple-element.61), channel_id=1, source_target_pairs={{2,0},{4,2},{6,4},{8,6},{10,8},{12,10},{14,12},{16,14},{18,16},{20... | collective-permute-start | bytes 786440 | tf_op jit(solution)/shard_map/ppermute | solution.py:417
  66.7 4.4 %collective-permute-done.17 = f32[160,256]{1,0:T(8,128)S(1)} collective-permute-done((f32[160,256]{1,0:T(8,128)S(1)}, f32[160,256]{1,0:T(8,128)S(1)}, u32[]{:S(2)}, u32[]{:S(2)}) %collective-permute-start.17) | collective-permute-done | bytes 163872 | tf_op jit(solution)/shard_map/ppermute | solution.py:400
  71.1 2.7 %collective-permute-done.18 = f32[160,256]{1,0:T(8,128)S(1)} collective-permute-done((f32[160,256]{1,0:T(8,128)S(1)}, f32[160,256]{1,0:T(8,128)S(1)}, u32[]{:S(2)}, u32[]{:S(2)}) %collective-permute-start.18) | collective-permute-done | bytes 163872 | tf_op jit(solution)/shard_map/ppermute | solution.py:400
  73.8 5.9 %collective-permute-done.19.below = f32[2,128,256]{2,1,0:T(8,128)S(1)} collective-permute-done((f32[2,128,256]{2,1,0:T(8,128)S(1)}, f32[2,128,256]{2,1,0:T(8,128)S(1)}, u32[]{:S(2)}, u32[]{:S(2)}) %collective-permute-start.19) | collective-permute-done | bytes 262176 | tf_op jit(solution)/shard_map/ppermute | solution.py:414
  79.7 2.2 %collective-permute-done.20.above = f32[2,128,256]{2,1,0:T(8,128)S(1)} collective-permute-done((f32[2,128,256]{2,1,0:T(8,128)S(1)}, f32[2,128,256]{2,1,0:T(8,128)S(1)}, u32[]{:S(2)}, u32[]{:S(2)}) %collective-permute-start.20) | collective-permute-done | bytes 262176 | tf_op jit(solution)/shard_map/ppermute | solution.py:417
  81.9 3.5 %collective-permute-start.23 = (f32[160,256]{1,0:T(8,128)S(1)}, f32[160,256]{1,0:T(8,128)S(1)}, u32[]{:S(2)}, u32[]{:S(2)}) collective-permute-start(f32[160,256]{1,0:T(8,128)S(1)} %add_add_fusion.1), channel_id=1, source_target_pairs={{0,12},{2,14},{4,8},{6,10},{8,4},{10,6},{12,0},{14,2},{16,28},{18,... | collective-permute-start | bytes 491528 | tf_op jit(solution)/shard_map/ppermute | solution.py:400
  85.4 3.6 %collective-permute-done.21 = f32[160,256]{1,0:T(8,128)S(1)} collective-permute-done((f32[160,256]{1,0:T(8,128)S(1)}, f32[160,256]{1,0:T(8,128)S(1)}, u32[]{:S(2)}, u32[]{:S(2)}) %collective-permute-start.21) | collective-permute-done | bytes 163872 | tf_op jit(solution)/shard_map/ppermute | solution.py:400
  89.0 1.9 %collective-permute-done.23 = f32[160,256]{1,0:T(8,128)S(1)} collective-permute-done((f32[160,256]{1,0:T(8,128)S(1)}, f32[160,256]{1,0:T(8,128)S(1)}, u32[]{:S(2)}, u32[]{:S(2)}) %collective-permute-start.23) | collective-permute-done | bytes 163872 | tf_op jit(solution)/shard_map/ppermute | solution.py:400
  92.0 1.1 collective-permute-done.24.other_totals
  93.8 4.5 %field.3 = (f32[2,256,256]{2,1,0:T(8,128)S(1)}, f32[2,128,256]{2,1,0:T(8,128)S(1)}, f32[2,128,256]{2,1,0:T(8,128)S(1)}, f32[4,160,256]{2,1,0:T(8,128)S(1)}, f32[4,160,256]{2,1,0:T(8,128)S(1)}) custom-call(s32[26]{0:T(128)S(1)} %concatenate.8.info, f32[2,256,256]{2,1,0:T(8,128)S(1)} %patch.1.strip_ref, f32[2,256,256]{2,1,0:T(8,128)S(1)} %get-tuple-element.65.refs_0_.own, ...), custom_call_target="tpu_custom_call" | custom-call | flops 3221225472 | bytes 4980840 | tf_op jit(solution)/shard_map/field/pallas_call | solution.py:371
  98.5 2.0 %collective-permute-done.25 = f32[4,160,256]{2,1,0:T(8,128)S(1)} collective-permute-done((f32[4,160,256]{2,1,0:T(8,128)S(1)}, f32[4,160,256]{2,1,0:T(8,128)S(1)}, u32[]{:S(2)}, u32[]{:S(2)}) %collective-permute-start.25) | collective-permute-done | bytes 655392 | tf_op jit(solution)/shard_map/ppermute | solution.py:397
  102.0 2.2 %collective-permute-start.28 = (f32[160,256]{1,0:T(8,128)S(1)}, f32[160,256]{1,0:T(8,128)S(1)}, u32[]{:S(2)}, u32[]{:S(2)}) collective-permute-start(f32[160,256]{1,0:T(8,128)S(1)} %get-tuple-element.79), channel_id=1, source_target_pairs={{0,12},{2,14},{4,8},{6,10},{8,4},{10,6},{12,0},{14,2},{16,28},{18,... | collective-permute-start | bytes 491528 | tf_op jit(solution)/shard_map/ppermute | solution.py:400
  104.1 4.0 %collective-permute-start.35 = (f32[2,128,256]{2,1,0:T(8,128)S(1)}, f32[2,128,256]{2,1,0:T(8,128)S(1)}, u32[]{:S(2)}, u32[]{:S(2)}) collective-permute-start(f32[2,128,256]{2,1,0:T(8,128)S(1)} %get-tuple-element.70), channel_id=1, source_target_pairs={{0,2},{2,4},{4,6},{6,8},{8,10},{10,12},{12,14},{14,16},{16,18},{18... | collective-permute-start | bytes 786440 | tf_op jit(solution)/shard_map/ppermute | solution.py:414
  108.1 1.3 collective-permute-start.36
  109.4 2.1 %collective-permute-done.28 = f32[160,256]{1,0:T(8,128)S(1)} collective-permute-done((f32[160,256]{1,0:T(8,128)S(1)}, f32[160,256]{1,0:T(8,128)S(1)}, u32[]{:S(2)}, u32[]{:S(2)}) %collective-permute-start.28) | collective-permute-done | bytes 163872 | tf_op jit(solution)/shard_map/ppermute | solution.py:400
  111.6 2.1 %collective-permute-start.29 = (f32[160,256]{1,0:T(8,128)S(1)}, f32[160,256]{1,0:T(8,128)S(1)}, u32[]{:S(2)}, u32[]{:S(2)}) collective-permute-start(f32[160,256]{1,0:T(8,128)S(1)} %fusion.6), channel_id=1, source_target_pairs={{0,2},{2,0},{4,6},{6,4},{8,10},{10,8},{12,14},{14,12},{16,18},{18,... | collective-permute-start | bytes 491528 | tf_op jit(solution)/shard_map/ppermute | solution.py:400
  113.8 2.0 %collective-permute-start.30 = (f32[160,256]{1,0:T(8,128)S(1)}, f32[160,256]{1,0:T(8,128)S(1)}, u32[]{:S(2)}, u32[]{:S(2)}) collective-permute-start(f32[160,256]{1,0:T(8,128)S(1)} %fusion.6), channel_id=1, source_target_pairs={{0,16},{2,18},{4,20},{6,22},{8,24},{10,26},{12,28},{14,30},{16,0},... | collective-permute-start | bytes 491528 | tf_op jit(solution)/shard_map/ppermute | solution.py:400
  115.8 1.4 collective-permute-start.31
  117.2 1.7 %illumination.3.illum = f32[256,512]{1,0:T(8,128)S(1)} custom-call(s32[26]{0:T(128)S(1)} %concatenate.9.info, f32[2,256,256]{2,1,0:T(8,128)S(1)} %get-tuple-element.65.refs_0_.own, f32[2,256,256]{2,1,0:T(8,128)S(1)} %get-tuple-element.66.refs_1_.other), custom_call_target="tpu_custom_call" | custom-call | bytes 1572968 | tf_op jit(solution)/shard_map/illumination/pallas_call | solution.py:371
  118.8 1.6 %collective-permute-done.35.b0 = f32[2,128,256]{2,1,0:T(8,128)S(1)} collective-permute-done((f32[2,128,256]{2,1,0:T(8,128)S(1)}, f32[2,128,256]{2,1,0:T(8,128)S(1)}, u32[]{:S(2)}, u32[]{:S(2)}) %collective-permute-start.35) | collective-permute-done | bytes 262176 | tf_op jit(solution)/shard_map/ppermute | solution.py:414
  120.5 2.4 %collective-permute-done.36.a0 = f32[2,128,256]{2,1,0:T(8,128)S(1)} collective-permute-done((f32[2,128,256]{2,1,0:T(8,128)S(1)}, f32[2,128,256]{2,1,0:T(8,128)S(1)}, u32[]{:S(2)}, u32[]{:S(2)}) %collective-permute-start.36) | collective-permute-done | bytes 262176 | tf_op jit(solution)/shard_map/ppermute | solution.py:417
  123.4 1.7 %collective-permute-done.29 = f32[160,256]{1,0:T(8,128)S(1)} collective-permute-done((f32[160,256]{1,0:T(8,128)S(1)}, f32[160,256]{1,0:T(8,128)S(1)}, u32[]{:S(2)}, u32[]{:S(2)}) %collective-permute-start.29) | collective-permute-done | bytes 163872 | tf_op jit(solution)/shard_map/ppermute | solution.py:400
  125.2 6.4 %collective-permute-done.30 = f32[160,256]{1,0:T(8,128)S(1)} collective-permute-done((f32[160,256]{1,0:T(8,128)S(1)}, f32[160,256]{1,0:T(8,128)S(1)}, u32[]{:S(2)}, u32[]{:S(2)}) %collective-permute-start.30) | collective-permute-done | bytes 163872 | tf_op jit(solution)/shard_map/ppermute | solution.py:400
  131.8 3.4 %collective-permute-start.34 = (f32[160,256]{1,0:T(8,128)S(1)}, f32[160,256]{1,0:T(8,128)S(1)}, u32[]{:S(2)}, u32[]{:S(2)}) collective-permute-start(f32[160,256]{1,0:T(8,128)S(1)} %add_add_fusion), channel_id=1, source_target_pairs={{0,12},{2,14},{4,8},{6,10},{8,4},{10,6},{12,0},{14,2},{16,28},{18,... | collective-permute-start | bytes 491528 | tf_op jit(solution)/shard_map/ppermute | solution.py:400
  135.2 3.1 %update.3 = f32[2,256,512]{2,1,0:T(8,128)} custom-call(s32[26]{0:T(128)S(1)} %concatenate.9.info, f32[2,256,512]{2,1,0:T(8,128)S(1)} %get-tuple-element.57.strip_ref, f32[256,512]{1,0:T(8,128)S(1)} %illumination.3.illum, f32[2,256,256]{2,1,0:T(8,128)S(1)} %get-tuple-element.73.own, f32[2,256,256]{2,1,0:T(8,128)S(1)} %collective-permute-done.37.other, ...), custom_call_target="tpu_custom_call" | custom-call | bytes 4718696 | tf_op jit(solution)/shard_map/update/pallas_call | solution.py:371
  138.6 1.7 %collective-permute-done.34 = f32[160,256]{1,0:T(8,128)S(1)} collective-permute-done((f32[160,256]{1,0:T(8,128)S(1)}, f32[160,256]{1,0:T(8,128)S(1)}, u32[]{:S(2)}, u32[]{:S(2)}) %collective-permute-start.34) | collective-permute-done | bytes 163872 | tf_op jit(solution)/shard_map/ppermute | solution.py:400
  140.5 1.3 collective-permute-done.40.other_totals
  141.8 1.4 probe.3
  (85 shorter events, 13.9 us)
Async XLA Ops:
  0.6 14.4 %copy-start.1 = (f32[2,2,256,256]{3,2,1,0:T(8,128)S(1)}, f32[2,2,256,256]{3,2,1,0:T(8,128)}, u32[]{:S(2)}) copy-start(f32[2,2,256,256]{3,2,1,0:T(8,128)} %measured.1) | copy-start | bytes 3145732
  2.6 6.4 %copy-start.9 = (s32[2,2,2]{2,1,0:T(2,128)S(1)}, s32[2,2,2]{2,1,0:T(2,128)}, u32[]{:S(2)}) copy-start(s32[2,2,2]{2,1,0:T(2,128)} %param.7) | copy-start | bytes 100
  2.6 18.4 %collective-permute-start = (f32[128,512]{1,0:T(8,128)}, f32[128,512]{1,0:T(8,128)S(1)}, u32[]{:S(2)}, u32[]{:S(2)}) collective-permute-start(f32[128,512]{1,0:T(8,128)} %get-tuple-element.85), channel_id=1, source_target_pairs={{0,2},{2,4},{4,6},{6,8},{8,10},{10,12},{12,14},{14,16},{16,18},{18... | collective-permute-start | bytes 786440 | tf_op jit(solution)/shard_map/ppermute | solution.py:414
  7.6 13.5 %collective-permute-start.1 = (f32[128,512]{1,0:T(8,128)}, f32[128,512]{1,0:T(8,128)}, u32[]{:S(2)}, u32[]{:S(2)}) collective-permute-start(f32[128,512]{1,0:T(8,128)} %get-tuple-element.84), channel_id=1, source_target_pairs={{2,0},{4,2},{6,4},{8,6},{10,8},{12,10},{14,12},{16,14},{18,16},{20... | collective-permute-start | bytes 786440 | tf_op jit(solution)/shard_map/ppermute | solution.py:417
  8.9 14.4 %collective-permute-start.6 = (f32[2,256,256]{2,1,0:T(8,128)}, f32[2,256,256]{2,1,0:T(8,128)S(1)}, u32[]{:S(2)}, u32[]{:S(2)}) collective-permute-start(f32[2,256,256]{2,1,0:T(8,128)} %bitcast.44), channel_id=1, source_target_pairs={{0,1},{1,0},{2,3},{3,2},{4,5},{5,4},{6,7},{7,6},{8,9},{9,8},{10,11... | collective-permute-start | bytes 1572872 | tf_op jit(solution)/shard_map/ppermute | solution.py:397
  9.0 10.1 %collective-permute-start.2 = (s32[2,2,2]{2,1,0:T(2,128)S(1)}, s32[2,2,2]{2,1,0:T(2,128)S(1)}, u32[]{:S(2)}, u32[]{:S(2)}) collective-permute-start(s32[2,2,2]{2,1,0:T(2,128)S(1)} %copy-done.9), channel_id=1, source_target_pairs={{0,2},{2,4},{4,6},{6,8},{8,10},{10,12},{12,14},{14,16},{16,18},{18... | collective-permute-start | bytes 104 | tf_op jit(solution)/shard_map/ppermute | solution.py:414
  13.5 7.5 %collective-permute-start.3 = (s32[2,2,2]{2,1,0:T(2,128)S(1)}, s32[2,2,2]{2,1,0:T(2,128)S(1)}, u32[]{:S(2)}, u32[]{:S(2)}) collective-permute-start(s32[2,2,2]{2,1,0:T(2,128)S(1)} %copy-done.9), channel_id=1, source_target_pairs={{2,0},{4,2},{6,4},{8,6},{10,8},{12,10},{14,12},{16,14},{18,16},{20... | collective-permute-start | bytes 104 | tf_op jit(solution)/shard_map/ppermute | solution.py:417
  17.1 6.2 %copy-start = (f32[2,256,512]{2,1,0:T(8,128)S(1)}, f32[2,256,512]{2,1,0:T(8,128)}, u32[]{:S(2)}) copy-start(f32[2,256,512]{2,1,0:T(8,128)} %strip_ref.3) | copy-start | bytes 3145732
  17.8 11.9 %copy-start.4 = (f32[2,256,256]{2,1,0:T(8,128)}, f32[2,256,256]{2,1,0:T(8,128)S(1)}, u32[]{:S(2)}) copy-start(f32[2,256,256]{2,1,0:T(8,128)S(1)} %get-tuple-element.48.refs_6_.refs_2_) | copy-start | bytes 1572868
  17.8 11.9 %copy-start.6 = (bf16[4,256,256]{2,1,0:T(8,128)(2,1)}, bf16[4,256,256]{2,1,0:T(8,128)(2,1)S(1)}, u32[]{:S(2)}) copy-start(bf16[4,256,256]{2,1,0:T(8,128)(2,1)S(1)} %get-tuple-element.49.refs_7_.refs_3_) | copy-start | bytes 1572868
  21.0 2.2 %copy-start.10 = (s32[2,2,2]{2,1,0:T(2,128)}, s32[2,2,2]{2,1,0:T(2,128)S(1)}, u32[]{:S(2)}) copy-start(s32[2,2,2]{2,1,0:T(2,128)S(1)} %collective-permute-done.3) | copy-start | bytes 100
  21.0 1.6 %collective-permute-start.4 = (f32[128,512]{1,0:T(8,128)S(1)}, f32[128,512]{1,0:T(8,128)S(1)}, u32[]{:S(2)}, u32[]{:S(2)}) collective-permute-start(f32[128,512]{1,0:T(8,128)S(1)} %collective-permute-done.refs_0_), channel_id=1, source_target_pairs={{0,1},{1,0},{2,3},{3,2},{4,5},{5,4},{6,7},{7,6},{8,9},{9,8},{10,11... | collective-permute-start | bytes 786440 | tf_op jit(solution)/shard_map/ppermute | solution.py:397
  21.1 2.1 %collective-permute-start.5 = (f32[128,512]{1,0:T(8,128)}, f32[128,512]{1,0:T(8,128)S(1)}, u32[]{:S(2)}, u32[]{:S(2)}) collective-permute-start(f32[128,512]{1,0:T(8,128)} %collective-permute-done.1.refs_2_), channel_id=1, source_target_pairs={{0,1},{1,0},{2,3},{3,2},{4,5},{5,4},{6,7},{7,6},{8,9},{9,8},{10,11... | collective-permute-start | bytes 786440 | tf_op jit(solution)/shard_map/ppermute | solution.py:397
  29.7 4.9 %collective-permute-start.12 = (f32[4,160,256]{2,1,0:T(8,128)S(1)}, f32[4,160,256]{2,1,0:T(8,128)S(1)}, u32[]{:S(2)}, u32[]{:S(2)}) collective-permute-start(f32[4,160,256]{2,1,0:T(8,128)S(1)} %get-tuple-element.59), channel_id=1, source_target_pairs={{0,1},{1,0},{2,3},{3,2},{4,5},{5,4},{6,7},{7,6},{8,9},{9,8},{10,11... | collective-permute-start | bytes 1966088 | tf_op jit(solution)/shard_map/ppermute | solution.py:397
  29.8 16.9 %collective-permute-start.7 = (f32[2,128,256]{2,1,0:T(8,128)}, f32[2,128,256]{2,1,0:T(8,128)S(1)}, u32[]{:S(2)}, u32[]{:S(2)}) collective-permute-start(f32[2,128,256]{2,1,0:T(8,128)} %get-tuple-element.51), channel_id=1, source_target_pairs={{0,2},{2,4},{4,6},{6,8},{8,10},{10,12},{12,14},{14,16},{16,18},{18... | collective-permute-start | bytes 786440 | tf_op jit(solution)/shard_map/ppermute | solution.py:414
  33.2 13.8 %collective-permute-start.8 = (f32[2,128,256]{2,1,0:T(8,128)}, f32[2,128,256]{2,1,0:T(8,128)}, u32[]{:S(2)}, u32[]{:S(2)}) collective-permute-start(f32[2,128,256]{2,1,0:T(8,128)} %get-tuple-element.52), channel_id=1, source_target_pairs={{2,0},{4,2},{6,4},{8,6},{10,8},{12,10},{14,12},{16,14},{18,16},{20... | collective-permute-start | bytes 786440 | tf_op jit(solution)/shard_map/ppermute | solution.py:417
  35.5 12.0 %collective-permute-start.13 = (f32[160,256]{1,0:T(8,128)}, f32[160,256]{1,0:T(8,128)}, u32[]{:S(2)}, u32[]{:S(2)}) collective-permute-start(f32[160,256]{1,0:T(8,128)} %get-tuple-element.81), channel_id=1, source_target_pairs={{0,4},{2,6},{4,0},{6,2},{8,12},{10,14},{12,8},{14,10},{16,20},{18,... | collective-permute-start | bytes 491528 | tf_op jit(solution)/shard_map/ppermute | solution.py:400
  39.2 4.4 %copy-start.11 = (s32[2,2,2]{2,1,0:T(2,128)S(1)}, s32[2,2,2]{2,1,0:T(2,128)}, u32[]{:S(2)}) copy-start(s32[2,2,2]{2,1,0:T(2,128)} %copy-done.10) | copy-start | bytes 100
  39.2 12.4 %collective-permute-start.14 = (f32[160,256]{1,0:T(8,128)}, f32[160,256]{1,0:T(8,128)}, u32[]{:S(2)}, u32[]{:S(2)}) collective-permute-start(f32[160,256]{1,0:T(8,128)} %get-tuple-element.83), channel_id=1, source_target_pairs={{0,8},{2,10},{4,12},{6,14},{8,0},{10,2},{12,4},{14,6},{16,24},{18,... | collective-permute-start | bytes 491528 | tf_op jit(solution)/shard_map/ppermute | solution.py:400
  41.6 10.0 %collective-permute-start.15 = (f32[160,256]{1,0:T(8,128)}, f32[160,256]{1,0:T(8,128)}, u32[]{:S(2)}, u32[]{:S(2)}) collective-permute-start(f32[160,256]{1,0:T(8,128)} %get-tuple-element.82), channel_id=1, source_target_pairs={{0,12},{2,14},{4,8},{6,10},{8,4},{10,6},{12,0},{14,2},{16,28},{18,... | collective-permute-start | bytes 491528 | tf_op jit(solution)/shard_map/ppermute | solution.py:400
  47.0 11.7 %collective-permute-start.9 = (f32[2,256,256]{2,1,0:T(8,128)S(1)}, f32[2,256,256]{2,1,0:T(8,128)S(1)}, u32[]{:S(2)}, u32[]{:S(2)}) collective-permute-start(f32[2,256,256]{2,1,0:T(8,128)S(1)} %get-tuple-element.54.own), channel_id=1, source_target_pairs={{0,1},{1,0},{2,3},{3,2},{4,5},{5,4},{6,7},{7,6},{8,9},{9,8},{10,11... | collective-permute-start | bytes 1572872 | tf_op jit(solution)/shard_map/ppermute | solution.py:397
  47.0 11.7 %collective-permute-start.10 = (f32[2,128,256]{2,1,0:T(8,128)S(1)}, f32[2,128,256]{2,1,0:T(8,128)S(1)}, u32[]{:S(2)}, u32[]{:S(2)}) collective-permute-start(f32[2,128,256]{2,1,0:T(8,128)S(1)} %collective-permute-done.7.b0), channel_id=1, source_target_pairs={{0,1},{1,0},{2,3},{3,2},{4,5},{5,4},{6,7},{7,6},{8,9},{9,8},{10,11... | collective-permute-start | bytes 786440 | tf_op jit(solution)/shard_map/ppermute | solution.py:397
  47.6 11.2 %collective-permute-start.11 = (f32[2,128,256]{2,1,0:T(8,128)}, f32[2,128,256]{2,1,0:T(8,128)S(1)}, u32[]{:S(2)}, u32[]{:S(2)}) collective-permute-start(f32[2,128,256]{2,1,0:T(8,128)} %collective-permute-done.8.a0), channel_id=1, source_target_pairs={{0,1},{1,0},{2,3},{3,2},{4,5},{5,4},{6,7},{7,6},{8,9},{9,8},{10,11... | collective-permute-start | bytes 786440 | tf_op jit(solution)/shard_map/ppermute | solution.py:397
  52.8 13.9 %collective-permute-start.16 = (f32[160,256]{1,0:T(8,128)S(1)}, f32[160,256]{1,0:T(8,128)S(1)}, u32[]{:S(2)}, u32[]{:S(2)}) collective-permute-start(f32[160,256]{1,0:T(8,128)S(1)} %fusion.13), channel_id=1, source_target_pairs={{0,2},{2,0},{4,6},{6,4},{8,10},{10,8},{12,14},{14,12},{16,18},{18,... | collective-permute-start | bytes 491528 | tf_op jit(solution)/shard_map/ppermute | solution.py:400
  56.1 15.0 %collective-permute-start.17 = (f32[160,256]{1,0:T(8,128)S(1)}, f32[160,256]{1,0:T(8,128)S(1)}, u32[]{:S(2)}, u32[]{:S(2)}) collective-permute-start(f32[160,256]{1,0:T(8,128)S(1)} %fusion.13), channel_id=1, source_target_pairs={{0,16},{2,18},{4,20},{6,22},{8,24},{10,26},{12,28},{14,30},{16,0},... | collective-permute-start | bytes 491528 | tf_op jit(solution)/shard_map/ppermute | solution.py:400
  58.7 15.0 %collective-permute-start.18 = (f32[160,256]{1,0:T(8,128)S(1)}, f32[160,256]{1,0:T(8,128)S(1)}, u32[]{:S(2)}, u32[]{:S(2)}) collective-permute-start(f32[160,256]{1,0:T(8,128)S(1)} %fusion.13), channel_id=1, source_target_pairs={{0,18},{2,16},{4,22},{6,20},{8,26},{10,24},{12,30},{14,28},{16,2},... | collective-permute-start | bytes 491528 | tf_op jit(solution)/shard_map/ppermute | solution.py:400
  61.5 18.2 %collective-permute-start.19 = (f32[2,128,256]{2,1,0:T(8,128)S(1)}, f32[2,128,256]{2,1,0:T(8,128)S(1)}, u32[]{:S(2)}, u32[]{:S(2)}) collective-permute-start(f32[2,128,256]{2,1,0:T(8,128)S(1)} %get-tuple-element.60), channel_id=1, source_target_pairs={{0,2},{2,4},{4,6},{6,8},{8,10},{10,12},{12,14},{14,16},{16,18},{18... | collective-permute-start | bytes 786440 | tf_op jit(solution)/shard_map/ppermute | solution.py:414
  65.2 16.7 %collective-permute-start.20 = (f32[2,128,256]{2,1,0:T(8,128)S(1)}, f32[2,128,256]{2,1,0:T(8,128)S(1)}, u32[]{:S(2)}, u32[]{:S(2)}) collective-permute-start(f32[2,128,256]{2,1,0:T(8,128)S(1)} %get-tuple-element.61), channel_id=1, source_target_pairs={{2,0},{4,2},{6,4},{8,6},{10,8},{12,10},{14,12},{16,14},{18,16},{20... | collective-permute-start | bytes 786440 | tf_op jit(solution)/shard_map/ppermute | solution.py:417
  81.9 7.1 %collective-permute-start.21 = (f32[160,256]{1,0:T(8,128)S(1)}, f32[160,256]{1,0:T(8,128)S(1)}, u32[]{:S(2)}, u32[]{:S(2)}) collective-permute-start(f32[160,256]{1,0:T(8,128)S(1)} %add_add_fusion.1), channel_id=1, source_target_pairs={{0,4},{2,6},{4,0},{6,2},{8,12},{10,14},{12,8},{14,10},{16,20},{18,... | collective-permute-start | bytes 491528 | tf_op jit(solution)/shard_map/ppermute | solution.py:400
  81.9 7.1 %collective-permute-start.22 = (f32[160,256]{1,0:T(8,128)S(1)}, f32[160,256]{1,0:T(8,128)S(1)}, u32[]{:S(2)}, u32[]{:S(2)}) collective-permute-start(f32[160,256]{1,0:T(8,128)S(1)} %add_add_fusion.1), channel_id=1, source_target_pairs={{0,8},{2,10},{4,12},{6,14},{8,0},{10,2},{12,4},{14,6},{16,24},{18,... | collective-permute-start | bytes 491528 | tf_op jit(solution)/shard_map/ppermute | solution.py:400
  81.9 9.0 %collective-permute-start.23 = (f32[160,256]{1,0:T(8,128)S(1)}, f32[160,256]{1,0:T(8,128)S(1)}, u32[]{:S(2)}, u32[]{:S(2)}) collective-permute-start(f32[160,256]{1,0:T(8,128)S(1)} %add_add_fusion.1), channel_id=1, source_target_pairs={{0,12},{2,14},{4,8},{6,10},{8,4},{10,6},{12,0},{14,2},{16,28},{18,... | collective-permute-start | bytes 491528 | tf_op jit(solution)/shard_map/ppermute | solution.py:400
  90.9 2.2 %collective-permute-start.24 = (f32[4,160,256]{2,1,0:T(8,128)S(1)}, f32[4,160,256]{2,1,0:T(8,128)S(1)}, u32[]{:S(2)}, u32[]{:S(2)}) collective-permute-start(f32[4,160,256]{2,1,0:T(8,128)S(1)} %pad_maximum_fusion.own_totals), channel_id=1, source_target_pairs={{0,1},{1,0},{2,3},{3,2},{4,5},{5,4},{6,7},{7,6},{8,9},{9,8},{10,11... | collective-permute-start | bytes 1966088 | tf_op jit(solution)/shard_map/ppermute | solution.py:397
  98.3 2.2 %collective-permute-start.25 = (f32[4,160,256]{2,1,0:T(8,128)S(1)}, f32[4,160,256]{2,1,0:T(8,128)S(1)}, u32[]{:S(2)}, u32[]{:S(2)}) collective-permute-start(f32[4,160,256]{2,1,0:T(8,128)S(1)} %get-tuple-element.68), channel_id=1, source_target_pairs={{0,1},{1,0},{2,3},{3,2},{4,5},{5,4},{6,7},{7,6},{8,9},{9,8},{10,11... | collective-permute-start | bytes 1966088 | tf_op jit(solution)/shard_map/ppermute | solution.py:397
  100.6 8.8 %collective-permute-start.26 = (f32[160,256]{1,0:T(8,128)S(1)}, f32[160,256]{1,0:T(8,128)S(1)}, u32[]{:S(2)}, u32[]{:S(2)}) collective-permute-start(f32[160,256]{1,0:T(8,128)S(1)} %get-tuple-element.78), channel_id=1, source_target_pairs={{0,4},{2,6},{4,0},{6,2},{8,12},{10,14},{12,8},{14,10},{16,20},{18,... | collective-permute-start | bytes 491528 | tf_op jit(solution)/shard_map/ppermute | solution.py:400
  100.9 8.5 %collective-permute-start.27 = (f32[160,256]{1,0:T(8,128)S(1)}, f32[160,256]{1,0:T(8,128)S(1)}, u32[]{:S(2)}, u32[]{:S(2)}) collective-permute-start(f32[160,256]{1,0:T(8,128)S(1)} %get-tuple-element.80), channel_id=1, source_target_pairs={{0,8},{2,10},{4,12},{6,14},{8,0},{10,2},{12,4},{14,6},{16,24},{18,... | collective-permute-start | bytes 491528 | tf_op jit(solution)/shard_map/ppermute | solution.py:400
  102.0 9.6 %collective-permute-start.28 = (f32[160,256]{1,0:T(8,128)S(1)}, f32[160,256]{1,0:T(8,128)S(1)}, u32[]{:S(2)}, u32[]{:S(2)}) collective-permute-start(f32[160,256]{1,0:T(8,128)S(1)} %get-tuple-element.79), channel_id=1, source_target_pairs={{0,12},{2,14},{4,8},{6,10},{8,4},{10,6},{12,0},{14,2},{16,28},{18,... | collective-permute-start | bytes 491528 | tf_op jit(solution)/shard_map/ppermute | solution.py:400
  104.1 16.3 %collective-permute-start.35 = (f32[2,128,256]{2,1,0:T(8,128)S(1)}, f32[2,128,256]{2,1,0:T(8,128)S(1)}, u32[]{:S(2)}, u32[]{:S(2)}) collective-permute-start(f32[2,128,256]{2,1,0:T(8,128)S(1)} %get-tuple-element.70), channel_id=1, source_target_pairs={{0,2},{2,4},{4,6},{6,8},{8,10},{10,12},{12,14},{14,16},{16,18},{18... | collective-permute-start | bytes 786440 | tf_op jit(solution)/shard_map/ppermute | solution.py:414
  108.1 14.8 %collective-permute-start.36 = (f32[2,128,256]{2,1,0:T(8,128)S(1)}, f32[2,128,256]{2,1,0:T(8,128)S(1)}, u32[]{:S(2)}, u32[]{:S(2)}) collective-permute-start(f32[2,128,256]{2,1,0:T(8,128)S(1)} %get-tuple-element.71), channel_id=1, source_target_pairs={{2,0},{4,2},{6,4},{8,6},{10,8},{12,10},{14,12},{16,14},{18,16},{20... | collective-permute-start | bytes 786440 | tf_op jit(solution)/shard_map/ppermute | solution.py:417
  111.6 13.5 %collective-permute-start.29 = (f32[160,256]{1,0:T(8,128)S(1)}, f32[160,256]{1,0:T(8,128)S(1)}, u32[]{:S(2)}, u32[]{:S(2)}) collective-permute-start(f32[160,256]{1,0:T(8,128)S(1)} %fusion.6), channel_id=1, source_target_pairs={{0,2},{2,0},{4,6},{6,4},{8,10},{10,8},{12,14},{14,12},{16,18},{18,... | collective-permute-start | bytes 491528 | tf_op jit(solution)/shard_map/ppermute | solution.py:400
  113.8 17.8 %collective-permute-start.30 = (f32[160,256]{1,0:T(8,128)S(1)}, f32[160,256]{1,0:T(8,128)S(1)}, u32[]{:S(2)}, u32[]{:S(2)}) collective-permute-start(f32[160,256]{1,0:T(8,128)S(1)} %fusion.6), channel_id=1, source_target_pairs={{0,16},{2,18},{4,20},{6,22},{8,24},{10,26},{12,28},{14,30},{16,0},... | collective-permute-start | bytes 491528 | tf_op jit(solution)/shard_map/ppermute | solution.py:400
  115.8 15.8 %collective-permute-start.31 = (f32[160,256]{1,0:T(8,128)S(1)}, f32[160,256]{1,0:T(8,128)S(1)}, u32[]{:S(2)}, u32[]{:S(2)}) collective-permute-start(f32[160,256]{1,0:T(8,128)S(1)} %fusion.6), channel_id=1, source_target_pairs={{0,18},{2,16},{4,22},{6,20},{8,26},{10,24},{12,30},{14,28},{16,2},... | collective-permute-start | bytes 491528 | tf_op jit(solution)/shard_map/ppermute | solution.py:400
  122.9 12.3 %collective-permute-start.37 = (f32[2,256,256]{2,1,0:T(8,128)S(1)}, f32[2,256,256]{2,1,0:T(8,128)S(1)}, u32[]{:S(2)}, u32[]{:S(2)}) collective-permute-start(f32[2,256,256]{2,1,0:T(8,128)S(1)} %get-tuple-element.73.own), channel_id=1, source_target_pairs={{0,1},{1,0},{2,3},{3,2},{4,5},{5,4},{6,7},{7,6},{8,9},{9,8},{10,11... | collective-permute-start | bytes 1572872 | tf_op jit(solution)/shard_map/ppermute | solution.py:397
  122.9 8.9 %collective-permute-start.38 = (f32[2,128,256]{2,1,0:T(8,128)S(1)}, f32[2,128,256]{2,1,0:T(8,128)S(1)}, u32[]{:S(2)}, u32[]{:S(2)}) collective-permute-start(f32[2,128,256]{2,1,0:T(8,128)S(1)} %collective-permute-done.35.b0), channel_id=1, source_target_pairs={{0,1},{1,0},{2,3},{3,2},{4,5},{5,4},{6,7},{7,6},{8,9},{9,8},{10,11... | collective-permute-start | bytes 786440 | tf_op jit(solution)/shard_map/ppermute | solution.py:397
  125.2 10.0 %collective-permute-start.39 = (f32[2,128,256]{2,1,0:T(8,128)S(1)}, f32[2,128,256]{2,1,0:T(8,128)S(1)}, u32[]{:S(2)}, u32[]{:S(2)}) collective-permute-start(f32[2,128,256]{2,1,0:T(8,128)S(1)} %collective-permute-done.36.a0), channel_id=1, source_target_pairs={{0,1},{1,0},{2,3},{3,2},{4,5},{5,4},{6,7},{7,6},{8,9},{9,8},{10,11... | collective-permute-start | bytes 786440 | tf_op jit(solution)/shard_map/ppermute | solution.py:397
  131.6 6.9 %collective-permute-start.32 = (f32[160,256]{1,0:T(8,128)S(1)}, f32[160,256]{1,0:T(8,128)S(1)}, u32[]{:S(2)}, u32[]{:S(2)}) collective-permute-start(f32[160,256]{1,0:T(8,128)S(1)} %add_add_fusion), channel_id=1, source_target_pairs={{0,4},{2,6},{4,0},{6,2},{8,12},{10,14},{12,8},{14,10},{16,20},{18,... | collective-permute-start | bytes 491528 | tf_op jit(solution)/shard_map/ppermute | solution.py:400
  131.8 6.8 %collective-permute-start.33 = (f32[160,256]{1,0:T(8,128)S(1)}, f32[160,256]{1,0:T(8,128)S(1)}, u32[]{:S(2)}, u32[]{:S(2)}) collective-permute-start(f32[160,256]{1,0:T(8,128)S(1)} %add_add_fusion), channel_id=1, source_target_pairs={{0,8},{2,10},{4,12},{6,14},{8,0},{10,2},{12,4},{14,6},{16,24},{18,... | collective-permute-start | bytes 491528 | tf_op jit(solution)/shard_map/ppermute | solution.py:400
  131.8 8.5 %collective-permute-start.34 = (f32[160,256]{1,0:T(8,128)S(1)}, f32[160,256]{1,0:T(8,128)S(1)}, u32[]{:S(2)}, u32[]{:S(2)}) collective-permute-start(f32[160,256]{1,0:T(8,128)S(1)} %add_add_fusion), channel_id=1, source_target_pairs={{0,12},{2,14},{4,8},{6,10},{8,4},{10,6},{12,0},{14,2},{16,28},{18,... | collective-permute-start | bytes 491528 | tf_op jit(solution)/shard_map/ppermute | solution.py:400
  140.4 1.4 collective-permute-start.40
  (6 other events, 7.3 us)

commit v4 on v3

--- a/solution.py
+++ b/solution.py
@@ -221,8 +221,11 @@
         )
 
 
-def ready_kernel(info, probe, measured, table, own, observed, split):
+def ready_kernel(size, info, strip_ref, probe, measured, table, columns, own, observed, split):
     own[...] = probe[...]
+    column = spot(info, size, 0, 0, info[25])[1]
+    for part in range(2):
+        columns[part] = take_columns(strip_ref[part], column, size[2])
     for minibatch in range(2):
         observed[minibatch] = measured[minibatch, info[25]]
     for i in range(2):
@@ -422,18 +425,21 @@
     tile, slot = lax.axis_index("tile"), lax.axis_index("mode")
     index = jnp.stack([tile, slot]).astype(jnp.int32)
     here = jnp.concatenate([positions.ravel()] * 3 + [index])
-    one_part = lax.dynamic_index_in_dim(object_field, slot, 0, keepdims=False)
-    edges = [from_below(one_part[strip - half :]), from_above(one_part[:half])]
+    first = slot == 0
+    edges = [
+        from_below(jnp.where(first, object_field[0, strip - half :], object_field[1, strip - half :])),
+        from_above(jnp.where(first, object_field[0, :half], object_field[1, :half])),
+    ]
     below, above = from_below(positions), from_above(positions)
     other = swap(probe[0])
-    own, observed, table = call(
-        ready_kernel,
+    columns, own, observed, table = call(
+        bind(ready_kernel, size),
         "ready",
-        [field, field, jax.ShapeDtypeStruct((4, pattern, pattern), BF16)],
-        (here, probe[0], measured, jnp.asarray(table_of(pattern))),
-    )
-    *edges, below, above, own, observed, table = lax.optimization_barrier(
-        (*edges, below, above, own, observed, table)
+        [(2, strip, pattern), field, field, jax.ShapeDtypeStruct((4, pattern, pattern), BF16)],
+        (here, object_field, probe[0], measured, jnp.asarray(table_of(pattern))),
+    )
+    *edges, below, above, columns, own, observed, table = lax.optimization_barrier(
+        (*edges, below, above, columns, own, observed, table)
     )
     edges = [edges[0], swap(edges[0]), edges[1], swap(edges[1])]
     info = jnp.concatenate([below.ravel(), positions.ravel(), above.ravel(), index])
@@ -442,8 +448,9 @@
         last = minibatch == 1
         rows = pattern // GROUP
         blocks = (GROUP, 2 * rows + rows // 2, pattern)
-        cut = (object_field, *edges)
+        cut = (columns, *edges)
         if last:
+            cut = (object_field, *edges)
             cut = call(
                 bind(patch_kernel, size, minibatch), "patch", [field], (here, *cut), [window], 10**10
             )

time: 145 us -> 146 us (level)
  waiting for transfers between devices: 50.6 us -> 48.4 us
  other arithmetic: 2.37 us -> 4.44 us
    select_n x0 -> x1, other arithmetic: none -> 2.09 us  [shards_by_position(): jnp.where(first, object_field[0, :half], object_field[1, :half])]
    slice x1 -> x0, local copies, waits for them, and re-layouts: 1.94 us -> none  [shards_by_position(): edges = [from_below(one_part[strip - half:]), from_above(one_part[:half])]]
    unnamed x26 -> x30, local copies, waits for them, and re-layouts: 2.24 us -> 4.09 us
where the time goes in v4:
time: 146 us; the launch traced here: 144 us
  starting transfers between devices  60 us (41%)
  waiting for transfers between devices  48.4 us (33%)
  Pallas kernels  23.5 us (16%)
  local copies, waits for them, and re-layouts  6.32 us (4%)
  other arithmetic  4.44 us (3%)
    ppermute x18, starting transfers between devices, across(): return lax.ppermute(value, 'tile', [(i, i ^ k) for i in range(tiles)])  30.2 us
    ppermute x18, waiting for transfers between devices, across(): return lax.ppermute(value, 'tile', [(i, i ^ k) for i in range(tiles)])  28.6 us
    pallas_call x10, Pallas kernels, call(): pl.pallas_call(kernel, out_shape=shapes, in_specs=[smem] + [vmem] * (len(...  23.5 us
    ppermute x5, starting transfers between devices, from_below(): return lax.ppermute(value, 'tile', up)  20.9 us
    ppermute x5, waiting for transfers between devices, from_below(): return lax.ppermute(value, 'tile', up)  8.24 us
    ppermute x5, starting transfers between devices, from_above(): return lax.ppermute(value, 'tile', down)  6.64 us
    ppermute x5, waiting for transfers between devices, from_above(): return lax.ppermute(value, 'tile', down)  6.46 us
    ppermute x13, waiting for transfers between devices, swap(): return lax.ppermute(value, 'mode', [(0, 1), (1, 0)])  5.09 us
  transfers between devices with their start and end apart: 41, of which 23 were waited for; matrix products, arithmetic and copies ran while one was open for 3% of the time, Pallas kernels for 8%

profile of v4, /device:TPU:0, one launch (start us, length us, event | category | flops | bytes accessed | tf_op | source)
XLA Modules:
  0.0 143.6 jit_solution(4750699348027629230)
XLA Ops:
  0.7 2.1 %select_bitcast_fusion = (f32[128,512]{1,0:T(8,128)S(1)}, f32[128,512]{1,0:T(8,128)}) fusion(f32[2,256,512]{2,1,0:T(8,128)} %strip_ref.3, pred[]{:T(512)S(6)} %eq.3), kind=kLoop, calls=%fused_computation.2 | loop fusion | flops 131072 | bytes 1572865 | tf_op jit(solution)/shard_map/jit(_where)/select_n | solution.py:431
  2.7 5.0 %collective-permute-start = (f32[128,512]{1,0:T(8,128)}, f32[128,512]{1,0:T(8,128)S(1)}, u32[]{:S(2)}, u32[]{:S(2)}) collective-permute-start(f32[128,512]{1,0:T(8,128)} %get-tuple-element.89), channel_id=1, source_target_pairs={{0,2},{2,4},{4,6},{6,8},{8,10},{10,12},{12,14},{14,16},{16,18},{18... | collective-permute-start | bytes 786440 | tf_op jit(solution)/shard_map/ppermute | solution.py:417
  7.7 1.3 collective-permute-start.1
  9.1 4.5 %collective-permute-start.2 = (s32[2,2,2]{2,1,0:T(2,128)S(1)}, s32[2,2,2]{2,1,0:T(2,128)S(1)}, u32[]{:S(2)}, u32[]{:S(2)}) collective-permute-start(s32[2,2,2]{2,1,0:T(2,128)S(1)} %copy-done.11), channel_id=1, source_target_pairs={{0,2},{2,4},{4,6},{6,8},{8,10},{10,12},{12,14},{14,16},{16,18},{18... | collective-permute-start | bytes 104 | tf_op jit(solution)/shard_map/ppermute | solution.py:417
  13.7 1.3 collective-permute-start.3
  15.2 1.2 copy-done.1
  19.2 1.9 %collective-permute-done.3 = s32[2,2,2]{2,1,0:T(2,128)S(1)} collective-permute-done((s32[2,2,2]{2,1,0:T(2,128)S(1)}, s32[2,2,2]{2,1,0:T(2,128)S(1)}, u32[]{:S(2)}, u32[]{:S(2)}) %collective-permute-start.3) | collective-permute-done | bytes 64 | tf_op jit(solution)/shard_map/ppermute | solution.py:420
  24.1 5.7 %field.2 = (f32[2,256,256]{2,1,0:T(8,128)S(1)}, f32[2,128,256]{2,1,0:T(8,128)}, f32[2,128,256]{2,1,0:T(8,128)}, f32[4,160,256]{2,1,0:T(8,128)S(1)}, f32[4,160,256]{2,1,0:T(8,128)S(1)}) custom-call(s32[26]{0:T(128)S(1)} %concatenate.8.info, f32[2,256,256]{2,1,0:T(8,128)S(1)} %get-tuple-element.48.strip_ref, f32[128,512]{1,0:T(8,128)S(1)} %collective-permute-done.refs_0_, ...), custom_call_target="tpu_custom_call" | custom-call | flops 3221225472 | bytes 6029416 | tf_op jit(solution)/shard_map/field/pallas_call | solution.py:374
  29.9 3.4 %collective-permute-start.7 = (f32[2,128,256]{2,1,0:T(8,128)}, f32[2,128,256]{2,1,0:T(8,128)S(1)}, u32[]{:S(2)}, u32[]{:S(2)}) collective-permute-start(f32[2,128,256]{2,1,0:T(8,128)} %get-tuple-element.55), channel_id=1, source_target_pairs={{0,2},{2,4},{4,6},{6,8},{8,10},{10,12},{12,14},{14,16},{16,18},{18... | collective-permute-start | bytes 786440 | tf_op jit(solution)/shard_map/ppermute | solution.py:417
  33.3 1.3 collective-permute-start.8
  35.6 3.9 %collective-permute-start.13 = (f32[160,256]{1,0:T(8,128)}, f32[160,256]{1,0:T(8,128)}, u32[]{:S(2)}, u32[]{:S(2)}) collective-permute-start(f32[160,256]{1,0:T(8,128)} %get-tuple-element.85), channel_id=1, source_target_pairs={{0,4},{2,6},{4,0},{6,2},{8,12},{10,14},{12,8},{14,10},{16,20},{18,... | collective-permute-start | bytes 491528 | tf_op jit(solution)/shard_map/ppermute | solution.py:403
  39.6 2.8 %collective-permute-start.14 = (f32[160,256]{1,0:T(8,128)}, f32[160,256]{1,0:T(8,128)}, u32[]{:S(2)}, u32[]{:S(2)}) collective-permute-start(f32[160,256]{1,0:T(8,128)} %get-tuple-element.87), channel_id=1, source_target_pairs={{0,8},{2,10},{4,12},{6,14},{8,0},{10,2},{12,4},{14,6},{16,24},{18,... | collective-permute-start | bytes 491528 | tf_op jit(solution)/shard_map/ppermute | solution.py:403
  42.3 1.5 %collective-permute-start.15 = (f32[160,256]{1,0:T(8,128)}, f32[160,256]{1,0:T(8,128)}, u32[]{:S(2)}, u32[]{:S(2)}) collective-permute-start(f32[160,256]{1,0:T(8,128)} %get-tuple-element.86), channel_id=1, source_target_pairs={{0,12},{2,14},{4,8},{6,10},{8,4},{10,6},{12,0},{14,2},{16,28},{18,... | collective-permute-start | bytes 491528 | tf_op jit(solution)/shard_map/ppermute | solution.py:403
  45.8 1.7 %illumination.2.illum = f32[256,512]{1,0:T(8,128)S(1)} custom-call(s32[26]{0:T(128)S(1)} %concatenate.9.info, f32[2,256,256]{2,1,0:T(8,128)S(1)} %get-tuple-element.51.refs_4_.own.refs_0_, f32[2,256,256]{2,1,0:T(8,128)S(1)} %collective-permute-done.6.refs_5_.other.refs_1_), custom_call_target="tpu_custom_call" | custom-call | bytes 1572968 | tf_op jit(solution)/shard_map/illumination/pallas_call | solution.py:374
  48.2 4.1 %collective-permute-done.14 = f32[160,256]{1,0:T(8,128)} collective-permute-done((f32[160,256]{1,0:T(8,128)}, f32[160,256]{1,0:T(8,128)}, u32[]{:S(2)}, u32[]{:S(2)}) %collective-permute-start.14) | collective-permute-done | bytes 163872 | tf_op jit(solution)/shard_map/ppermute | solution.py:403
  52.3 1.2 fusion.13
  53.5 3.1 %collective-permute-start.16 = (f32[160,256]{1,0:T(8,128)S(1)}, f32[160,256]{1,0:T(8,128)S(1)}, u32[]{:S(2)}, u32[]{:S(2)}) collective-permute-start(f32[160,256]{1,0:T(8,128)S(1)} %fusion.13), channel_id=1, source_target_pairs={{0,2},{2,0},{4,6},{6,4},{8,10},{10,8},{12,14},{14,12},{16,18},{18,... | collective-permute-start | bytes 491528 | tf_op jit(solution)/shard_map/ppermute | solution.py:403
  56.6 2.6 %collective-permute-start.17 = (f32[160,256]{1,0:T(8,128)S(1)}, f32[160,256]{1,0:T(8,128)S(1)}, u32[]{:S(2)}, u32[]{:S(2)}) collective-permute-start(f32[160,256]{1,0:T(8,128)S(1)} %fusion.13), channel_id=1, source_target_pairs={{0,16},{2,18},{4,20},{6,22},{8,24},{10,26},{12,28},{14,30},{16,0},... | collective-permute-start | bytes 491528 | tf_op jit(solution)/shard_map/ppermute | solution.py:403
  59.2 2.8 %update.2 = (f32[2,256,512]{2,1,0:T(8,128)S(1)}, f32[2,128,256]{2,1,0:T(8,128)S(1)}, f32[2,128,256]{2,1,0:T(8,128)S(1)}) custom-call(s32[26]{0:T(128)S(1)} %concatenate.9.info, f32[2,256,512]{2,1,0:T(8,128)S(1)} %copy-done, f32[256,512]{1,0:T(8,128)S(1)} %illumination.2.illum, f32[2,256,256]{2,1,0:T(8,128)S(1)} %get-tuple-element.58.own, ...), custom_call_target="tpu_custom_call" | custom-call | bytes 5242984 | tf_op jit(solution)/shard_map/update/pallas_call | solution.py:374
  62.0 3.7 %collective-permute-start.19 = (f32[2,128,256]{2,1,0:T(8,128)S(1)}, f32[2,128,256]{2,1,0:T(8,128)S(1)}, u32[]{:S(2)}, u32[]{:S(2)}) collective-permute-start(f32[2,128,256]{2,1,0:T(8,128)S(1)} %get-tuple-element.64), channel_id=1, source_target_pairs={{0,2},{2,4},{4,6},{6,8},{8,10},{10,12},{12,14},{14,16},{16,18},{18... | collective-permute-start | bytes 786440 | tf_op jit(solution)/shard_map/ppermute | solution.py:417
  65.7 1.5 %collective-permute-start.20 = (f32[2,128,256]{2,1,0:T(8,128)S(1)}, f32[2,128,256]{2,1,0:T(8,128)S(1)}, u32[]{:S(2)}, u32[]{:S(2)}) collective-permute-start(f32[2,128,256]{2,1,0:T(8,128)S(1)} %get-tuple-element.65), channel_id=1, source_target_pairs={{2,0},{4,2},{6,4},{8,6},{10,8},{12,10},{14,12},{16,14},{18,16},{20... | collective-permute-start | bytes 786440 | tf_op jit(solution)/shard_map/ppermute | solution.py:420
  67.2 4.4 %collective-permute-done.17 = f32[160,256]{1,0:T(8,128)S(1)} collective-permute-done((f32[160,256]{1,0:T(8,128)S(1)}, f32[160,256]{1,0:T(8,128)S(1)}, u32[]{:S(2)}, u32[]{:S(2)}) %collective-permute-start.17) | collective-permute-done | bytes 163872 | tf_op jit(solution)/shard_map/ppermute | solution.py:403
  71.6 2.7 %collective-permute-done.18 = f32[160,256]{1,0:T(8,128)S(1)} collective-permute-done((f32[160,256]{1,0:T(8,128)S(1)}, f32[160,256]{1,0:T(8,128)S(1)}, u32[]{:S(2)}, u32[]{:S(2)}) %collective-permute-start.18) | collective-permute-done | bytes 163872 | tf_op jit(solution)/shard_map/ppermute | solution.py:403
  74.3 5.9 %collective-permute-done.19.below = f32[2,128,256]{2,1,0:T(8,128)S(1)} collective-permute-done((f32[2,128,256]{2,1,0:T(8,128)S(1)}, f32[2,128,256]{2,1,0:T(8,128)S(1)}, u32[]{:S(2)}, u32[]{:S(2)}) %collective-permute-start.19) | collective-permute-done | bytes 262176 | tf_op jit(solution)/shard_map/ppermute | solution.py:417
  80.2 2.2 %collective-permute-done.20.above = f32[2,128,256]{2,1,0:T(8,128)S(1)} collective-permute-done((f32[2,128,256]{2,1,0:T(8,128)S(1)}, f32[2,128,256]{2,1,0:T(8,128)S(1)}, u32[]{:S(2)}, u32[]{:S(2)}) %collective-permute-start.20) | collective-permute-done | bytes 262176 | tf_op jit(solution)/shard_map/ppermute | solution.py:420
  82.4 3.5 %collective-permute-start.23 = (f32[160,256]{1,0:T(8,128)S(1)}, f32[160,256]{1,0:T(8,128)S(1)}, u32[]{:S(2)}, u32[]{:S(2)}) collective-permute-start(f32[160,256]{1,0:T(8,128)S(1)} %add_add_fusion.1), channel_id=1, source_target_pairs={{0,12},{2,14},{4,8},{6,10},{8,4},{10,6},{12,0},{14,2},{16,28},{18,... | collective-permute-start | bytes 491528 | tf_op jit(solution)/shard_map/ppermute | solution.py:403
  85.8 3.5 %collective-permute-done.21 = f32[160,256]{1,0:T(8,128)S(1)} collective-permute-done((f32[160,256]{1,0:T(8,128)S(1)}, f32[160,256]{1,0:T(8,128)S(1)}, u32[]{:S(2)}, u32[]{:S(2)}) %collective-permute-start.21) | collective-permute-done | bytes 163872 | tf_op jit(solution)/shard_map/ppermute | solution.py:403
  89.3 1.8 %collective-permute-done.23 = f32[160,256]{1,0:T(8,128)S(1)} collective-permute-done((f32[160,256]{1,0:T(8,128)S(1)}, f32[160,256]{1,0:T(8,128)S(1)}, u32[]{:S(2)}, u32[]{:S(2)}) %collective-permute-start.23) | collective-permute-done | bytes 163872 | tf_op jit(solution)/shard_map/ppermute | solution.py:403
  94.0 4.5 %field.3 = (f32[2,256,256]{2,1,0:T(8,128)S(1)}, f32[2,128,256]{2,1,0:T(8,128)S(1)}, f32[2,128,256]{2,1,0:T(8,128)S(1)}, f32[4,160,256]{2,1,0:T(8,128)S(1)}, f32[4,160,256]{2,1,0:T(8,128)S(1)}) custom-call(s32[26]{0:T(128)S(1)} %concatenate.8.info, f32[2,256,256]{2,1,0:T(8,128)S(1)} %patch.1.strip_ref, f32[2,256,256]{2,1,0:T(8,128)S(1)} %get-tuple-element.69.refs_0_.own, ...), custom_call_target="tpu_custom_call" | custom-call | flops 3221225472 | bytes 4980840 | tf_op jit(solution)/shard_map/field/pallas_call | solution.py:374
  98.7 1.9 %collective-permute-done.25 = f32[4,160,256]{2,1,0:T(8,128)S(1)} collective-permute-done((f32[4,160,256]{2,1,0:T(8,128)S(1)}, f32[4,160,256]{2,1,0:T(8,128)S(1)}, u32[]{:S(2)}, u32[]{:S(2)}) %collective-permute-start.25) | collective-permute-done | bytes 655392 | tf_op jit(solution)/shard_map/ppermute | solution.py:400
  101.3 1.1 collective-permute-start.27
  102.4 1.9 %collective-permute-start.28 = (f32[160,256]{1,0:T(8,128)S(1)}, f32[160,256]{1,0:T(8,128)S(1)}, u32[]{:S(2)}, u32[]{:S(2)}) collective-permute-start(f32[160,256]{1,0:T(8,128)S(1)} %get-tuple-element.83), channel_id=1, source_target_pairs={{0,12},{2,14},{4,8},{6,10},{8,4},{10,6},{12,0},{14,2},{16,28},{18,... | collective-permute-start | bytes 491528 | tf_op jit(solution)/shard_map/ppermute | solution.py:403
  104.3 4.3 %collective-permute-start.35 = (f32[2,128,256]{2,1,0:T(8,128)S(1)}, f32[2,128,256]{2,1,0:T(8,128)S(1)}, u32[]{:S(2)}, u32[]{:S(2)}) collective-permute-start(f32[2,128,256]{2,1,0:T(8,128)S(1)} %get-tuple-element.74), channel_id=1, source_target_pairs={{0,2},{2,4},{4,6},{6,8},{8,10},{10,12},{12,14},{14,16},{16,18},{18... | collective-permute-start | bytes 786440 | tf_op jit(solution)/shard_map/ppermute | solution.py:417
  108.6 1.3 collective-permute-start.36
  109.9 1.9 %collective-permute-done.28 = f32[160,256]{1,0:T(8,128)S(1)} collective-permute-done((f32[160,256]{1,0:T(8,128)S(1)}, f32[160,256]{1,0:T(8,128)S(1)}, u32[]{:S(2)}, u32[]{:S(2)}) %collective-permute-start.28) | collective-permute-done | bytes 163872 | tf_op jit(solution)/shard_map/ppermute | solution.py:403
  111.8 2.4 %collective-permute-start.29 = (f32[160,256]{1,0:T(8,128)S(1)}, f32[160,256]{1,0:T(8,128)S(1)}, u32[]{:S(2)}, u32[]{:S(2)}) collective-permute-start(f32[160,256]{1,0:T(8,128)S(1)} %fusion.6), channel_id=1, source_target_pairs={{0,2},{2,0},{4,6},{6,4},{8,10},{10,8},{12,14},{14,12},{16,18},{18,... | collective-permute-start | bytes 491528 | tf_op jit(solution)/shard_map/ppermute | solution.py:403
  114.2 2.0 %collective-permute-start.30 = (f32[160,256]{1,0:T(8,128)S(1)}, f32[160,256]{1,0:T(8,128)S(1)}, u32[]{:S(2)}, u32[]{:S(2)}) collective-permute-start(f32[160,256]{1,0:T(8,128)S(1)} %fusion.6), channel_id=1, source_target_pairs={{0,16},{2,18},{4,20},{6,22},{8,24},{10,26},{12,28},{14,30},{16,0},... | collective-permute-start | bytes 491528 | tf_op jit(solution)/shard_map/ppermute | solution.py:403
  116.2 1.4 collective-permute-start.31
  117.6 1.7 %illumination.3.illum = f32[256,512]{1,0:T(8,128)S(1)} custom-call(s32[26]{0:T(128)S(1)} %concatenate.9.info, f32[2,256,256]{2,1,0:T(8,128)S(1)} %get-tuple-element.69.refs_0_.own, f32[2,256,256]{2,1,0:T(8,128)S(1)} %get-tuple-element.70.refs_1_.other), custom_call_target="tpu_custom_call" | custom-call | bytes 1572968 | tf_op jit(solution)/shard_map/illumination/pallas_call | solution.py:374
  119.3 1.6 %collective-permute-done.35.b0 = f32[2,128,256]{2,1,0:T(8,128)S(1)} collective-permute-done((f32[2,128,256]{2,1,0:T(8,128)S(1)}, f32[2,128,256]{2,1,0:T(8,128)S(1)}, u32[]{:S(2)}, u32[]{:S(2)}) %collective-permute-start.35) | collective-permute-done | bytes 262176 | tf_op jit(solution)/shard_map/ppermute | solution.py:417
  120.9 2.3 %collective-permute-done.36.a0 = f32[2,128,256]{2,1,0:T(8,128)S(1)} collective-permute-done((f32[2,128,256]{2,1,0:T(8,128)S(1)}, f32[2,128,256]{2,1,0:T(8,128)S(1)}, u32[]{:S(2)}, u32[]{:S(2)}) %collective-permute-start.36) | collective-permute-done | bytes 262176 | tf_op jit(solution)/shard_map/ppermute | solution.py:420
  123.7 1.7 %collective-permute-done.29 = f32[160,256]{1,0:T(8,128)S(1)} collective-permute-done((f32[160,256]{1,0:T(8,128)S(1)}, f32[160,256]{1,0:T(8,128)S(1)}, u32[]{:S(2)}, u32[]{:S(2)}) %collective-permute-start.29) | collective-permute-done | bytes 163872 | tf_op jit(solution)/shard_map/ppermute | solution.py:403
  125.5 6.5 %collective-permute-done.30 = f32[160,256]{1,0:T(8,128)S(1)} collective-permute-done((f32[160,256]{1,0:T(8,128)S(1)}, f32[160,256]{1,0:T(8,128)S(1)}, u32[]{:S(2)}, u32[]{:S(2)}) %collective-permute-start.30) | collective-permute-done | bytes 163872 | tf_op jit(solution)/shard_map/ppermute | solution.py:403
  132.3 3.3 %collective-permute-start.34 = (f32[160,256]{1,0:T(8,128)S(1)}, f32[160,256]{1,0:T(8,128)S(1)}, u32[]{:S(2)}, u32[]{:S(2)}) collective-permute-start(f32[160,256]{1,0:T(8,128)S(1)} %add_add_fusion), channel_id=1, source_target_pairs={{0,12},{2,14},{4,8},{6,10},{8,4},{10,6},{12,0},{14,2},{16,28},{18,... | collective-permute-start | bytes 491528 | tf_op jit(solution)/shard_map/ppermute | solution.py:403
  135.6 3.1 %update.3 = f32[2,256,512]{2,1,0:T(8,128)} custom-call(s32[26]{0:T(128)S(1)} %concatenate.9.info, f32[2,256,512]{2,1,0:T(8,128)S(1)} %get-tuple-element.61.strip_ref, f32[256,512]{1,0:T(8,128)S(1)} %illumination.3.illum, f32[2,256,256]{2,1,0:T(8,128)S(1)} %get-tuple-element.77.own, f32[2,256,256]{2,1,0:T(8,128)S(1)} %collective-permute-done.37.other, ...), custom_call_target="tpu_custom_call" | custom-call | bytes 4718696 | tf_op jit(solution)/shard_map/update/pallas_call | solution.py:374
  139.1 1.7 %collective-permute-done.34 = f32[160,256]{1,0:T(8,128)S(1)} collective-permute-done((f32[160,256]{1,0:T(8,128)S(1)}, f32[160,256]{1,0:T(8,128)S(1)}, u32[]{:S(2)}, u32[]{:S(2)}) %collective-permute-start.34) | collective-permute-done | bytes 163872 | tf_op jit(solution)/shard_map/ppermute | solution.py:403
  140.9 1.3 collective-permute-done.40.other_totals
  142.2 1.4 probe.3
  (89 shorter events, 14.9 us)
Async XLA Ops:
  0.6 14.5 %copy-start = (f32[2,256,512]{2,1,0:T(8,128)S(1)}, f32[2,256,512]{2,1,0:T(8,128)}, u32[]{:S(2)}) copy-start(f32[2,256,512]{2,1,0:T(8,128)} %strip_ref.3) | copy-start | bytes 3145732
  0.6 8.4 %copy-start.2 = (f32[1,2,256,256]{3,2,1,0:T(8,128)S(1)}, f32[1,2,256,256]{3,2,1,0:T(8,128)}, u32[]{:S(2)}) copy-start(f32[1,2,256,256]{3,2,1,0:T(8,128)} %param.6) | copy-start | bytes 1572868
  2.7 6.4 %copy-start.11 = (s32[2,2,2]{2,1,0:T(2,128)S(1)}, s32[2,2,2]{2,1,0:T(2,128)}, u32[]{:S(2)}) copy-start(s32[2,2,2]{2,1,0:T(2,128)} %param.7) | copy-start | bytes 100
  2.7 18.4 %collective-permute-start = (f32[128,512]{1,0:T(8,128)}, f32[128,512]{1,0:T(8,128)S(1)}, u32[]{:S(2)}, u32[]{:S(2)}) collective-permute-start(f32[128,512]{1,0:T(8,128)} %get-tuple-element.89), channel_id=1, source_target_pairs={{0,2},{2,4},{4,6},{6,8},{8,10},{10,12},{12,14},{14,16},{16,18},{18... | collective-permute-start | bytes 786440 | tf_op jit(solution)/shard_map/ppermute | solution.py:417
  7.7 13.4 %collective-permute-start.1 = (f32[128,512]{1,0:T(8,128)S(1)}, f32[128,512]{1,0:T(8,128)S(1)}, u32[]{:S(2)}, u32[]{:S(2)}) collective-permute-start(f32[128,512]{1,0:T(8,128)S(1)} %get-tuple-element.88), channel_id=1, source_target_pairs={{2,0},{4,2},{6,4},{8,6},{10,8},{12,10},{14,12},{16,14},{18,16},{20... | collective-permute-start | bytes 786440 | tf_op jit(solution)/shard_map/ppermute | solution.py:420
  9.0 14.1 %collective-permute-start.6 = (f32[2,256,256]{2,1,0:T(8,128)S(1)}, f32[2,256,256]{2,1,0:T(8,128)S(1)}, u32[]{:S(2)}, u32[]{:S(2)}) collective-permute-start(f32[2,256,256]{2,1,0:T(8,128)S(1)} %bitcast.44), channel_id=1, source_target_pairs={{0,1},{1,0},{2,3},{3,2},{4,5},{5,4},{6,7},{7,6},{8,9},{9,8},{10,11... | collective-permute-start | bytes 1572872 | tf_op jit(solution)/shard_map/ppermute | solution.py:400
  9.1 10.1 %collective-permute-start.2 = (s32[2,2,2]{2,1,0:T(2,128)S(1)}, s32[2,2,2]{2,1,0:T(2,128)S(1)}, u32[]{:S(2)}, u32[]{:S(2)}) collective-permute-start(s32[2,2,2]{2,1,0:T(2,128)S(1)} %copy-done.11), channel_id=1, source_target_pairs={{0,2},{2,4},{4,6},{6,8},{8,10},{10,12},{12,14},{14,16},{16,18},{18... | collective-permute-start | bytes 104 | tf_op jit(solution)/shard_map/ppermute | solution.py:417
  13.7 7.4 %collective-permute-start.3 = (s32[2,2,2]{2,1,0:T(2,128)S(1)}, s32[2,2,2]{2,1,0:T(2,128)S(1)}, u32[]{:S(2)}, u32[]{:S(2)}) collective-permute-start(s32[2,2,2]{2,1,0:T(2,128)S(1)} %copy-done.11), channel_id=1, source_target_pairs={{2,0},{4,2},{6,4},{8,6},{10,8},{12,10},{14,12},{16,14},{18,16},{20... | collective-permute-start | bytes 104 | tf_op jit(solution)/shard_map/ppermute | solution.py:420
  18.5 11.3 %copy-start.4 = (f32[2,256,256]{2,1,0:T(8,128)}, f32[2,256,256]{2,1,0:T(8,128)S(1)}, u32[]{:S(2)}) copy-start(f32[2,256,256]{2,1,0:T(8,128)S(1)} %get-tuple-element.52.refs_6_.refs_2_) | copy-start | bytes 1572868
  18.5 11.3 %copy-start.6 = (bf16[4,256,256]{2,1,0:T(8,128)(2,1)}, bf16[4,256,256]{2,1,0:T(8,128)(2,1)S(1)}, u32[]{:S(2)}) copy-start(bf16[4,256,256]{2,1,0:T(8,128)(2,1)S(1)} %get-tuple-element.53.refs_7_.refs_3_) | copy-start | bytes 1572868
  21.1 2.0 %copy-start.12 = (s32[2,2,2]{2,1,0:T(2,128)}, s32[2,2,2]{2,1,0:T(2,128)S(1)}, u32[]{:S(2)}) copy-start(s32[2,2,2]{2,1,0:T(2,128)S(1)} %collective-permute-done.3) | copy-start | bytes 100
  21.1 1.6 %collective-permute-start.4 = (f32[128,512]{1,0:T(8,128)S(1)}, f32[128,512]{1,0:T(8,128)S(1)}, u32[]{:S(2)}, u32[]{:S(2)}) collective-permute-start(f32[128,512]{1,0:T(8,128)S(1)} %collective-permute-done.refs_0_), channel_id=1, source_target_pairs={{0,1},{1,0},{2,3},{3,2},{4,5},{5,4},{6,7},{7,6},{8,9},{9,8},{10,11... | collective-permute-start | bytes 786440 | tf_op jit(solution)/shard_map/ppermute | solution.py:400
  21.2 1.9 %collective-permute-start.5 = (f32[128,512]{1,0:T(8,128)S(1)}, f32[128,512]{1,0:T(8,128)S(1)}, u32[]{:S(2)}, u32[]{:S(2)}) collective-permute-start(f32[128,512]{1,0:T(8,128)S(1)} %collective-permute-done.1.refs_2_), channel_id=1, source_target_pairs={{0,1},{1,0},{2,3},{3,2},{4,5},{5,4},{6,7},{7,6},{8,9},{9,8},{10,11... | collective-permute-start | bytes 786440 | tf_op jit(solution)/shard_map/ppermute | solution.py:400
  29.8 4.9 %collective-permute-start.12 = (f32[4,160,256]{2,1,0:T(8,128)S(1)}, f32[4,160,256]{2,1,0:T(8,128)S(1)}, u32[]{:S(2)}, u32[]{:S(2)}) collective-permute-start(f32[4,160,256]{2,1,0:T(8,128)S(1)} %get-tuple-element.63), channel_id=1, source_target_pairs={{0,1},{1,0},{2,3},{3,2},{4,5},{5,4},{6,7},{7,6},{8,9},{9,8},{10,11... | collective-permute-start | bytes 1966088 | tf_op jit(solution)/shard_map/ppermute | solution.py:400
  29.9 17.6 %collective-permute-start.7 = (f32[2,128,256]{2,1,0:T(8,128)}, f32[2,128,256]{2,1,0:T(8,128)S(1)}, u32[]{:S(2)}, u32[]{:S(2)}) collective-permute-start(f32[2,128,256]{2,1,0:T(8,128)} %get-tuple-element.55), channel_id=1, source_target_pairs={{0,2},{2,4},{4,6},{6,8},{8,10},{10,12},{12,14},{14,16},{16,18},{18... | collective-permute-start | bytes 786440 | tf_op jit(solution)/shard_map/ppermute | solution.py:417
  33.3 14.3 %collective-permute-start.8 = (f32[2,128,256]{2,1,0:T(8,128)}, f32[2,128,256]{2,1,0:T(8,128)}, u32[]{:S(2)}, u32[]{:S(2)}) collective-permute-start(f32[2,128,256]{2,1,0:T(8,128)} %get-tuple-element.56), channel_id=1, source_target_pairs={{2,0},{4,2},{6,4},{8,6},{10,8},{12,10},{14,12},{16,14},{18,16},{20... | collective-permute-start | bytes 786440 | tf_op jit(solution)/shard_map/ppermute | solution.py:420
  35.6 12.5 %collective-permute-start.13 = (f32[160,256]{1,0:T(8,128)}, f32[160,256]{1,0:T(8,128)}, u32[]{:S(2)}, u32[]{:S(2)}) collective-permute-start(f32[160,256]{1,0:T(8,128)} %get-tuple-element.85), channel_id=1, source_target_pairs={{0,4},{2,6},{4,0},{6,2},{8,12},{10,14},{12,8},{14,10},{16,20},{18,... | collective-permute-start | bytes 491528 | tf_op jit(solution)/shard_map/ppermute | solution.py:403
  39.6 4.9 %copy-start.13 = (s32[2,2,2]{2,1,0:T(2,128)S(1)}, s32[2,2,2]{2,1,0:T(2,128)}, u32[]{:S(2)}) copy-start(s32[2,2,2]{2,1,0:T(2,128)} %copy-done.12) | copy-start | bytes 100
  39.6 12.7 %collective-permute-start.14 = (f32[160,256]{1,0:T(8,128)}, f32[160,256]{1,0:T(8,128)}, u32[]{:S(2)}, u32[]{:S(2)}) collective-permute-start(f32[160,256]{1,0:T(8,128)} %get-tuple-element.87), channel_id=1, source_target_pairs={{0,8},{2,10},{4,12},{6,14},{8,0},{10,2},{12,4},{14,6},{16,24},{18,... | collective-permute-start | bytes 491528 | tf_op jit(solution)/shard_map/ppermute | solution.py:403
  42.3 10.0 %collective-permute-start.15 = (f32[160,256]{1,0:T(8,128)}, f32[160,256]{1,0:T(8,128)}, u32[]{:S(2)}, u32[]{:S(2)}) collective-permute-start(f32[160,256]{1,0:T(8,128)} %get-tuple-element.86), channel_id=1, source_target_pairs={{0,12},{2,14},{4,8},{6,10},{8,4},{10,6},{12,0},{14,2},{16,28},{18,... | collective-permute-start | bytes 491528 | tf_op jit(solution)/shard_map/ppermute | solution.py:403
  47.6 11.6 %collective-permute-start.9 = (f32[2,256,256]{2,1,0:T(8,128)S(1)}, f32[2,256,256]{2,1,0:T(8,128)S(1)}, u32[]{:S(2)}, u32[]{:S(2)}) collective-permute-start(f32[2,256,256]{2,1,0:T(8,128)S(1)} %get-tuple-element.58.own), channel_id=1, source_target_pairs={{0,1},{1,0},{2,3},{3,2},{4,5},{5,4},{6,7},{7,6},{8,9},{9,8},{10,11... | collective-permute-start | bytes 1572872 | tf_op jit(solution)/shard_map/ppermute | solution.py:400
  47.6 11.6 %collective-permute-start.10 = (f32[2,128,256]{2,1,0:T(8,128)S(1)}, f32[2,128,256]{2,1,0:T(8,128)S(1)}, u32[]{:S(2)}, u32[]{:S(2)}) collective-permute-start(f32[2,128,256]{2,1,0:T(8,128)S(1)} %collective-permute-done.7.b0), channel_id=1, source_target_pairs={{0,1},{1,0},{2,3},{3,2},{4,5},{5,4},{6,7},{7,6},{8,9},{9,8},{10,11... | collective-permute-start | bytes 786440 | tf_op jit(solution)/shard_map/ppermute | solution.py:400
  48.1 11.1 %collective-permute-start.11 = (f32[2,128,256]{2,1,0:T(8,128)}, f32[2,128,256]{2,1,0:T(8,128)S(1)}, u32[]{:S(2)}, u32[]{:S(2)}) collective-permute-start(f32[2,128,256]{2,1,0:T(8,128)} %collective-permute-done.8.a0), channel_id=1, source_target_pairs={{0,1},{1,0},{2,3},{3,2},{4,5},{5,4},{6,7},{7,6},{8,9},{9,8},{10,11... | collective-permute-start | bytes 786440 | tf_op jit(solution)/shard_map/ppermute | solution.py:400
  53.5 13.7 %collective-permute-start.16 = (f32[160,256]{1,0:T(8,128)S(1)}, f32[160,256]{1,0:T(8,128)S(1)}, u32[]{:S(2)}, u32[]{:S(2)}) collective-permute-start(f32[160,256]{1,0:T(8,128)S(1)} %fusion.13), channel_id=1, source_target_pairs={{0,2},{2,0},{4,6},{6,4},{8,10},{10,8},{12,14},{14,12},{16,18},{18,... | collective-permute-start | bytes 491528 | tf_op jit(solution)/shard_map/ppermute | solution.py:403
  56.6 15.0 %collective-permute-start.17 = (f32[160,256]{1,0:T(8,128)S(1)}, f32[160,256]{1,0:T(8,128)S(1)}, u32[]{:S(2)}, u32[]{:S(2)}) collective-permute-start(f32[160,256]{1,0:T(8,128)S(1)} %fusion.13), channel_id=1, source_target_pairs={{0,16},{2,18},{4,20},{6,22},{8,24},{10,26},{12,28},{14,30},{16,0},... | collective-permute-start | bytes 491528 | tf_op jit(solution)/shard_map/ppermute | solution.py:403
  59.2 15.1 %collective-permute-start.18 = (f32[160,256]{1,0:T(8,128)S(1)}, f32[160,256]{1,0:T(8,128)S(1)}, u32[]{:S(2)}, u32[]{:S(2)}) collective-permute-start(f32[160,256]{1,0:T(8,128)S(1)} %fusion.13), channel_id=1, source_target_pairs={{0,18},{2,16},{4,22},{6,20},{8,26},{10,24},{12,30},{14,28},{16,2},... | collective-permute-start | bytes 491528 | tf_op jit(solution)/shard_map/ppermute | solution.py:403
  62.0 18.2 %collective-permute-start.19 = (f32[2,128,256]{2,1,0:T(8,128)S(1)}, f32[2,128,256]{2,1,0:T(8,128)S(1)}, u32[]{:S(2)}, u32[]{:S(2)}) collective-permute-start(f32[2,128,256]{2,1,0:T(8,128)S(1)} %get-tuple-element.64), channel_id=1, source_target_pairs={{0,2},{2,4},{4,6},{6,8},{8,10},{10,12},{12,14},{14,16},{16,18},{18... | collective-permute-start | bytes 786440 | tf_op jit(solution)/shard_map/ppermute | solution.py:417
  65.7 16.6 %collective-permute-start.20 = (f32[2,128,256]{2,1,0:T(8,128)S(1)}, f32[2,128,256]{2,1,0:T(8,128)S(1)}, u32[]{:S(2)}, u32[]{:S(2)}) collective-permute-start(f32[2,128,256]{2,1,0:T(8,128)S(1)} %get-tuple-element.65), channel_id=1, source_target_pairs={{2,0},{4,2},{6,4},{8,6},{10,8},{12,10},{14,12},{16,14},{18,16},{20... | collective-permute-start | bytes 786440 | tf_op jit(solution)/shard_map/ppermute | solution.py:420
  82.3 7.0 %collective-permute-start.21 = (f32[160,256]{1,0:T(8,128)S(1)}, f32[160,256]{1,0:T(8,128)S(1)}, u32[]{:S(2)}, u32[]{:S(2)}) collective-permute-start(f32[160,256]{1,0:T(8,128)S(1)} %add_add_fusion.1), channel_id=1, source_target_pairs={{0,4},{2,6},{4,0},{6,2},{8,12},{10,14},{12,8},{14,10},{16,20},{18,... | collective-permute-start | bytes 491528 | tf_op jit(solution)/shard_map/ppermute | solution.py:403
  82.3 7.0 %collective-permute-start.22 = (f32[160,256]{1,0:T(8,128)S(1)}, f32[160,256]{1,0:T(8,128)S(1)}, u32[]{:S(2)}, u32[]{:S(2)}) collective-permute-start(f32[160,256]{1,0:T(8,128)S(1)} %add_add_fusion.1), channel_id=1, source_target_pairs={{0,8},{2,10},{4,12},{6,14},{8,0},{10,2},{12,4},{14,6},{16,24},{18,... | collective-permute-start | bytes 491528 | tf_op jit(solution)/shard_map/ppermute | solution.py:403
  82.4 8.7 %collective-permute-start.23 = (f32[160,256]{1,0:T(8,128)S(1)}, f32[160,256]{1,0:T(8,128)S(1)}, u32[]{:S(2)}, u32[]{:S(2)}) collective-permute-start(f32[160,256]{1,0:T(8,128)S(1)} %add_add_fusion.1), channel_id=1, source_target_pairs={{0,12},{2,14},{4,8},{6,10},{8,4},{10,6},{12,0},{14,2},{16,28},{18,... | collective-permute-start | bytes 491528 | tf_op jit(solution)/shard_map/ppermute | solution.py:403
  91.1 2.2 %collective-permute-start.24 = (f32[4,160,256]{2,1,0:T(8,128)S(1)}, f32[4,160,256]{2,1,0:T(8,128)S(1)}, u32[]{:S(2)}, u32[]{:S(2)}) collective-permute-start(f32[4,160,256]{2,1,0:T(8,128)S(1)} %pad_maximum_fusion.own_totals), channel_id=1, source_target_pairs={{0,1},{1,0},{2,3},{3,2},{4,5},{5,4},{6,7},{7,6},{8,9},{9,8},{10,11... | collective-permute-start | bytes 1966088 | tf_op jit(solution)/shard_map/ppermute | solution.py:400
  98.5 2.2 %collective-permute-start.25 = (f32[4,160,256]{2,1,0:T(8,128)S(1)}, f32[4,160,256]{2,1,0:T(8,128)S(1)}, u32[]{:S(2)}, u32[]{:S(2)}) collective-permute-start(f32[4,160,256]{2,1,0:T(8,128)S(1)} %get-tuple-element.72), channel_id=1, source_target_pairs={{0,1},{1,0},{2,3},{3,2},{4,5},{5,4},{6,7},{7,6},{8,9},{9,8},{10,11... | collective-permute-start | bytes 1966088 | tf_op jit(solution)/shard_map/ppermute | solution.py:400
  100.7 9.1 %collective-permute-start.26 = (f32[160,256]{1,0:T(8,128)S(1)}, f32[160,256]{1,0:T(8,128)S(1)}, u32[]{:S(2)}, u32[]{:S(2)}) collective-permute-start(f32[160,256]{1,0:T(8,128)S(1)} %get-tuple-element.82), channel_id=1, source_target_pairs={{0,4},{2,6},{4,0},{6,2},{8,12},{10,14},{12,8},{14,10},{16,20},{18,... | collective-permute-start | bytes 491528 | tf_op jit(solution)/shard_map/ppermute | solution.py:403
  101.3 8.6 %collective-permute-start.27 = (f32[160,256]{1,0:T(8,128)S(1)}, f32[160,256]{1,0:T(8,128)S(1)}, u32[]{:S(2)}, u32[]{:S(2)}) collective-permute-start(f32[160,256]{1,0:T(8,128)S(1)} %get-tuple-element.84), channel_id=1, source_target_pairs={{0,8},{2,10},{4,12},{6,14},{8,0},{10,2},{12,4},{14,6},{16,24},{18,... | collective-permute-start | bytes 491528 | tf_op jit(solution)/shard_map/ppermute | solution.py:403
  102.4 9.3 %collective-permute-start.28 = (f32[160,256]{1,0:T(8,128)S(1)}, f32[160,256]{1,0:T(8,128)S(1)}, u32[]{:S(2)}, u32[]{:S(2)}) collective-permute-start(f32[160,256]{1,0:T(8,128)S(1)} %get-tuple-element.83), channel_id=1, source_target_pairs={{0,12},{2,14},{4,8},{6,10},{8,4},{10,6},{12,0},{14,2},{16,28},{18,... | collective-permute-start | bytes 491528 | tf_op jit(solution)/shard_map/ppermute | solution.py:403
  104.3 16.6 %collective-permute-start.35 = (f32[2,128,256]{2,1,0:T(8,128)S(1)}, f32[2,128,256]{2,1,0:T(8,128)S(1)}, u32[]{:S(2)}, u32[]{:S(2)}) collective-permute-start(f32[2,128,256]{2,1,0:T(8,128)S(1)} %get-tuple-element.74), channel_id=1, source_target_pairs={{0,2},{2,4},{4,6},{6,8},{8,10},{10,12},{12,14},{14,16},{16,18},{18... | collective-permute-start | bytes 786440 | tf_op jit(solution)/shard_map/ppermute | solution.py:417
  108.6 14.6 %collective-permute-start.36 = (f32[2,128,256]{2,1,0:T(8,128)S(1)}, f32[2,128,256]{2,1,0:T(8,128)S(1)}, u32[]{:S(2)}, u32[]{:S(2)}) collective-permute-start(f32[2,128,256]{2,1,0:T(8,128)S(1)} %get-tuple-element.75), channel_id=1, source_target_pairs={{2,0},{4,2},{6,4},{8,6},{10,8},{12,10},{14,12},{16,14},{18,16},{20... | collective-permute-start | bytes 786440 | tf_op jit(solution)/shard_map/ppermute | solution.py:420
  111.8 13.6 %collective-permute-start.29 = (f32[160,256]{1,0:T(8,128)S(1)}, f32[160,256]{1,0:T(8,128)S(1)}, u32[]{:S(2)}, u32[]{:S(2)}) collective-permute-start(f32[160,256]{1,0:T(8,128)S(1)} %fusion.6), channel_id=1, source_target_pairs={{0,2},{2,0},{4,6},{6,4},{8,10},{10,8},{12,14},{14,12},{16,18},{18,... | collective-permute-start | bytes 491528 | tf_op jit(solution)/shard_map/ppermute | solution.py:403
  114.2 17.8 %collective-permute-start.30 = (f32[160,256]{1,0:T(8,128)S(1)}, f32[160,256]{1,0:T(8,128)S(1)}, u32[]{:S(2)}, u32[]{:S(2)}) collective-permute-start(f32[160,256]{1,0:T(8,128)S(1)} %fusion.6), channel_id=1, source_target_pairs={{0,16},{2,18},{4,20},{6,22},{8,24},{10,26},{12,28},{14,30},{16,0},... | collective-permute-start | bytes 491528 | tf_op jit(solution)/shard_map/ppermute | solution.py:403
  116.2 15.8 %collective-permute-start.31 = (f32[160,256]{1,0:T(8,128)S(1)}, f32[160,256]{1,0:T(8,128)S(1)}, u32[]{:S(2)}, u32[]{:S(2)}) collective-permute-start(f32[160,256]{1,0:T(8,128)S(1)} %fusion.6), channel_id=1, source_target_pairs={{0,18},{2,16},{4,22},{6,20},{8,26},{10,24},{12,30},{14,28},{16,2},... | collective-permute-start | bytes 491528 | tf_op jit(solution)/shard_map/ppermute | solution.py:403
  123.2 12.4 %collective-permute-start.37 = (f32[2,256,256]{2,1,0:T(8,128)S(1)}, f32[2,256,256]{2,1,0:T(8,128)S(1)}, u32[]{:S(2)}, u32[]{:S(2)}) collective-permute-start(f32[2,256,256]{2,1,0:T(8,128)S(1)} %get-tuple-element.77.own), channel_id=1, source_target_pairs={{0,1},{1,0},{2,3},{3,2},{4,5},{5,4},{6,7},{7,6},{8,9},{9,8},{10,11... | collective-permute-start | bytes 1572872 | tf_op jit(solution)/shard_map/ppermute | solution.py:400
  123.2 9.1 %collective-permute-start.38 = (f32[2,128,256]{2,1,0:T(8,128)S(1)}, f32[2,128,256]{2,1,0:T(8,128)S(1)}, u32[]{:S(2)}, u32[]{:S(2)}) collective-permute-start(f32[2,128,256]{2,1,0:T(8,128)S(1)} %collective-permute-done.35.b0), channel_id=1, source_target_pairs={{0,1},{1,0},{2,3},{3,2},{4,5},{5,4},{6,7},{7,6},{8,9},{9,8},{10,11... | collective-permute-start | bytes 786440 | tf_op jit(solution)/shard_map/ppermute | solution.py:400
  125.4 10.2 %collective-permute-start.39 = (f32[2,128,256]{2,1,0:T(8,128)S(1)}, f32[2,128,256]{2,1,0:T(8,128)S(1)}, u32[]{:S(2)}, u32[]{:S(2)}) collective-permute-start(f32[2,128,256]{2,1,0:T(8,128)S(1)} %collective-permute-done.36.a0), channel_id=1, source_target_pairs={{0,1},{1,0},{2,3},{3,2},{4,5},{5,4},{6,7},{7,6},{8,9},{9,8},{10,11... | collective-permute-start | bytes 786440 | tf_op jit(solution)/shard_map/ppermute | solution.py:400
  132.0 6.9 %collective-permute-start.32 = (f32[160,256]{1,0:T(8,128)S(1)}, f32[160,256]{1,0:T(8,128)S(1)}, u32[]{:S(2)}, u32[]{:S(2)}) collective-permute-start(f32[160,256]{1,0:T(8,128)S(1)} %add_add_fusion), channel_id=1, source_target_pairs={{0,4},{2,6},{4,0},{6,2},{8,12},{10,14},{12,8},{14,10},{16,20},{18,... | collective-permute-start | bytes 491528 | tf_op jit(solution)/shard_map/ppermute | solution.py:403
  132.3 6.8 %collective-permute-start.33 = (f32[160,256]{1,0:T(8,128)S(1)}, f32[160,256]{1,0:T(8,128)S(1)}, u32[]{:S(2)}, u32[]{:S(2)}) collective-permute-start(f32[160,256]{1,0:T(8,128)S(1)} %add_add_fusion), channel_id=1, source_target_pairs={{0,8},{2,10},{4,12},{6,14},{8,0},{10,2},{12,4},{14,6},{16,24},{18,... | collective-permute-start | bytes 491528 | tf_op jit(solution)/shard_map/ppermute | solution.py:403
  132.3 8.5 %collective-permute-start.34 = (f32[160,256]{1,0:T(8,128)S(1)}, f32[160,256]{1,0:T(8,128)S(1)}, u32[]{:S(2)}, u32[]{:S(2)}) collective-permute-start(f32[160,256]{1,0:T(8,128)S(1)} %add_add_fusion), channel_id=1, source_target_pairs={{0,12},{2,14},{4,8},{6,10},{8,4},{10,6},{12,0},{14,2},{16,28},{18,... | collective-permute-start | bytes 491528 | tf_op jit(solution)/shard_map/ppermute | solution.py:403
  140.8 1.4 collective-permute-start.40
  (8 other events, 9.2 us)

commit v5 on v3

--- a/solution.py
+++ b/solution.py
@@ -202,9 +202,9 @@
 
 def illumination_kernel(size, minibatch, info, own, other, out, tall):
     tiles, strip, pattern = size
-    half = pattern // 2
-    kept = slice(pattern + half, pattern + half + strip)
-    tall[kept] = jnp.zeros((strip, tall.shape[1]), F32)
+    begin = pattern + (pattern + strip - out.shape[0]) // 2
+    kept = slice(begin, begin + out.shape[0])
+    tall[kept] = jnp.zeros(out.shape, F32)
     (pr0, pi0), (pr1, pi1) = ((ref[0], ref[1]) for ref in (own, other))
     power = pr0 * pr0 + pi0 * pi0 + (pr1 * pr1 + pi1 * pi1)
     for side in (-1, 0, 1):
@@ -214,11 +214,13 @@
     out[...] = tall[kept]
 
 
-def patch_kernel(size, minibatch, info, strip_ref, below, above, patch, window):
+def edges_kernel(size, info, strip_ref, low, high):
+    half, width = low.shape[1:]
+    column_below = spot(info, size, 1, -1, info[25])[1]
+    column_above = spot(info, size, 1, 1, info[25])[1]
     for part in range(2):
-        patch[part] = cut_patch(
-            size, info, minibatch, strip_ref, below[part], above[part], window, part
-        )
+        low[part] = take_columns(strip_ref[part, :half], column_below, width)
+        high[part] = take_columns(strip_ref[part, strip_ref.shape[1] - half :], column_above, width)
 
 
 def ready_kernel(info, probe, measured, table, own, observed, split):
@@ -236,8 +238,8 @@
         own, other, measured, table, gradient, top, bottom, step_own, step_other = refs
         obj_real, obj_imag = strip_ref[0], strip_ref[1]
     else:
-        *edges, own, other, measured, table = refs[:-6]
-        gradient, top, bottom, step_own, step_other, window = refs[-6:]
+        *edges, own, other, measured, table = refs[:-4]
+        gradient, step_own, step_other, window = refs[-4:]
         sides = (jnp.where(slot == 0, edges[i][...], edges[i + 1][...]) for i in (0, 2))
         others = (jnp.where(slot == 0, edges[i + 1][...], edges[i][...]) for i in (0, 2))
         obj_real, obj_imag = (
@@ -286,12 +288,14 @@
     chi = both([(factor * fr, factor * fi) for fr, fi in far], second, first)
     (pr0, pi0), (pr1, pi1) = probes
     (cr0, ci0), (cr1, ci1) = chi
-    half = top.shape[1]
+    half = pattern // 2
     for part, value in (
         (0, (pr0 * cr0 + pi0 * ci0) + (pr1 * cr1 + pi1 * ci1)),
         (1, (pr0 * ci0 - pi0 * cr0) + (pr1 * ci1 - pi1 * cr1)),
     ):
-        gradient[part], top[part], bottom[part] = value, value[:half], value[half:]
+        gradient[part] = value
+        if minibatch:
+            top[part], bottom[part] = value[:half], value[half:]
     coverage = obj_real * obj_real + obj_imag * obj_imag
     rows = pattern // GROUP
     mate = lax.rem(lax.div(info[24], NEAR_STEP), GROUP)
@@ -309,32 +313,45 @@
             )
 
 
-def update_kernel(size, minibatch, info, strip_ref, illum, own, other, b0, a0, b1, a1, *outs):
-    strip_out, *edges, tall = outs
+def place_all(size, minibatch, info, refs, part, tall, kept, start_below):
+    own, other, b0, a0, b1, a1 = refs
+    slot = info[25]
+    tall[kept] = jnp.zeros((kept.stop - kept.start, tall.shape[1]), F32)
+    for side, place, ref, start in (
+        (0, slot, own, 0),
+        (0, 1 - slot, other, 0),
+        (-1, slot, b0, start_below),
+        (1, slot, a0, 0),
+        (-1, 1 - slot, b1, start_below),
+        (1, 1 - slot, a1, 0),
+    ):
+        row, column = spot(info, size, minibatch, side, place)
+        add_at(tall, ref[part], row + size[2] + start, column)
+
+
+def update_kernel(size, info, strip_ref, below, above, illum, *refs):
+    grads, (strip_out, patch, tall, window) = refs[:-4], refs[-4:]
     tiles, strip, pattern = size
     half = pattern // 2
-    slot = info[25]
+    kept = slice(pattern, 2 * pattern + strip)
+    row, column = spot(info, size, 1, 0, info[25])
+    for part in range(2):
+        place_all(size, 0, info, grads, part, tall, kept, 0)
+        change = tall[kept] / (illum[...] + 1.0)
+        strip_out[part] = strip_ref[part] + change[half : half + strip]
+        old = cut_patch(size, info, 1, strip_ref, below[part], above[part], window, part)
+        window[: pattern + strip] = take_columns(change, column, pattern)
+        patch[part] = old + rows_at(window, row, pattern)
+
+
+def final_kernel(size, info, strip_ref, illum, *refs):
+    grads, (strip_out, tall) = refs[:-2], refs[-2:]
+    tiles, strip, pattern = size
+    half = pattern // 2
     kept = slice(pattern + half, pattern + half + strip)
-    grads = (
-        (0, slot, own, 0),
-        (0, 1 - slot, other, 0),
-        (-1, slot, b0, half),
-        (1, slot, a0, 0),
-        (-1, 1 - slot, b1, half),
-        (1, 1 - slot, a1, 0),
-    )
     for part in range(2):
-        tall[kept] = jnp.zeros((strip, tall.shape[1]), F32)
-        for side, place, ref, start in grads:
-            row, column = spot(info, size, minibatch, side, place)
-            add_at(tall, ref[part], row + pattern + start, column)
-        fresh = strip_ref[part] + tall[kept] / (illum[...] + 1.0)
-        strip_out[part] = fresh
-        if edges:
-            column_below = spot(info, size, minibatch + 1, -1, slot)[1]
-            column_above = spot(info, size, minibatch + 1, 1, slot)[1]
-            edges[0][part] = take_columns(fresh[:half], column_below, pattern)
-            edges[1][part] = take_columns(fresh[strip - half :], column_above, pattern)
+        place_all(size, 1, info, grads, part, tall, kept, half)
+        strip_out[part] = strip_ref[part] + tall[kept] / (illum[...] + 1.0)
 
 
 def probe_kernel(info, own_totals, other_totals, *refs):
@@ -432,56 +449,76 @@
         [field, field, jax.ShapeDtypeStruct((4, pattern, pattern), BF16)],
         (here, probe[0], measured, jnp.asarray(table_of(pattern))),
     )
-    *edges, below, above, own, observed, table = lax.optimization_barrier(
-        (*edges, below, above, own, observed, table)
+    info = jnp.concatenate([below.ravel(), positions.ravel(), above.ravel(), index])
+    low, high = call(
+        bind(edges_kernel, size), "edges", [(2, half, pattern)] * 2, (info, object_field)
+    )
+    *edges, low, high, own, observed, table = lax.optimization_barrier(
+        (*edges, low, high, own, observed, table)
     )
     edges = [edges[0], swap(edges[0]), edges[1], swap(edges[1])]
-    info = jnp.concatenate([below.ravel(), positions.ravel(), above.ravel(), index])
+    old_below, old_above = from_below(high), from_above(low)
+    cut = (object_field, *edges)
 
     for minibatch in range(2):
         last = minibatch == 1
         rows = pattern // GROUP
         blocks = (GROUP, 2 * rows + rows // 2, pattern)
-        cut = (object_field, *edges)
-        if last:
-            cut = call(
-                bind(patch_kernel, size, minibatch), "patch", [field], (here, *cut), [window], 10**10
-            )
-        rim = (2, half, pattern)
-        gradient, top, bottom, step_own, step_other = call(
+        rims = [(2, half, pattern)] * 2 if last else []
+        gradient, *rims, step_own, step_other = call(
             bind(field_kernel, size, minibatch),
             "field",
-            [field, rim, rim, blocks, blocks],
+            [field, *rims, blocks, blocks],
             (here, *cut, own, other, observed, table),
             [] if last else [window],
-            flops=2 * 12 * 512**3,
+            flops=2 * 12 * 512**3 if last else 2 * 10**10,
         )
         (illum,) = call(
             bind(illumination_kernel, size, minibatch),
             "illumination",
-            [(strip, width)],
+            [(strip if last else strip + pattern, width)],
             (info, own, other),
             [tall],
         )
+        if not last:
+            step_other, old_below, old_above = lax.optimization_barrier(
+                (step_other, old_below, old_above)
+            )
         brought = swap(step_other)
         steps = [step_own[k] + brought[k] for k in range(GROUP)]
+        if last:
+            from_low, from_high = from_below(rims[1]), from_above(rims[0])
+        else:
+            from_low, from_high = from_below(gradient), from_above(gradient)
         piece = scatter(steps, NEAR_STEP)
-        rim_below, rim_above = from_below(bottom), from_above(top)
-        gradient, rim_below, rim_above, illum = lax.optimization_barrier(
-            (gradient, rim_below, rim_above, illum)
-        )
-        rims = (gradient, swap(gradient), rim_below, rim_above, swap(rim_below), swap(rim_above))
-        object_field, *edges = call(
-            bind(update_kernel, size, minibatch),
-            "update",
-            [object_field.shape] + ([] if last else [rim] * 2),
-            (info, object_field, illum, *rims),
-            [tall],
-        )
-        piece = exchange(piece)
-        if not last:
-            edges = [from_below(edges[1]), from_above(edges[0])]
-            piece, *edges = lax.optimization_barrier((piece, *edges))
+        if last:
+            gradient, from_low, from_high, illum = lax.optimization_barrier(
+                (gradient, from_low, from_high, illum)
+            )
+            piece = exchange(piece)
+        else:
+            piece = exchange(piece)
+            gradient, from_low, from_high, illum, piece = lax.optimization_barrier(
+                (gradient, from_low, from_high, illum, piece)
+            )
+        grads = (gradient, swap(gradient), from_low, from_high, swap(from_low), swap(from_high))
+        if last:
+            (object_field,) = call(
+                bind(final_kernel, size),
+                "final",
+                [object_field.shape],
+                (info, object_field, illum, *grads),
+                [tall],
+            )
+        else:
+            object_field, *cut = call(
+                bind(update_kernel, size),
+                "update",
+                [object_field.shape, field],
+                (info, object_field, old_below, old_above, illum, *grads),
+                [tall, window],
+                flops=10**10,
+            )
         totals = gather(piece, NEAR_STEP)
         if last:
             totals, object_field = lax.optimization_barrier((totals, object_field))

time: 145 us -> 155 us (1.069)
  waiting for transfers between devices: 50.6 us -> 57.2 us
  starting transfers between devices: 59 us -> 65.6 us
  other arithmetic: 2.37 us -> 0.41 us
    ppermute x18, waiting for transfers between devices: 28.9 us -> 42.7 us  [across(): return lax.ppermute(value, 'tile', [(i, i ^ k) for i in range(tiles)])]
    ppermute x5, waiting for transfers between devices: 8.82 us -> 0.01 us  [from_below(): return lax.ppermute(value, 'tile', up)]
    ppermute x18, starting transfers between devices: 29.6 us -> 37 us  [across(): return lax.ppermute(value, 'tile', [(i, i ^ k) for i in range(tiles)])]
    ppermute x5, waiting for transfers between devices: 6.85 us -> 9.26 us  [from_above(): return lax.ppermute(value, 'tile', down)]
    unnamed x26 -> x18, local copies, waits for them, and re-layouts: 2.24 us -> 3.69 us
  transfers between devices with their start and end apart: 41 -> 41, of which waited for: 23 -> 19; matrix products, arithmetic and copies ran while one was open for 3% -> 0% of each run, Pallas kernels for 8% -> 11%
where the time goes in v5:
time: 155 us
  starting transfers between devices  65.6 us (42%)
  waiting for transfers between devices  57.2 us (37%)
  Pallas kernels  24.3 us (16%)
  local copies, waits for them, and re-layouts  6.07 us (4%)
    ppermute x18, waiting for transfers between devices, across(): return lax.ppermute(value, 'tile', [(i, i ^ k) for i in range(tiles)])  42.7 us
    ppermute x18, starting transfers between devices, across(): return lax.ppermute(value, 'tile', [(i, i ^ k) for i in range(tiles)])  37 us
    pallas_call x10, Pallas kernels, call(): pl.pallas_call(kernel, out_shape=shapes, in_specs=[smem] + [vmem] * (len(...  24.3 us
    ppermute x5, starting transfers between devices, from_below(): return lax.ppermute(value, 'tile', up)  19.1 us
    ppermute x5, waiting for transfers between devices, from_above(): return lax.ppermute(value, 'tile', down)  9.26 us
    ppermute x5, starting transfers between devices, from_above(): return lax.ppermute(value, 'tile', down)  6.86 us
    ppermute x13, waiting for transfers between devices, swap(): return lax.ppermute(value, 'mode', [(0, 1), (1, 0)])  5.18 us
    unnamed x18, local copies, waits for them, and re-layouts  3.69 us
  transfers between devices with their start and end apart: 41, of which 19 were waited for; matrix products, arithmetic and copies ran while one was open for 0% of the time, Pallas kernels for 11%

profile of v5, /device:TPU:0, one launch (start us, length us, event | category | flops | bytes accessed | tf_op | source)
XLA Modules:
  0.0 154.6 jit_solution(611076368159787450)
XLA Ops:
  0.6 2.0 %dynamic-slice_bitcast_fusion = (f32[128,512]{1,0:T(8,128)}, f32[128,512]{1,0:T(8,128)}) fusion(f32[2,256,512]{2,1,0:T(8,128)} %strip_ref.5, s32[]{:T(128)S(6)} %select_n.4, s32[]{:T(128)S(6)} %add.117), kind=kLoop, calls=%fused_computation.2 | loop fusion | bytes 1048584 | tf_op jit(solution)/shard_map/slice | solution.py:443
  2.6 5.0 %collective-permute-start.2 = (f32[128,512]{1,0:T(8,128)}, f32[128,512]{1,0:T(8,128)S(1)}, u32[]{:S(2)}, u32[]{:S(2)}) collective-permute-start(f32[128,512]{1,0:T(8,128)} %get-tuple-element.85), channel_id=1, source_target_pairs={{0,2},{2,4},{4,6},{6,8},{8,10},{10,12},{12,14},{14,16},{16,18},{18... | collective-permute-start | bytes 786440 | tf_op jit(solution)/shard_map/ppermute | solution.py:431
  7.6 1.3 collective-permute-start.3
  9.0 4.5 %collective-permute-start = (s32[2,2,2]{2,1,0:T(2,128)S(1)}, s32[2,2,2]{2,1,0:T(2,128)S(1)}, u32[]{:S(2)}, u32[]{:S(2)}) collective-permute-start(s32[2,2,2]{2,1,0:T(2,128)S(1)} %copy-done.8), channel_id=1, source_target_pairs={{0,2},{2,4},{4,6},{6,8},{8,10},{10,12},{12,14},{14,16},{16,18},{18... | collective-permute-start | bytes 104 | tf_op jit(solution)/shard_map/ppermute | solution.py:431
  13.5 1.3 collective-permute-start.1
  15.0 1.0 copy-done.2
  16.1 1.0 copy-done.3
  17.8 0.8 copy-done.4
  18.6 0.8 copy-done.6
  19.5 1.6 %collective-permute-done.1 = s32[2,2,2]{2,1,0:T(2,128)S(1)} collective-permute-done((s32[2,2,2]{2,1,0:T(2,128)S(1)}, s32[2,2,2]{2,1,0:T(2,128)S(1)}, u32[]{:S(2)}, u32[]{:S(2)}) %collective-permute-start.1) | collective-permute-done | bytes 64 | tf_op jit(solution)/shard_map/ppermute | solution.py:434
  21.2 0.9 edges.1
  22.7 3.4 %collective-permute-start.7 = (f32[2,128,256]{2,1,0:T(8,128)S(1)}, f32[2,128,256]{2,1,0:T(8,128)S(1)}, u32[]{:S(2)}, u32[]{:S(2)}) collective-permute-start(f32[2,128,256]{2,1,0:T(8,128)S(1)} %get-tuple-element.51), channel_id=1, source_target_pairs={{0,2},{2,4},{4,6},{6,8},{8,10},{10,12},{12,14},{14,16},{16,18},{18... | collective-permute-start | bytes 786440 | tf_op jit(solution)/shard_map/ppermute | solution.py:431
  26.1 1.3 collective-permute-start.8
  27.5 5.7 %field.2 = (f32[2,256,256]{2,1,0:T(8,128)S(1)}, f32[4,160,256]{2,1,0:T(8,128)S(1)}, f32[4,160,256]{2,1,0:T(8,128)S(1)}) custom-call(s32[26]{0:T(128)S(1)} %concatenate.8.info, f32[2,256,512]{2,1,0:T(8,128)S(1)} %copy-done, f32[128,512]{1,0:T(8,128)S(1)} %collective-permute-done.2.refs_0_, f32[128,512]{1,0:T(8,128)S(1)} %collective-permute-done.4.refs_1_, ...), custom_call_target="tpu_custom_call" | custom-call | flops 20000000000 | bytes 6029416 | tf_op jit(solution)/shard_map/field/pallas_call | solution.py:388
  33.2 7.7 %collective-permute-done.8.above = f32[2,128,256]{2,1,0:T(8,128)S(1)} collective-permute-done((f32[2,128,256]{2,1,0:T(8,128)S(1)}, f32[2,128,256]{2,1,0:T(8,128)S(1)}, u32[]{:S(2)}, u32[]{:S(2)}) %collective-permute-start.8) | collective-permute-done | bytes 262176 | tf_op jit(solution)/shard_map/ppermute | solution.py:434
  40.8 2.1 %collective-permute-done.11 = f32[4,160,256]{2,1,0:T(8,128)S(1)} collective-permute-done((f32[4,160,256]{2,1,0:T(8,128)S(1)}, f32[4,160,256]{2,1,0:T(8,128)S(1)}, u32[]{:S(2)}, u32[]{:S(2)}) %collective-permute-start.11) | collective-permute-done | bytes 655392 | tf_op jit(solution)/shard_map/ppermute | solution.py:414
  43.0 4.3 %collective-permute-start.14 = (f32[160,256]{1,0:T(8,128)S(1)}, f32[160,256]{1,0:T(8,128)S(1)}, u32[]{:S(2)}, u32[]{:S(2)}) collective-permute-start(f32[160,256]{1,0:T(8,128)S(1)} %get-tuple-element.82), channel_id=1, source_target_pairs={{0,12},{2,14},{4,8},{6,10},{8,4},{10,6},{12,0},{14,2},{16,28},{18,... | collective-permute-start | bytes 491528 | tf_op jit(solution)/shard_map/ppermute | solution.py:417
  47.9 2.2 %collective-permute-start.9 = (f32[2,256,256]{2,1,0:T(8,128)S(1)}, f32[2,256,256]{2,1,0:T(8,128)S(1)}, u32[]{:S(2)}, u32[]{:S(2)}) collective-permute-start(f32[2,256,256]{2,1,0:T(8,128)S(1)} %get-tuple-element.59.refs_0_), channel_id=1, source_target_pairs={{0,2},{2,4},{4,6},{6,8},{8,10},{10,12},{12,14},{14,16},{16,18},{18... | collective-permute-start | bytes 1572872 | tf_op jit(solution)/shard_map/ppermute | solution.py:431
  50.2 1.5 collective-permute-start.10
  52.3 2.3 %collective-permute-done.13 = f32[160,256]{1,0:T(8,128)S(1)} collective-permute-done((f32[160,256]{1,0:T(8,128)S(1)}, f32[160,256]{1,0:T(8,128)S(1)}, u32[]{:S(2)}, u32[]{:S(2)}) %collective-permute-start.13) | collective-permute-done | bytes 163872 | tf_op jit(solution)/shard_map/ppermute | solution.py:417
  55.4 13.0 %collective-permute-start.16 = (f32[160,256]{1,0:T(8,128)S(1)}, f32[160,256]{1,0:T(8,128)S(1)}, u32[]{:S(2)}, u32[]{:S(2)}) collective-permute-start(f32[160,256]{1,0:T(8,128)S(1)} %fusion.13), channel_id=1, source_target_pairs={{0,16},{2,18},{4,20},{6,22},{8,24},{10,26},{12,28},{14,30},{16,0},... | collective-permute-start | bytes 491528 | tf_op jit(solution)/shard_map/ppermute | solution.py:417
  68.4 1.5 collective-permute-start.15
  69.9 1.7 %illumination.2.illum = f32[512,512]{1,0:T(8,128)S(1)} custom-call(s32[26]{0:T(128)S(1)} %concatenate.9.info, f32[2,256,256]{2,1,0:T(8,128)S(1)} %get-tuple-element.47.refs_4_.own.refs_0_, f32[2,256,256]{2,1,0:T(8,128)S(1)} %collective-permute-done.6.refs_5_.other.refs_1_), custom_call_target="tpu_custom_call" | custom-call | bytes 2097256 | tf_op jit(solution)/shard_map/illumination/pallas_call | solution.py:388
  71.7 8.8 %collective-permute-done.16 = f32[160,256]{1,0:T(8,128)S(1)} collective-permute-done((f32[160,256]{1,0:T(8,128)S(1)}, f32[160,256]{1,0:T(8,128)S(1)}, u32[]{:S(2)}, u32[]{:S(2)}) %collective-permute-start.16) | collective-permute-done | bytes 163872 | tf_op jit(solution)/shard_map/ppermute | solution.py:417
  80.4 1.9 %collective-permute-done.15 = f32[160,256]{1,0:T(8,128)S(1)} collective-permute-done((f32[160,256]{1,0:T(8,128)S(1)}, f32[160,256]{1,0:T(8,128)S(1)}, u32[]{:S(2)}, u32[]{:S(2)}) %collective-permute-start.15) | collective-permute-done | bytes 163872 | tf_op jit(solution)/shard_map/ppermute | solution.py:417
  83.0 3.6 %collective-permute-start.23 = (f32[160,256]{1,0:T(8,128)S(1)}, f32[160,256]{1,0:T(8,128)S(1)}, u32[]{:S(2)}, u32[]{:S(2)}) collective-permute-start(f32[160,256]{1,0:T(8,128)S(1)} %add_add_fusion.1), channel_id=1, source_target_pairs={{0,12},{2,14},{4,8},{6,10},{8,4},{10,6},{12,0},{14,2},{16,28},{18,... | collective-permute-start | bytes 491528 | tf_op jit(solution)/shard_map/ppermute | solution.py:417
  86.6 5.0 %collective-permute-done.23 = f32[160,256]{1,0:T(8,128)S(1)} collective-permute-done((f32[160,256]{1,0:T(8,128)S(1)}, f32[160,256]{1,0:T(8,128)S(1)}, u32[]{:S(2)}, u32[]{:S(2)}) %collective-permute-start.23) | collective-permute-done | bytes 163872 | tf_op jit(solution)/shard_map/ppermute | solution.py:417
  91.7 2.5 %collective-permute-done.22 = f32[160,256]{1,0:T(8,128)S(1)} collective-permute-done((f32[160,256]{1,0:T(8,128)S(1)}, f32[160,256]{1,0:T(8,128)S(1)}, u32[]{:S(2)}, u32[]{:S(2)}) %collective-permute-start.22) | collective-permute-done | bytes 163872 | tf_op jit(solution)/shard_map/ppermute | solution.py:417
  94.2 3.2 %collective-permute-done.21 = f32[160,256]{1,0:T(8,128)S(1)} collective-permute-done((f32[160,256]{1,0:T(8,128)S(1)}, f32[160,256]{1,0:T(8,128)S(1)}, u32[]{:S(2)}, u32[]{:S(2)}) %collective-permute-start.21) | collective-permute-done | bytes 163872 | tf_op jit(solution)/shard_map/ppermute | solution.py:417
  97.5 4.0 %update.1 = (f32[2,256,512]{2,1,0:T(8,128)S(1)}, f32[2,256,256]{2,1,0:T(8,128)S(1)}) custom-call(s32[26]{0:T(128)S(1)} %concatenate.9.info, f32[2,256,512]{2,1,0:T(8,128)S(1)} %copy-done, f32[2,128,256]{2,1,0:T(8,128)S(1)} %collective-permute-done.7.below, f32[2,128,256]{2,1,0:T(8,128)S(1)} %collective-permute-done.8.above, ...), custom_call_target="tpu_custom_call" | custom-call | flops 10000000000 | bytes 7340136 | tf_op jit(solution)/shard_map/update/pallas_call | solution.py:388
  102.2 4.5 %field.3 = (f32[2,256,256]{2,1,0:T(8,128)S(1)}, f32[2,128,256]{2,1,0:T(8,128)S(1)}, f32[2,128,256]{2,1,0:T(8,128)S(1)}, f32[4,160,256]{2,1,0:T(8,128)S(1)}, f32[4,160,256]{2,1,0:T(8,128)S(1)}) custom-call(s32[26]{0:T(128)S(1)} %concatenate.8.info, f32[2,256,256]{2,1,0:T(8,128)S(1)} %get-tuple-element.62.strip_ref, ...), custom_call_target="tpu_custom_call" | custom-call | flops 3221225472 | bytes 4980840 | tf_op jit(solution)/shard_map/field/pallas_call | solution.py:388
  107.3 1.7 %collective-permute-done.25 = f32[4,160,256]{2,1,0:T(8,128)S(1)} collective-permute-done((f32[4,160,256]{2,1,0:T(8,128)S(1)}, f32[4,160,256]{2,1,0:T(8,128)S(1)}, u32[]{:S(2)}, u32[]{:S(2)}) %collective-permute-start.25) | collective-permute-done | bytes 655392 | tf_op jit(solution)/shard_map/ppermute | solution.py:414
  109.1 2.6 %collective-permute-start.28 = (f32[160,256]{1,0:T(8,128)S(1)}, f32[160,256]{1,0:T(8,128)S(1)}, u32[]{:S(2)}, u32[]{:S(2)}) collective-permute-start(f32[160,256]{1,0:T(8,128)S(1)} %get-tuple-element.79), channel_id=1, source_target_pairs={{0,12},{2,14},{4,8},{6,10},{8,4},{10,6},{12,0},{14,2},{16,28},{18,... | collective-permute-start | bytes 491528 | tf_op jit(solution)/shard_map/ppermute | solution.py:417
  111.6 1.0 collective-permute-start.26
  112.6 4.0 %collective-permute-start.35 = (f32[2,128,256]{2,1,0:T(8,128)S(1)}, f32[2,128,256]{2,1,0:T(8,128)S(1)}, u32[]{:S(2)}, u32[]{:S(2)}) collective-permute-start(f32[2,128,256]{2,1,0:T(8,128)S(1)} %get-tuple-element.70), channel_id=1, source_target_pairs={{0,2},{2,4},{4,6},{6,8},{8,10},{10,12},{12,14},{14,16},{16,18},{18... | collective-permute-start | bytes 786440 | tf_op jit(solution)/shard_map/ppermute | solution.py:431
  116.6 1.5 collective-permute-start.36
  118.2 1.0 collective-permute-done.27
  119.2 4.3 %collective-permute-done.26 = f32[160,256]{1,0:T(8,128)S(1)} collective-permute-done((f32[160,256]{1,0:T(8,128)S(1)}, f32[160,256]{1,0:T(8,128)S(1)}, u32[]{:S(2)}, u32[]{:S(2)}) %collective-permute-start.26) | collective-permute-done | bytes 163872 | tf_op jit(solution)/shard_map/ppermute | solution.py:417
  123.5 3.9 %collective-permute-start.30 = (f32[160,256]{1,0:T(8,128)S(1)}, f32[160,256]{1,0:T(8,128)S(1)}, u32[]{:S(2)}, u32[]{:S(2)}) collective-permute-start(f32[160,256]{1,0:T(8,128)S(1)} %fusion.6), channel_id=1, source_target_pairs={{0,16},{2,18},{4,20},{6,22},{8,24},{10,26},{12,28},{14,30},{16,0},... | collective-permute-start | bytes 491528 | tf_op jit(solution)/shard_map/ppermute | solution.py:417
  127.4 1.5 collective-permute-start.29
  128.9 1.7 %illumination.3.illum = f32[256,512]{1,0:T(8,128)S(1)} custom-call(s32[26]{0:T(128)S(1)} %concatenate.9.info, f32[2,256,256]{2,1,0:T(8,128)S(1)} %get-tuple-element.64.refs_0_.own, f32[2,256,256]{2,1,0:T(8,128)S(1)} %get-tuple-element.65.refs_1_.other), custom_call_target="tpu_custom_call" | custom-call | bytes 1572968 | tf_op jit(solution)/shard_map/illumination/pallas_call | solution.py:388
  131.2 8.2 %collective-permute-done.30 = f32[160,256]{1,0:T(8,128)S(1)} collective-permute-done((f32[160,256]{1,0:T(8,128)S(1)}, f32[160,256]{1,0:T(8,128)S(1)}, u32[]{:S(2)}, u32[]{:S(2)}) %collective-permute-start.30) | collective-permute-done | bytes 163872 | tf_op jit(solution)/shard_map/ppermute | solution.py:417
  139.5 4.3 %collective-permute-start.34 = (f32[160,256]{1,0:T(8,128)S(1)}, f32[160,256]{1,0:T(8,128)S(1)}, u32[]{:S(2)}, u32[]{:S(2)}) collective-permute-start(f32[160,256]{1,0:T(8,128)S(1)} %add_add_fusion), channel_id=1, source_target_pairs={{0,12},{2,14},{4,8},{6,10},{8,4},{10,6},{12,0},{14,2},{16,28},{18,... | collective-permute-start | bytes 491528 | tf_op jit(solution)/shard_map/ppermute | solution.py:417
  144.5 3.1 %final.1 = f32[2,256,512]{2,1,0:T(8,128)} custom-call(s32[26]{0:T(128)S(1)} %concatenate.9.info, f32[2,256,512]{2,1,0:T(8,128)S(1)} %get-tuple-element.68.strip_ref, f32[256,512]{1,0:T(8,128)S(1)} %illumination.3.illum, f32[2,256,256]{2,1,0:T(8,128)S(1)} %get-tuple-element.73.refs_0_, f32[2,256,256]{2,1,0:T(8,128)S(1)} %collective-permute-done.37.refs_1_, ...), custom_call_target="tpu_custom_call" | custom-call | bytes 4718696 | tf_op jit(solution)/shard_map/final/pallas_call | solution.py:388
  147.6 1.3 collective-permute-done.34
  148.8 2.2 %collective-permute-done.33 = f32[160,256]{1,0:T(8,128)S(1)} collective-permute-done((f32[160,256]{1,0:T(8,128)S(1)}, f32[160,256]{1,0:T(8,128)S(1)}, u32[]{:S(2)}, u32[]{:S(2)}) %collective-permute-start.33) | collective-permute-done | bytes 163872 | tf_op jit(solution)/shard_map/ppermute | solution.py:417
  151.9 1.3 collective-permute-done.40.other_totals
  153.2 1.4 probe.3
  (77 shorter events, 8.2 us)
Async XLA Ops:
  0.6 14.4 %copy-start.1 = (f32[2,2,256,256]{3,2,1,0:T(8,128)S(1)}, f32[2,2,256,256]{3,2,1,0:T(8,128)}, u32[]{:S(2)}) copy-start(f32[2,2,256,256]{3,2,1,0:T(8,128)} %measured.1) | copy-start | bytes 3145732
  2.6 6.4 %copy-start.8 = (s32[2,2,2]{2,1,0:T(2,128)S(1)}, s32[2,2,2]{2,1,0:T(2,128)}, u32[]{:S(2)}) copy-start(s32[2,2,2]{2,1,0:T(2,128)} %param.7) | copy-start | bytes 100
  2.6 19.5 %collective-permute-start.2 = (f32[128,512]{1,0:T(8,128)}, f32[128,512]{1,0:T(8,128)S(1)}, u32[]{:S(2)}, u32[]{:S(2)}) collective-permute-start(f32[128,512]{1,0:T(8,128)} %get-tuple-element.85), channel_id=1, source_target_pairs={{0,2},{2,4},{4,6},{6,8},{8,10},{10,12},{12,14},{14,16},{16,18},{18... | collective-permute-start | bytes 786440 | tf_op jit(solution)/shard_map/ppermute | solution.py:431
  7.6 14.5 %collective-permute-start.3 = (f32[128,512]{1,0:T(8,128)}, f32[128,512]{1,0:T(8,128)}, u32[]{:S(2)}, u32[]{:S(2)}) collective-permute-start(f32[128,512]{1,0:T(8,128)} %get-tuple-element.84), channel_id=1, source_target_pairs={{2,0},{4,2},{6,4},{8,6},{10,8},{12,10},{14,12},{16,14},{18,16},{20... | collective-permute-start | bytes 786440 | tf_op jit(solution)/shard_map/ppermute | solution.py:434
  8.9 18.6 %collective-permute-start.6 = (f32[2,256,256]{2,1,0:T(8,128)}, f32[2,256,256]{2,1,0:T(8,128)S(1)}, u32[]{:S(2)}, u32[]{:S(2)}) collective-permute-start(f32[2,256,256]{2,1,0:T(8,128)} %bitcast.44), channel_id=1, source_target_pairs={{0,1},{1,0},{2,3},{3,2},{4,5},{5,4},{6,7},{7,6},{8,9},{9,8},{10,11... | collective-permute-start | bytes 1572872 | tf_op jit(solution)/shard_map/ppermute | solution.py:414
  9.0 10.4 %collective-permute-start = (s32[2,2,2]{2,1,0:T(2,128)S(1)}, s32[2,2,2]{2,1,0:T(2,128)S(1)}, u32[]{:S(2)}, u32[]{:S(2)}) collective-permute-start(s32[2,2,2]{2,1,0:T(2,128)S(1)} %copy-done.8), channel_id=1, source_target_pairs={{0,2},{2,4},{4,6},{6,8},{8,10},{10,12},{12,14},{14,16},{16,18},{18... | collective-permute-start | bytes 104 | tf_op jit(solution)/shard_map/ppermute | solution.py:431
  13.5 7.5 %collective-permute-start.1 = (s32[2,2,2]{2,1,0:T(2,128)S(1)}, s32[2,2,2]{2,1,0:T(2,128)S(1)}, u32[]{:S(2)}, u32[]{:S(2)}) collective-permute-start(s32[2,2,2]{2,1,0:T(2,128)S(1)} %copy-done.8), channel_id=1, source_target_pairs={{2,0},{4,2},{6,4},{8,6},{10,8},{12,10},{14,12},{16,14},{18,16},{20... | collective-permute-start | bytes 104 | tf_op jit(solution)/shard_map/ppermute | solution.py:434
  15.0 1.0 copy-start.2
  16.1 1.0 copy-start.3
  17.1 4.1 %copy-start = (f32[2,256,512]{2,1,0:T(8,128)S(1)}, f32[2,256,512]{2,1,0:T(8,128)}, u32[]{:S(2)}) copy-start(f32[2,256,512]{2,1,0:T(8,128)} %strip_ref.5) | copy-start | bytes 3145732
  21.2 6.2 %copy-start.5 = (f32[2,256,256]{2,1,0:T(8,128)S(1)}, f32[2,256,256]{2,1,0:T(8,128)}, u32[]{:S(2)}) copy-start(f32[2,256,256]{2,1,0:T(8,128)} %copy-done.4) | copy-start | bytes 1572868
  21.2 6.3 %copy-start.7 = (bf16[4,256,256]{2,1,0:T(8,128)(2,1)S(1)}, bf16[4,256,256]{2,1,0:T(8,128)(2,1)}, u32[]{:S(2)}) copy-start(bf16[4,256,256]{2,1,0:T(8,128)(2,1)} %copy-done.6) | copy-start | bytes 1572868
  22.1 5.3 %collective-permute-start.4 = (f32[128,512]{1,0:T(8,128)S(1)}, f32[128,512]{1,0:T(8,128)S(1)}, u32[]{:S(2)}, u32[]{:S(2)}) collective-permute-start(f32[128,512]{1,0:T(8,128)S(1)} %collective-permute-done.2.refs_0_), channel_id=1, source_target_pairs={{0,1},{1,0},{2,3},{3,2},{4,5},{5,4},{6,7},{7,6},{8,9},{9,8},{10,11... | collective-permute-start | bytes 786440 | tf_op jit(solution)/shard_map/ppermute | solution.py:414
  22.2 5.2 %collective-permute-start.5 = (f32[128,512]{1,0:T(8,128)}, f32[128,512]{1,0:T(8,128)S(1)}, u32[]{:S(2)}, u32[]{:S(2)}) collective-permute-start(f32[128,512]{1,0:T(8,128)} %collective-permute-done.3.refs_2_), channel_id=1, source_target_pairs={{0,1},{1,0},{2,3},{3,2},{4,5},{5,4},{6,7},{7,6},{8,9},{9,8},{10,11... | collective-permute-start | bytes 786440 | tf_op jit(solution)/shard_map/ppermute | solution.py:414
  22.7 10.4 %collective-permute-start.7 = (f32[2,128,256]{2,1,0:T(8,128)S(1)}, f32[2,128,256]{2,1,0:T(8,128)S(1)}, u32[]{:S(2)}, u32[]{:S(2)}) collective-permute-start(f32[2,128,256]{2,1,0:T(8,128)S(1)} %get-tuple-element.51), channel_id=1, source_target_pairs={{0,2},{2,4},{4,6},{6,8},{8,10},{10,12},{12,14},{14,16},{16,18},{18... | collective-permute-start | bytes 786440 | tf_op jit(solution)/shard_map/ppermute | solution.py:431
  26.1 14.7 %collective-permute-start.8 = (f32[2,128,256]{2,1,0:T(8,128)S(1)}, f32[2,128,256]{2,1,0:T(8,128)S(1)}, u32[]{:S(2)}, u32[]{:S(2)}) collective-permute-start(f32[2,128,256]{2,1,0:T(8,128)S(1)} %get-tuple-element.52), channel_id=1, source_target_pairs={{2,0},{4,2},{6,4},{8,6},{10,8},{12,10},{14,12},{16,14},{18,16},{20... | collective-permute-start | bytes 786440 | tf_op jit(solution)/shard_map/ppermute | solution.py:434
  40.8 2.1 %collective-permute-start.11 = (f32[4,160,256]{2,1,0:T(8,128)S(1)}, f32[4,160,256]{2,1,0:T(8,128)S(1)}, u32[]{:S(2)}, u32[]{:S(2)}) collective-permute-start(f32[4,160,256]{2,1,0:T(8,128)S(1)} %get-tuple-element.57), channel_id=1, source_target_pairs={{0,1},{1,0},{2,3},{3,2},{4,5},{5,4},{6,7},{7,6},{8,9},{9,8},{10,11... | collective-permute-start | bytes 1966088 | tf_op jit(solution)/shard_map/ppermute | solution.py:414
  43.0 9.3 %collective-permute-start.14 = (f32[160,256]{1,0:T(8,128)S(1)}, f32[160,256]{1,0:T(8,128)S(1)}, u32[]{:S(2)}, u32[]{:S(2)}) collective-permute-start(f32[160,256]{1,0:T(8,128)S(1)} %get-tuple-element.82), channel_id=1, source_target_pairs={{0,12},{2,14},{4,8},{6,10},{8,4},{10,6},{12,0},{14,2},{16,28},{18,... | collective-permute-start | bytes 491528 | tf_op jit(solution)/shard_map/ppermute | solution.py:417
  47.3 7.3 %collective-permute-start.13 = (f32[160,256]{1,0:T(8,128)S(1)}, f32[160,256]{1,0:T(8,128)S(1)}, u32[]{:S(2)}, u32[]{:S(2)}) collective-permute-start(f32[160,256]{1,0:T(8,128)S(1)} %get-tuple-element.83), channel_id=1, source_target_pairs={{0,8},{2,10},{4,12},{6,14},{8,0},{10,2},{12,4},{14,6},{16,24},{18,... | collective-permute-start | bytes 491528 | tf_op jit(solution)/shard_map/ppermute | solution.py:417
  47.3 8.0 %collective-permute-start.12 = (f32[160,256]{1,0:T(8,128)S(1)}, f32[160,256]{1,0:T(8,128)S(1)}, u32[]{:S(2)}, u32[]{:S(2)}) collective-permute-start(f32[160,256]{1,0:T(8,128)S(1)} %get-tuple-element.81), channel_id=1, source_target_pairs={{0,4},{2,6},{4,0},{6,2},{8,12},{10,14},{12,8},{14,10},{16,20},{18,... | collective-permute-start | bytes 491528 | tf_op jit(solution)/shard_map/ppermute | solution.py:417
  47.9 34.4 %collective-permute-start.9 = (f32[2,256,256]{2,1,0:T(8,128)S(1)}, f32[2,256,256]{2,1,0:T(8,128)S(1)}, u32[]{:S(2)}, u32[]{:S(2)}) collective-permute-start(f32[2,256,256]{2,1,0:T(8,128)S(1)} %get-tuple-element.59.refs_0_), channel_id=1, source_target_pairs={{0,2},{2,4},{4,6},{6,8},{8,10},{10,12},{12,14},{14,16},{16,18},{18... | collective-permute-start | bytes 1572872 | tf_op jit(solution)/shard_map/ppermute | solution.py:431
  50.2 32.2 %collective-permute-start.10 = (f32[2,256,256]{2,1,0:T(8,128)S(1)}, f32[2,256,256]{2,1,0:T(8,128)S(1)}, u32[]{:S(2)}, u32[]{:S(2)}) collective-permute-start(f32[2,256,256]{2,1,0:T(8,128)S(1)} %get-tuple-element.59.refs_0_), channel_id=1, source_target_pairs={{2,0},{4,2},{6,4},{8,6},{10,8},{12,10},{14,12},{16,14},{18,16},{20... | collective-permute-start | bytes 1572872 | tf_op jit(solution)/shard_map/ppermute | solution.py:434
  55.4 25.1 %collective-permute-start.16 = (f32[160,256]{1,0:T(8,128)S(1)}, f32[160,256]{1,0:T(8,128)S(1)}, u32[]{:S(2)}, u32[]{:S(2)}) collective-permute-start(f32[160,256]{1,0:T(8,128)S(1)} %fusion.13), channel_id=1, source_target_pairs={{0,16},{2,18},{4,20},{6,22},{8,24},{10,26},{12,28},{14,30},{16,0},... | collective-permute-start | bytes 491528 | tf_op jit(solution)/shard_map/ppermute | solution.py:417
  68.4 12.0 %collective-permute-start.17 = (f32[160,256]{1,0:T(8,128)S(1)}, f32[160,256]{1,0:T(8,128)S(1)}, u32[]{:S(2)}, u32[]{:S(2)}) collective-permute-start(f32[160,256]{1,0:T(8,128)S(1)} %fusion.13), channel_id=1, source_target_pairs={{0,18},{2,16},{4,22},{6,20},{8,26},{10,24},{12,30},{14,28},{16,2},... | collective-permute-start | bytes 491528 | tf_op jit(solution)/shard_map/ppermute | solution.py:417
  68.4 13.9 %collective-permute-start.15 = (f32[160,256]{1,0:T(8,128)S(1)}, f32[160,256]{1,0:T(8,128)S(1)}, u32[]{:S(2)}, u32[]{:S(2)}) collective-permute-start(f32[160,256]{1,0:T(8,128)S(1)} %fusion.13), channel_id=1, source_target_pairs={{0,2},{2,0},{4,6},{6,4},{8,10},{10,8},{12,14},{14,12},{16,18},{18,... | collective-permute-start | bytes 491528 | tf_op jit(solution)/shard_map/ppermute | solution.py:417
  82.4 15.1 %collective-permute-start.18 = (f32[2,256,256]{2,1,0:T(8,128)S(1)}, f32[2,256,256]{2,1,0:T(8,128)S(1)}, u32[]{:S(2)}, u32[]{:S(2)}) collective-permute-start(f32[2,256,256]{2,1,0:T(8,128)S(1)} %get-tuple-element.59.refs_0_), channel_id=1, source_target_pairs={{0,1},{1,0},{2,3},{3,2},{4,5},{5,4},{6,7},{7,6},{8,9},{9,8},{10,11... | collective-permute-start | bytes 1572872 | tf_op jit(solution)/shard_map/ppermute | solution.py:414
  82.4 15.1 %collective-permute-start.19 = (f32[2,256,256]{2,1,0:T(8,128)S(1)}, f32[2,256,256]{2,1,0:T(8,128)S(1)}, u32[]{:S(2)}, u32[]{:S(2)}) collective-permute-start(f32[2,256,256]{2,1,0:T(8,128)S(1)} %collective-permute-done.9.refs_2_), channel_id=1, source_target_pairs={{0,1},{1,0},{2,3},{3,2},{4,5},{5,4},{6,7},{7,6},{8,9},{9,8},{10,11... | collective-permute-start | bytes 1572872 | tf_op jit(solution)/shard_map/ppermute | solution.py:414
  82.9 14.6 %collective-permute-start.20 = (f32[2,256,256]{2,1,0:T(8,128)S(1)}, f32[2,256,256]{2,1,0:T(8,128)S(1)}, u32[]{:S(2)}, u32[]{:S(2)}) collective-permute-start(f32[2,256,256]{2,1,0:T(8,128)S(1)} %collective-permute-done.10.refs_3_), channel_id=1, source_target_pairs={{0,1},{1,0},{2,3},{3,2},{4,5},{5,4},{6,7},{7,6},{8,9},{9,8},{10,11... | collective-permute-start | bytes 1572872 | tf_op jit(solution)/shard_map/ppermute | solution.py:414
  83.0 8.7 %collective-permute-start.23 = (f32[160,256]{1,0:T(8,128)S(1)}, f32[160,256]{1,0:T(8,128)S(1)}, u32[]{:S(2)}, u32[]{:S(2)}) collective-permute-start(f32[160,256]{1,0:T(8,128)S(1)} %add_add_fusion.1), channel_id=1, source_target_pairs={{0,12},{2,14},{4,8},{6,10},{8,4},{10,6},{12,0},{14,2},{16,28},{18,... | collective-permute-start | bytes 491528 | tf_op jit(solution)/shard_map/ppermute | solution.py:417
  86.6 7.6 %collective-permute-start.22 = (f32[160,256]{1,0:T(8,128)S(1)}, f32[160,256]{1,0:T(8,128)S(1)}, u32[]{:S(2)}, u32[]{:S(2)}) collective-permute-start(f32[160,256]{1,0:T(8,128)S(1)} %add_add_fusion.1), channel_id=1, source_target_pairs={{0,8},{2,10},{4,12},{6,14},{8,0},{10,2},{12,4},{14,6},{16,24},{18,... | collective-permute-start | bytes 491528 | tf_op jit(solution)/shard_map/ppermute | solution.py:417
  91.7 5.7 %collective-permute-start.21 = (f32[160,256]{1,0:T(8,128)S(1)}, f32[160,256]{1,0:T(8,128)S(1)}, u32[]{:S(2)}, u32[]{:S(2)}) collective-permute-start(f32[160,256]{1,0:T(8,128)S(1)} %add_add_fusion.1), channel_id=1, source_target_pairs={{0,4},{2,6},{4,0},{6,2},{8,12},{10,14},{12,8},{14,10},{16,20},{18,... | collective-permute-start | bytes 491528 | tf_op jit(solution)/shard_map/ppermute | solution.py:417
  97.4 4.1 %collective-permute-start.24 = (f32[4,160,256]{2,1,0:T(8,128)S(1)}, f32[4,160,256]{2,1,0:T(8,128)S(1)}, u32[]{:S(2)}, u32[]{:S(2)}) collective-permute-start(f32[4,160,256]{2,1,0:T(8,128)S(1)} %pad_maximum_fusion.own_totals), channel_id=1, source_target_pairs={{0,1},{1,0},{2,3},{3,2},{4,5},{5,4},{6,7},{7,6},{8,9},{9,8},{10,11... | collective-permute-start | bytes 1966088 | tf_op jit(solution)/shard_map/ppermute | solution.py:414
  106.7 2.3 %collective-permute-start.25 = (f32[4,160,256]{2,1,0:T(8,128)S(1)}, f32[4,160,256]{2,1,0:T(8,128)S(1)}, u32[]{:S(2)}, u32[]{:S(2)}) collective-permute-start(f32[4,160,256]{2,1,0:T(8,128)S(1)} %get-tuple-element.67), channel_id=1, source_target_pairs={{0,1},{1,0},{2,3},{3,2},{4,5},{5,4},{6,7},{7,6},{8,9},{9,8},{10,11... | collective-permute-start | bytes 1966088 | tf_op jit(solution)/shard_map/ppermute | solution.py:414
  109.1 9.1 %collective-permute-start.28 = (f32[160,256]{1,0:T(8,128)S(1)}, f32[160,256]{1,0:T(8,128)S(1)}, u32[]{:S(2)}, u32[]{:S(2)}) collective-permute-start(f32[160,256]{1,0:T(8,128)S(1)} %get-tuple-element.79), channel_id=1, source_target_pairs={{0,12},{2,14},{4,8},{6,10},{8,4},{10,6},{12,0},{14,2},{16,28},{18,... | collective-permute-start | bytes 491528 | tf_op jit(solution)/shard_map/ppermute | solution.py:417
  111.6 7.5 %collective-permute-start.27 = (f32[160,256]{1,0:T(8,128)S(1)}, f32[160,256]{1,0:T(8,128)S(1)}, u32[]{:S(2)}, u32[]{:S(2)}) collective-permute-start(f32[160,256]{1,0:T(8,128)S(1)} %get-tuple-element.80), channel_id=1, source_target_pairs={{0,8},{2,10},{4,12},{6,14},{8,0},{10,2},{12,4},{14,6},{16,24},{18,... | collective-permute-start | bytes 491528 | tf_op jit(solution)/shard_map/ppermute | solution.py:417
  111.6 11.8 %collective-permute-start.26 = (f32[160,256]{1,0:T(8,128)S(1)}, f32[160,256]{1,0:T(8,128)S(1)}, u32[]{:S(2)}, u32[]{:S(2)}) collective-permute-start(f32[160,256]{1,0:T(8,128)S(1)} %get-tuple-element.78), channel_id=1, source_target_pairs={{0,4},{2,6},{4,0},{6,2},{8,12},{10,14},{12,8},{14,10},{16,20},{18,... | collective-permute-start | bytes 491528 | tf_op jit(solution)/shard_map/ppermute | solution.py:417
  112.6 18.0 %collective-permute-start.35 = (f32[2,128,256]{2,1,0:T(8,128)S(1)}, f32[2,128,256]{2,1,0:T(8,128)S(1)}, u32[]{:S(2)}, u32[]{:S(2)}) collective-permute-start(f32[2,128,256]{2,1,0:T(8,128)S(1)} %get-tuple-element.70), channel_id=1, source_target_pairs={{0,2},{2,4},{4,6},{6,8},{8,10},{10,12},{12,14},{14,16},{16,18},{18... | collective-permute-start | bytes 786440 | tf_op jit(solution)/shard_map/ppermute | solution.py:431
  116.6 14.0 %collective-permute-start.36 = (f32[2,128,256]{2,1,0:T(8,128)S(1)}, f32[2,128,256]{2,1,0:T(8,128)S(1)}, u32[]{:S(2)}, u32[]{:S(2)}) collective-permute-start(f32[2,128,256]{2,1,0:T(8,128)S(1)} %get-tuple-element.71), channel_id=1, source_target_pairs={{2,0},{4,2},{6,4},{8,6},{10,8},{12,10},{14,12},{16,14},{18,16},{20... | collective-permute-start | bytes 786440 | tf_op jit(solution)/shard_map/ppermute | solution.py:434
  123.5 15.9 %collective-permute-start.30 = (f32[160,256]{1,0:T(8,128)S(1)}, f32[160,256]{1,0:T(8,128)S(1)}, u32[]{:S(2)}, u32[]{:S(2)}) collective-permute-start(f32[160,256]{1,0:T(8,128)S(1)} %fusion.6), channel_id=1, source_target_pairs={{0,16},{2,18},{4,20},{6,22},{8,24},{10,26},{12,28},{14,30},{16,0},... | collective-permute-start | bytes 491528 | tf_op jit(solution)/shard_map/ppermute | solution.py:417
  127.4 12.0 %collective-permute-start.31 = (f32[160,256]{1,0:T(8,128)S(1)}, f32[160,256]{1,0:T(8,128)S(1)}, u32[]{:S(2)}, u32[]{:S(2)}) collective-permute-start(f32[160,256]{1,0:T(8,128)S(1)} %fusion.6), channel_id=1, source_target_pairs={{0,18},{2,16},{4,22},{6,20},{8,26},{10,24},{12,30},{14,28},{16,2},... | collective-permute-start | bytes 491528 | tf_op jit(solution)/shard_map/ppermute | solution.py:417
  127.4 12.0 %collective-permute-start.29 = (f32[160,256]{1,0:T(8,128)S(1)}, f32[160,256]{1,0:T(8,128)S(1)}, u32[]{:S(2)}, u32[]{:S(2)}) collective-permute-start(f32[160,256]{1,0:T(8,128)S(1)} %fusion.6), channel_id=1, source_target_pairs={{0,2},{2,0},{4,6},{6,4},{8,10},{10,8},{12,14},{14,12},{16,18},{18,... | collective-permute-start | bytes 491528 | tf_op jit(solution)/shard_map/ppermute | solution.py:417
  130.6 13.8 %collective-permute-start.37 = (f32[2,256,256]{2,1,0:T(8,128)S(1)}, f32[2,256,256]{2,1,0:T(8,128)S(1)}, u32[]{:S(2)}, u32[]{:S(2)}) collective-permute-start(f32[2,256,256]{2,1,0:T(8,128)S(1)} %get-tuple-element.73.refs_0_), channel_id=1, source_target_pairs={{0,1},{1,0},{2,3},{3,2},{4,5},{5,4},{6,7},{7,6},{8,9},{9,8},{10,11... | collective-permute-start | bytes 1572872 | tf_op jit(solution)/shard_map/ppermute | solution.py:414
  130.7 13.1 %collective-permute-start.38 = (f32[2,128,256]{2,1,0:T(8,128)S(1)}, f32[2,128,256]{2,1,0:T(8,128)S(1)}, u32[]{:S(2)}, u32[]{:S(2)}) collective-permute-start(f32[2,128,256]{2,1,0:T(8,128)S(1)} %collective-permute-done.35.refs_2_), channel_id=1, source_target_pairs={{0,1},{1,0},{2,3},{3,2},{4,5},{5,4},{6,7},{7,6},{8,9},{9,8},{10,11... | collective-permute-start | bytes 786440 | tf_op jit(solution)/shard_map/ppermute | solution.py:414
  139.4 5.0 %collective-permute-start.39 = (f32[2,128,256]{2,1,0:T(8,128)S(1)}, f32[2,128,256]{2,1,0:T(8,128)S(1)}, u32[]{:S(2)}, u32[]{:S(2)}) collective-permute-start(f32[2,128,256]{2,1,0:T(8,128)S(1)} %collective-permute-done.36.refs_3_), channel_id=1, source_target_pairs={{0,1},{1,0},{2,3},{3,2},{4,5},{5,4},{6,7},{7,6},{8,9},{9,8},{10,11... | collective-permute-start | bytes 786440 | tf_op jit(solution)/shard_map/ppermute | solution.py:414
  139.5 9.3 %collective-permute-start.34 = (f32[160,256]{1,0:T(8,128)S(1)}, f32[160,256]{1,0:T(8,128)S(1)}, u32[]{:S(2)}, u32[]{:S(2)}) collective-permute-start(f32[160,256]{1,0:T(8,128)S(1)} %add_add_fusion), channel_id=1, source_target_pairs={{0,12},{2,14},{4,8},{6,10},{8,4},{10,6},{12,0},{14,2},{16,28},{18,... | collective-permute-start | bytes 491528 | tf_op jit(solution)/shard_map/ppermute | solution.py:417
  143.8 7.2 %collective-permute-start.33 = (f32[160,256]{1,0:T(8,128)S(1)}, f32[160,256]{1,0:T(8,128)S(1)}, u32[]{:S(2)}, u32[]{:S(2)}) collective-permute-start(f32[160,256]{1,0:T(8,128)S(1)} %add_add_fusion), channel_id=1, source_target_pairs={{0,8},{2,10},{4,12},{6,14},{8,0},{10,2},{12,4},{14,6},{16,24},{18,... | collective-permute-start | bytes 491528 | tf_op jit(solution)/shard_map/ppermute | solution.py:417
  143.8 7.9 %collective-permute-start.32 = (f32[160,256]{1,0:T(8,128)S(1)}, f32[160,256]{1,0:T(8,128)S(1)}, u32[]{:S(2)}, u32[]{:S(2)}) collective-permute-start(f32[160,256]{1,0:T(8,128)S(1)} %add_add_fusion), channel_id=1, source_target_pairs={{0,4},{2,6},{4,0},{6,2},{8,12},{10,14},{12,8},{14,10},{16,20},{18,... | collective-permute-start | bytes 491528 | tf_op jit(solution)/shard_map/ppermute | solution.py:417
  151.8 1.4 collective-permute-start.40
  (2 other events, 1.6 us)

commit v6 on v3

--- a/solution.py
+++ b/solution.py
@@ -481,7 +481,7 @@
         piece = exchange(piece)
         if not last:
             edges = [from_below(edges[1]), from_above(edges[0])]
-            piece, *edges = lax.optimization_barrier((piece, *edges))
+            piece, edges[0] = lax.optimization_barrier((piece, edges[0]))
         totals = gather(piece, NEAR_STEP)
         if last:
             totals, object_field = lax.optimization_barrier((totals, object_field))

time: 145 us -> 145 us (level); the launches traced: 143 us -> 145 us
  starting transfers between devices: 59 us -> 66 us
  waiting for transfers between devices: 50.6 us -> 44.7 us
    ppermute x5, waiting for transfers between devices: 8.82 us -> 2.09 us  [from_below(): return lax.ppermute(value, 'tile', up)]
    ppermute x18, starting transfers between devices: 29.6 us -> 35 us  [across(): return lax.ppermute(value, 'tile', [(i, i ^ k) for i in range(tiles)])]
    ppermute x5, starting transfers between devices: 20.6 us -> 22.4 us  [from_below(): return lax.ppermute(value, 'tile', up)]
    ppermute x18, waiting for transfers between devices: 28.9 us -> 30.6 us  [across(): return lax.ppermute(value, 'tile', [(i, i ^ k) for i in range(tiles)])]
  transfers between devices with their start and end apart: 41 -> 41, of which waited for: 23 -> 22; matrix products, arithmetic and copies ran while one was open for 3% -> 3% of each run, Pallas kernels for 8% -> 7%
where the time goes in v6:
time: 145 us
  starting transfers between devices  66 us (46%)
  waiting for transfers between devices  44.7 us (31%)
  Pallas kernels  23.9 us (16%)
  local copies, waits for them, and re-layouts  6.84 us (5%)
  other arithmetic  2.38 us (2%)
    ppermute x18, starting transfers between devices, across(): return lax.ppermute(value, 'tile', [(i, i ^ k) for i in range(tiles)])  35 us
    ppermute x18, waiting for transfers between devices, across(): return lax.ppermute(value, 'tile', [(i, i ^ k) for i in range(tiles)])  30.6 us
    pallas_call x10, Pallas kernels, call(): pl.pallas_call(kernel, out_shape=shapes, in_specs=[smem] + [vmem] * (len(...  23.9 us
    ppermute x5, starting transfers between devices, from_below(): return lax.ppermute(value, 'tile', up)  22.4 us
    ppermute x5, waiting for transfers between devices, from_above(): return lax.ppermute(value, 'tile', down)  7.01 us
    ppermute x5, starting transfers between devices, from_above(): return lax.ppermute(value, 'tile', down)  6.63 us
    ppermute x13, waiting for transfers between devices, swap(): return lax.ppermute(value, 'mode', [(0, 1), (1, 0)])  5.05 us
  transfers between devices with their start and end apart: 41, of which 22 were waited for; matrix products, arithmetic and copies ran while one was open for 3% of the time, Pallas kernels for 7%

profile of v6, /device:TPU:0, one launch (start us, length us, event | category | flops | bytes accessed | tf_op | source)
XLA Modules:
  0.0 144.8 jit_solution(10736540254987798971)
XLA Ops:
  0.6 1.9 %dynamic-slice_bitcast_fusion = (f32[128,512]{1,0:T(8,128)}, f32[128,512]{1,0:T(8,128)}) fusion(f32[2,256,512]{2,1,0:T(8,128)} %strip_ref.3, s32[]{:T(128)S(6)} %select_n.4, s32[]{:T(128)S(6)} %add.117), kind=kLoop, calls=%fused_computation.2 | loop fusion | bytes 1048584 | tf_op jit(solution)/shard_map/slice | solution.py:426
  2.6 5.0 %collective-permute-start = (f32[128,512]{1,0:T(8,128)}, f32[128,512]{1,0:T(8,128)S(1)}, u32[]{:S(2)}, u32[]{:S(2)}) collective-permute-start(f32[128,512]{1,0:T(8,128)} %get-tuple-element.83), channel_id=1, source_target_pairs={{0,2},{2,4},{4,6},{6,8},{8,10},{10,12},{12,14},{14,16},{16,18},{18... | collective-permute-start | bytes 786440 | tf_op jit(solution)/shard_map/ppermute | solution.py:414
  7.6 1.3 collective-permute-start.1
  9.0 4.5 %collective-permute-start.2 = (s32[2,2,2]{2,1,0:T(2,128)S(1)}, s32[2,2,2]{2,1,0:T(2,128)S(1)}, u32[]{:S(2)}, u32[]{:S(2)}) collective-permute-start(s32[2,2,2]{2,1,0:T(2,128)S(1)} %copy-done.9), channel_id=1, source_target_pairs={{0,2},{2,4},{4,6},{6,8},{8,10},{10,12},{12,14},{14,16},{16,18},{18... | collective-permute-start | bytes 104 | tf_op jit(solution)/shard_map/ppermute | solution.py:414
  13.5 1.3 collective-permute-start.3
  15.0 1.0 copy-done.2
  17.8 1.3 collective-permute-done.2
  19.1 1.9 %collective-permute-done.3 = s32[2,2,2]{2,1,0:T(2,128)S(1)} collective-permute-done((s32[2,2,2]{2,1,0:T(2,128)S(1)}, s32[2,2,2]{2,1,0:T(2,128)S(1)}, u32[]{:S(2)}, u32[]{:S(2)}) %collective-permute-start.3) | collective-permute-done | bytes 64 | tf_op jit(solution)/shard_map/ppermute | solution.py:417
  23.2 6.4 %field.2 = (f32[2,256,256]{2,1,0:T(8,128)S(1)}, f32[2,128,256]{2,1,0:T(8,128)}, f32[2,128,256]{2,1,0:T(8,128)}, f32[4,160,256]{2,1,0:T(8,128)S(1)}, f32[4,160,256]{2,1,0:T(8,128)S(1)}) custom-call(s32[26]{0:T(128)S(1)} %concatenate.8.info, f32[2,256,512]{2,1,0:T(8,128)S(1)} %copy-done, f32[128,512]{1,0:T(8,128)S(1)} %collective-permute-done.refs_0_, ...), custom_call_target="tpu_custom_call" | custom-call | flops 3221225472 | bytes 6553704 | tf_op jit(solution)/shard_map/field/pallas_call | solution.py:371
  29.8 3.4 %collective-permute-start.7 = (f32[2,128,256]{2,1,0:T(8,128)}, f32[2,128,256]{2,1,0:T(8,128)S(1)}, u32[]{:S(2)}, u32[]{:S(2)}) collective-permute-start(f32[2,128,256]{2,1,0:T(8,128)} %get-tuple-element.50), channel_id=1, source_target_pairs={{0,2},{2,4},{4,6},{6,8},{8,10},{10,12},{12,14},{14,16},{16,18},{18... | collective-permute-start | bytes 786440 | tf_op jit(solution)/shard_map/ppermute | solution.py:414
  33.2 1.3 collective-permute-start.8
  35.5 3.7 %collective-permute-start.13 = (f32[160,256]{1,0:T(8,128)}, f32[160,256]{1,0:T(8,128)}, u32[]{:S(2)}, u32[]{:S(2)}) collective-permute-start(f32[160,256]{1,0:T(8,128)} %get-tuple-element.79), channel_id=1, source_target_pairs={{0,4},{2,6},{4,0},{6,2},{8,12},{10,14},{12,8},{14,10},{16,20},{18,... | collective-permute-start | bytes 491528 | tf_op jit(solution)/shard_map/ppermute | solution.py:400
  39.3 2.4 %collective-permute-start.14 = (f32[160,256]{1,0:T(8,128)}, f32[160,256]{1,0:T(8,128)}, u32[]{:S(2)}, u32[]{:S(2)}) collective-permute-start(f32[160,256]{1,0:T(8,128)} %get-tuple-element.81), channel_id=1, source_target_pairs={{0,8},{2,10},{4,12},{6,14},{8,0},{10,2},{12,4},{14,6},{16,24},{18,... | collective-permute-start | bytes 491528 | tf_op jit(solution)/shard_map/ppermute | solution.py:400
  41.6 1.5 %collective-permute-start.15 = (f32[160,256]{1,0:T(8,128)}, f32[160,256]{1,0:T(8,128)}, u32[]{:S(2)}, u32[]{:S(2)}) collective-permute-start(f32[160,256]{1,0:T(8,128)} %get-tuple-element.80), channel_id=1, source_target_pairs={{0,12},{2,14},{4,8},{6,10},{8,4},{10,6},{12,0},{14,2},{16,28},{18,... | collective-permute-start | bytes 491528 | tf_op jit(solution)/shard_map/ppermute | solution.py:400
  45.1 1.7 %illumination.2.illum = f32[256,512]{1,0:T(8,128)S(1)} custom-call(s32[26]{0:T(128)S(1)} %concatenate.9.info, f32[2,256,256]{2,1,0:T(8,128)S(1)} %get-tuple-element.46.refs_4_.own.refs_0_, f32[2,256,256]{2,1,0:T(8,128)S(1)} %collective-permute-done.6.refs_5_.other.refs_1_), custom_call_target="tpu_custom_call" | custom-call | bytes 1572968 | tf_op jit(solution)/shard_map/illumination/pallas_call | solution.py:371
  47.6 4.0 %collective-permute-done.14 = f32[160,256]{1,0:T(8,128)} collective-permute-done((f32[160,256]{1,0:T(8,128)}, f32[160,256]{1,0:T(8,128)}, u32[]{:S(2)}, u32[]{:S(2)}) %collective-permute-start.14) | collective-permute-done | bytes 163872 | tf_op jit(solution)/shard_map/ppermute | solution.py:400
  51.6 1.2 fusion.13
  52.8 3.3 %collective-permute-start.16 = (f32[160,256]{1,0:T(8,128)S(1)}, f32[160,256]{1,0:T(8,128)S(1)}, u32[]{:S(2)}, u32[]{:S(2)}) collective-permute-start(f32[160,256]{1,0:T(8,128)S(1)} %fusion.13), channel_id=1, source_target_pairs={{0,2},{2,0},{4,6},{6,4},{8,10},{10,8},{12,14},{14,12},{16,18},{18,... | collective-permute-start | bytes 491528 | tf_op jit(solution)/shard_map/ppermute | solution.py:400
  56.2 2.6 %collective-permute-start.17 = (f32[160,256]{1,0:T(8,128)S(1)}, f32[160,256]{1,0:T(8,128)S(1)}, u32[]{:S(2)}, u32[]{:S(2)}) collective-permute-start(f32[160,256]{1,0:T(8,128)S(1)} %fusion.13), channel_id=1, source_target_pairs={{0,16},{2,18},{4,20},{6,22},{8,24},{10,26},{12,28},{14,30},{16,0},... | collective-permute-start | bytes 491528 | tf_op jit(solution)/shard_map/ppermute | solution.py:400
  58.8 2.8 %update.2 = (f32[2,256,512]{2,1,0:T(8,128)S(1)}, f32[2,128,256]{2,1,0:T(8,128)S(1)}, f32[2,128,256]{2,1,0:T(8,128)S(1)}) custom-call(s32[26]{0:T(128)S(1)} %concatenate.9.info, f32[2,256,512]{2,1,0:T(8,128)S(1)} %copy-done, f32[256,512]{1,0:T(8,128)S(1)} %illumination.2.illum, f32[2,256,256]{2,1,0:T(8,128)S(1)} %get-tuple-element.53.own, ...), custom_call_target="tpu_custom_call" | custom-call | bytes 5242984 | tf_op jit(solution)/shard_map/update/pallas_call | solution.py:371
  61.5 3.7 %collective-permute-start.19 = (f32[2,128,256]{2,1,0:T(8,128)S(1)}, f32[2,128,256]{2,1,0:T(8,128)S(1)}, u32[]{:S(2)}, u32[]{:S(2)}) collective-permute-start(f32[2,128,256]{2,1,0:T(8,128)S(1)} %get-tuple-element.59), channel_id=1, source_target_pairs={{0,2},{2,4},{4,6},{6,8},{8,10},{10,12},{12,14},{14,16},{16,18},{18... | collective-permute-start | bytes 786440 | tf_op jit(solution)/shard_map/ppermute | solution.py:414
  65.3 5.8 %collective-permute-done.17 = f32[160,256]{1,0:T(8,128)S(1)} collective-permute-done((f32[160,256]{1,0:T(8,128)S(1)}, f32[160,256]{1,0:T(8,128)S(1)}, u32[]{:S(2)}, u32[]{:S(2)}) %collective-permute-start.17) | collective-permute-done | bytes 163872 | tf_op jit(solution)/shard_map/ppermute | solution.py:400
  71.1 2.7 %collective-permute-done.18 = f32[160,256]{1,0:T(8,128)S(1)} collective-permute-done((f32[160,256]{1,0:T(8,128)S(1)}, f32[160,256]{1,0:T(8,128)S(1)}, u32[]{:S(2)}, u32[]{:S(2)}) %collective-permute-start.18) | collective-permute-done | bytes 163872 | tf_op jit(solution)/shard_map/ppermute | solution.py:400
  74.1 3.6 %collective-permute-start.21 = (f32[160,256]{1,0:T(8,128)S(1)}, f32[160,256]{1,0:T(8,128)S(1)}, u32[]{:S(2)}, u32[]{:S(2)}) collective-permute-start(f32[160,256]{1,0:T(8,128)S(1)} %add_add_fusion.1), channel_id=1, source_target_pairs={{0,4},{2,6},{4,0},{6,2},{8,12},{10,14},{12,8},{14,10},{16,20},{18,... | collective-permute-start | bytes 491528 | tf_op jit(solution)/shard_map/ppermute | solution.py:400
  77.7 1.5 %collective-permute-start.23 = (f32[160,256]{1,0:T(8,128)S(1)}, f32[160,256]{1,0:T(8,128)S(1)}, u32[]{:S(2)}, u32[]{:S(2)}) collective-permute-start(f32[160,256]{1,0:T(8,128)S(1)} %add_add_fusion.1), channel_id=1, source_target_pairs={{0,12},{2,14},{4,8},{6,10},{8,4},{10,6},{12,0},{14,2},{16,28},{18,... | collective-permute-start | bytes 491528 | tf_op jit(solution)/shard_map/ppermute | solution.py:400
  79.2 1.5 %collective-permute-start.20 = (f32[2,128,256]{2,1,0:T(8,128)S(1)}, f32[2,128,256]{2,1,0:T(8,128)S(1)}, u32[]{:S(2)}, u32[]{:S(2)}) collective-permute-start(f32[2,128,256]{2,1,0:T(8,128)S(1)} %get-tuple-element.61), channel_id=1, source_target_pairs={{2,0},{4,2},{6,4},{8,6},{10,8},{12,10},{14,12},{16,14},{18,16},{20... | collective-permute-start | bytes 786440 | tf_op jit(solution)/shard_map/ppermute | solution.py:417
  80.7 2.1 %collective-permute-done.21 = f32[160,256]{1,0:T(8,128)S(1)} collective-permute-done((f32[160,256]{1,0:T(8,128)S(1)}, f32[160,256]{1,0:T(8,128)S(1)}, u32[]{:S(2)}, u32[]{:S(2)}) %collective-permute-start.21) | collective-permute-done | bytes 163872 | tf_op jit(solution)/shard_map/ppermute | solution.py:400
  83.5 1.5 %collective-permute-done.23 = f32[160,256]{1,0:T(8,128)S(1)} collective-permute-done((f32[160,256]{1,0:T(8,128)S(1)}, f32[160,256]{1,0:T(8,128)S(1)}, u32[]{:S(2)}, u32[]{:S(2)}) %collective-permute-start.23) | collective-permute-done | bytes 163872 | tf_op jit(solution)/shard_map/ppermute | solution.py:400
  85.1 2.8 %collective-permute-done.20.above = f32[2,128,256]{2,1,0:T(8,128)S(1)} collective-permute-done((f32[2,128,256]{2,1,0:T(8,128)S(1)}, f32[2,128,256]{2,1,0:T(8,128)S(1)}, u32[]{:S(2)}, u32[]{:S(2)}) %collective-permute-start.20) | collective-permute-done | bytes 262176 | tf_op jit(solution)/shard_map/ppermute | solution.py:417
  90.1 4.5 %field.3 = (f32[2,256,256]{2,1,0:T(8,128)S(1)}, f32[2,128,256]{2,1,0:T(8,128)S(1)}, f32[2,128,256]{2,1,0:T(8,128)S(1)}, f32[4,160,256]{2,1,0:T(8,128)S(1)}, f32[4,160,256]{2,1,0:T(8,128)S(1)}) custom-call(s32[26]{0:T(128)S(1)} %concatenate.8.info, f32[2,256,256]{2,1,0:T(8,128)S(1)} %patch.1.strip_ref, f32[2,256,256]{2,1,0:T(8,128)S(1)} %get-tuple-element.63.refs_0_.own, ...), custom_call_target="tpu_custom_call" | custom-call | flops 3221225472 | bytes 4980840 | tf_op jit(solution)/shard_map/field/pallas_call | solution.py:371
  94.7 2.1 %collective-permute-done.25 = f32[4,160,256]{2,1,0:T(8,128)S(1)} collective-permute-done((f32[4,160,256]{2,1,0:T(8,128)S(1)}, f32[4,160,256]{2,1,0:T(8,128)S(1)}, u32[]{:S(2)}, u32[]{:S(2)}) %collective-permute-start.25) | collective-permute-done | bytes 655392 | tf_op jit(solution)/shard_map/ppermute | solution.py:397
  96.8 3.2 %collective-permute-start.26 = (f32[160,256]{1,0:T(8,128)S(1)}, f32[160,256]{1,0:T(8,128)S(1)}, u32[]{:S(2)}, u32[]{:S(2)}) collective-permute-start(f32[160,256]{1,0:T(8,128)S(1)} %get-tuple-element.76), channel_id=1, source_target_pairs={{0,4},{2,6},{4,0},{6,2},{8,12},{10,14},{12,8},{14,10},{16,20},{18,... | collective-permute-start | bytes 491528 | tf_op jit(solution)/shard_map/ppermute | solution.py:400
  100.0 1.6 %collective-permute-start.27 = (f32[160,256]{1,0:T(8,128)S(1)}, f32[160,256]{1,0:T(8,128)S(1)}, u32[]{:S(2)}, u32[]{:S(2)}) collective-permute-start(f32[160,256]{1,0:T(8,128)S(1)} %get-tuple-element.78), channel_id=1, source_target_pairs={{0,8},{2,10},{4,12},{6,14},{8,0},{10,2},{12,4},{14,6},{16,24},{18,... | collective-permute-start | bytes 491528 | tf_op jit(solution)/shard_map/ppermute | solution.py:400
  101.7 5.7 %collective-permute-start.35 = (f32[2,128,256]{2,1,0:T(8,128)S(1)}, f32[2,128,256]{2,1,0:T(8,128)S(1)}, u32[]{:S(2)}, u32[]{:S(2)}) collective-permute-start(f32[2,128,256]{2,1,0:T(8,128)S(1)} %get-tuple-element.68), channel_id=1, source_target_pairs={{0,2},{2,4},{4,6},{6,8},{8,10},{10,12},{12,14},{14,16},{16,18},{18... | collective-permute-start | bytes 786440 | tf_op jit(solution)/shard_map/ppermute | solution.py:414
  107.4 1.3 collective-permute-start.36
  109.5 3.6 %collective-permute-start.29 = (f32[160,256]{1,0:T(8,128)S(1)}, f32[160,256]{1,0:T(8,128)S(1)}, u32[]{:S(2)}, u32[]{:S(2)}) collective-permute-start(f32[160,256]{1,0:T(8,128)S(1)} %fusion.6), channel_id=1, source_target_pairs={{0,2},{2,0},{4,6},{6,4},{8,10},{10,8},{12,14},{14,12},{16,18},{18,... | collective-permute-start | bytes 491528 | tf_op jit(solution)/shard_map/ppermute | solution.py:400
  113.2 4.3 %collective-permute-start.30 = (f32[160,256]{1,0:T(8,128)S(1)}, f32[160,256]{1,0:T(8,128)S(1)}, u32[]{:S(2)}, u32[]{:S(2)}) collective-permute-start(f32[160,256]{1,0:T(8,128)S(1)} %fusion.6), channel_id=1, source_target_pairs={{0,16},{2,18},{4,20},{6,22},{8,24},{10,26},{12,28},{14,30},{16,0},... | collective-permute-start | bytes 491528 | tf_op jit(solution)/shard_map/ppermute | solution.py:400
  117.6 1.7 %illumination.3.illum = f32[256,512]{1,0:T(8,128)S(1)} custom-call(s32[26]{0:T(128)S(1)} %concatenate.9.info, f32[2,256,256]{2,1,0:T(8,128)S(1)} %get-tuple-element.63.refs_0_.own, f32[2,256,256]{2,1,0:T(8,128)S(1)} %get-tuple-element.64.refs_1_.other), custom_call_target="tpu_custom_call" | custom-call | bytes 1572968 | tf_op jit(solution)/shard_map/illumination/pallas_call | solution.py:371
  119.8 2.0 %collective-permute-done.36.a0 = f32[2,128,256]{2,1,0:T(8,128)S(1)} collective-permute-done((f32[2,128,256]{2,1,0:T(8,128)S(1)}, f32[2,128,256]{2,1,0:T(8,128)S(1)}, u32[]{:S(2)}, u32[]{:S(2)}) %collective-permute-start.36) | collective-permute-done | bytes 262176 | tf_op jit(solution)/shard_map/ppermute | solution.py:417
  122.3 1.9 %collective-permute-done.29 = f32[160,256]{1,0:T(8,128)S(1)} collective-permute-done((f32[160,256]{1,0:T(8,128)S(1)}, f32[160,256]{1,0:T(8,128)S(1)}, u32[]{:S(2)}, u32[]{:S(2)}) %collective-permute-start.29) | collective-permute-done | bytes 163872 | tf_op jit(solution)/shard_map/ppermute | solution.py:400
  124.2 7.3 %collective-permute-done.30 = f32[160,256]{1,0:T(8,128)S(1)} collective-permute-done((f32[160,256]{1,0:T(8,128)S(1)}, f32[160,256]{1,0:T(8,128)S(1)}, u32[]{:S(2)}, u32[]{:S(2)}) %collective-permute-start.30) | collective-permute-done | bytes 163872 | tf_op jit(solution)/shard_map/ppermute | solution.py:400
  131.6 1.1 collective-permute-start.32
  132.7 2.4 %collective-permute-start.34 = (f32[160,256]{1,0:T(8,128)S(1)}, f32[160,256]{1,0:T(8,128)S(1)}, u32[]{:S(2)}, u32[]{:S(2)}) collective-permute-start(f32[160,256]{1,0:T(8,128)S(1)} %add_add_fusion), channel_id=1, source_target_pairs={{0,12},{2,14},{4,8},{6,10},{8,4},{10,6},{12,0},{14,2},{16,28},{18,... | collective-permute-start | bytes 491528 | tf_op jit(solution)/shard_map/ppermute | solution.py:400
  135.1 3.1 %update.3 = f32[2,256,512]{2,1,0:T(8,128)} custom-call(s32[26]{0:T(128)S(1)} %concatenate.9.info, f32[2,256,512]{2,1,0:T(8,128)S(1)} %get-tuple-element.56.strip_ref, f32[256,512]{1,0:T(8,128)S(1)} %illumination.3.illum, f32[2,256,256]{2,1,0:T(8,128)S(1)} %get-tuple-element.71.own, f32[2,256,256]{2,1,0:T(8,128)S(1)} %collective-permute-done.37.other, ...), custom_call_target="tpu_custom_call" | custom-call | bytes 4718696 | tf_op jit(solution)/shard_map/update/pallas_call | solution.py:371
  138.2 1.5 %collective-permute-done.33 = f32[160,256]{1,0:T(8,128)S(1)} collective-permute-done((f32[160,256]{1,0:T(8,128)S(1)}, f32[160,256]{1,0:T(8,128)S(1)}, u32[]{:S(2)}, u32[]{:S(2)}) %collective-permute-start.33) | collective-permute-done | bytes 163872 | tf_op jit(solution)/shard_map/ppermute | solution.py:400
  139.7 2.2 %collective-permute-done.34 = f32[160,256]{1,0:T(8,128)S(1)} collective-permute-done((f32[160,256]{1,0:T(8,128)S(1)}, f32[160,256]{1,0:T(8,128)S(1)}, u32[]{:S(2)}, u32[]{:S(2)}) %collective-permute-start.34) | collective-permute-done | bytes 163872 | tf_op jit(solution)/shard_map/ppermute | solution.py:400
  142.1 1.3 collective-permute-done.40.other_totals
  143.4 1.4 probe.3
  (85 shorter events, 13.9 us)
Async XLA Ops:
  0.6 14.4 %copy-start.1 = (f32[2,2,256,256]{3,2,1,0:T(8,128)S(1)}, f32[2,2,256,256]{3,2,1,0:T(8,128)}, u32[]{:S(2)}) copy-start(f32[2,2,256,256]{3,2,1,0:T(8,128)} %measured.1) | copy-start | bytes 3145732
  2.6 6.4 %copy-start.9 = (s32[2,2,2]{2,1,0:T(2,128)S(1)}, s32[2,2,2]{2,1,0:T(2,128)}, u32[]{:S(2)}) copy-start(s32[2,2,2]{2,1,0:T(2,128)} %param.7) | copy-start | bytes 100
  2.6 18.4 %collective-permute-start = (f32[128,512]{1,0:T(8,128)}, f32[128,512]{1,0:T(8,128)S(1)}, u32[]{:S(2)}, u32[]{:S(2)}) collective-permute-start(f32[128,512]{1,0:T(8,128)} %get-tuple-element.83), channel_id=1, source_target_pairs={{0,2},{2,4},{4,6},{6,8},{8,10},{10,12},{12,14},{14,16},{16,18},{18... | collective-permute-start | bytes 786440 | tf_op jit(solution)/shard_map/ppermute | solution.py:414
  7.6 13.5 %collective-permute-start.1 = (f32[128,512]{1,0:T(8,128)}, f32[128,512]{1,0:T(8,128)}, u32[]{:S(2)}, u32[]{:S(2)}) collective-permute-start(f32[128,512]{1,0:T(8,128)} %get-tuple-element.82), channel_id=1, source_target_pairs={{2,0},{4,2},{6,4},{8,6},{10,8},{12,10},{14,12},{16,14},{18,16},{20... | collective-permute-start | bytes 786440 | tf_op jit(solution)/shard_map/ppermute | solution.py:417
  8.9 14.4 %collective-permute-start.6 = (f32[2,256,256]{2,1,0:T(8,128)}, f32[2,256,256]{2,1,0:T(8,128)S(1)}, u32[]{:S(2)}, u32[]{:S(2)}) collective-permute-start(f32[2,256,256]{2,1,0:T(8,128)} %bitcast.44), channel_id=1, source_target_pairs={{0,1},{1,0},{2,3},{3,2},{4,5},{5,4},{6,7},{7,6},{8,9},{9,8},{10,11... | collective-permute-start | bytes 1572872 | tf_op jit(solution)/shard_map/ppermute | solution.py:397
  9.0 10.1 %collective-permute-start.2 = (s32[2,2,2]{2,1,0:T(2,128)S(1)}, s32[2,2,2]{2,1,0:T(2,128)S(1)}, u32[]{:S(2)}, u32[]{:S(2)}) collective-permute-start(s32[2,2,2]{2,1,0:T(2,128)S(1)} %copy-done.9), channel_id=1, source_target_pairs={{0,2},{2,4},{4,6},{6,8},{8,10},{10,12},{12,14},{14,16},{16,18},{18... | collective-permute-start | bytes 104 | tf_op jit(solution)/shard_map/ppermute | solution.py:414
  13.5 7.5 %collective-permute-start.3 = (s32[2,2,2]{2,1,0:T(2,128)S(1)}, s32[2,2,2]{2,1,0:T(2,128)S(1)}, u32[]{:S(2)}, u32[]{:S(2)}) collective-permute-start(s32[2,2,2]{2,1,0:T(2,128)S(1)} %copy-done.9), channel_id=1, source_target_pairs={{2,0},{4,2},{6,4},{8,6},{10,8},{12,10},{14,12},{16,14},{18,16},{20... | collective-permute-start | bytes 104 | tf_op jit(solution)/shard_map/ppermute | solution.py:417
  17.1 6.2 %copy-start = (f32[2,256,512]{2,1,0:T(8,128)S(1)}, f32[2,256,512]{2,1,0:T(8,128)}, u32[]{:S(2)}) copy-start(f32[2,256,512]{2,1,0:T(8,128)} %strip_ref.3) | copy-start | bytes 3145732
  17.8 11.9 %copy-start.4 = (f32[2,256,256]{2,1,0:T(8,128)}, f32[2,256,256]{2,1,0:T(8,128)S(1)}, u32[]{:S(2)}) copy-start(f32[2,256,256]{2,1,0:T(8,128)S(1)} %get-tuple-element.47.refs_6_.refs_2_) | copy-start | bytes 1572868
  17.8 11.9 %copy-start.6 = (bf16[4,256,256]{2,1,0:T(8,128)(2,1)}, bf16[4,256,256]{2,1,0:T(8,128)(2,1)S(1)}, u32[]{:S(2)}) copy-start(bf16[4,256,256]{2,1,0:T(8,128)(2,1)S(1)} %get-tuple-element.48.refs_7_.refs_3_) | copy-start | bytes 1572868
  21.0 2.2 %copy-start.10 = (s32[2,2,2]{2,1,0:T(2,128)}, s32[2,2,2]{2,1,0:T(2,128)S(1)}, u32[]{:S(2)}) copy-start(s32[2,2,2]{2,1,0:T(2,128)S(1)} %collective-permute-done.3) | copy-start | bytes 100
  21.0 1.6 %collective-permute-start.4 = (f32[128,512]{1,0:T(8,128)S(1)}, f32[128,512]{1,0:T(8,128)S(1)}, u32[]{:S(2)}, u32[]{:S(2)}) collective-permute-start(f32[128,512]{1,0:T(8,128)S(1)} %collective-permute-done.refs_0_), channel_id=1, source_target_pairs={{0,1},{1,0},{2,3},{3,2},{4,5},{5,4},{6,7},{7,6},{8,9},{9,8},{10,11... | collective-permute-start | bytes 786440 | tf_op jit(solution)/shard_map/ppermute | solution.py:397
  21.1 2.1 %collective-permute-start.5 = (f32[128,512]{1,0:T(8,128)}, f32[128,512]{1,0:T(8,128)S(1)}, u32[]{:S(2)}, u32[]{:S(2)}) collective-permute-start(f32[128,512]{1,0:T(8,128)} %collective-permute-done.1.refs_2_), channel_id=1, source_target_pairs={{0,1},{1,0},{2,3},{3,2},{4,5},{5,4},{6,7},{7,6},{8,9},{9,8},{10,11... | collective-permute-start | bytes 786440 | tf_op jit(solution)/shard_map/ppermute | solution.py:397
  29.7 4.9 %collective-permute-start.12 = (f32[4,160,256]{2,1,0:T(8,128)S(1)}, f32[4,160,256]{2,1,0:T(8,128)S(1)}, u32[]{:S(2)}, u32[]{:S(2)}) collective-permute-start(f32[4,160,256]{2,1,0:T(8,128)S(1)} %get-tuple-element.58), channel_id=1, source_target_pairs={{0,1},{1,0},{2,3},{3,2},{4,5},{5,4},{6,7},{7,6},{8,9},{9,8},{10,11... | collective-permute-start | bytes 1966088 | tf_op jit(solution)/shard_map/ppermute | solution.py:397
  29.8 16.9 %collective-permute-start.7 = (f32[2,128,256]{2,1,0:T(8,128)}, f32[2,128,256]{2,1,0:T(8,128)S(1)}, u32[]{:S(2)}, u32[]{:S(2)}) collective-permute-start(f32[2,128,256]{2,1,0:T(8,128)} %get-tuple-element.50), channel_id=1, source_target_pairs={{0,2},{2,4},{4,6},{6,8},{8,10},{10,12},{12,14},{14,16},{16,18},{18... | collective-permute-start | bytes 786440 | tf_op jit(solution)/shard_map/ppermute | solution.py:414
  33.2 13.8 %collective-permute-start.8 = (f32[2,128,256]{2,1,0:T(8,128)}, f32[2,128,256]{2,1,0:T(8,128)}, u32[]{:S(2)}, u32[]{:S(2)}) collective-permute-start(f32[2,128,256]{2,1,0:T(8,128)} %get-tuple-element.51), channel_id=1, source_target_pairs={{2,0},{4,2},{6,4},{8,6},{10,8},{12,10},{14,12},{16,14},{18,16},{20... | collective-permute-start | bytes 786440 | tf_op jit(solution)/shard_map/ppermute | solution.py:417
  35.5 12.0 %collective-permute-start.13 = (f32[160,256]{1,0:T(8,128)}, f32[160,256]{1,0:T(8,128)}, u32[]{:S(2)}, u32[]{:S(2)}) collective-permute-start(f32[160,256]{1,0:T(8,128)} %get-tuple-element.79), channel_id=1, source_target_pairs={{0,4},{2,6},{4,0},{6,2},{8,12},{10,14},{12,8},{14,10},{16,20},{18,... | collective-permute-start | bytes 491528 | tf_op jit(solution)/shard_map/ppermute | solution.py:400
  39.3 4.4 %copy-start.11 = (s32[2,2,2]{2,1,0:T(2,128)S(1)}, s32[2,2,2]{2,1,0:T(2,128)}, u32[]{:S(2)}) copy-start(s32[2,2,2]{2,1,0:T(2,128)} %copy-done.10) | copy-start | bytes 100
  39.3 12.4 %collective-permute-start.14 = (f32[160,256]{1,0:T(8,128)}, f32[160,256]{1,0:T(8,128)}, u32[]{:S(2)}, u32[]{:S(2)}) collective-permute-start(f32[160,256]{1,0:T(8,128)} %get-tuple-element.81), channel_id=1, source_target_pairs={{0,8},{2,10},{4,12},{6,14},{8,0},{10,2},{12,4},{14,6},{16,24},{18,... | collective-permute-start | bytes 491528 | tf_op jit(solution)/shard_map/ppermute | solution.py:400
  41.6 10.0 %collective-permute-start.15 = (f32[160,256]{1,0:T(8,128)}, f32[160,256]{1,0:T(8,128)}, u32[]{:S(2)}, u32[]{:S(2)}) collective-permute-start(f32[160,256]{1,0:T(8,128)} %get-tuple-element.80), channel_id=1, source_target_pairs={{0,12},{2,14},{4,8},{6,10},{8,4},{10,6},{12,0},{14,2},{16,28},{18,... | collective-permute-start | bytes 491528 | tf_op jit(solution)/shard_map/ppermute | solution.py:400
  47.0 11.7 %collective-permute-start.9 = (f32[2,256,256]{2,1,0:T(8,128)S(1)}, f32[2,256,256]{2,1,0:T(8,128)S(1)}, u32[]{:S(2)}, u32[]{:S(2)}) collective-permute-start(f32[2,256,256]{2,1,0:T(8,128)S(1)} %get-tuple-element.53.own), channel_id=1, source_target_pairs={{0,1},{1,0},{2,3},{3,2},{4,5},{5,4},{6,7},{7,6},{8,9},{9,8},{10,11... | collective-permute-start | bytes 1572872 | tf_op jit(solution)/shard_map/ppermute | solution.py:397
  47.0 11.7 %collective-permute-start.10 = (f32[2,128,256]{2,1,0:T(8,128)S(1)}, f32[2,128,256]{2,1,0:T(8,128)S(1)}, u32[]{:S(2)}, u32[]{:S(2)}) collective-permute-start(f32[2,128,256]{2,1,0:T(8,128)S(1)} %collective-permute-done.7.b0), channel_id=1, source_target_pairs={{0,1},{1,0},{2,3},{3,2},{4,5},{5,4},{6,7},{7,6},{8,9},{9,8},{10,11... | collective-permute-start | bytes 786440 | tf_op jit(solution)/shard_map/ppermute | solution.py:397
  47.6 11.2 %collective-permute-start.11 = (f32[2,128,256]{2,1,0:T(8,128)}, f32[2,128,256]{2,1,0:T(8,128)S(1)}, u32[]{:S(2)}, u32[]{:S(2)}) collective-permute-start(f32[2,128,256]{2,1,0:T(8,128)} %collective-permute-done.8.a0), channel_id=1, source_target_pairs={{0,1},{1,0},{2,3},{3,2},{4,5},{5,4},{6,7},{7,6},{8,9},{9,8},{10,11... | collective-permute-start | bytes 786440 | tf_op jit(solution)/shard_map/ppermute | solution.py:397
  52.8 12.4 %collective-permute-start.16 = (f32[160,256]{1,0:T(8,128)S(1)}, f32[160,256]{1,0:T(8,128)S(1)}, u32[]{:S(2)}, u32[]{:S(2)}) collective-permute-start(f32[160,256]{1,0:T(8,128)S(1)} %fusion.13), channel_id=1, source_target_pairs={{0,2},{2,0},{4,6},{6,4},{8,10},{10,8},{12,14},{14,12},{16,18},{18,... | collective-permute-start | bytes 491528 | tf_op jit(solution)/shard_map/ppermute | solution.py:400
  56.2 15.0 %collective-permute-start.17 = (f32[160,256]{1,0:T(8,128)S(1)}, f32[160,256]{1,0:T(8,128)S(1)}, u32[]{:S(2)}, u32[]{:S(2)}) collective-permute-start(f32[160,256]{1,0:T(8,128)S(1)} %fusion.13), channel_id=1, source_target_pairs={{0,16},{2,18},{4,20},{6,22},{8,24},{10,26},{12,28},{14,30},{16,0},... | collective-permute-start | bytes 491528 | tf_op jit(solution)/shard_map/ppermute | solution.py:400
  58.7 15.1 %collective-permute-start.18 = (f32[160,256]{1,0:T(8,128)S(1)}, f32[160,256]{1,0:T(8,128)S(1)}, u32[]{:S(2)}, u32[]{:S(2)}) collective-permute-start(f32[160,256]{1,0:T(8,128)S(1)} %fusion.13), channel_id=1, source_target_pairs={{0,18},{2,16},{4,22},{6,20},{8,26},{10,24},{12,30},{14,28},{16,2},... | collective-permute-start | bytes 491528 | tf_op jit(solution)/shard_map/ppermute | solution.py:400
  61.5 12.6 %collective-permute-start.19 = (f32[2,128,256]{2,1,0:T(8,128)S(1)}, f32[2,128,256]{2,1,0:T(8,128)S(1)}, u32[]{:S(2)}, u32[]{:S(2)}) collective-permute-start(f32[2,128,256]{2,1,0:T(8,128)S(1)} %get-tuple-element.59), channel_id=1, source_target_pairs={{0,2},{2,4},{4,6},{6,8},{8,10},{10,12},{12,14},{14,16},{16,18},{18... | collective-permute-start | bytes 786440 | tf_op jit(solution)/shard_map/ppermute | solution.py:414
  74.1 8.7 %collective-permute-start.21 = (f32[160,256]{1,0:T(8,128)S(1)}, f32[160,256]{1,0:T(8,128)S(1)}, u32[]{:S(2)}, u32[]{:S(2)}) collective-permute-start(f32[160,256]{1,0:T(8,128)S(1)} %add_add_fusion.1), channel_id=1, source_target_pairs={{0,4},{2,6},{4,0},{6,2},{8,12},{10,14},{12,8},{14,10},{16,20},{18,... | collective-permute-start | bytes 491528 | tf_op jit(solution)/shard_map/ppermute | solution.py:400
  77.7 5.8 %collective-permute-start.22 = (f32[160,256]{1,0:T(8,128)S(1)}, f32[160,256]{1,0:T(8,128)S(1)}, u32[]{:S(2)}, u32[]{:S(2)}) collective-permute-start(f32[160,256]{1,0:T(8,128)S(1)} %add_add_fusion.1), channel_id=1, source_target_pairs={{0,8},{2,10},{4,12},{6,14},{8,0},{10,2},{12,4},{14,6},{16,24},{18,... | collective-permute-start | bytes 491528 | tf_op jit(solution)/shard_map/ppermute | solution.py:400
  77.7 7.2 %collective-permute-start.23 = (f32[160,256]{1,0:T(8,128)S(1)}, f32[160,256]{1,0:T(8,128)S(1)}, u32[]{:S(2)}, u32[]{:S(2)}) collective-permute-start(f32[160,256]{1,0:T(8,128)S(1)} %add_add_fusion.1), channel_id=1, source_target_pairs={{0,12},{2,14},{4,8},{6,10},{8,4},{10,6},{12,0},{14,2},{16,28},{18,... | collective-permute-start | bytes 491528 | tf_op jit(solution)/shard_map/ppermute | solution.py:400
  79.2 8.7 %collective-permute-start.20 = (f32[2,128,256]{2,1,0:T(8,128)S(1)}, f32[2,128,256]{2,1,0:T(8,128)S(1)}, u32[]{:S(2)}, u32[]{:S(2)}) collective-permute-start(f32[2,128,256]{2,1,0:T(8,128)S(1)} %get-tuple-element.61), channel_id=1, source_target_pairs={{2,0},{4,2},{6,4},{8,6},{10,8},{12,10},{14,12},{16,14},{18,16},{20... | collective-permute-start | bytes 786440 | tf_op jit(solution)/shard_map/ppermute | solution.py:417
  85.0 3.9 %collective-permute-start.24 = (f32[4,160,256]{2,1,0:T(8,128)S(1)}, f32[4,160,256]{2,1,0:T(8,128)S(1)}, u32[]{:S(2)}, u32[]{:S(2)}) collective-permute-start(f32[4,160,256]{2,1,0:T(8,128)S(1)} %pad_maximum_fusion.own_totals), channel_id=1, source_target_pairs={{0,1},{1,0},{2,3},{3,2},{4,5},{5,4},{6,7},{7,6},{8,9},{9,8},{10,11... | collective-permute-start | bytes 1966088 | tf_op jit(solution)/shard_map/ppermute | solution.py:397
  94.6 2.2 %collective-permute-start.25 = (f32[4,160,256]{2,1,0:T(8,128)S(1)}, f32[4,160,256]{2,1,0:T(8,128)S(1)}, u32[]{:S(2)}, u32[]{:S(2)}) collective-permute-start(f32[4,160,256]{2,1,0:T(8,128)S(1)} %get-tuple-element.66), channel_id=1, source_target_pairs={{0,1},{1,0},{2,3},{3,2},{4,5},{5,4},{6,7},{7,6},{8,9},{9,8},{10,11... | collective-permute-start | bytes 1966088 | tf_op jit(solution)/shard_map/ppermute | solution.py:397
  96.8 11.9 %collective-permute-start.26 = (f32[160,256]{1,0:T(8,128)S(1)}, f32[160,256]{1,0:T(8,128)S(1)}, u32[]{:S(2)}, u32[]{:S(2)}) collective-permute-start(f32[160,256]{1,0:T(8,128)S(1)} %get-tuple-element.76), channel_id=1, source_target_pairs={{0,4},{2,6},{4,0},{6,2},{8,12},{10,14},{12,8},{14,10},{16,20},{18,... | collective-permute-start | bytes 491528 | tf_op jit(solution)/shard_map/ppermute | solution.py:400
  100.0 8.7 %collective-permute-start.27 = (f32[160,256]{1,0:T(8,128)S(1)}, f32[160,256]{1,0:T(8,128)S(1)}, u32[]{:S(2)}, u32[]{:S(2)}) collective-permute-start(f32[160,256]{1,0:T(8,128)S(1)} %get-tuple-element.78), channel_id=1, source_target_pairs={{0,8},{2,10},{4,12},{6,14},{8,0},{10,2},{12,4},{14,6},{16,24},{18,... | collective-permute-start | bytes 491528 | tf_op jit(solution)/shard_map/ppermute | solution.py:400
  101.6 7.8 %collective-permute-start.28 = (f32[160,256]{1,0:T(8,128)S(1)}, f32[160,256]{1,0:T(8,128)S(1)}, u32[]{:S(2)}, u32[]{:S(2)}) collective-permute-start(f32[160,256]{1,0:T(8,128)S(1)} %get-tuple-element.77), channel_id=1, source_target_pairs={{0,12},{2,14},{4,8},{6,10},{8,4},{10,6},{12,0},{14,2},{16,28},{18,... | collective-permute-start | bytes 491528 | tf_op jit(solution)/shard_map/ppermute | solution.py:400
  101.7 18.0 %collective-permute-start.35 = (f32[2,128,256]{2,1,0:T(8,128)S(1)}, f32[2,128,256]{2,1,0:T(8,128)S(1)}, u32[]{:S(2)}, u32[]{:S(2)}) collective-permute-start(f32[2,128,256]{2,1,0:T(8,128)S(1)} %get-tuple-element.68), channel_id=1, source_target_pairs={{0,2},{2,4},{4,6},{6,8},{8,10},{10,12},{12,14},{14,16},{16,18},{18... | collective-permute-start | bytes 786440 | tf_op jit(solution)/shard_map/ppermute | solution.py:414
  107.4 14.3 %collective-permute-start.36 = (f32[2,128,256]{2,1,0:T(8,128)S(1)}, f32[2,128,256]{2,1,0:T(8,128)S(1)}, u32[]{:S(2)}, u32[]{:S(2)}) collective-permute-start(f32[2,128,256]{2,1,0:T(8,128)S(1)} %get-tuple-element.69), channel_id=1, source_target_pairs={{2,0},{4,2},{6,4},{8,6},{10,8},{12,10},{14,12},{16,14},{18,16},{20... | collective-permute-start | bytes 786440 | tf_op jit(solution)/shard_map/ppermute | solution.py:417
  109.5 14.7 %collective-permute-start.29 = (f32[160,256]{1,0:T(8,128)S(1)}, f32[160,256]{1,0:T(8,128)S(1)}, u32[]{:S(2)}, u32[]{:S(2)}) collective-permute-start(f32[160,256]{1,0:T(8,128)S(1)} %fusion.6), channel_id=1, source_target_pairs={{0,2},{2,0},{4,6},{6,4},{8,10},{10,8},{12,14},{14,12},{16,18},{18,... | collective-permute-start | bytes 491528 | tf_op jit(solution)/shard_map/ppermute | solution.py:400
  113.2 18.3 %collective-permute-start.30 = (f32[160,256]{1,0:T(8,128)S(1)}, f32[160,256]{1,0:T(8,128)S(1)}, u32[]{:S(2)}, u32[]{:S(2)}) collective-permute-start(f32[160,256]{1,0:T(8,128)S(1)} %fusion.6), channel_id=1, source_target_pairs={{0,16},{2,18},{4,20},{6,22},{8,24},{10,26},{12,28},{14,30},{16,0},... | collective-permute-start | bytes 491528 | tf_op jit(solution)/shard_map/ppermute | solution.py:400
  117.4 14.1 %collective-permute-start.31 = (f32[160,256]{1,0:T(8,128)S(1)}, f32[160,256]{1,0:T(8,128)S(1)}, u32[]{:S(2)}, u32[]{:S(2)}) collective-permute-start(f32[160,256]{1,0:T(8,128)S(1)} %fusion.6), channel_id=1, source_target_pairs={{0,18},{2,16},{4,22},{6,20},{8,26},{10,24},{12,30},{14,28},{16,2},... | collective-permute-start | bytes 491528 | tf_op jit(solution)/shard_map/ppermute | solution.py:400
  121.8 13.4 %collective-permute-start.37 = (f32[2,256,256]{2,1,0:T(8,128)S(1)}, f32[2,256,256]{2,1,0:T(8,128)S(1)}, u32[]{:S(2)}, u32[]{:S(2)}) collective-permute-start(f32[2,256,256]{2,1,0:T(8,128)S(1)} %get-tuple-element.71.own), channel_id=1, source_target_pairs={{0,1},{1,0},{2,3},{3,2},{4,5},{5,4},{6,7},{7,6},{8,9},{9,8},{10,11... | collective-permute-start | bytes 1572872 | tf_op jit(solution)/shard_map/ppermute | solution.py:397
  121.8 10.9 %collective-permute-start.38 = (f32[2,128,256]{2,1,0:T(8,128)S(1)}, f32[2,128,256]{2,1,0:T(8,128)S(1)}, u32[]{:S(2)}, u32[]{:S(2)}) collective-permute-start(f32[2,128,256]{2,1,0:T(8,128)S(1)} %collective-permute-done.35.b0), channel_id=1, source_target_pairs={{0,1},{1,0},{2,3},{3,2},{4,5},{5,4},{6,7},{7,6},{8,9},{9,8},{10,11... | collective-permute-start | bytes 786440 | tf_op jit(solution)/shard_map/ppermute | solution.py:397
  124.2 10.9 %collective-permute-start.39 = (f32[2,128,256]{2,1,0:T(8,128)S(1)}, f32[2,128,256]{2,1,0:T(8,128)S(1)}, u32[]{:S(2)}, u32[]{:S(2)}) collective-permute-start(f32[2,128,256]{2,1,0:T(8,128)S(1)} %collective-permute-done.36.a0), channel_id=1, source_target_pairs={{0,1},{1,0},{2,3},{3,2},{4,5},{5,4},{6,7},{7,6},{8,9},{9,8},{10,11... | collective-permute-start | bytes 786440 | tf_op jit(solution)/shard_map/ppermute | solution.py:397
  131.6 6.7 %collective-permute-start.32 = (f32[160,256]{1,0:T(8,128)S(1)}, f32[160,256]{1,0:T(8,128)S(1)}, u32[]{:S(2)}, u32[]{:S(2)}) collective-permute-start(f32[160,256]{1,0:T(8,128)S(1)} %add_add_fusion), channel_id=1, source_target_pairs={{0,4},{2,6},{4,0},{6,2},{8,12},{10,14},{12,8},{14,10},{16,20},{18,... | collective-permute-start | bytes 491528 | tf_op jit(solution)/shard_map/ppermute | solution.py:400
  132.6 7.1 %collective-permute-start.33 = (f32[160,256]{1,0:T(8,128)S(1)}, f32[160,256]{1,0:T(8,128)S(1)}, u32[]{:S(2)}, u32[]{:S(2)}) collective-permute-start(f32[160,256]{1,0:T(8,128)S(1)} %add_add_fusion), channel_id=1, source_target_pairs={{0,8},{2,10},{4,12},{6,14},{8,0},{10,2},{12,4},{14,6},{16,24},{18,... | collective-permute-start | bytes 491528 | tf_op jit(solution)/shard_map/ppermute | solution.py:400
  132.7 9.2 %collective-permute-start.34 = (f32[160,256]{1,0:T(8,128)S(1)}, f32[160,256]{1,0:T(8,128)S(1)}, u32[]{:S(2)}, u32[]{:S(2)}) collective-permute-start(f32[160,256]{1,0:T(8,128)S(1)} %add_add_fusion), channel_id=1, source_target_pairs={{0,12},{2,14},{4,8},{6,10},{8,4},{10,6},{12,0},{14,2},{16,28},{18,... | collective-permute-start | bytes 491528 | tf_op jit(solution)/shard_map/ppermute | solution.py:400
  142.0 1.4 collective-permute-start.40
  (6 other events, 6.0 us)

commit v7 on v4

--- a/solution.py
+++ b/solution.py
@@ -11,7 +11,7 @@
 
 F32 = jnp.float32
 BF16 = jnp.bfloat16
-VMEM_BYTES = 16 * 1024 * 1024
+VMEM_BYTES = 12 * 1024 * 1024
 GROUP = 4
 NEAR_STEP = 2
 FAR_STEPS = (1, 8, 9)
@@ -425,11 +425,8 @@
     tile, slot = lax.axis_index("tile"), lax.axis_index("mode")
     index = jnp.stack([tile, slot]).astype(jnp.int32)
     here = jnp.concatenate([positions.ravel()] * 3 + [index])
-    first = slot == 0
-    edges = [
-        from_below(jnp.where(first, object_field[0, strip - half :], object_field[1, strip - half :])),
-        from_above(jnp.where(first, object_field[0, :half], object_field[1, :half])),
-    ]
+    one_part = lax.dynamic_index_in_dim(object_field, slot, 0, keepdims=False)
+    edges = [from_below(one_part[strip - half :]), from_above(one_part[:half])]
     below, above = from_below(positions), from_above(positions)
     other = swap(probe[0])
     columns, own, observed, table = call(
@@ -488,7 +485,7 @@
         piece = exchange(piece)
         if not last:
             edges = [from_below(edges[1]), from_above(edges[0])]
-            piece, *edges = lax.optimization_barrier((piece, *edges))
+            piece, edges[0] = lax.optimization_barrier((piece, edges[0]))
         totals = gather(piece, NEAR_STEP)
         if last:
             totals, object_field = lax.optimization_barrier((totals, object_field))

time: 146 us -> 146 us (level); the launches traced: 144 us -> 145 us
  starting transfers between devices: 60 us -> 67.6 us
  waiting for transfers between devices: 48.4 us -> 41.8 us
  local copies, waits for them, and re-layouts: 6.32 us -> 8.99 us
  other arithmetic: 4.44 us -> 2.36 us
    ppermute x5, waiting for transfers between devices: 8.24 us -> 0.81 us  [from_below(): return lax.ppermute(value, 'tile', up)]
    ppermute x18, starting transfers between devices: 30.2 us -> 36.5 us  [across(): return lax.ppermute(value, 'tile', [(i, i ^ k) for i in range(tiles)])]
    select_n x1 -> x0, other arithmetic: 2.09 us -> none  [shards_by_position(): jnp.where(first, object_field[0, :half], object_field[1, :half])]
    ppermute x18, waiting for transfers between devices: 28.6 us -> 30.4 us  [across(): return lax.ppermute(value, 'tile', [(i, i ^ k) for i in range(tiles)])]
    ppermute x5, starting transfers between devices: 20.9 us -> 22.4 us  [from_below(): return lax.ppermute(value, 'tile', up)]
    unnamed x30, local copies, waits for them, and re-layouts: 4.09 us -> 5.62 us
  transfers between devices with their start and end apart: 41 -> 41, of which waited for: 23 -> 21; matrix products, arithmetic and copies ran while one was open for 3% -> 3% of each run, Pallas kernels for 8% -> 8%
where the time goes in v7:
time: 146 us; the launch traced here: 145 us
  starting transfers between devices  67.6 us (46%)
  waiting for transfers between devices  41.8 us (29%)
  Pallas kernels  23.5 us (16%)
  local copies, waits for them, and re-layouts  8.99 us (6%)
  other arithmetic  2.36 us (2%)
    ppermute x18, starting transfers between devices, across(): return lax.ppermute(value, 'tile', [(i, i ^ k) for i in range(tiles)])  36.5 us
    ppermute x18, waiting for transfers between devices, across(): return lax.ppermute(value, 'tile', [(i, i ^ k) for i in range(tiles)])  30.4 us
    pallas_call x10, Pallas kernels, call(): pl.pallas_call(kernel, out_shape=shapes, in_specs=[smem] + [vmem] * (len(...  23.5 us
    ppermute x5, starting transfers between devices, from_below(): return lax.ppermute(value, 'tile', up)  22.4 us
    ppermute x5, starting transfers between devices, from_above(): return lax.ppermute(value, 'tile', down)  6.63 us
    ppermute x5, waiting for transfers between devices, from_above(): return lax.ppermute(value, 'tile', down)  6.45 us
    unnamed x30, local copies, waits for them, and re-layouts  5.62 us
    ppermute x13, waiting for transfers between devices, swap(): return lax.ppermute(value, 'mode', [(0, 1), (1, 0)])  4.14 us
  transfers between devices with their start and end apart: 41, of which 21 were waited for; matrix products, arithmetic and copies ran while one was open for 3% of the time, Pallas kernels for 8%

profile of v7, /device:TPU:0, one launch (start us, length us, event | category | flops | bytes accessed | tf_op | source)
XLA Modules:
  0.0 145.2 jit_solution(9190599167393065610)
XLA Ops:
  0.6 1.2 dynamic-slice_bitcast_fusion
  1.8 4.9 %collective-permute-start = (f32[128,512]{1,0:T(8,128)S(1)}, f32[128,512]{1,0:T(8,128)S(1)}, u32[]{:S(2)}, u32[]{:S(2)}) collective-permute-start(f32[128,512]{1,0:T(8,128)S(1)} %get-tuple-element.87), channel_id=1, source_target_pairs={{0,2},{2,4},{4,6},{6,8},{8,10},{10,12},{12,14},{14,16},{16,18},{18... | collective-permute-start | bytes 786440 | tf_op jit(solution)/shard_map/ppermute | solution.py:417
  6.7 1.3 collective-permute-start.1
  8.1 4.5 %collective-permute-start.2 = (s32[2,2,2]{2,1,0:T(2,128)S(1)}, s32[2,2,2]{2,1,0:T(2,128)S(1)}, u32[]{:S(2)}, u32[]{:S(2)}) collective-permute-start(s32[2,2,2]{2,1,0:T(2,128)S(1)} %copy-done.11), channel_id=1, source_target_pairs={{0,2},{2,4},{4,6},{6,8},{8,10},{10,12},{12,14},{14,16},{16,18},{18... | collective-permute-start | bytes 104 | tf_op jit(solution)/shard_map/ppermute | solution.py:417
  12.6 1.3 collective-permute-start.3
  14.1 1.2 copy-done.1
  16.4 1.0 copy-done.3
  18.5 1.4 collective-permute-done.3
  22.8 5.7 %field.2 = (f32[2,256,256]{2,1,0:T(8,128)S(1)}, f32[2,128,256]{2,1,0:T(8,128)}, f32[2,128,256]{2,1,0:T(8,128)}, f32[4,160,256]{2,1,0:T(8,128)S(1)}, f32[4,160,256]{2,1,0:T(8,128)S(1)}) custom-call(s32[26]{0:T(128)S(1)} %concatenate.8.info, f32[2,256,256]{2,1,0:T(8,128)S(1)} %get-tuple-element.47.strip_ref, f32[128,512]{1,0:T(8,128)S(1)} %collective-permute-done.refs_0_, ...), custom_call_target="tpu_custom_call" | custom-call | flops 3221225472 | bytes 6029416 | tf_op jit(solution)/shard_map/field/pallas_call | solution.py:374
  28.7 3.6 %collective-permute-start.7 = (f32[2,128,256]{2,1,0:T(8,128)}, f32[2,128,256]{2,1,0:T(8,128)S(1)}, u32[]{:S(2)}, u32[]{:S(2)}) collective-permute-start(f32[2,128,256]{2,1,0:T(8,128)} %get-tuple-element.54), channel_id=1, source_target_pairs={{0,2},{2,4},{4,6},{6,8},{8,10},{10,12},{12,14},{14,16},{16,18},{18... | collective-permute-start | bytes 786440 | tf_op jit(solution)/shard_map/ppermute | solution.py:417
  32.3 1.3 collective-permute-start.8
  34.6 4.9 %collective-permute-start.13 = (f32[160,256]{1,0:T(8,128)}, f32[160,256]{1,0:T(8,128)}, u32[]{:S(2)}, u32[]{:S(2)}) collective-permute-start(f32[160,256]{1,0:T(8,128)} %get-tuple-element.83), channel_id=1, source_target_pairs={{0,4},{2,6},{4,0},{6,2},{8,12},{10,14},{12,8},{14,10},{16,20},{18,... | collective-permute-start | bytes 491528 | tf_op jit(solution)/shard_map/ppermute | solution.py:403
  39.6 2.8 %collective-permute-start.14 = (f32[160,256]{1,0:T(8,128)}, f32[160,256]{1,0:T(8,128)}, u32[]{:S(2)}, u32[]{:S(2)}) collective-permute-start(f32[160,256]{1,0:T(8,128)} %get-tuple-element.85), channel_id=1, source_target_pairs={{0,8},{2,10},{4,12},{6,14},{8,0},{10,2},{12,4},{14,6},{16,24},{18,... | collective-permute-start | bytes 491528 | tf_op jit(solution)/shard_map/ppermute | solution.py:403
  42.3 1.5 %collective-permute-start.15 = (f32[160,256]{1,0:T(8,128)}, f32[160,256]{1,0:T(8,128)}, u32[]{:S(2)}, u32[]{:S(2)}) collective-permute-start(f32[160,256]{1,0:T(8,128)} %get-tuple-element.84), channel_id=1, source_target_pairs={{0,12},{2,14},{4,8},{6,10},{8,4},{10,6},{12,0},{14,2},{16,28},{18,... | collective-permute-start | bytes 491528 | tf_op jit(solution)/shard_map/ppermute | solution.py:403
  45.8 1.7 %illumination.2.illum = f32[256,512]{1,0:T(8,128)S(1)} custom-call(s32[26]{0:T(128)S(1)} %concatenate.9.info, f32[2,256,256]{2,1,0:T(8,128)S(1)} %get-tuple-element.50.refs_4_.own.refs_0_, f32[2,256,256]{2,1,0:T(8,128)S(1)} %collective-permute-done.6.refs_5_.other.refs_1_), custom_call_target="tpu_custom_call" | custom-call | bytes 1572968 | tf_op jit(solution)/shard_map/illumination/pallas_call | solution.py:374
  48.2 4.1 %collective-permute-done.14 = f32[160,256]{1,0:T(8,128)} collective-permute-done((f32[160,256]{1,0:T(8,128)}, f32[160,256]{1,0:T(8,128)}, u32[]{:S(2)}, u32[]{:S(2)}) %collective-permute-start.14) | collective-permute-done | bytes 163872 | tf_op jit(solution)/shard_map/ppermute | solution.py:403
  52.3 1.2 fusion.13
  53.5 3.1 %collective-permute-start.16 = (f32[160,256]{1,0:T(8,128)S(1)}, f32[160,256]{1,0:T(8,128)S(1)}, u32[]{:S(2)}, u32[]{:S(2)}) collective-permute-start(f32[160,256]{1,0:T(8,128)S(1)} %fusion.13), channel_id=1, source_target_pairs={{0,2},{2,0},{4,6},{6,4},{8,10},{10,8},{12,14},{14,12},{16,18},{18,... | collective-permute-start | bytes 491528 | tf_op jit(solution)/shard_map/ppermute | solution.py:403
  56.6 2.6 %collective-permute-start.17 = (f32[160,256]{1,0:T(8,128)S(1)}, f32[160,256]{1,0:T(8,128)S(1)}, u32[]{:S(2)}, u32[]{:S(2)}) collective-permute-start(f32[160,256]{1,0:T(8,128)S(1)} %fusion.13), channel_id=1, source_target_pairs={{0,16},{2,18},{4,20},{6,22},{8,24},{10,26},{12,28},{14,30},{16,0},... | collective-permute-start | bytes 491528 | tf_op jit(solution)/shard_map/ppermute | solution.py:403
  59.2 2.8 %update.2 = (f32[2,256,512]{2,1,0:T(8,128)S(1)}, f32[2,128,256]{2,1,0:T(8,128)S(1)}, f32[2,128,256]{2,1,0:T(8,128)S(1)}) custom-call(s32[26]{0:T(128)S(1)} %concatenate.9.info, f32[2,256,512]{2,1,0:T(8,128)S(1)} %copy-done, f32[256,512]{1,0:T(8,128)S(1)} %illumination.2.illum, f32[2,256,256]{2,1,0:T(8,128)S(1)} %get-tuple-element.57.own, ...), custom_call_target="tpu_custom_call" | custom-call | bytes 5242984 | tf_op jit(solution)/shard_map/update/pallas_call | solution.py:374
  62.0 3.7 %collective-permute-start.19 = (f32[2,128,256]{2,1,0:T(8,128)S(1)}, f32[2,128,256]{2,1,0:T(8,128)S(1)}, u32[]{:S(2)}, u32[]{:S(2)}) collective-permute-start(f32[2,128,256]{2,1,0:T(8,128)S(1)} %get-tuple-element.63), channel_id=1, source_target_pairs={{0,2},{2,4},{4,6},{6,8},{8,10},{10,12},{12,14},{14,16},{16,18},{18... | collective-permute-start | bytes 786440 | tf_op jit(solution)/shard_map/ppermute | solution.py:417
  65.7 5.8 %collective-permute-done.17 = f32[160,256]{1,0:T(8,128)S(1)} collective-permute-done((f32[160,256]{1,0:T(8,128)S(1)}, f32[160,256]{1,0:T(8,128)S(1)}, u32[]{:S(2)}, u32[]{:S(2)}) %collective-permute-start.17) | collective-permute-done | bytes 163872 | tf_op jit(solution)/shard_map/ppermute | solution.py:403
  71.5 2.7 %collective-permute-done.18 = f32[160,256]{1,0:T(8,128)S(1)} collective-permute-done((f32[160,256]{1,0:T(8,128)S(1)}, f32[160,256]{1,0:T(8,128)S(1)}, u32[]{:S(2)}, u32[]{:S(2)}) %collective-permute-start.18) | collective-permute-done | bytes 163872 | tf_op jit(solution)/shard_map/ppermute | solution.py:403
  74.6 3.6 %collective-permute-start.21 = (f32[160,256]{1,0:T(8,128)S(1)}, f32[160,256]{1,0:T(8,128)S(1)}, u32[]{:S(2)}, u32[]{:S(2)}) collective-permute-start(f32[160,256]{1,0:T(8,128)S(1)} %add_add_fusion.1), channel_id=1, source_target_pairs={{0,4},{2,6},{4,0},{6,2},{8,12},{10,14},{12,8},{14,10},{16,20},{18,... | collective-permute-start | bytes 491528 | tf_op jit(solution)/shard_map/ppermute | solution.py:403
  78.2 1.5 %collective-permute-start.23 = (f32[160,256]{1,0:T(8,128)S(1)}, f32[160,256]{1,0:T(8,128)S(1)}, u32[]{:S(2)}, u32[]{:S(2)}) collective-permute-start(f32[160,256]{1,0:T(8,128)S(1)} %add_add_fusion.1), channel_id=1, source_target_pairs={{0,12},{2,14},{4,8},{6,10},{8,4},{10,6},{12,0},{14,2},{16,28},{18,... | collective-permute-start | bytes 491528 | tf_op jit(solution)/shard_map/ppermute | solution.py:403
  79.7 1.5 %collective-permute-start.20 = (f32[2,128,256]{2,1,0:T(8,128)S(1)}, f32[2,128,256]{2,1,0:T(8,128)S(1)}, u32[]{:S(2)}, u32[]{:S(2)}) collective-permute-start(f32[2,128,256]{2,1,0:T(8,128)S(1)} %get-tuple-element.65), channel_id=1, source_target_pairs={{2,0},{4,2},{6,4},{8,6},{10,8},{12,10},{14,12},{16,14},{18,16},{20... | collective-permute-start | bytes 786440 | tf_op jit(solution)/shard_map/ppermute | solution.py:420
  81.1 2.1 %collective-permute-done.21 = f32[160,256]{1,0:T(8,128)S(1)} collective-permute-done((f32[160,256]{1,0:T(8,128)S(1)}, f32[160,256]{1,0:T(8,128)S(1)}, u32[]{:S(2)}, u32[]{:S(2)}) %collective-permute-start.21) | collective-permute-done | bytes 163872 | tf_op jit(solution)/shard_map/ppermute | solution.py:403
  83.7 1.5 %collective-permute-done.23 = f32[160,256]{1,0:T(8,128)S(1)} collective-permute-done((f32[160,256]{1,0:T(8,128)S(1)}, f32[160,256]{1,0:T(8,128)S(1)}, u32[]{:S(2)}, u32[]{:S(2)}) %collective-permute-start.23) | collective-permute-done | bytes 163872 | tf_op jit(solution)/shard_map/ppermute | solution.py:403
  85.4 3.0 %collective-permute-done.20.above = f32[2,128,256]{2,1,0:T(8,128)S(1)} collective-permute-done((f32[2,128,256]{2,1,0:T(8,128)S(1)}, f32[2,128,256]{2,1,0:T(8,128)S(1)}, u32[]{:S(2)}, u32[]{:S(2)}) %collective-permute-start.20) | collective-permute-done | bytes 262176 | tf_op jit(solution)/shard_map/ppermute | solution.py:420
  90.5 4.5 %field.3 = (f32[2,256,256]{2,1,0:T(8,128)S(1)}, f32[2,128,256]{2,1,0:T(8,128)S(1)}, f32[2,128,256]{2,1,0:T(8,128)S(1)}, f32[4,160,256]{2,1,0:T(8,128)S(1)}, f32[4,160,256]{2,1,0:T(8,128)S(1)}) custom-call(s32[26]{0:T(128)S(1)} %concatenate.8.info, f32[2,256,256]{2,1,0:T(8,128)S(1)} %patch.1.strip_ref, f32[2,256,256]{2,1,0:T(8,128)S(1)} %get-tuple-element.67.refs_0_.own, ...), custom_call_target="tpu_custom_call" | custom-call | flops 3221225472 | bytes 4980840 | tf_op jit(solution)/shard_map/field/pallas_call | solution.py:374
  95.1 2.1 %collective-permute-done.25 = f32[4,160,256]{2,1,0:T(8,128)S(1)} collective-permute-done((f32[4,160,256]{2,1,0:T(8,128)S(1)}, f32[4,160,256]{2,1,0:T(8,128)S(1)}, u32[]{:S(2)}, u32[]{:S(2)}) %collective-permute-start.25) | collective-permute-done | bytes 655392 | tf_op jit(solution)/shard_map/ppermute | solution.py:400
  97.2 3.2 %collective-permute-start.26 = (f32[160,256]{1,0:T(8,128)S(1)}, f32[160,256]{1,0:T(8,128)S(1)}, u32[]{:S(2)}, u32[]{:S(2)}) collective-permute-start(f32[160,256]{1,0:T(8,128)S(1)} %get-tuple-element.80), channel_id=1, source_target_pairs={{0,4},{2,6},{4,0},{6,2},{8,12},{10,14},{12,8},{14,10},{16,20},{18,... | collective-permute-start | bytes 491528 | tf_op jit(solution)/shard_map/ppermute | solution.py:403
  100.5 1.6 %collective-permute-start.27 = (f32[160,256]{1,0:T(8,128)S(1)}, f32[160,256]{1,0:T(8,128)S(1)}, u32[]{:S(2)}, u32[]{:S(2)}) collective-permute-start(f32[160,256]{1,0:T(8,128)S(1)} %get-tuple-element.82), channel_id=1, source_target_pairs={{0,8},{2,10},{4,12},{6,14},{8,0},{10,2},{12,4},{14,6},{16,24},{18,... | collective-permute-start | bytes 491528 | tf_op jit(solution)/shard_map/ppermute | solution.py:403
  102.2 5.7 %collective-permute-start.35 = (f32[2,128,256]{2,1,0:T(8,128)S(1)}, f32[2,128,256]{2,1,0:T(8,128)S(1)}, u32[]{:S(2)}, u32[]{:S(2)}) collective-permute-start(f32[2,128,256]{2,1,0:T(8,128)S(1)} %get-tuple-element.72), channel_id=1, source_target_pairs={{0,2},{2,4},{4,6},{6,8},{8,10},{10,12},{12,14},{14,16},{16,18},{18... | collective-permute-start | bytes 786440 | tf_op jit(solution)/shard_map/ppermute | solution.py:417
  107.8 1.3 collective-permute-start.36
  109.9 3.6 %collective-permute-start.29 = (f32[160,256]{1,0:T(8,128)S(1)}, f32[160,256]{1,0:T(8,128)S(1)}, u32[]{:S(2)}, u32[]{:S(2)}) collective-permute-start(f32[160,256]{1,0:T(8,128)S(1)} %fusion.6), channel_id=1, source_target_pairs={{0,2},{2,0},{4,6},{6,4},{8,10},{10,8},{12,14},{14,12},{16,18},{18,... | collective-permute-start | bytes 491528 | tf_op jit(solution)/shard_map/ppermute | solution.py:403
  113.6 4.3 %collective-permute-start.30 = (f32[160,256]{1,0:T(8,128)S(1)}, f32[160,256]{1,0:T(8,128)S(1)}, u32[]{:S(2)}, u32[]{:S(2)}) collective-permute-start(f32[160,256]{1,0:T(8,128)S(1)} %fusion.6), channel_id=1, source_target_pairs={{0,16},{2,18},{4,20},{6,22},{8,24},{10,26},{12,28},{14,30},{16,0},... | collective-permute-start | bytes 491528 | tf_op jit(solution)/shard_map/ppermute | solution.py:403
  118.0 1.7 %illumination.3.illum = f32[256,512]{1,0:T(8,128)S(1)} custom-call(s32[26]{0:T(128)S(1)} %concatenate.9.info, f32[2,256,256]{2,1,0:T(8,128)S(1)} %get-tuple-element.67.refs_0_.own, f32[2,256,256]{2,1,0:T(8,128)S(1)} %get-tuple-element.68.refs_1_.other), custom_call_target="tpu_custom_call" | custom-call | bytes 1572968 | tf_op jit(solution)/shard_map/illumination/pallas_call | solution.py:374
  120.2 2.0 %collective-permute-done.36.a0 = f32[2,128,256]{2,1,0:T(8,128)S(1)} collective-permute-done((f32[2,128,256]{2,1,0:T(8,128)S(1)}, f32[2,128,256]{2,1,0:T(8,128)S(1)}, u32[]{:S(2)}, u32[]{:S(2)}) %collective-permute-start.36) | collective-permute-done | bytes 262176 | tf_op jit(solution)/shard_map/ppermute | solution.py:420
  122.7 1.9 %collective-permute-done.29 = f32[160,256]{1,0:T(8,128)S(1)} collective-permute-done((f32[160,256]{1,0:T(8,128)S(1)}, f32[160,256]{1,0:T(8,128)S(1)}, u32[]{:S(2)}, u32[]{:S(2)}) %collective-permute-start.29) | collective-permute-done | bytes 163872 | tf_op jit(solution)/shard_map/ppermute | solution.py:403
  124.6 7.3 %collective-permute-done.30 = f32[160,256]{1,0:T(8,128)S(1)} collective-permute-done((f32[160,256]{1,0:T(8,128)S(1)}, f32[160,256]{1,0:T(8,128)S(1)}, u32[]{:S(2)}, u32[]{:S(2)}) %collective-permute-start.30) | collective-permute-done | bytes 163872 | tf_op jit(solution)/shard_map/ppermute | solution.py:403
  132.0 1.1 collective-permute-start.32
  133.1 2.4 %collective-permute-start.34 = (f32[160,256]{1,0:T(8,128)S(1)}, f32[160,256]{1,0:T(8,128)S(1)}, u32[]{:S(2)}, u32[]{:S(2)}) collective-permute-start(f32[160,256]{1,0:T(8,128)S(1)} %add_add_fusion), channel_id=1, source_target_pairs={{0,12},{2,14},{4,8},{6,10},{8,4},{10,6},{12,0},{14,2},{16,28},{18,... | collective-permute-start | bytes 491528 | tf_op jit(solution)/shard_map/ppermute | solution.py:403
  135.5 3.1 %update.3 = f32[2,256,512]{2,1,0:T(8,128)} custom-call(s32[26]{0:T(128)S(1)} %concatenate.9.info, f32[2,256,512]{2,1,0:T(8,128)S(1)} %get-tuple-element.60.strip_ref, f32[256,512]{1,0:T(8,128)S(1)} %illumination.3.illum, f32[2,256,256]{2,1,0:T(8,128)S(1)} %get-tuple-element.75.own, f32[2,256,256]{2,1,0:T(8,128)S(1)} %collective-permute-done.37.other, ...), custom_call_target="tpu_custom_call" | custom-call | bytes 4718696 | tf_op jit(solution)/shard_map/update/pallas_call | solution.py:374
  138.6 1.5 %collective-permute-done.33 = f32[160,256]{1,0:T(8,128)S(1)} collective-permute-done((f32[160,256]{1,0:T(8,128)S(1)}, f32[160,256]{1,0:T(8,128)S(1)}, u32[]{:S(2)}, u32[]{:S(2)}) %collective-permute-start.33) | collective-permute-done | bytes 163872 | tf_op jit(solution)/shard_map/ppermute | solution.py:403
  140.1 2.2 %collective-permute-done.34 = f32[160,256]{1,0:T(8,128)S(1)} collective-permute-done((f32[160,256]{1,0:T(8,128)S(1)}, f32[160,256]{1,0:T(8,128)S(1)}, u32[]{:S(2)}, u32[]{:S(2)}) %collective-permute-start.34) | collective-permute-done | bytes 163872 | tf_op jit(solution)/shard_map/ppermute | solution.py:403
  142.5 1.3 collective-permute-done.40.other_totals
  143.8 1.4 probe.3
  (89 shorter events, 14.6 us)
Async XLA Ops:
  0.6 13.5 %copy-start = (f32[2,256,512]{2,1,0:T(8,128)S(1)}, f32[2,256,512]{2,1,0:T(8,128)}, u32[]{:S(2)}) copy-start(f32[2,256,512]{2,1,0:T(8,128)} %strip_ref.3) | copy-start | bytes 3145732
  1.8 6.3 %copy-start.11 = (s32[2,2,2]{2,1,0:T(2,128)S(1)}, s32[2,2,2]{2,1,0:T(2,128)}, u32[]{:S(2)}) copy-start(s32[2,2,2]{2,1,0:T(2,128)} %param.7) | copy-start | bytes 100
  1.8 18.1 %collective-permute-start = (f32[128,512]{1,0:T(8,128)S(1)}, f32[128,512]{1,0:T(8,128)S(1)}, u32[]{:S(2)}, u32[]{:S(2)}) collective-permute-start(f32[128,512]{1,0:T(8,128)S(1)} %get-tuple-element.87), channel_id=1, source_target_pairs={{0,2},{2,4},{4,6},{6,8},{8,10},{10,12},{12,14},{14,16},{16,18},{18... | collective-permute-start | bytes 786440 | tf_op jit(solution)/shard_map/ppermute | solution.py:417
  6.7 13.2 %collective-permute-start.1 = (f32[128,512]{1,0:T(8,128)S(1)}, f32[128,512]{1,0:T(8,128)S(1)}, u32[]{:S(2)}, u32[]{:S(2)}) collective-permute-start(f32[128,512]{1,0:T(8,128)S(1)} %get-tuple-element.86), channel_id=1, source_target_pairs={{2,0},{4,2},{6,4},{8,6},{10,8},{12,10},{14,12},{16,14},{18,16},{20... | collective-permute-start | bytes 786440 | tf_op jit(solution)/shard_map/ppermute | solution.py:420
  8.0 13.9 %collective-permute-start.6 = (f32[2,256,256]{2,1,0:T(8,128)}, f32[2,256,256]{2,1,0:T(8,128)S(1)}, u32[]{:S(2)}, u32[]{:S(2)}) collective-permute-start(f32[2,256,256]{2,1,0:T(8,128)} %bitcast.44), channel_id=1, source_target_pairs={{0,1},{1,0},{2,3},{3,2},{4,5},{5,4},{6,7},{7,6},{8,9},{9,8},{10,11... | collective-permute-start | bytes 1572872 | tf_op jit(solution)/shard_map/ppermute | solution.py:400
  8.1 10.4 %collective-permute-start.2 = (s32[2,2,2]{2,1,0:T(2,128)S(1)}, s32[2,2,2]{2,1,0:T(2,128)S(1)}, u32[]{:S(2)}, u32[]{:S(2)}) collective-permute-start(s32[2,2,2]{2,1,0:T(2,128)S(1)} %copy-done.11), channel_id=1, source_target_pairs={{0,2},{2,4},{4,6},{6,8},{8,10},{10,12},{12,14},{14,16},{16,18},{18... | collective-permute-start | bytes 104 | tf_op jit(solution)/shard_map/ppermute | solution.py:417
  12.6 7.2 %collective-permute-start.3 = (s32[2,2,2]{2,1,0:T(2,128)S(1)}, s32[2,2,2]{2,1,0:T(2,128)S(1)}, u32[]{:S(2)}, u32[]{:S(2)}) collective-permute-start(s32[2,2,2]{2,1,0:T(2,128)S(1)} %copy-done.11), channel_id=1, source_target_pairs={{2,0},{4,2},{6,4},{8,6},{10,8},{12,10},{14,12},{16,14},{18,16},{20... | collective-permute-start | bytes 104 | tf_op jit(solution)/shard_map/ppermute | solution.py:420
  14.1 1.2 copy-start.1
  18.5 10.1 %copy-start.4 = (f32[2,256,256]{2,1,0:T(8,128)}, f32[2,256,256]{2,1,0:T(8,128)S(1)}, u32[]{:S(2)}) copy-start(f32[2,256,256]{2,1,0:T(8,128)S(1)} %get-tuple-element.51.refs_6_.refs_2_) | copy-start | bytes 1572868
  18.5 10.1 %copy-start.6 = (bf16[4,256,256]{2,1,0:T(8,128)(2,1)}, bf16[4,256,256]{2,1,0:T(8,128)(2,1)S(1)}, u32[]{:S(2)}) copy-start(bf16[4,256,256]{2,1,0:T(8,128)(2,1)S(1)} %get-tuple-element.52.refs_7_.refs_3_) | copy-start | bytes 1572868
  19.9 2.0 %copy-start.12 = (s32[2,2,2]{2,1,0:T(2,128)}, s32[2,2,2]{2,1,0:T(2,128)S(1)}, u32[]{:S(2)}) copy-start(s32[2,2,2]{2,1,0:T(2,128)S(1)} %collective-permute-done.3) | copy-start | bytes 100
  19.9 1.6 %collective-permute-start.4 = (f32[128,512]{1,0:T(8,128)S(1)}, f32[128,512]{1,0:T(8,128)S(1)}, u32[]{:S(2)}, u32[]{:S(2)}) collective-permute-start(f32[128,512]{1,0:T(8,128)S(1)} %collective-permute-done.refs_0_), channel_id=1, source_target_pairs={{0,1},{1,0},{2,3},{3,2},{4,5},{5,4},{6,7},{7,6},{8,9},{9,8},{10,11... | collective-permute-start | bytes 786440 | tf_op jit(solution)/shard_map/ppermute | solution.py:400
  20.0 1.9 %collective-permute-start.5 = (f32[128,512]{1,0:T(8,128)S(1)}, f32[128,512]{1,0:T(8,128)S(1)}, u32[]{:S(2)}, u32[]{:S(2)}) collective-permute-start(f32[128,512]{1,0:T(8,128)S(1)} %collective-permute-done.1.refs_2_), channel_id=1, source_target_pairs={{0,1},{1,0},{2,3},{3,2},{4,5},{5,4},{6,7},{7,6},{8,9},{9,8},{10,11... | collective-permute-start | bytes 786440 | tf_op jit(solution)/shard_map/ppermute | solution.py:400
  28.5 5.1 %collective-permute-start.12 = (f32[4,160,256]{2,1,0:T(8,128)S(1)}, f32[4,160,256]{2,1,0:T(8,128)S(1)}, u32[]{:S(2)}, u32[]{:S(2)}) collective-permute-start(f32[4,160,256]{2,1,0:T(8,128)S(1)} %get-tuple-element.62), channel_id=1, source_target_pairs={{0,1},{1,0},{2,3},{3,2},{4,5},{5,4},{6,7},{7,6},{8,9},{9,8},{10,11... | collective-permute-start | bytes 1966088 | tf_op jit(solution)/shard_map/ppermute | solution.py:400
  28.7 18.8 %collective-permute-start.7 = (f32[2,128,256]{2,1,0:T(8,128)}, f32[2,128,256]{2,1,0:T(8,128)S(1)}, u32[]{:S(2)}, u32[]{:S(2)}) collective-permute-start(f32[2,128,256]{2,1,0:T(8,128)} %get-tuple-element.54), channel_id=1, source_target_pairs={{0,2},{2,4},{4,6},{6,8},{8,10},{10,12},{12,14},{14,16},{16,18},{18... | collective-permute-start | bytes 786440 | tf_op jit(solution)/shard_map/ppermute | solution.py:417
  32.3 15.3 %collective-permute-start.8 = (f32[2,128,256]{2,1,0:T(8,128)}, f32[2,128,256]{2,1,0:T(8,128)}, u32[]{:S(2)}, u32[]{:S(2)}) collective-permute-start(f32[2,128,256]{2,1,0:T(8,128)} %get-tuple-element.55), channel_id=1, source_target_pairs={{2,0},{4,2},{6,4},{8,6},{10,8},{12,10},{14,12},{16,14},{18,16},{20... | collective-permute-start | bytes 786440 | tf_op jit(solution)/shard_map/ppermute | solution.py:420
  34.6 13.5 %collective-permute-start.13 = (f32[160,256]{1,0:T(8,128)}, f32[160,256]{1,0:T(8,128)}, u32[]{:S(2)}, u32[]{:S(2)}) collective-permute-start(f32[160,256]{1,0:T(8,128)} %get-tuple-element.83), channel_id=1, source_target_pairs={{0,4},{2,6},{4,0},{6,2},{8,12},{10,14},{12,8},{14,10},{16,20},{18,... | collective-permute-start | bytes 491528 | tf_op jit(solution)/shard_map/ppermute | solution.py:403
  39.6 4.9 %copy-start.13 = (s32[2,2,2]{2,1,0:T(2,128)S(1)}, s32[2,2,2]{2,1,0:T(2,128)}, u32[]{:S(2)}) copy-start(s32[2,2,2]{2,1,0:T(2,128)} %copy-done.12) | copy-start | bytes 100
  39.6 12.7 %collective-permute-start.14 = (f32[160,256]{1,0:T(8,128)}, f32[160,256]{1,0:T(8,128)}, u32[]{:S(2)}, u32[]{:S(2)}) collective-permute-start(f32[160,256]{1,0:T(8,128)} %get-tuple-element.85), channel_id=1, source_target_pairs={{0,8},{2,10},{4,12},{6,14},{8,0},{10,2},{12,4},{14,6},{16,24},{18,... | collective-permute-start | bytes 491528 | tf_op jit(solution)/shard_map/ppermute | solution.py:403
  42.3 10.0 %collective-permute-start.15 = (f32[160,256]{1,0:T(8,128)}, f32[160,256]{1,0:T(8,128)}, u32[]{:S(2)}, u32[]{:S(2)}) collective-permute-start(f32[160,256]{1,0:T(8,128)} %get-tuple-element.84), channel_id=1, source_target_pairs={{0,12},{2,14},{4,8},{6,10},{8,4},{10,6},{12,0},{14,2},{16,28},{18,... | collective-permute-start | bytes 491528 | tf_op jit(solution)/shard_map/ppermute | solution.py:403
  47.6 11.6 %collective-permute-start.9 = (f32[2,256,256]{2,1,0:T(8,128)S(1)}, f32[2,256,256]{2,1,0:T(8,128)S(1)}, u32[]{:S(2)}, u32[]{:S(2)}) collective-permute-start(f32[2,256,256]{2,1,0:T(8,128)S(1)} %get-tuple-element.57.own), channel_id=1, source_target_pairs={{0,1},{1,0},{2,3},{3,2},{4,5},{5,4},{6,7},{7,6},{8,9},{9,8},{10,11... | collective-permute-start | bytes 1572872 | tf_op jit(solution)/shard_map/ppermute | solution.py:400
  47.6 11.6 %collective-permute-start.10 = (f32[2,128,256]{2,1,0:T(8,128)S(1)}, f32[2,128,256]{2,1,0:T(8,128)S(1)}, u32[]{:S(2)}, u32[]{:S(2)}) collective-permute-start(f32[2,128,256]{2,1,0:T(8,128)S(1)} %collective-permute-done.7.b0), channel_id=1, source_target_pairs={{0,1},{1,0},{2,3},{3,2},{4,5},{5,4},{6,7},{7,6},{8,9},{9,8},{10,11... | collective-permute-start | bytes 786440 | tf_op jit(solution)/shard_map/ppermute | solution.py:400
  48.1 11.1 %collective-permute-start.11 = (f32[2,128,256]{2,1,0:T(8,128)}, f32[2,128,256]{2,1,0:T(8,128)S(1)}, u32[]{:S(2)}, u32[]{:S(2)}) collective-permute-start(f32[2,128,256]{2,1,0:T(8,128)} %collective-permute-done.8.a0), channel_id=1, source_target_pairs={{0,1},{1,0},{2,3},{3,2},{4,5},{5,4},{6,7},{7,6},{8,9},{9,8},{10,11... | collective-permute-start | bytes 786440 | tf_op jit(solution)/shard_map/ppermute | solution.py:400
  53.5 12.2 %collective-permute-start.16 = (f32[160,256]{1,0:T(8,128)S(1)}, f32[160,256]{1,0:T(8,128)S(1)}, u32[]{:S(2)}, u32[]{:S(2)}) collective-permute-start(f32[160,256]{1,0:T(8,128)S(1)} %fusion.13), channel_id=1, source_target_pairs={{0,2},{2,0},{4,6},{6,4},{8,10},{10,8},{12,14},{14,12},{16,18},{18,... | collective-permute-start | bytes 491528 | tf_op jit(solution)/shard_map/ppermute | solution.py:403
  56.6 15.0 %collective-permute-start.17 = (f32[160,256]{1,0:T(8,128)S(1)}, f32[160,256]{1,0:T(8,128)S(1)}, u32[]{:S(2)}, u32[]{:S(2)}) collective-permute-start(f32[160,256]{1,0:T(8,128)S(1)} %fusion.13), channel_id=1, source_target_pairs={{0,16},{2,18},{4,20},{6,22},{8,24},{10,26},{12,28},{14,30},{16,0},... | collective-permute-start | bytes 491528 | tf_op jit(solution)/shard_map/ppermute | solution.py:403
  59.2 15.0 %collective-permute-start.18 = (f32[160,256]{1,0:T(8,128)S(1)}, f32[160,256]{1,0:T(8,128)S(1)}, u32[]{:S(2)}, u32[]{:S(2)}) collective-permute-start(f32[160,256]{1,0:T(8,128)S(1)} %fusion.13), channel_id=1, source_target_pairs={{0,18},{2,16},{4,22},{6,20},{8,26},{10,24},{12,30},{14,28},{16,2},... | collective-permute-start | bytes 491528 | tf_op jit(solution)/shard_map/ppermute | solution.py:403
  62.0 12.6 %collective-permute-start.19 = (f32[2,128,256]{2,1,0:T(8,128)S(1)}, f32[2,128,256]{2,1,0:T(8,128)S(1)}, u32[]{:S(2)}, u32[]{:S(2)}) collective-permute-start(f32[2,128,256]{2,1,0:T(8,128)S(1)} %get-tuple-element.63), channel_id=1, source_target_pairs={{0,2},{2,4},{4,6},{6,8},{8,10},{10,12},{12,14},{14,16},{16,18},{18... | collective-permute-start | bytes 786440 | tf_op jit(solution)/shard_map/ppermute | solution.py:417
  74.6 8.7 %collective-permute-start.21 = (f32[160,256]{1,0:T(8,128)S(1)}, f32[160,256]{1,0:T(8,128)S(1)}, u32[]{:S(2)}, u32[]{:S(2)}) collective-permute-start(f32[160,256]{1,0:T(8,128)S(1)} %add_add_fusion.1), channel_id=1, source_target_pairs={{0,4},{2,6},{4,0},{6,2},{8,12},{10,14},{12,8},{14,10},{16,20},{18,... | collective-permute-start | bytes 491528 | tf_op jit(solution)/shard_map/ppermute | solution.py:403
  78.2 5.5 %collective-permute-start.22 = (f32[160,256]{1,0:T(8,128)S(1)}, f32[160,256]{1,0:T(8,128)S(1)}, u32[]{:S(2)}, u32[]{:S(2)}) collective-permute-start(f32[160,256]{1,0:T(8,128)S(1)} %add_add_fusion.1), channel_id=1, source_target_pairs={{0,8},{2,10},{4,12},{6,14},{8,0},{10,2},{12,4},{14,6},{16,24},{18,... | collective-permute-start | bytes 491528 | tf_op jit(solution)/shard_map/ppermute | solution.py:403
  78.2 7.0 %collective-permute-start.23 = (f32[160,256]{1,0:T(8,128)S(1)}, f32[160,256]{1,0:T(8,128)S(1)}, u32[]{:S(2)}, u32[]{:S(2)}) collective-permute-start(f32[160,256]{1,0:T(8,128)S(1)} %add_add_fusion.1), channel_id=1, source_target_pairs={{0,12},{2,14},{4,8},{6,10},{8,4},{10,6},{12,0},{14,2},{16,28},{18,... | collective-permute-start | bytes 491528 | tf_op jit(solution)/shard_map/ppermute | solution.py:403
  79.7 8.7 %collective-permute-start.20 = (f32[2,128,256]{2,1,0:T(8,128)S(1)}, f32[2,128,256]{2,1,0:T(8,128)S(1)}, u32[]{:S(2)}, u32[]{:S(2)}) collective-permute-start(f32[2,128,256]{2,1,0:T(8,128)S(1)} %get-tuple-element.65), channel_id=1, source_target_pairs={{2,0},{4,2},{6,4},{8,6},{10,8},{12,10},{14,12},{16,14},{18,16},{20... | collective-permute-start | bytes 786440 | tf_op jit(solution)/shard_map/ppermute | solution.py:420
  85.3 4.0 %collective-permute-start.24 = (f32[4,160,256]{2,1,0:T(8,128)S(1)}, f32[4,160,256]{2,1,0:T(8,128)S(1)}, u32[]{:S(2)}, u32[]{:S(2)}) collective-permute-start(f32[4,160,256]{2,1,0:T(8,128)S(1)} %pad_maximum_fusion.own_totals), channel_id=1, source_target_pairs={{0,1},{1,0},{2,3},{3,2},{4,5},{5,4},{6,7},{7,6},{8,9},{9,8},{10,11... | collective-permute-start | bytes 1966088 | tf_op jit(solution)/shard_map/ppermute | solution.py:400
  95.0 2.2 %collective-permute-start.25 = (f32[4,160,256]{2,1,0:T(8,128)S(1)}, f32[4,160,256]{2,1,0:T(8,128)S(1)}, u32[]{:S(2)}, u32[]{:S(2)}) collective-permute-start(f32[4,160,256]{2,1,0:T(8,128)S(1)} %get-tuple-element.70), channel_id=1, source_target_pairs={{0,1},{1,0},{2,3},{3,2},{4,5},{5,4},{6,7},{7,6},{8,9},{9,8},{10,11... | collective-permute-start | bytes 1966088 | tf_op jit(solution)/shard_map/ppermute | solution.py:400
  97.2 11.9 %collective-permute-start.26 = (f32[160,256]{1,0:T(8,128)S(1)}, f32[160,256]{1,0:T(8,128)S(1)}, u32[]{:S(2)}, u32[]{:S(2)}) collective-permute-start(f32[160,256]{1,0:T(8,128)S(1)} %get-tuple-element.80), channel_id=1, source_target_pairs={{0,4},{2,6},{4,0},{6,2},{8,12},{10,14},{12,8},{14,10},{16,20},{18,... | collective-permute-start | bytes 491528 | tf_op jit(solution)/shard_map/ppermute | solution.py:403
  100.5 8.7 %collective-permute-start.27 = (f32[160,256]{1,0:T(8,128)S(1)}, f32[160,256]{1,0:T(8,128)S(1)}, u32[]{:S(2)}, u32[]{:S(2)}) collective-permute-start(f32[160,256]{1,0:T(8,128)S(1)} %get-tuple-element.82), channel_id=1, source_target_pairs={{0,8},{2,10},{4,12},{6,14},{8,0},{10,2},{12,4},{14,6},{16,24},{18,... | collective-permute-start | bytes 491528 | tf_op jit(solution)/shard_map/ppermute | solution.py:403
  102.1 7.8 %collective-permute-start.28 = (f32[160,256]{1,0:T(8,128)S(1)}, f32[160,256]{1,0:T(8,128)S(1)}, u32[]{:S(2)}, u32[]{:S(2)}) collective-permute-start(f32[160,256]{1,0:T(8,128)S(1)} %get-tuple-element.81), channel_id=1, source_target_pairs={{0,12},{2,14},{4,8},{6,10},{8,4},{10,6},{12,0},{14,2},{16,28},{18,... | collective-permute-start | bytes 491528 | tf_op jit(solution)/shard_map/ppermute | solution.py:403
  102.2 18.0 %collective-permute-start.35 = (f32[2,128,256]{2,1,0:T(8,128)S(1)}, f32[2,128,256]{2,1,0:T(8,128)S(1)}, u32[]{:S(2)}, u32[]{:S(2)}) collective-permute-start(f32[2,128,256]{2,1,0:T(8,128)S(1)} %get-tuple-element.72), channel_id=1, source_target_pairs={{0,2},{2,4},{4,6},{6,8},{8,10},{10,12},{12,14},{14,16},{16,18},{18... | collective-permute-start | bytes 786440 | tf_op jit(solution)/shard_map/ppermute | solution.py:417
  107.8 14.3 %collective-permute-start.36 = (f32[2,128,256]{2,1,0:T(8,128)S(1)}, f32[2,128,256]{2,1,0:T(8,128)S(1)}, u32[]{:S(2)}, u32[]{:S(2)}) collective-permute-start(f32[2,128,256]{2,1,0:T(8,128)S(1)} %get-tuple-element.73), channel_id=1, source_target_pairs={{2,0},{4,2},{6,4},{8,6},{10,8},{12,10},{14,12},{16,14},{18,16},{20... | collective-permute-start | bytes 786440 | tf_op jit(solution)/shard_map/ppermute | solution.py:420
  109.9 14.7 %collective-permute-start.29 = (f32[160,256]{1,0:T(8,128)S(1)}, f32[160,256]{1,0:T(8,128)S(1)}, u32[]{:S(2)}, u32[]{:S(2)}) collective-permute-start(f32[160,256]{1,0:T(8,128)S(1)} %fusion.6), channel_id=1, source_target_pairs={{0,2},{2,0},{4,6},{6,4},{8,10},{10,8},{12,14},{14,12},{16,18},{18,... | collective-permute-start | bytes 491528 | tf_op jit(solution)/shard_map/ppermute | solution.py:403
  113.6 18.3 %collective-permute-start.30 = (f32[160,256]{1,0:T(8,128)S(1)}, f32[160,256]{1,0:T(8,128)S(1)}, u32[]{:S(2)}, u32[]{:S(2)}) collective-permute-start(f32[160,256]{1,0:T(8,128)S(1)} %fusion.6), channel_id=1, source_target_pairs={{0,16},{2,18},{4,20},{6,22},{8,24},{10,26},{12,28},{14,30},{16,0},... | collective-permute-start | bytes 491528 | tf_op jit(solution)/shard_map/ppermute | solution.py:403
  117.9 14.1 %collective-permute-start.31 = (f32[160,256]{1,0:T(8,128)S(1)}, f32[160,256]{1,0:T(8,128)S(1)}, u32[]{:S(2)}, u32[]{:S(2)}) collective-permute-start(f32[160,256]{1,0:T(8,128)S(1)} %fusion.6), channel_id=1, source_target_pairs={{0,18},{2,16},{4,22},{6,20},{8,26},{10,24},{12,30},{14,28},{16,2},... | collective-permute-start | bytes 491528 | tf_op jit(solution)/shard_map/ppermute | solution.py:403
  122.2 13.3 %collective-permute-start.37 = (f32[2,256,256]{2,1,0:T(8,128)S(1)}, f32[2,256,256]{2,1,0:T(8,128)S(1)}, u32[]{:S(2)}, u32[]{:S(2)}) collective-permute-start(f32[2,256,256]{2,1,0:T(8,128)S(1)} %get-tuple-element.75.own), channel_id=1, source_target_pairs={{0,1},{1,0},{2,3},{3,2},{4,5},{5,4},{6,7},{7,6},{8,9},{9,8},{10,11... | collective-permute-start | bytes 1572872 | tf_op jit(solution)/shard_map/ppermute | solution.py:400
  122.2 10.9 %collective-permute-start.38 = (f32[2,128,256]{2,1,0:T(8,128)S(1)}, f32[2,128,256]{2,1,0:T(8,128)S(1)}, u32[]{:S(2)}, u32[]{:S(2)}) collective-permute-start(f32[2,128,256]{2,1,0:T(8,128)S(1)} %collective-permute-done.35.b0), channel_id=1, source_target_pairs={{0,1},{1,0},{2,3},{3,2},{4,5},{5,4},{6,7},{7,6},{8,9},{9,8},{10,11... | collective-permute-start | bytes 786440 | tf_op jit(solution)/shard_map/ppermute | solution.py:400
  124.6 10.9 %collective-permute-start.39 = (f32[2,128,256]{2,1,0:T(8,128)S(1)}, f32[2,128,256]{2,1,0:T(8,128)S(1)}, u32[]{:S(2)}, u32[]{:S(2)}) collective-permute-start(f32[2,128,256]{2,1,0:T(8,128)S(1)} %collective-permute-done.36.a0), channel_id=1, source_target_pairs={{0,1},{1,0},{2,3},{3,2},{4,5},{5,4},{6,7},{7,6},{8,9},{9,8},{10,11... | collective-permute-start | bytes 786440 | tf_op jit(solution)/shard_map/ppermute | solution.py:400
  132.0 6.7 %collective-permute-start.32 = (f32[160,256]{1,0:T(8,128)S(1)}, f32[160,256]{1,0:T(8,128)S(1)}, u32[]{:S(2)}, u32[]{:S(2)}) collective-permute-start(f32[160,256]{1,0:T(8,128)S(1)} %add_add_fusion), channel_id=1, source_target_pairs={{0,4},{2,6},{4,0},{6,2},{8,12},{10,14},{12,8},{14,10},{16,20},{18,... | collective-permute-start | bytes 491528 | tf_op jit(solution)/shard_map/ppermute | solution.py:403
  133.0 7.1 %collective-permute-start.33 = (f32[160,256]{1,0:T(8,128)S(1)}, f32[160,256]{1,0:T(8,128)S(1)}, u32[]{:S(2)}, u32[]{:S(2)}) collective-permute-start(f32[160,256]{1,0:T(8,128)S(1)} %add_add_fusion), channel_id=1, source_target_pairs={{0,8},{2,10},{4,12},{6,14},{8,0},{10,2},{12,4},{14,6},{16,24},{18,... | collective-permute-start | bytes 491528 | tf_op jit(solution)/shard_map/ppermute | solution.py:403
  133.1 9.2 %collective-permute-start.34 = (f32[160,256]{1,0:T(8,128)S(1)}, f32[160,256]{1,0:T(8,128)S(1)}, u32[]{:S(2)}, u32[]{:S(2)}) collective-permute-start(f32[160,256]{1,0:T(8,128)S(1)} %add_add_fusion), channel_id=1, source_target_pairs={{0,12},{2,14},{4,8},{6,10},{8,4},{10,6},{12,0},{14,2},{16,28},{18,... | collective-permute-start | bytes 491528 | tf_op jit(solution)/shard_map/ppermute | solution.py:403
  142.4 1.4 collective-permute-start.40
  (8 other events, 7.6 us)

commit v8 on v3

--- a/solution.py
+++ b/solution.py
@@ -211,7 +211,7 @@
         for slot in range(2):
             row, column = spot(info, size, minibatch, side, slot)
             add_at(tall, power, row + pattern, column)
-    out[...] = tall[kept]
+    out[...] = 1.0 / (tall[kept] + 1.0)
 
 
 def patch_kernel(size, minibatch, info, strip_ref, below, above, patch, window):
@@ -328,7 +328,7 @@
         for side, place, ref, start in grads:
             row, column = spot(info, size, minibatch, side, place)
             add_at(tall, ref[part], row + pattern + start, column)
-        fresh = strip_ref[part] + tall[kept] / (illum[...] + 1.0)
+        fresh = strip_ref[part] + tall[kept] * illum[...]
         strip_out[part] = fresh
         if edges:
             column_below = spot(info, size, minibatch + 1, -1, slot)[1]

time: 145 us -> 145 us (level)
  transfers between devices with their start and end apart: 41 -> 41, of which waited for: 23 -> 22; matrix products, arithmetic and copies ran while one was open for 3% -> 3% of each run, Pallas kernels for 8% -> 8%
where the time goes in v8:
time: 145 us; the launch traced here: 143 us
  starting transfers between devices  59 us (41%)
  waiting for transfers between devices  50.5 us (35%)
  Pallas kernels  24 us (17%)
  local copies, waits for them, and re-layouts  6.36 us (4%)
  other arithmetic  2.37 us (2%)
    ppermute x18, starting transfers between devices, across(): return lax.ppermute(value, 'tile', [(i, i ^ k) for i in range(tiles)])  29.6 us
    ppermute x18, waiting for transfers between devices, across(): return lax.ppermute(value, 'tile', [(i, i ^ k) for i in range(tiles)])  28.8 us
    pallas_call x10, Pallas kernels, call(): pl.pallas_call(kernel, out_shape=shapes, in_specs=[smem] + [vmem] * (len(...  24 us
    ppermute x5, starting transfers between devices, from_below(): return lax.ppermute(value, 'tile', up)  20.7 us
    ppermute x5, waiting for transfers between devices, from_below(): return lax.ppermute(value, 'tile', up)  8.91 us
    ppermute x5, waiting for transfers between devices, from_above(): return lax.ppermute(value, 'tile', down)  6.71 us
    ppermute x5, starting transfers between devices, from_above(): return lax.ppermute(value, 'tile', down)  6.64 us
    ppermute x13, waiting for transfers between devices, swap(): return lax.ppermute(value, 'mode', [(0, 1), (1, 0)])  6.03 us
  transfers between devices with their start and end apart: 41, of which 22 were waited for; matrix products, arithmetic and copies ran while one was open for 3% of the time, Pallas kernels for 8%

profile of v8, /device:TPU:0, one launch (start us, length us, event | category | flops | bytes accessed | tf_op | source)
XLA Modules:
  0.0 143.2 jit_solution(4348664826953795364)
XLA Ops:
  0.6 1.9 %dynamic-slice_bitcast_fusion = (f32[128,512]{1,0:T(8,128)}, f32[128,512]{1,0:T(8,128)}) fusion(f32[2,256,512]{2,1,0:T(8,128)} %strip_ref.3, s32[]{:T(128)S(6)} %select_n.4, s32[]{:T(128)S(6)} %add.117), kind=kLoop, calls=%fused_computation.2 | loop fusion | bytes 1048584 | tf_op jit(solution)/shard_map/slice | solution.py:426
  2.6 5.0 %collective-permute-start = (f32[128,512]{1,0:T(8,128)}, f32[128,512]{1,0:T(8,128)S(1)}, u32[]{:S(2)}, u32[]{:S(2)}) collective-permute-start(f32[128,512]{1,0:T(8,128)} %get-tuple-element.85), channel_id=1, source_target_pairs={{0,2},{2,4},{4,6},{6,8},{8,10},{10,12},{12,14},{14,16},{16,18},{18... | collective-permute-start | bytes 786440 | tf_op jit(solution)/shard_map/ppermute | solution.py:414
  7.6 1.3 collective-permute-start.1
  9.0 4.5 %collective-permute-start.2 = (s32[2,2,2]{2,1,0:T(2,128)S(1)}, s32[2,2,2]{2,1,0:T(2,128)S(1)}, u32[]{:S(2)}, u32[]{:S(2)}) collective-permute-start(s32[2,2,2]{2,1,0:T(2,128)S(1)} %copy-done.9), channel_id=1, source_target_pairs={{0,2},{2,4},{4,6},{6,8},{8,10},{10,12},{12,14},{14,16},{16,18},{18... | collective-permute-start | bytes 104 | tf_op jit(solution)/shard_map/ppermute | solution.py:414
  13.5 1.3 collective-permute-start.3
  17.8 1.3 collective-permute-done.2
  19.1 1.9 %collective-permute-done.3 = s32[2,2,2]{2,1,0:T(2,128)S(1)} collective-permute-done((s32[2,2,2]{2,1,0:T(2,128)S(1)}, s32[2,2,2]{2,1,0:T(2,128)S(1)}, u32[]{:S(2)}, u32[]{:S(2)}) %collective-permute-start.3) | collective-permute-done | bytes 64 | tf_op jit(solution)/shard_map/ppermute | solution.py:417
  23.2 6.4 %field.2 = (f32[2,256,256]{2,1,0:T(8,128)S(1)}, f32[2,128,256]{2,1,0:T(8,128)}, f32[2,128,256]{2,1,0:T(8,128)}, f32[4,160,256]{2,1,0:T(8,128)S(1)}, f32[4,160,256]{2,1,0:T(8,128)S(1)}) custom-call(s32[26]{0:T(128)S(1)} %concatenate.8.info, f32[2,256,512]{2,1,0:T(8,128)S(1)} %copy-done, f32[128,512]{1,0:T(8,128)S(1)} %collective-permute-done.refs_0_, ...), custom_call_target="tpu_custom_call" | custom-call | flops 3221225472 | bytes 6553704 | tf_op jit(solution)/shard_map/field/pallas_call | solution.py:371
  29.8 3.4 %collective-permute-start.7 = (f32[2,128,256]{2,1,0:T(8,128)}, f32[2,128,256]{2,1,0:T(8,128)S(1)}, u32[]{:S(2)}, u32[]{:S(2)}) collective-permute-start(f32[2,128,256]{2,1,0:T(8,128)} %get-tuple-element.51), channel_id=1, source_target_pairs={{0,2},{2,4},{4,6},{6,8},{8,10},{10,12},{12,14},{14,16},{16,18},{18... | collective-permute-start | bytes 786440 | tf_op jit(solution)/shard_map/ppermute | solution.py:414
  33.2 1.3 collective-permute-start.8
  35.5 3.7 %collective-permute-start.13 = (f32[160,256]{1,0:T(8,128)}, f32[160,256]{1,0:T(8,128)}, u32[]{:S(2)}, u32[]{:S(2)}) collective-permute-start(f32[160,256]{1,0:T(8,128)} %get-tuple-element.81), channel_id=1, source_target_pairs={{0,4},{2,6},{4,0},{6,2},{8,12},{10,14},{12,8},{14,10},{16,20},{18,... | collective-permute-start | bytes 491528 | tf_op jit(solution)/shard_map/ppermute | solution.py:400
  39.3 2.4 %collective-permute-start.14 = (f32[160,256]{1,0:T(8,128)}, f32[160,256]{1,0:T(8,128)}, u32[]{:S(2)}, u32[]{:S(2)}) collective-permute-start(f32[160,256]{1,0:T(8,128)} %get-tuple-element.83), channel_id=1, source_target_pairs={{0,8},{2,10},{4,12},{6,14},{8,0},{10,2},{12,4},{14,6},{16,24},{18,... | collective-permute-start | bytes 491528 | tf_op jit(solution)/shard_map/ppermute | solution.py:400
  41.6 1.5 %collective-permute-start.15 = (f32[160,256]{1,0:T(8,128)}, f32[160,256]{1,0:T(8,128)}, u32[]{:S(2)}, u32[]{:S(2)}) collective-permute-start(f32[160,256]{1,0:T(8,128)} %get-tuple-element.82), channel_id=1, source_target_pairs={{0,12},{2,14},{4,8},{6,10},{8,4},{10,6},{12,0},{14,2},{16,28},{18,... | collective-permute-start | bytes 491528 | tf_op jit(solution)/shard_map/ppermute | solution.py:400
  45.1 1.7 %illumination.2.illum = f32[256,512]{1,0:T(8,128)S(1)} custom-call(s32[26]{0:T(128)S(1)} %concatenate.9.info, f32[2,256,256]{2,1,0:T(8,128)S(1)} %get-tuple-element.47.refs_4_.own.refs_0_, f32[2,256,256]{2,1,0:T(8,128)S(1)} %collective-permute-done.6.refs_5_.other.refs_1_), custom_call_target="tpu_custom_call" | custom-call | bytes 1572968 | tf_op jit(solution)/shard_map/illumination/pallas_call | solution.py:371
  47.6 4.0 %collective-permute-done.14 = f32[160,256]{1,0:T(8,128)} collective-permute-done((f32[160,256]{1,0:T(8,128)}, f32[160,256]{1,0:T(8,128)}, u32[]{:S(2)}, u32[]{:S(2)}) %collective-permute-start.14) | collective-permute-done | bytes 163872 | tf_op jit(solution)/shard_map/ppermute | solution.py:400
  51.6 1.2 fusion.13
  52.8 3.3 %collective-permute-start.16 = (f32[160,256]{1,0:T(8,128)S(1)}, f32[160,256]{1,0:T(8,128)S(1)}, u32[]{:S(2)}, u32[]{:S(2)}) collective-permute-start(f32[160,256]{1,0:T(8,128)S(1)} %fusion.13), channel_id=1, source_target_pairs={{0,2},{2,0},{4,6},{6,4},{8,10},{10,8},{12,14},{14,12},{16,18},{18,... | collective-permute-start | bytes 491528 | tf_op jit(solution)/shard_map/ppermute | solution.py:400
  56.2 2.6 %collective-permute-start.17 = (f32[160,256]{1,0:T(8,128)S(1)}, f32[160,256]{1,0:T(8,128)S(1)}, u32[]{:S(2)}, u32[]{:S(2)}) collective-permute-start(f32[160,256]{1,0:T(8,128)S(1)} %fusion.13), channel_id=1, source_target_pairs={{0,16},{2,18},{4,20},{6,22},{8,24},{10,26},{12,28},{14,30},{16,0},... | collective-permute-start | bytes 491528 | tf_op jit(solution)/shard_map/ppermute | solution.py:400
  58.8 2.8 %update.2 = (f32[2,256,512]{2,1,0:T(8,128)S(1)}, f32[2,128,256]{2,1,0:T(8,128)S(1)}, f32[2,128,256]{2,1,0:T(8,128)S(1)}) custom-call(s32[26]{0:T(128)S(1)} %concatenate.9.info, f32[2,256,512]{2,1,0:T(8,128)S(1)} %copy-done, f32[256,512]{1,0:T(8,128)S(1)} %illumination.2.illum, f32[2,256,256]{2,1,0:T(8,128)S(1)} %get-tuple-element.54.own, ...), custom_call_target="tpu_custom_call" | custom-call | bytes 5242984 | tf_op jit(solution)/shard_map/update/pallas_call | solution.py:371
  61.6 3.7 %collective-permute-start.19 = (f32[2,128,256]{2,1,0:T(8,128)S(1)}, f32[2,128,256]{2,1,0:T(8,128)S(1)}, u32[]{:S(2)}, u32[]{:S(2)}) collective-permute-start(f32[2,128,256]{2,1,0:T(8,128)S(1)} %get-tuple-element.60), channel_id=1, source_target_pairs={{0,2},{2,4},{4,6},{6,8},{8,10},{10,12},{12,14},{14,16},{16,18},{18... | collective-permute-start | bytes 786440 | tf_op jit(solution)/shard_map/ppermute | solution.py:414
  65.3 1.5 %collective-permute-start.20 = (f32[2,128,256]{2,1,0:T(8,128)S(1)}, f32[2,128,256]{2,1,0:T(8,128)S(1)}, u32[]{:S(2)}, u32[]{:S(2)}) collective-permute-start(f32[2,128,256]{2,1,0:T(8,128)S(1)} %get-tuple-element.61), channel_id=1, source_target_pairs={{2,0},{4,2},{6,4},{8,6},{10,8},{12,10},{14,12},{16,14},{18,16},{20... | collective-permute-start | bytes 786440 | tf_op jit(solution)/shard_map/ppermute | solution.py:417
  66.8 4.3 %collective-permute-done.17 = f32[160,256]{1,0:T(8,128)S(1)} collective-permute-done((f32[160,256]{1,0:T(8,128)S(1)}, f32[160,256]{1,0:T(8,128)S(1)}, u32[]{:S(2)}, u32[]{:S(2)}) %collective-permute-start.17) | collective-permute-done | bytes 163872 | tf_op jit(solution)/shard_map/ppermute | solution.py:400
  71.1 2.7 %collective-permute-done.18 = f32[160,256]{1,0:T(8,128)S(1)} collective-permute-done((f32[160,256]{1,0:T(8,128)S(1)}, f32[160,256]{1,0:T(8,128)S(1)}, u32[]{:S(2)}, u32[]{:S(2)}) %collective-permute-start.18) | collective-permute-done | bytes 163872 | tf_op jit(solution)/shard_map/ppermute | solution.py:400
  73.9 5.9 %collective-permute-done.19.below = f32[2,128,256]{2,1,0:T(8,128)S(1)} collective-permute-done((f32[2,128,256]{2,1,0:T(8,128)S(1)}, f32[2,128,256]{2,1,0:T(8,128)S(1)}, u32[]{:S(2)}, u32[]{:S(2)}) %collective-permute-start.19) | collective-permute-done | bytes 262176 | tf_op jit(solution)/shard_map/ppermute | solution.py:414
  79.8 2.1 %collective-permute-done.20.above = f32[2,128,256]{2,1,0:T(8,128)S(1)} collective-permute-done((f32[2,128,256]{2,1,0:T(8,128)S(1)}, f32[2,128,256]{2,1,0:T(8,128)S(1)}, u32[]{:S(2)}, u32[]{:S(2)}) %collective-permute-start.20) | collective-permute-done | bytes 262176 | tf_op jit(solution)/shard_map/ppermute | solution.py:417
  82.0 3.5 %collective-permute-start.23 = (f32[160,256]{1,0:T(8,128)S(1)}, f32[160,256]{1,0:T(8,128)S(1)}, u32[]{:S(2)}, u32[]{:S(2)}) collective-permute-start(f32[160,256]{1,0:T(8,128)S(1)} %add_add_fusion.1), channel_id=1, source_target_pairs={{0,12},{2,14},{4,8},{6,10},{8,4},{10,6},{12,0},{14,2},{16,28},{18,... | collective-permute-start | bytes 491528 | tf_op jit(solution)/shard_map/ppermute | solution.py:400
  85.4 3.6 %collective-permute-done.21 = f32[160,256]{1,0:T(8,128)S(1)} collective-permute-done((f32[160,256]{1,0:T(8,128)S(1)}, f32[160,256]{1,0:T(8,128)S(1)}, u32[]{:S(2)}, u32[]{:S(2)}) %collective-permute-start.21) | collective-permute-done | bytes 163872 | tf_op jit(solution)/shard_map/ppermute | solution.py:400
  89.0 1.9 %collective-permute-done.23 = f32[160,256]{1,0:T(8,128)S(1)} collective-permute-done((f32[160,256]{1,0:T(8,128)S(1)}, f32[160,256]{1,0:T(8,128)S(1)}, u32[]{:S(2)}, u32[]{:S(2)}) %collective-permute-start.23) | collective-permute-done | bytes 163872 | tf_op jit(solution)/shard_map/ppermute | solution.py:400
  92.0 1.1 collective-permute-done.24.other_totals
  93.8 4.5 %field.3 = (f32[2,256,256]{2,1,0:T(8,128)S(1)}, f32[2,128,256]{2,1,0:T(8,128)S(1)}, f32[2,128,256]{2,1,0:T(8,128)S(1)}, f32[4,160,256]{2,1,0:T(8,128)S(1)}, f32[4,160,256]{2,1,0:T(8,128)S(1)}) custom-call(s32[26]{0:T(128)S(1)} %concatenate.8.info, f32[2,256,256]{2,1,0:T(8,128)S(1)} %patch.1.strip_ref, f32[2,256,256]{2,1,0:T(8,128)S(1)} %get-tuple-element.65.refs_0_.own, ...), custom_call_target="tpu_custom_call" | custom-call | flops 3221225472 | bytes 4980840 | tf_op jit(solution)/shard_map/field/pallas_call | solution.py:371
  98.6 2.0 %collective-permute-done.25 = f32[4,160,256]{2,1,0:T(8,128)S(1)} collective-permute-done((f32[4,160,256]{2,1,0:T(8,128)S(1)}, f32[4,160,256]{2,1,0:T(8,128)S(1)}, u32[]{:S(2)}, u32[]{:S(2)}) %collective-permute-start.25) | collective-permute-done | bytes 655392 | tf_op jit(solution)/shard_map/ppermute | solution.py:397
  102.0 2.2 %collective-permute-start.28 = (f32[160,256]{1,0:T(8,128)S(1)}, f32[160,256]{1,0:T(8,128)S(1)}, u32[]{:S(2)}, u32[]{:S(2)}) collective-permute-start(f32[160,256]{1,0:T(8,128)S(1)} %get-tuple-element.79), channel_id=1, source_target_pairs={{0,12},{2,14},{4,8},{6,10},{8,4},{10,6},{12,0},{14,2},{16,28},{18,... | collective-permute-start | bytes 491528 | tf_op jit(solution)/shard_map/ppermute | solution.py:400
  104.2 4.0 %collective-permute-start.35 = (f32[2,128,256]{2,1,0:T(8,128)S(1)}, f32[2,128,256]{2,1,0:T(8,128)S(1)}, u32[]{:S(2)}, u32[]{:S(2)}) collective-permute-start(f32[2,128,256]{2,1,0:T(8,128)S(1)} %get-tuple-element.70), channel_id=1, source_target_pairs={{0,2},{2,4},{4,6},{6,8},{8,10},{10,12},{12,14},{14,16},{16,18},{18... | collective-permute-start | bytes 786440 | tf_op jit(solution)/shard_map/ppermute | solution.py:414
  108.2 1.3 collective-permute-start.36
  109.5 2.1 %collective-permute-done.28 = f32[160,256]{1,0:T(8,128)S(1)} collective-permute-done((f32[160,256]{1,0:T(8,128)S(1)}, f32[160,256]{1,0:T(8,128)S(1)}, u32[]{:S(2)}, u32[]{:S(2)}) %collective-permute-start.28) | collective-permute-done | bytes 163872 | tf_op jit(solution)/shard_map/ppermute | solution.py:400
  111.7 2.2 %collective-permute-start.29 = (f32[160,256]{1,0:T(8,128)S(1)}, f32[160,256]{1,0:T(8,128)S(1)}, u32[]{:S(2)}, u32[]{:S(2)}) collective-permute-start(f32[160,256]{1,0:T(8,128)S(1)} %fusion.6), channel_id=1, source_target_pairs={{0,2},{2,0},{4,6},{6,4},{8,10},{10,8},{12,14},{14,12},{16,18},{18,... | collective-permute-start | bytes 491528 | tf_op jit(solution)/shard_map/ppermute | solution.py:400
  113.8 1.9 %collective-permute-start.30 = (f32[160,256]{1,0:T(8,128)S(1)}, f32[160,256]{1,0:T(8,128)S(1)}, u32[]{:S(2)}, u32[]{:S(2)}) collective-permute-start(f32[160,256]{1,0:T(8,128)S(1)} %fusion.6), channel_id=1, source_target_pairs={{0,16},{2,18},{4,20},{6,22},{8,24},{10,26},{12,28},{14,30},{16,0},... | collective-permute-start | bytes 491528 | tf_op jit(solution)/shard_map/ppermute | solution.py:400
  115.8 1.4 collective-permute-start.31
  117.2 1.7 %illumination.3.illum = f32[256,512]{1,0:T(8,128)S(1)} custom-call(s32[26]{0:T(128)S(1)} %concatenate.9.info, f32[2,256,256]{2,1,0:T(8,128)S(1)} %get-tuple-element.65.refs_0_.own, f32[2,256,256]{2,1,0:T(8,128)S(1)} %get-tuple-element.66.refs_1_.other), custom_call_target="tpu_custom_call" | custom-call | bytes 1572968 | tf_op jit(solution)/shard_map/illumination/pallas_call | solution.py:371
  118.9 1.7 %collective-permute-done.35.b0 = f32[2,128,256]{2,1,0:T(8,128)S(1)} collective-permute-done((f32[2,128,256]{2,1,0:T(8,128)S(1)}, f32[2,128,256]{2,1,0:T(8,128)S(1)}, u32[]{:S(2)}, u32[]{:S(2)}) %collective-permute-start.35) | collective-permute-done | bytes 262176 | tf_op jit(solution)/shard_map/ppermute | solution.py:414
  120.5 2.4 %collective-permute-done.36.a0 = f32[2,128,256]{2,1,0:T(8,128)S(1)} collective-permute-done((f32[2,128,256]{2,1,0:T(8,128)S(1)}, f32[2,128,256]{2,1,0:T(8,128)S(1)}, u32[]{:S(2)}, u32[]{:S(2)}) %collective-permute-start.36) | collective-permute-done | bytes 262176 | tf_op jit(solution)/shard_map/ppermute | solution.py:417
  123.4 1.7 %collective-permute-done.29 = f32[160,256]{1,0:T(8,128)S(1)} collective-permute-done((f32[160,256]{1,0:T(8,128)S(1)}, f32[160,256]{1,0:T(8,128)S(1)}, u32[]{:S(2)}, u32[]{:S(2)}) %collective-permute-start.29) | collective-permute-done | bytes 163872 | tf_op jit(solution)/shard_map/ppermute | solution.py:400
  125.2 6.4 %collective-permute-done.30 = f32[160,256]{1,0:T(8,128)S(1)} collective-permute-done((f32[160,256]{1,0:T(8,128)S(1)}, f32[160,256]{1,0:T(8,128)S(1)}, u32[]{:S(2)}, u32[]{:S(2)}) %collective-permute-start.30) | collective-permute-done | bytes 163872 | tf_op jit(solution)/shard_map/ppermute | solution.py:400
  131.8 3.4 %collective-permute-start.34 = (f32[160,256]{1,0:T(8,128)S(1)}, f32[160,256]{1,0:T(8,128)S(1)}, u32[]{:S(2)}, u32[]{:S(2)}) collective-permute-start(f32[160,256]{1,0:T(8,128)S(1)} %add_add_fusion), channel_id=1, source_target_pairs={{0,12},{2,14},{4,8},{6,10},{8,4},{10,6},{12,0},{14,2},{16,28},{18,... | collective-permute-start | bytes 491528 | tf_op jit(solution)/shard_map/ppermute | solution.py:400
  135.2 3.1 %update.3 = f32[2,256,512]{2,1,0:T(8,128)} custom-call(s32[26]{0:T(128)S(1)} %concatenate.9.info, f32[2,256,512]{2,1,0:T(8,128)S(1)} %get-tuple-element.57.strip_ref, f32[256,512]{1,0:T(8,128)S(1)} %illumination.3.illum, f32[2,256,256]{2,1,0:T(8,128)S(1)} %get-tuple-element.73.own, f32[2,256,256]{2,1,0:T(8,128)S(1)} %collective-permute-done.37.other, ...), custom_call_target="tpu_custom_call" | custom-call | bytes 4718696 | tf_op jit(solution)/shard_map/update/pallas_call | solution.py:371
  138.6 1.7 %collective-permute-done.34 = f32[160,256]{1,0:T(8,128)S(1)} collective-permute-done((f32[160,256]{1,0:T(8,128)S(1)}, f32[160,256]{1,0:T(8,128)S(1)}, u32[]{:S(2)}, u32[]{:S(2)}) %collective-permute-start.34) | collective-permute-done | bytes 163872 | tf_op jit(solution)/shard_map/ppermute | solution.py:400
  140.5 1.3 collective-permute-done.40.other_totals
  141.8 1.4 probe.3
  (85 shorter events, 13.9 us)
Async XLA Ops:
  0.6 14.4 %copy-start.1 = (f32[2,2,256,256]{3,2,1,0:T(8,128)S(1)}, f32[2,2,256,256]{3,2,1,0:T(8,128)}, u32[]{:S(2)}) copy-start(f32[2,2,256,256]{3,2,1,0:T(8,128)} %measured.1) | copy-start | bytes 3145732
  2.6 6.4 %copy-start.9 = (s32[2,2,2]{2,1,0:T(2,128)S(1)}, s32[2,2,2]{2,1,0:T(2,128)}, u32[]{:S(2)}) copy-start(s32[2,2,2]{2,1,0:T(2,128)} %param.7) | copy-start | bytes 100
  2.6 18.4 %collective-permute-start = (f32[128,512]{1,0:T(8,128)}, f32[128,512]{1,0:T(8,128)S(1)}, u32[]{:S(2)}, u32[]{:S(2)}) collective-permute-start(f32[128,512]{1,0:T(8,128)} %get-tuple-element.85), channel_id=1, source_target_pairs={{0,2},{2,4},{4,6},{6,8},{8,10},{10,12},{12,14},{14,16},{16,18},{18... | collective-permute-start | bytes 786440 | tf_op jit(solution)/shard_map/ppermute | solution.py:414
  7.6 13.5 %collective-permute-start.1 = (f32[128,512]{1,0:T(8,128)}, f32[128,512]{1,0:T(8,128)}, u32[]{:S(2)}, u32[]{:S(2)}) collective-permute-start(f32[128,512]{1,0:T(8,128)} %get-tuple-element.84), channel_id=1, source_target_pairs={{2,0},{4,2},{6,4},{8,6},{10,8},{12,10},{14,12},{16,14},{18,16},{20... | collective-permute-start | bytes 786440 | tf_op jit(solution)/shard_map/ppermute | solution.py:417
  8.9 14.4 %collective-permute-start.6 = (f32[2,256,256]{2,1,0:T(8,128)}, f32[2,256,256]{2,1,0:T(8,128)S(1)}, u32[]{:S(2)}, u32[]{:S(2)}) collective-permute-start(f32[2,256,256]{2,1,0:T(8,128)} %bitcast.44), channel_id=1, source_target_pairs={{0,1},{1,0},{2,3},{3,2},{4,5},{5,4},{6,7},{7,6},{8,9},{9,8},{10,11... | collective-permute-start | bytes 1572872 | tf_op jit(solution)/shard_map/ppermute | solution.py:397
  9.0 10.1 %collective-permute-start.2 = (s32[2,2,2]{2,1,0:T(2,128)S(1)}, s32[2,2,2]{2,1,0:T(2,128)S(1)}, u32[]{:S(2)}, u32[]{:S(2)}) collective-permute-start(s32[2,2,2]{2,1,0:T(2,128)S(1)} %copy-done.9), channel_id=1, source_target_pairs={{0,2},{2,4},{4,6},{6,8},{8,10},{10,12},{12,14},{14,16},{16,18},{18... | collective-permute-start | bytes 104 | tf_op jit(solution)/shard_map/ppermute | solution.py:414
  13.5 7.5 %collective-permute-start.3 = (s32[2,2,2]{2,1,0:T(2,128)S(1)}, s32[2,2,2]{2,1,0:T(2,128)S(1)}, u32[]{:S(2)}, u32[]{:S(2)}) collective-permute-start(s32[2,2,2]{2,1,0:T(2,128)S(1)} %copy-done.9), channel_id=1, source_target_pairs={{2,0},{4,2},{6,4},{8,6},{10,8},{12,10},{14,12},{16,14},{18,16},{20... | collective-permute-start | bytes 104 | tf_op jit(solution)/shard_map/ppermute | solution.py:417
  17.1 6.2 %copy-start = (f32[2,256,512]{2,1,0:T(8,128)S(1)}, f32[2,256,512]{2,1,0:T(8,128)}, u32[]{:S(2)}) copy-start(f32[2,256,512]{2,1,0:T(8,128)} %strip_ref.3) | copy-start | bytes 3145732
  17.8 11.9 %copy-start.4 = (f32[2,256,256]{2,1,0:T(8,128)}, f32[2,256,256]{2,1,0:T(8,128)S(1)}, u32[]{:S(2)}) copy-start(f32[2,256,256]{2,1,0:T(8,128)S(1)} %get-tuple-element.48.refs_6_.refs_2_) | copy-start | bytes 1572868
  17.8 11.9 %copy-start.6 = (bf16[4,256,256]{2,1,0:T(8,128)(2,1)}, bf16[4,256,256]{2,1,0:T(8,128)(2,1)S(1)}, u32[]{:S(2)}) copy-start(bf16[4,256,256]{2,1,0:T(8,128)(2,1)S(1)} %get-tuple-element.49.refs_7_.refs_3_) | copy-start | bytes 1572868
  21.0 2.2 %copy-start.10 = (s32[2,2,2]{2,1,0:T(2,128)}, s32[2,2,2]{2,1,0:T(2,128)S(1)}, u32[]{:S(2)}) copy-start(s32[2,2,2]{2,1,0:T(2,128)S(1)} %collective-permute-done.3) | copy-start | bytes 100
  21.0 1.6 %collective-permute-start.4 = (f32[128,512]{1,0:T(8,128)S(1)}, f32[128,512]{1,0:T(8,128)S(1)}, u32[]{:S(2)}, u32[]{:S(2)}) collective-permute-start(f32[128,512]{1,0:T(8,128)S(1)} %collective-permute-done.refs_0_), channel_id=1, source_target_pairs={{0,1},{1,0},{2,3},{3,2},{4,5},{5,4},{6,7},{7,6},{8,9},{9,8},{10,11... | collective-permute-start | bytes 786440 | tf_op jit(solution)/shard_map/ppermute | solution.py:397
  21.1 2.1 %collective-permute-start.5 = (f32[128,512]{1,0:T(8,128)}, f32[128,512]{1,0:T(8,128)S(1)}, u32[]{:S(2)}, u32[]{:S(2)}) collective-permute-start(f32[128,512]{1,0:T(8,128)} %collective-permute-done.1.refs_2_), channel_id=1, source_target_pairs={{0,1},{1,0},{2,3},{3,2},{4,5},{5,4},{6,7},{7,6},{8,9},{9,8},{10,11... | collective-permute-start | bytes 786440 | tf_op jit(solution)/shard_map/ppermute | solution.py:397
  29.7 4.9 %collective-permute-start.12 = (f32[4,160,256]{2,1,0:T(8,128)S(1)}, f32[4,160,256]{2,1,0:T(8,128)S(1)}, u32[]{:S(2)}, u32[]{:S(2)}) collective-permute-start(f32[4,160,256]{2,1,0:T(8,128)S(1)} %get-tuple-element.59), channel_id=1, source_target_pairs={{0,1},{1,0},{2,3},{3,2},{4,5},{5,4},{6,7},{7,6},{8,9},{9,8},{10,11... | collective-permute-start | bytes 1966088 | tf_op jit(solution)/shard_map/ppermute | solution.py:397
  29.8 17.0 %collective-permute-start.7 = (f32[2,128,256]{2,1,0:T(8,128)}, f32[2,128,256]{2,1,0:T(8,128)S(1)}, u32[]{:S(2)}, u32[]{:S(2)}) collective-permute-start(f32[2,128,256]{2,1,0:T(8,128)} %get-tuple-element.51), channel_id=1, source_target_pairs={{0,2},{2,4},{4,6},{6,8},{8,10},{10,12},{12,14},{14,16},{16,18},{18... | collective-permute-start | bytes 786440 | tf_op jit(solution)/shard_map/ppermute | solution.py:414
  33.2 13.8 %collective-permute-start.8 = (f32[2,128,256]{2,1,0:T(8,128)}, f32[2,128,256]{2,1,0:T(8,128)}, u32[]{:S(2)}, u32[]{:S(2)}) collective-permute-start(f32[2,128,256]{2,1,0:T(8,128)} %get-tuple-element.52), channel_id=1, source_target_pairs={{2,0},{4,2},{6,4},{8,6},{10,8},{12,10},{14,12},{16,14},{18,16},{20... | collective-permute-start | bytes 786440 | tf_op jit(solution)/shard_map/ppermute | solution.py:417
  35.5 12.0 %collective-permute-start.13 = (f32[160,256]{1,0:T(8,128)}, f32[160,256]{1,0:T(8,128)}, u32[]{:S(2)}, u32[]{:S(2)}) collective-permute-start(f32[160,256]{1,0:T(8,128)} %get-tuple-element.81), channel_id=1, source_target_pairs={{0,4},{2,6},{4,0},{6,2},{8,12},{10,14},{12,8},{14,10},{16,20},{18,... | collective-permute-start | bytes 491528 | tf_op jit(solution)/shard_map/ppermute | solution.py:400
  39.3 4.4 %copy-start.11 = (s32[2,2,2]{2,1,0:T(2,128)S(1)}, s32[2,2,2]{2,1,0:T(2,128)}, u32[]{:S(2)}) copy-start(s32[2,2,2]{2,1,0:T(2,128)} %copy-done.10) | copy-start | bytes 100
  39.3 12.4 %collective-permute-start.14 = (f32[160,256]{1,0:T(8,128)}, f32[160,256]{1,0:T(8,128)}, u32[]{:S(2)}, u32[]{:S(2)}) collective-permute-start(f32[160,256]{1,0:T(8,128)} %get-tuple-element.83), channel_id=1, source_target_pairs={{0,8},{2,10},{4,12},{6,14},{8,0},{10,2},{12,4},{14,6},{16,24},{18,... | collective-permute-start | bytes 491528 | tf_op jit(solution)/shard_map/ppermute | solution.py:400
  41.6 10.0 %collective-permute-start.15 = (f32[160,256]{1,0:T(8,128)}, f32[160,256]{1,0:T(8,128)}, u32[]{:S(2)}, u32[]{:S(2)}) collective-permute-start(f32[160,256]{1,0:T(8,128)} %get-tuple-element.82), channel_id=1, source_target_pairs={{0,12},{2,14},{4,8},{6,10},{8,4},{10,6},{12,0},{14,2},{16,28},{18,... | collective-permute-start | bytes 491528 | tf_op jit(solution)/shard_map/ppermute | solution.py:400
  47.0 11.7 %collective-permute-start.9 = (f32[2,256,256]{2,1,0:T(8,128)S(1)}, f32[2,256,256]{2,1,0:T(8,128)S(1)}, u32[]{:S(2)}, u32[]{:S(2)}) collective-permute-start(f32[2,256,256]{2,1,0:T(8,128)S(1)} %get-tuple-element.54.own), channel_id=1, source_target_pairs={{0,1},{1,0},{2,3},{3,2},{4,5},{5,4},{6,7},{7,6},{8,9},{9,8},{10,11... | collective-permute-start | bytes 1572872 | tf_op jit(solution)/shard_map/ppermute | solution.py:397
  47.0 11.7 %collective-permute-start.10 = (f32[2,128,256]{2,1,0:T(8,128)S(1)}, f32[2,128,256]{2,1,0:T(8,128)S(1)}, u32[]{:S(2)}, u32[]{:S(2)}) collective-permute-start(f32[2,128,256]{2,1,0:T(8,128)S(1)} %collective-permute-done.7.b0), channel_id=1, source_target_pairs={{0,1},{1,0},{2,3},{3,2},{4,5},{5,4},{6,7},{7,6},{8,9},{9,8},{10,11... | collective-permute-start | bytes 786440 | tf_op jit(solution)/shard_map/ppermute | solution.py:397
  47.6 11.2 %collective-permute-start.11 = (f32[2,128,256]{2,1,0:T(8,128)}, f32[2,128,256]{2,1,0:T(8,128)S(1)}, u32[]{:S(2)}, u32[]{:S(2)}) collective-permute-start(f32[2,128,256]{2,1,0:T(8,128)} %collective-permute-done.8.a0), channel_id=1, source_target_pairs={{0,1},{1,0},{2,3},{3,2},{4,5},{5,4},{6,7},{7,6},{8,9},{9,8},{10,11... | collective-permute-start | bytes 786440 | tf_op jit(solution)/shard_map/ppermute | solution.py:397
  52.8 14.0 %collective-permute-start.16 = (f32[160,256]{1,0:T(8,128)S(1)}, f32[160,256]{1,0:T(8,128)S(1)}, u32[]{:S(2)}, u32[]{:S(2)}) collective-permute-start(f32[160,256]{1,0:T(8,128)S(1)} %fusion.13), channel_id=1, source_target_pairs={{0,2},{2,0},{4,6},{6,4},{8,10},{10,8},{12,14},{14,12},{16,18},{18,... | collective-permute-start | bytes 491528 | tf_op jit(solution)/shard_map/ppermute | solution.py:400
  56.2 15.0 %collective-permute-start.17 = (f32[160,256]{1,0:T(8,128)S(1)}, f32[160,256]{1,0:T(8,128)S(1)}, u32[]{:S(2)}, u32[]{:S(2)}) collective-permute-start(f32[160,256]{1,0:T(8,128)S(1)} %fusion.13), channel_id=1, source_target_pairs={{0,16},{2,18},{4,20},{6,22},{8,24},{10,26},{12,28},{14,30},{16,0},... | collective-permute-start | bytes 491528 | tf_op jit(solution)/shard_map/ppermute | solution.py:400
  58.7 15.1 %collective-permute-start.18 = (f32[160,256]{1,0:T(8,128)S(1)}, f32[160,256]{1,0:T(8,128)S(1)}, u32[]{:S(2)}, u32[]{:S(2)}) collective-permute-start(f32[160,256]{1,0:T(8,128)S(1)} %fusion.13), channel_id=1, source_target_pairs={{0,18},{2,16},{4,22},{6,20},{8,26},{10,24},{12,30},{14,28},{16,2},... | collective-permute-start | bytes 491528 | tf_op jit(solution)/shard_map/ppermute | solution.py:400
  61.6 18.2 %collective-permute-start.19 = (f32[2,128,256]{2,1,0:T(8,128)S(1)}, f32[2,128,256]{2,1,0:T(8,128)S(1)}, u32[]{:S(2)}, u32[]{:S(2)}) collective-permute-start(f32[2,128,256]{2,1,0:T(8,128)S(1)} %get-tuple-element.60), channel_id=1, source_target_pairs={{0,2},{2,4},{4,6},{6,8},{8,10},{10,12},{12,14},{14,16},{16,18},{18... | collective-permute-start | bytes 786440 | tf_op jit(solution)/shard_map/ppermute | solution.py:414
  65.3 16.6 %collective-permute-start.20 = (f32[2,128,256]{2,1,0:T(8,128)S(1)}, f32[2,128,256]{2,1,0:T(8,128)S(1)}, u32[]{:S(2)}, u32[]{:S(2)}) collective-permute-start(f32[2,128,256]{2,1,0:T(8,128)S(1)} %get-tuple-element.61), channel_id=1, source_target_pairs={{2,0},{4,2},{6,4},{8,6},{10,8},{12,10},{14,12},{16,14},{18,16},{20... | collective-permute-start | bytes 786440 | tf_op jit(solution)/shard_map/ppermute | solution.py:417
  81.9 7.1 %collective-permute-start.21 = (f32[160,256]{1,0:T(8,128)S(1)}, f32[160,256]{1,0:T(8,128)S(1)}, u32[]{:S(2)}, u32[]{:S(2)}) collective-permute-start(f32[160,256]{1,0:T(8,128)S(1)} %add_add_fusion.1), channel_id=1, source_target_pairs={{0,4},{2,6},{4,0},{6,2},{8,12},{10,14},{12,8},{14,10},{16,20},{18,... | collective-permute-start | bytes 491528 | tf_op jit(solution)/shard_map/ppermute | solution.py:400
  82.0 7.1 %collective-permute-start.22 = (f32[160,256]{1,0:T(8,128)S(1)}, f32[160,256]{1,0:T(8,128)S(1)}, u32[]{:S(2)}, u32[]{:S(2)}) collective-permute-start(f32[160,256]{1,0:T(8,128)S(1)} %add_add_fusion.1), channel_id=1, source_target_pairs={{0,8},{2,10},{4,12},{6,14},{8,0},{10,2},{12,4},{14,6},{16,24},{18,... | collective-permute-start | bytes 491528 | tf_op jit(solution)/shard_map/ppermute | solution.py:400
  82.0 9.0 %collective-permute-start.23 = (f32[160,256]{1,0:T(8,128)S(1)}, f32[160,256]{1,0:T(8,128)S(1)}, u32[]{:S(2)}, u32[]{:S(2)}) collective-permute-start(f32[160,256]{1,0:T(8,128)S(1)} %add_add_fusion.1), channel_id=1, source_target_pairs={{0,12},{2,14},{4,8},{6,10},{8,4},{10,6},{12,0},{14,2},{16,28},{18,... | collective-permute-start | bytes 491528 | tf_op jit(solution)/shard_map/ppermute | solution.py:400
  91.0 2.2 %collective-permute-start.24 = (f32[4,160,256]{2,1,0:T(8,128)S(1)}, f32[4,160,256]{2,1,0:T(8,128)S(1)}, u32[]{:S(2)}, u32[]{:S(2)}) collective-permute-start(f32[4,160,256]{2,1,0:T(8,128)S(1)} %pad_maximum_fusion.own_totals), channel_id=1, source_target_pairs={{0,1},{1,0},{2,3},{3,2},{4,5},{5,4},{6,7},{7,6},{8,9},{9,8},{10,11... | collective-permute-start | bytes 1966088 | tf_op jit(solution)/shard_map/ppermute | solution.py:397
  98.4 2.2 %collective-permute-start.25 = (f32[4,160,256]{2,1,0:T(8,128)S(1)}, f32[4,160,256]{2,1,0:T(8,128)S(1)}, u32[]{:S(2)}, u32[]{:S(2)}) collective-permute-start(f32[4,160,256]{2,1,0:T(8,128)S(1)} %get-tuple-element.68), channel_id=1, source_target_pairs={{0,1},{1,0},{2,3},{3,2},{4,5},{5,4},{6,7},{7,6},{8,9},{9,8},{10,11... | collective-permute-start | bytes 1966088 | tf_op jit(solution)/shard_map/ppermute | solution.py:397
  100.6 8.9 %collective-permute-start.26 = (f32[160,256]{1,0:T(8,128)S(1)}, f32[160,256]{1,0:T(8,128)S(1)}, u32[]{:S(2)}, u32[]{:S(2)}) collective-permute-start(f32[160,256]{1,0:T(8,128)S(1)} %get-tuple-element.78), channel_id=1, source_target_pairs={{0,4},{2,6},{4,0},{6,2},{8,12},{10,14},{12,8},{14,10},{16,20},{18,... | collective-permute-start | bytes 491528 | tf_op jit(solution)/shard_map/ppermute | solution.py:400
  101.0 8.5 %collective-permute-start.27 = (f32[160,256]{1,0:T(8,128)S(1)}, f32[160,256]{1,0:T(8,128)S(1)}, u32[]{:S(2)}, u32[]{:S(2)}) collective-permute-start(f32[160,256]{1,0:T(8,128)S(1)} %get-tuple-element.80), channel_id=1, source_target_pairs={{0,8},{2,10},{4,12},{6,14},{8,0},{10,2},{12,4},{14,6},{16,24},{18,... | collective-permute-start | bytes 491528 | tf_op jit(solution)/shard_map/ppermute | solution.py:400
  102.0 9.6 %collective-permute-start.28 = (f32[160,256]{1,0:T(8,128)S(1)}, f32[160,256]{1,0:T(8,128)S(1)}, u32[]{:S(2)}, u32[]{:S(2)}) collective-permute-start(f32[160,256]{1,0:T(8,128)S(1)} %get-tuple-element.79), channel_id=1, source_target_pairs={{0,12},{2,14},{4,8},{6,10},{8,4},{10,6},{12,0},{14,2},{16,28},{18,... | collective-permute-start | bytes 491528 | tf_op jit(solution)/shard_map/ppermute | solution.py:400
  104.2 16.4 %collective-permute-start.35 = (f32[2,128,256]{2,1,0:T(8,128)S(1)}, f32[2,128,256]{2,1,0:T(8,128)S(1)}, u32[]{:S(2)}, u32[]{:S(2)}) collective-permute-start(f32[2,128,256]{2,1,0:T(8,128)S(1)} %get-tuple-element.70), channel_id=1, source_target_pairs={{0,2},{2,4},{4,6},{6,8},{8,10},{10,12},{12,14},{14,16},{16,18},{18... | collective-permute-start | bytes 786440 | tf_op jit(solution)/shard_map/ppermute | solution.py:414
  108.2 14.7 %collective-permute-start.36 = (f32[2,128,256]{2,1,0:T(8,128)S(1)}, f32[2,128,256]{2,1,0:T(8,128)S(1)}, u32[]{:S(2)}, u32[]{:S(2)}) collective-permute-start(f32[2,128,256]{2,1,0:T(8,128)S(1)} %get-tuple-element.71), channel_id=1, source_target_pairs={{2,0},{4,2},{6,4},{8,6},{10,8},{12,10},{14,12},{16,14},{18,16},{20... | collective-permute-start | bytes 786440 | tf_op jit(solution)/shard_map/ppermute | solution.py:417
  111.7 13.5 %collective-permute-start.29 = (f32[160,256]{1,0:T(8,128)S(1)}, f32[160,256]{1,0:T(8,128)S(1)}, u32[]{:S(2)}, u32[]{:S(2)}) collective-permute-start(f32[160,256]{1,0:T(8,128)S(1)} %fusion.6), channel_id=1, source_target_pairs={{0,2},{2,0},{4,6},{6,4},{8,10},{10,8},{12,14},{14,12},{16,18},{18,... | collective-permute-start | bytes 491528 | tf_op jit(solution)/shard_map/ppermute | solution.py:400
  113.8 17.7 %collective-permute-start.30 = (f32[160,256]{1,0:T(8,128)S(1)}, f32[160,256]{1,0:T(8,128)S(1)}, u32[]{:S(2)}, u32[]{:S(2)}) collective-permute-start(f32[160,256]{1,0:T(8,128)S(1)} %fusion.6), channel_id=1, source_target_pairs={{0,16},{2,18},{4,20},{6,22},{8,24},{10,26},{12,28},{14,30},{16,0},... | collective-permute-start | bytes 491528 | tf_op jit(solution)/shard_map/ppermute | solution.py:400
  115.8 15.8 %collective-permute-start.31 = (f32[160,256]{1,0:T(8,128)S(1)}, f32[160,256]{1,0:T(8,128)S(1)}, u32[]{:S(2)}, u32[]{:S(2)}) collective-permute-start(f32[160,256]{1,0:T(8,128)S(1)} %fusion.6), channel_id=1, source_target_pairs={{0,18},{2,16},{4,22},{6,20},{8,26},{10,24},{12,30},{14,28},{16,2},... | collective-permute-start | bytes 491528 | tf_op jit(solution)/shard_map/ppermute | solution.py:400
  122.9 12.3 %collective-permute-start.37 = (f32[2,256,256]{2,1,0:T(8,128)S(1)}, f32[2,256,256]{2,1,0:T(8,128)S(1)}, u32[]{:S(2)}, u32[]{:S(2)}) collective-permute-start(f32[2,256,256]{2,1,0:T(8,128)S(1)} %get-tuple-element.73.own), channel_id=1, source_target_pairs={{0,1},{1,0},{2,3},{3,2},{4,5},{5,4},{6,7},{7,6},{8,9},{9,8},{10,11... | collective-permute-start | bytes 1572872 | tf_op jit(solution)/shard_map/ppermute | solution.py:397
  122.9 8.9 %collective-permute-start.38 = (f32[2,128,256]{2,1,0:T(8,128)S(1)}, f32[2,128,256]{2,1,0:T(8,128)S(1)}, u32[]{:S(2)}, u32[]{:S(2)}) collective-permute-start(f32[2,128,256]{2,1,0:T(8,128)S(1)} %collective-permute-done.35.b0), channel_id=1, source_target_pairs={{0,1},{1,0},{2,3},{3,2},{4,5},{5,4},{6,7},{7,6},{8,9},{9,8},{10,11... | collective-permute-start | bytes 786440 | tf_op jit(solution)/shard_map/ppermute | solution.py:397
  125.2 10.0 %collective-permute-start.39 = (f32[2,128,256]{2,1,0:T(8,128)S(1)}, f32[2,128,256]{2,1,0:T(8,128)S(1)}, u32[]{:S(2)}, u32[]{:S(2)}) collective-permute-start(f32[2,128,256]{2,1,0:T(8,128)S(1)} %collective-permute-done.36.a0), channel_id=1, source_target_pairs={{0,1},{1,0},{2,3},{3,2},{4,5},{5,4},{6,7},{7,6},{8,9},{9,8},{10,11... | collective-permute-start | bytes 786440 | tf_op jit(solution)/shard_map/ppermute | solution.py:397
  131.6 6.9 %collective-permute-start.32 = (f32[160,256]{1,0:T(8,128)S(1)}, f32[160,256]{1,0:T(8,128)S(1)}, u32[]{:S(2)}, u32[]{:S(2)}) collective-permute-start(f32[160,256]{1,0:T(8,128)S(1)} %add_add_fusion), channel_id=1, source_target_pairs={{0,4},{2,6},{4,0},{6,2},{8,12},{10,14},{12,8},{14,10},{16,20},{18,... | collective-permute-start | bytes 491528 | tf_op jit(solution)/shard_map/ppermute | solution.py:400
  131.8 6.8 %collective-permute-start.33 = (f32[160,256]{1,0:T(8,128)S(1)}, f32[160,256]{1,0:T(8,128)S(1)}, u32[]{:S(2)}, u32[]{:S(2)}) collective-permute-start(f32[160,256]{1,0:T(8,128)S(1)} %add_add_fusion), channel_id=1, source_target_pairs={{0,8},{2,10},{4,12},{6,14},{8,0},{10,2},{12,4},{14,6},{16,24},{18,... | collective-permute-start | bytes 491528 | tf_op jit(solution)/shard_map/ppermute | solution.py:400
  131.8 8.5 %collective-permute-start.34 = (f32[160,256]{1,0:T(8,128)S(1)}, f32[160,256]{1,0:T(8,128)S(1)}, u32[]{:S(2)}, u32[]{:S(2)}) collective-permute-start(f32[160,256]{1,0:T(8,128)S(1)} %add_add_fusion), channel_id=1, source_target_pairs={{0,12},{2,14},{4,8},{6,10},{8,4},{10,6},{12,0},{14,2},{16,28},{18,... | collective-permute-start | bytes 491528 | tf_op jit(solution)/shard_map/ppermute | solution.py:400
  140.4 1.4 collective-permute-start.40
  (6 other events, 7.3 us)
